TPU v7x, 32 devices: a whole 2x2x4 slice. The times are simulated.
32 devices in a mesh: seq: 8 (over z, y), head: 4 (over x, core).
Axes of the slice: x: 2, y: 2, z: 4, core: 2. Of those that a mesh axis runs over, the one named last changes fastest.
Arguments:
- hidden_in: bfloat16 [2048, 2304], P(('seq', 'head')), may hold values from -6 to 6
- qkv_weight: bfloat16 [2304, 3, 2048], P(None, None, 'head'), may hold values from -0.125 to 0.125
- conv_weight: bfloat16 [3, 4, 2048], P(None, None, 'head'), may hold values from -3 to 3
- decay_log: float32 [16], P('head'), may hold values from -9 to -3
- dt_bias: float32 [2048], P('head'), may hold values from -3 to 3
- decay_down: bfloat16 [2304, 128], replicated, may hold values from -0.125 to 0.125
- decay_up: bfloat16 [128, 2048], P(None, 'head'), may hold values from -0.5 to 0.5
- beta_weight: bfloat16 [2304, 16], P(None, 'head'), may hold values from -0.125 to 0.125
- gate_down: bfloat16 [2304, 128], replicated, may hold values from -0.125 to 0.125
- gate_up: bfloat16 [128, 2048], P(None, 'head'), may hold values from -0.5 to 0.5
- norm_gain: float32 [128], replicated, may hold values from 0.1 to 1.9
- out_weight: bfloat16 [2048, 2304], P('head'), may hold values from -0.125 to 0.125
Outputs:
- layer_out: bfloat16 [2048, 2304], P(('seq', 'head'))
All inputs are finite; a program needn't handle non-finite values.
Results may differ from a plain program's by a relative error of at most 0.015.
Values may be sent and summed in bfloat16 or wider, within the bound.
No kernel may reach another device: no remote copies, remote signals or barrier semaphores. Data moves between devices by JAX's collectives and lax.ppermute only.
A program may use at most 128 MiB of HBM per device.

v0:
```python
import math

import jax
import jax.numpy as jnp
from jax import lax
from jax.sharding import PartitionSpec as P

exact_precision = lax.Precision.HIGHEST


def passed_along(block, axis, distance):
    devices = range(lax.axis_size(axis))
    route = [(i - distance, i) for i in devices if i - distance in devices]
    return lax.ppermute(block, axis, route)


def entering(value, axis, combine, identity):
    devices, here = (lax.axis_size(axis), lax.axis_index(axis))
    everything = jax.tree.map(
        lambda part, kind: lax.all_gather(part.astype(kind), axis),
        value,
        jax.tree.map(lambda a: jnp.bfloat16 if a.dtype == jnp.float32 else a.dtype, value),
    )
    start = jax.tree.map(
        lambda part, zero: jnp.broadcast_to(jnp.asarray(zero, part.dtype), part.shape),
        value,
        identity,
    )

    def turn(k, before):
        reached = k < here
        new = combine(
            before, jax.tree.map(lambda part, own: part[k].astype(own.dtype), everything, value)
        )
        return jax.tree.map(lambda a, b: jnp.where(reached, a, b), new, before)

    return lax.fori_loop(0, devices, turn, start)


def l2_normalize(values):
    return values * lax.rsqrt(jnp.sum(values * values, axis=-1, keepdims=True) + 1e-06)


def product(left, right):
    return jnp.einsum("hij,hjk->hik", left, right, precision=exact_precision)


def compose(earlier, later):
    first_map, first_shift = earlier
    second_map, second_shift = later
    return (product(second_map, first_map), product(second_map, first_shift) + second_shift)


def compose_single(earlier, later):
    first_map, first_shift = earlier
    second_map, second_shift = later
    return (
        jnp.dot(second_map, first_map, precision=exact_precision),
        jnp.dot(second_map, first_shift, precision=exact_precision) + second_shift,
    )


def block_terms(queries, key_rows, value_rows, log_decay, strength):
    row_count = key_rows.shape[1]
    head_size = key_rows.shape[2]
    cumulative = jnp.cumsum(log_decay, axis=1)
    middle = cumulative[:, row_count // 2 : row_count // 2 + 1]
    block_end = cumulative[:, row_count - 1 :]
    key_rise = key_rows * jnp.exp(cumulative - middle)
    key_fall = key_rows * jnp.exp(middle - cumulative)
    query_rise = queries * jnp.exp(cumulative - middle)
    positions = jnp.arange(row_count)
    strict_lower = positions[:, None] > positions[None, :]
    inclusive = positions[:, None] >= positions[None, :]
    key_mixing = jnp.where(
        strict_lower,
        jnp.einsum("htk,hjk->htj", key_rise, key_fall, precision=exact_precision)
        * strength[:, None, :],
        0.0,
    )
    attend = jnp.where(
        inclusive,
        jnp.einsum("htk,hjk->htj", query_rise, key_fall, precision=exact_precision)
        * strength[:, None, :],
        0.0,
    )
    nilpotent = -key_mixing
    inverse = jnp.eye(row_count, dtype=jnp.float32)[None] + nilpotent
    for _ in range(1, (row_count - 1).bit_length()):
        nilpotent = product(nilpotent, nilpotent)
        inverse = inverse + product(inverse, nilpotent)
    key_start = key_rows * jnp.exp(cumulative)
    query_start = queries * jnp.exp(cumulative)
    state_correction = product(inverse, value_rows)
    erasure = product(inverse, key_start)
    output_rows = product(attend, state_correction)
    raised_tensor = query_start - product(attend, erasure)
    key_stop_index = key_rows * jnp.exp(block_end - cumulative) * strength[:, :, None]
    eye_keys = jnp.eye(head_size, dtype=jnp.float32)
    transition = jnp.exp(block_end[:, 0])[:, :, None] * eye_keys[None] - jnp.einsum(
        "hjk,hjl->hkl", key_stop_index, erasure, precision=exact_precision
    )
    position_shift = jnp.einsum(
        "xpd,xpb->xdb", key_stop_index, state_correction, precision=exact_precision
    )
    return (output_rows, raised_tensor, transition, position_shift)


def recur(query_in, key_in, value_in, log_decay, strength, entry_state):
    row_count, head_count, head_size = key_in.shape
    queries = l2_normalize(query_in.astype(jnp.float32)) * head_size ** (-0.5)
    key_rows = l2_normalize(key_in.astype(jnp.float32))
    value_rows = value_in.astype(jnp.float32)
    block_len = math.gcd(row_count, 64)
    block_count = row_count // block_len

    def to_blocks(values):
        return values.reshape(block_count, block_len, head_count, -1).transpose(0, 2, 1, 3)

    strength_blocks = strength.reshape(block_count, block_len, head_count).transpose(0, 2, 1)
    eye_keys = jnp.eye(head_size, dtype=jnp.float32)
    neutral = (
        jnp.broadcast_to(eye_keys, (head_count, head_size, head_size)),
        jnp.zeros((head_count, head_size, head_size), jnp.float32),
    )

    def advance(carry, inputs):
        so_far_map, so_far_shift = carry
        output_rows, raised_tensor, transition, position_shift = block_terms(*inputs)
        output_rows = output_rows + product(raised_tensor, so_far_shift)
        raised_tensor = product(raised_tensor, so_far_map)
        return (compose(carry, (transition, position_shift)), (output_rows, raised_tensor))

    whole_pair, stacked = lax.scan(
        advance,
        neutral,
        (
            to_blocks(queries),
            to_blocks(key_rows),
            to_blocks(value_rows),
            to_blocks(log_decay),
            strength_blocks,
        ),
    )
    output_rows, raised_tensor = stacked
    incoming_state = entry_state(whole_pair)
    output_rows = output_rows + jnp.einsum(
        "owfp,wpc->owfc", raised_tensor, incoming_state, precision=exact_precision
    )
    return output_rows.transpose(0, 2, 1, 3).reshape(row_count, head_count, -1)


def shards(
    hidden_in,
    qkv_weight,
    conv_weight,
    decay_log,
    dt_bias,
    decay_down,
    decay_up,
    beta_weight,
    gate_down,
    gate_up,
    norm_gain,
    out_weight,
):
    gathered = lax.all_gather(hidden_in, "head", axis=0, tiled=True)
    row_count = gathered.shape[0]
    head_count = decay_log.shape[0]
    head_size = norm_gain.shape[0]
    full_width = head_count * head_size
    tap_count = conv_weight.shape[1]
    projected = jnp.dot(
        gathered,
        qkv_weight.reshape(qkv_weight.shape[0], 3 * full_width),
        preferred_element_type=jnp.float32,
    ).astype(jnp.bfloat16)
    projected = projected.reshape(row_count, 3, full_width)
    rim_rows = passed_along(projected[row_count - (tap_count - 1) :], "seq", 1)
    padded = jnp.concatenate([rim_rows, projected], axis=0).astype(jnp.float32)
    taps = conv_weight.astype(jnp.float32)
    convolved = jnp.zeros((row_count, 3, full_width), jnp.float32)
    for tap_index in range(tap_count):
        convolved = convolved + padded[tap_index : tap_index + row_count] * taps[:, tap_index][None]
    convolved = jax.nn.silu(convolved).astype(jnp.bfloat16)
    query_in = convolved[:, 0].reshape(row_count, head_count, head_size)
    key_in = convolved[:, 1].reshape(row_count, head_count, head_size)
    value_in = convolved[:, 2].reshape(row_count, head_count, head_size)
    decay_low = jnp.dot(gathered, decay_down, preferred_element_type=jnp.float32).astype(
        jnp.bfloat16
    )
    raw_decay = jnp.dot(decay_low, decay_up, preferred_element_type=jnp.float32) + dt_bias
    log_decay = -jnp.exp(decay_log)[None, :, None] * jax.nn.softplus(raw_decay).reshape(
        row_count, head_count, head_size
    )
    strength = jax.nn.sigmoid(jnp.dot(gathered, beta_weight, preferred_element_type=jnp.float32))
    gate_low = jnp.dot(gathered, gate_down, preferred_element_type=jnp.float32).astype(jnp.bfloat16)
    out_gate = jax.nn.sigmoid(
        jnp.dot(gate_low, gate_up, preferred_element_type=jnp.float32)
    ).reshape(row_count, head_count, head_size)
    eye_single = jnp.eye(head_size, dtype=jnp.float32)
    zero_single = jnp.zeros((head_size, head_size), jnp.float32)

    def block_single(single_pair):
        return entering(single_pair, "seq", compose_single, (eye_single, zero_single))[1]

    def block_entry(transfer_pair):
        return lax.map(block_single, transfer_pair)

    attended = recur(query_in, key_in, value_in, log_decay, strength, block_entry)
    inverse_rms = lax.rsqrt(jnp.mean(attended * attended, axis=-1, keepdims=True) + 1e-05)
    normed = (
        (attended * inverse_rms * norm_gain * out_gate)
        .astype(jnp.bfloat16)
        .reshape(row_count, full_width)
    )
    own_rows = lax.all_to_all(normed, "head", split_axis=0, concat_axis=1, tiled=True)
    summed = jnp.dot(
        own_rows,
        lax.all_gather(out_weight, "head", axis=0, tiled=True),
        preferred_element_type=jnp.float32,
    )
    return summed.astype(jnp.bfloat16)


def solution(mesh):
    return jax.shard_map(
        shards,
        mesh=mesh,
        in_specs=(
            P(("seq", "head"), None),
            P(None, None, "head"),
            P(None, None, "head"),
            P("head"),
            P("head"),
            P(),
            P(None, "head"),
            P(None, "head"),
            P(),
            P(None, "head"),
            P(),
            P("head", None),
        ),
        out_specs=P(("seq", "head"), None),
        check_vma=False,
    )
```

profile of v0, /device:TPU:0, one launch (start us, length us, event | category | flops | bytes accessed | tf_op | source)
XLA Modules:
  0.0 381.9 jit_solution(17871264039645350192)
XLA Ops:
  6.5 0.7 all-gather.3.cloned.1.call-update
  7.3 0.7 all-gather.5.cloned.1.call-update
  8.1 9.7 %copy.35 = bf16[2304,3,512]{0,2,1:T(8,128)(2,1)} copy(bf16[2304,3,512]{2,0,1:T(8,128)(2,1)} %param.19) | data formatting | bytes 14155776 | tf_op args[1]
  17.9 11.2 %all-gather.3.cloned.1.call-done = bf16[256,2304]{1,0:T(8,128)(2,1)} async-done(((bf16[64,2304]{1,0:T(8,128)(2,1)}), bf16[256,2304]{1,0:T(8,128)(2,1)}) %all-gather.3.cloned.1.call-update) | async-done | bytes 1179664 | tf_op jit(solution)/shard_map/all_gather | solution.py:167
  29.1 5.5 %convolution_convert_fusion.1 = bf16[256,1536]{1,0:T(8,128)(2,1)S(1)} fusion(bf16[256,2304]{1,0:T(8,128)(2,1)} %all-gather.3.cloned.1.call-done, bf16[2304,1536]{0,1:T(8,128)(2,1)} %bitcast.266), kind=kOutput, calls=%fused_computation.67 | convolution fusion | flops 1812332544 | bytes 9043968 | tf_op jit(solution)/shard_map/dot_general | solution.py:173
  34.6 1.0 copy.53
  35.6 4.3 %collective-permute-start = (bf16[3,3,512]{0,2,1:T(8,128)(2,1)}, bf16[3,3,512]{0,2,1:T(8,128)(2,1)}, u32[]{:S(2)}, u32[]{:S(2)}) collective-permute-start(bf16[3,3,512]{0,2,1:T(8,128)(2,1)} %bitcast.3), channel_id=1, source_target_pairs={{0,4},{4,8},{8,12},{12,16},{16,20},{20,24},{24,28},{1,5},{5,9},{9,... | collective-permute-start | bytes 27656 | tf_op jit(solution)/shard_map/ppermute | solution.py:14
  39.9 1.6 compare_select_fusion
  41.5 1.4 reshape.118
  43.3 1.0 fusion.49
  44.7 3.5 collective-permute-done
  48.2 1.5 maximum_convert_fusion
  49.7 2.6 multiply_convert_fusion
  52.3 0.9 slice_convert_fusion
  53.8 0.8 copy.55
  54.5 1.2 copy.38
  57.6 39.7 %while.43 = (s32[]{:T(128)}, f32[4,128,128]{2,1,0:T(8,128)S(1)}, f32[4,128,128]{2,1,0:T(8,128)S(1)}, f32[4,4,64,128]{3,2,0,1:T(8,128)}, f32[4,4,64,128]{3,2,0,1:...) while((s32[]{:T(128)}, f32[4,128,128]{2,1,0:T(8,128)S(1)}, ...), condition=%wide.region_4.5_spmd.clone, body=%wide.region_2.4_spmd.clone.sunk | while | flops 682688512 | bytes 10499228 | solution.py:134
  57.6 0.9 dynamic-slice_bitcast_fusion.4
  63.3 1.1 fusion.222
  64.3 0.7 convolution_subtract_fusion.4
  65.1 0.4 fusion.218
  65.5 0.7 convolution_add_fusion.20
  66.2 1.0 fusion.223
  67.2 0.4 fusion.217
  67.6 0.9 dynamic-slice_bitcast_fusion.4
  73.2 1.0 fusion.222
  74.3 0.7 convolution_subtract_fusion.4
  75.0 0.4 fusion.218
  75.4 0.7 convolution_add_fusion.20
  76.1 1.0 fusion.223
  77.5 0.9 dynamic-slice_bitcast_fusion.4
  83.2 1.0 fusion.222
  84.2 0.7 convolution_subtract_fusion.4
  84.9 0.4 fusion.218
  85.3 0.7 convolution_add_fusion.20
  86.0 1.0 fusion.223
  87.0 0.4 fusion.217
  87.4 0.9 dynamic-slice_bitcast_fusion.4
  93.1 1.0 fusion.222
  94.1 0.7 convolution_subtract_fusion.4
  94.8 0.4 fusion.218
  95.2 0.7 convolution_add_fusion.20
  95.9 1.0 fusion.223
  97.4 258.5 %while.42 = (s32[]{:T(128)}, f32[4,128,128]{2,1,0:T(8,128)}, bf16[4,128,128]{2,1,0:T(8,128)(2,1)S(1)}, bf16[4,128,128]{2,1,0:T(8,128)(2,1)S(1)}, s32[]{:T(128)},...) while((s32[]{:T(128)}, f32[4,128,128]{2,1,0:T(8,128)}, bf16[4,128,128]{2,1,0:T(8,128)(2,1)S(1)}, ...), condition=%wide.region_8.9_spmd, body=%wide.region_5.8_spmd.sunk | while | flops 25247752 | bytes 1248556 | solution.py:208
  97.5 32.9 %all_gather.18 = bf16[8,128,128]{2,1,0:T(8,128)(2,1)S(1)} all-gather(bf16[1,128,128]{2,1,0:T(8,128)(2,1)S(1)} %dynamic-slice_convert_fusion.4), channel_id=1, replica_groups=mesh['seq'=8,'head'=4] {'seq'}, dimensions={0}, use_global_device_ids=true | all-gather | bytes 294912 | tf_op jit(solution)/shard_map/while/body/eval_jaxpr/all_gather | solution.py:20
  130.4 30.9 %all_gather.19 = bf16[8,128,128]{2,1,0:T(8,128)(2,1)S(1)} all-gather(bf16[1,128,128]{2,1,0:T(8,128)(2,1)S(1)} %dynamic-slice_convert_fusion.5), channel_id=1, replica_groups=mesh['seq'=8,'head'=4] {'seq'}, dimensions={0}, use_global_device_ids=true | all-gather | bytes 294912 | tf_op jit(solution)/shard_map/while/body/eval_jaxpr/all_gather | solution.py:20
  161.3 1.8 while.44
  163.1 0.6 bitcast_dynamic-update-slice_fusion.2
  163.8 30.8 %all_gather.18 = bf16[8,128,128]{2,1,0:T(8,128)(2,1)S(1)} all-gather(bf16[1,128,128]{2,1,0:T(8,128)(2,1)S(1)} %dynamic-slice_convert_fusion.4), channel_id=1, replica_groups=mesh['seq'=8,'head'=4] {'seq'}, dimensions={0}, use_global_device_ids=true | all-gather | bytes 294912 | tf_op jit(solution)/shard_map/while/body/eval_jaxpr/all_gather | solution.py:20
  194.6 30.7 %all_gather.19 = bf16[8,128,128]{2,1,0:T(8,128)(2,1)S(1)} all-gather(bf16[1,128,128]{2,1,0:T(8,128)(2,1)S(1)} %dynamic-slice_convert_fusion.5), channel_id=1, replica_groups=mesh['seq'=8,'head'=4] {'seq'}, dimensions={0}, use_global_device_ids=true | all-gather | bytes 294912 | tf_op jit(solution)/shard_map/while/body/eval_jaxpr/all_gather | solution.py:20
  225.4 1.8 while.44
  227.2 0.6 bitcast_dynamic-update-slice_fusion.2
  227.9 30.8 %all_gather.18 = bf16[8,128,128]{2,1,0:T(8,128)(2,1)S(1)} all-gather(bf16[1,128,128]{2,1,0:T(8,128)(2,1)S(1)} %dynamic-slice_convert_fusion.4), channel_id=1, replica_groups=mesh['seq'=8,'head'=4] {'seq'}, dimensions={0}, use_global_device_ids=true | all-gather | bytes 294912 | tf_op jit(solution)/shard_map/while/body/eval_jaxpr/all_gather | solution.py:20
  258.7 30.8 %all_gather.19 = bf16[8,128,128]{2,1,0:T(8,128)(2,1)S(1)} all-gather(bf16[1,128,128]{2,1,0:T(8,128)(2,1)S(1)} %dynamic-slice_convert_fusion.5), channel_id=1, replica_groups=mesh['seq'=8,'head'=4] {'seq'}, dimensions={0}, use_global_device_ids=true | all-gather | bytes 294912 | tf_op jit(solution)/shard_map/while/body/eval_jaxpr/all_gather | solution.py:20
  289.5 1.8 while.44
  291.4 0.6 bitcast_dynamic-update-slice_fusion.2
  292.0 30.7 %all_gather.18 = bf16[8,128,128]{2,1,0:T(8,128)(2,1)S(1)} all-gather(bf16[1,128,128]{2,1,0:T(8,128)(2,1)S(1)} %dynamic-slice_convert_fusion.4), channel_id=1, replica_groups=mesh['seq'=8,'head'=4] {'seq'}, dimensions={0}, use_global_device_ids=true | all-gather | bytes 294912 | tf_op jit(solution)/shard_map/while/body/eval_jaxpr/all_gather | solution.py:20
  322.7 30.7 %all_gather.19 = bf16[8,128,128]{2,1,0:T(8,128)(2,1)S(1)} all-gather(bf16[1,128,128]{2,1,0:T(8,128)(2,1)S(1)} %dynamic-slice_convert_fusion.5), channel_id=1, replica_groups=mesh['seq'=8,'head'=4] {'seq'}, dimensions={0}, use_global_device_ids=true | all-gather | bytes 294912 | tf_op jit(solution)/shard_map/while/body/eval_jaxpr/all_gather | solution.py:20
  353.5 1.8 while.44
  355.3 0.6 bitcast_dynamic-update-slice_fusion.2
  356.0 1.9 multiply_reduce_fusion
  358.7 1.8 fusion.44
  360.5 8.4 %all_to_all.19 = bf16[4,64,512]{2,1,0:T(8,128)(2,1)S(1)} all-to-all(bf16[4,64,512]{2,1,0:T(8,128)(2,1)S(1)} %bitcast.283), channel_id=1, replica_groups=mesh['seq'=8,'head'=4] {'head'}, dimensions={0} | all-to-all | bytes 524288 | tf_op jit(solution)/shard_map/all_to_all | solution.py:217
  369.0 6.1 %convolution_convert_fusion = bf16[64,2304]{1,0:T(8,128)(2,1)} fusion(bf16[64,2048]{1,0:T(8,128)(2,1)S(1)} %bitcast.271, bf16[2048,2304]{1,0:T(8,128)(2,1)} %all-gather.5.cloned.1.call-done), kind=kOutput, calls=%fused_computation.66 | convolution fusion | flops 604127232 | bytes 9994240 | tf_op jit(solution)/shard_map/dot_general | solution.py:218
  (249 shorter events, 29.4 us)
Async XLA Ops:
  6.5 33.4 %copy-start = (bf16[2304,128]{1,0:T(8,128)(2,1)S(1)}, bf16[2304,128]{1,0:T(8,128)(2,1)}, u32[]{:S(2)}) copy-start(bf16[2304,128]{1,0:T(8,128)(2,1)} %param.23) | copy-start | bytes 1769476
  6.5 22.6 %all-gather.3.cloned.1.call-start = ((), (), s32[]{:S(2)}) async-start(), calls=%async_computation.1 | async-start | bytes 1474560 | tf_op jit(solution)/shard_map/all_gather | solution.py:167
  7.3 361.7 %all-gather.5.cloned.1.call-start = ((), (), s32[]{:S(2)}) async-start(), calls=%async_computation.2 | async-start | bytes 11796480 | tf_op jit(solution)/shard_map/all_gather | solution.py:220
  8.1 9.8 %copy-start.5 = (bf16[3,4,512]{2,1,0:T(4,128)(2,1)S(1)}, bf16[3,4,512]{2,1,0:T(4,128)(2,1)}, u32[]{:S(2)}) copy-start(bf16[3,4,512]{2,1,0:T(4,128)(2,1)} %param.20) | copy-start | bytes 36868
  8.1 9.8 %copy-start.11 = (f32[4]{0:T(128)S(1)}, f32[4]{0:T(128)}, u32[]{:S(2)}) copy-start(f32[4]{0:T(128)} %param.21) | copy-start | bytes 52
  8.1 9.8 %copy-start.7 = (f32[128]{0:T(128)S(1)}, f32[128]{0:T(128)}, u32[]{:S(2)}) copy-start(f32[128]{0:T(128)} %param.28) | copy-start | bytes 1540
  29.1 10.8 %copy-start.1 = (bf16[256,2304]{1,0:T(8,128)(2,1)S(1)}, bf16[256,2304]{1,0:T(8,128)(2,1)}, u32[]{:S(2)}) copy-start(bf16[256,2304]{1,0:T(8,128)(2,1)} %all-gather.3.cloned.1.call-done) | copy-start | bytes 3538948
  29.1 10.8 %copy-start.8 = (bf16[128,512]{1,0:T(8,128)(2,1)S(1)}, bf16[128,512]{1,0:T(8,128)(2,1)}, u32[]{:S(2)}) copy-start(bf16[128,512]{1,0:T(8,128)(2,1)} %param.24) | copy-start | bytes 393220
  29.1 10.8 %copy-start.10 = (f32[512]{0:T(512)S(1)}, f32[512]{0:T(512)}, u32[]{:S(2)}) copy-start(f32[512]{0:T(512)} %param.22) | copy-start | bytes 6148
  35.6 7.3 %copy-start.6 = (bf16[2304,4]{0,1:T(4,128)(2,1)S(1)}, bf16[2304,4]{0,1:T(4,128)(2,1)}, u32[]{:S(2)}) copy-start(bf16[2304,4]{0,1:T(4,128)(2,1)} %param.25) | copy-start | bytes 55300
  35.6 12.6 %collective-permute-start = (bf16[3,3,512]{0,2,1:T(8,128)(2,1)}, bf16[3,3,512]{0,2,1:T(8,128)(2,1)}, u32[]{:S(2)}, u32[]{:S(2)}) collective-permute-start(bf16[3,3,512]{0,2,1:T(8,128)(2,1)} %bitcast.3), channel_id=1, source_target_pairs={{0,4},{4,8},{8,12},{12,16},{16,20},{20,24},{24,28},{1,5},{5,9},{9,... | collective-permute-start | bytes 27656 | tf_op jit(solution)/shard_map/ppermute | solution.py:14
  56.0 0.9 copy-start.4
  97.4 258.5 %copy-start.3 = (f32[4,4,64,128]{3,2,0,1:T(8,128)S(1)}, f32[4,4,64,128]{3,2,0,1:T(8,128)}, u32[]{:S(2)}) copy-start(f32[4,4,64,128]{3,2,0,1:T(8,128)} %get-tuple-element.176) | copy-start | bytes 1572868
  356.0 2.8 copy-start.2
  356.0 2.8 copy-start.9
Sparse Core Ops, SparseCore 0:
  8.9 20.1 all-gather.2
  30.7 64.2 all-gather.4
where the time goes:
time: 383 us; the launch traced here: 382 us
  blocking collectives  257 us (67%)
  matrix products  57.4 us (15%)
  local copies, waits for them, and re-layouts  23.6 us (6%)
  waiting for transfers between devices  16.1 us (4%)
  between operations  13.8 us (4%)
  other arithmetic  7.67 us (2%)
  starting transfers between devices  4.33 us (1%)
    all_gather x8, blocking collectives, entering(): lax.all_gather(part.astype(kind), axis)  248 us
    dot_general x72, matrix products, product(): return jnp.einsum('hij,hjk->hik', left, right, precision=exact_precision)  25.7 us
    all_gather x1, waiting for transfers between devices, shards(): gathered = lax.all_gather(hidden_in, 'head', axis=0, tiled=True)  11.2 us
    unnamed x27, local copies, waits for them, and re-layouts  10.1 us
    all_to_all x1, blocking collectives, shards(): lax.all_to_all(normed, 'head', split_axis=0, concat_axis=1, tiled=True)  8.42 us
  transfers between devices with their start and end apart: 3, of which 2 were waited for; matrix products, arithmetic and copies ran while one was open for 22% of the time, Pallas kernels for 0%

commit v1 on v0

v1 whole, which is shorter than its diff:
```python
import functools
import math

import jax
import jax.numpy as jnp
from jax import lax
from jax.experimental import pallas as pl
from jax.experimental.pallas import tpu as pltpu
from jax.sharding import PartitionSpec as P

RIM = 16
BASE = 16
VMEM_LIMIT = 40 * 1024 * 1024
f32 = jnp.float32
bf16 = jnp.bfloat16


def dot(left, right, contract=((1,), (0,))):
    return lax.dot_general(left, right, (contract, ((), ())), preferred_element_type=f32)


def passed_along(block, axis, distance):
    size = lax.axis_size(axis)
    return lax.ppermute(block, axis, [(i, i + distance) for i in range(size - distance)])


def swapped(block, axis, bit):
    return lax.ppermute(block, axis, [(i, i ^ bit) for i in range(lax.axis_size(axis))])


def bits_of(size):
    assert size & (size - 1) == 0
    return [1 << i for i in range(size.bit_length() - 1)]


def reversed_order(size):
    width = size.bit_length() - 1
    return sorted(range(size), key=lambda k: int(f"{k:0{width}b}"[::-1], 2) if width else 0)


def slabs_of(own, axis):
    size = lax.axis_size(axis)
    slabs = {0: own}
    for bit in reversed(bits_of(size)):
        for k in sorted(slabs):
            slabs[k ^ bit] = swapped(slabs[k], axis, bit)
    return [slabs[k] for k in range(size)]


def rim_of(own, size_rows):
    heads, seqs = lax.axis_size("head"), lax.axis_size("seq")
    tail = own[own.shape[0] - size_rows :]
    rim = jnp.zeros_like(tail)
    for k in range(heads):
        route = [(s * heads + heads - 1, (s + 1) * heads + k) for s in range(seqs - 1)]
        rim = rim + lax.ppermute(tail, ("seq", "head"), route)
    return rim


def vmem_call(body, out_shape, args, scratch=(), in_specs=None, flops=0, moved=0):
    return pl.pallas_call(
        body,
        out_shape=out_shape,
        in_specs=in_specs or [pl.BlockSpec(memory_space=pltpu.VMEM)] * len(args),
        out_specs=jax.tree.map(lambda _: pl.BlockSpec(memory_space=pltpu.VMEM), out_shape),
        scratch_shapes=list(scratch),
        compiler_params=pltpu.CompilerParams(vmem_limit_bytes=VMEM_LIMIT),
        cost_estimate=pl.CostEstimate(flops=flops, bytes_accessed=moved, transcendentals=0),
    )(*args)


def front_body(
    slab_count,
    order_ref,
    rim_ref,
    *refs,
):
    slab_refs = refs[:slab_count]
    (
        weight_ref,
        small_ref,
        taps_ref,
        rate_ref,
        bias_ref,
        decay_up_ref,
        pair_ref,
        solved_ref,
        attend_ref,
        start_ref,
        gate_ref,
        rows_ref,
        weights,
        projected,
        mixing,
        inverse,
        inverse_low,
        row_sem,
        weight_sem,
    ) = refs[slab_count:]
    slab_rows = slab_refs[0].shape[0]
    heads, size = pair_ref.shape[0], pair_ref.shape[1]
    count = start_ref.shape[1]
    tap_count = taps_ref.shape[0] // 3
    chunk = math.gcd(count, 64)
    chunks = count // chunk

    copies = [pltpu.make_async_copy(rim_ref, rows_ref.at[pl.ds(0, RIM)], row_sem.at[slab_count])]
    for k in range(slab_count):
        begin = pl.multiple_of(RIM + order_ref[k] * slab_rows, 16)
        copies.append(
            pltpu.make_async_copy(
                slab_refs[k], rows_ref.at[pl.ds(begin, slab_rows)], row_sem.at[k]
            )
        )
    loads = [
        pltpu.make_async_copy(weight_ref.at[c], weights.at[c], weight_sem.at[c]) for c in range(3)
    ]
    for copy in copies + loads:
        copy.start()
    for copy in copies:
        copy.wait()

    low = dot(rows_ref[RIM:, :], small_ref[...])
    rank = decay_up_ref.shape[0]
    decay_low = low[:, :rank].astype(bf16)
    gate_ref[...] = low[:, rank : 2 * rank].astype(bf16)
    strength = jax.nn.sigmoid(low[:, 2 * rank :])
    raw = dot(decay_low, decay_up_ref[...]) + bias_ref[...]
    softplus = jnp.maximum(raw, 0.0) + jnp.log1p(jnp.exp(-jnp.abs(raw)))
    log_decay = -rate_ref[...] * softplus
    row = lax.broadcasted_iota(jnp.int32, (count, count), 0)
    col = lax.broadcasted_iota(jnp.int32, (count, count), 1)
    lower = jnp.where(row >= col, 1.0, 0.0).astype(bf16)
    high = log_decay.astype(bf16)
    cumulative = dot(lower, high) + dot(lower, (log_decay - high.astype(f32)).astype(bf16))

    convolved = []
    for c in range(3):
        loads[c].wait()
        projected[c] = dot(rows_ref[...], weights[c]).astype(bf16).astype(f32)
        total = None
        for i in range(tap_count):
            term = projected[c, pl.ds(RIM - tap_count + 1 + i, count), :] * taps_ref[
                pl.ds(c * tap_count + i, 1), :
            ]
            total = term if total is None else total + term
        convolved.append((total / (1.0 + jnp.exp(-total))).astype(bf16).astype(f32))

    def by_chunk(rows):
        return jnp.concatenate([jnp.broadcast_to(r, (chunk, size)) for r in rows], axis=0)

    eye = row == col
    stops, sides = [], []
    for h in range(heads):
        lanes = slice(h * size, (h + 1) * size)
        queries, keys, values = (part[:, lanes] for part in convolved)
        queries = queries * lax.rsqrt(jnp.sum(queries * queries, -1, keepdims=True) + 1e-06)
        queries = queries * size ** (-0.5)
        keys = keys * lax.rsqrt(jnp.sum(keys * keys, -1, keepdims=True) + 1e-06)
        running = cumulative[:, lanes]
        middles = [running[a * chunk + chunk // 2 : a * chunk + chunk // 2 + 1] for a in range(chunks)]
        middle = by_chunk(middles)
        rise = jnp.exp(running - middle)
        key_rise, query_rise = keys * rise, queries * rise
        key_fall = keys * strength[:, h : h + 1] * jnp.exp(middle - running)
        last = running[count - 1 :]
        stops.append(
            ((key_fall * by_chunk([jnp.exp(last - m) for m in middles])).astype(bf16), jnp.exp(last))
        )
        entry = by_chunk([jnp.exp(m) for m in middles])
        start_ref[h] = query_rise * entry
        sides.append(
            jnp.concatenate([(key_rise * entry).astype(bf16), values.astype(bf16)], axis=1)
        )
        for a in range(chunks):
            here = slice(a * chunk, (a + 1) * chunk)
            left = jnp.concatenate([key_rise[here], query_rise[here]], axis=0).astype(bf16)
            falls = []
            for b in range(chunks):
                there = slice(b * chunk, (b + 1) * chunk)
                if b < a:
                    falls.append(key_fall[there] * jnp.exp(middles[a] - middles[b]))
                elif b == a:
                    falls.append(key_fall[there])
                else:
                    falls.append(jnp.zeros((chunk, size), f32))
            right = jnp.concatenate(falls, axis=0).astype(bf16)
            scores = dot(left, right, ((1,), (1,)))
            mixing[h, here, :] = jnp.where(row[here] > col[here], scores[:chunk], 0.0).astype(bf16)
            attend_ref[h, here, :] = jnp.where(row[here] >= col[here], scores[chunk:], 0.0).astype(
                bf16
            )

    base = math.gcd(count, BASE)
    same = row // base == col // base
    powers = [None] * heads
    for h in range(heads):
        nilpotent = jnp.where(same, -mixing[h].astype(f32), 0.0)
        powers[h] = nilpotent.astype(bf16)
        inverse[h] = jnp.where(eye, 1.0, nilpotent)
    for _ in range(1, (base - 1).bit_length()):
        for h in range(heads):
            powers[h] = dot(powers[h], powers[h]).astype(bf16)
        for h in range(heads):
            inverse[h] = inverse[h] + dot(inverse[h].astype(bf16), powers[h])
    for h in range(heads):
        inverse_low[h] = inverse[h].astype(bf16)
    width = base
    while width < count:
        odd = [slice(i, i + width) for i in range(width, count, 2 * width)]
        pair_mask = jnp.where(
            (row // width % 2 == 1) & (col // width == row // width - 1), 1.0, 0.0
        ).astype(bf16)
        halves = []
        for h in range(heads):
            chosen = jnp.concatenate([inverse_low[h, rows, :] for rows in odd], axis=0)
            halves.append(dot(chosen, mixing[h] * pair_mask).astype(bf16))
        for h in range(heads):
            change = dot(halves[h], inverse_low[h])
            for i, rows in enumerate(odd):
                new = inverse_low[h, rows, :].astype(f32) - change[i * width : (i + 1) * width]
                inverse_low[h, rows, :] = new.astype(bf16)
        width *= 2

    for h in range(heads):
        solved = dot(inverse_low[h], sides[h]).astype(bf16)
        solved_ref[h] = solved
        stop, fade = stops[h]
        moved = dot(stop, solved, ((0,), (0,)))
        diagonal = jnp.where(eye[:size, :size], jnp.broadcast_to(fade, (size, size)), 0.0)
        pair_ref[h, :, :size] = (diagonal - moved[:, :size]).astype(bf16)
        pair_ref[h, :, size:] = moved[:, size:].astype(bf16)


def front(order, rim, slabs, weight, small, taps, rate, bias, decay_up, heads, size):
    slab_count, slab_rows = len(slabs), slabs[0].shape[0]
    count = slab_count * slab_rows
    width = weight.shape[1]
    channels = heads * size
    vm, anywhere = pl.BlockSpec(memory_space=pltpu.VMEM), pl.BlockSpec(memory_space=pl.ANY)
    args = (order, rim, *slabs, weight, small, taps, rate, bias, decay_up)
    specs = [pl.BlockSpec(memory_space=pltpu.SMEM)] + [anywhere] * (slab_count + 2) + [vm] * 5
    return vmem_call(
        functools.partial(front_body, slab_count),
        (
            jax.ShapeDtypeStruct((heads, size, 2 * size), bf16),
            jax.ShapeDtypeStruct((heads, count, 2 * size), bf16),
            jax.ShapeDtypeStruct((heads, count, count), bf16),
            jax.ShapeDtypeStruct((heads, count, size), f32),
            jax.ShapeDtypeStruct((count, decay_up.shape[0]), bf16),
        ),
        args,
        scratch=[
            pltpu.VMEM((RIM + count, width), bf16),
            pltpu.VMEM((3, width, channels), bf16),
            pltpu.VMEM((3, RIM + count, channels), f32),
            pltpu.VMEM((heads, count, count), bf16),
            pltpu.VMEM((heads, count, count), f32),
            pltpu.VMEM((heads, count, count), bf16),
            pltpu.SemaphoreType.DMA((slab_count + 1,)),
            pltpu.SemaphoreType.DMA((3,)),
        ],
        in_specs=specs,
        flops=2 * count * width * channels * 4,
        moved=2 * 4 * width * channels,
    )


def rows_body(attend_ref, solved_ref, start_ref, low_ref, up_ref, raised_ref, output_ref, gate_ref):
    heads, _, size = start_ref.shape
    gate_ref[...] = jax.nn.sigmoid(dot(low_ref[...], up_ref[...]))
    for h in range(heads):
        both = dot(attend_ref[h], solved_ref[h])
        raised_ref[h] = (start_ref[h] - both[:, :size]).astype(bf16)
        output_ref[:, h * size : (h + 1) * size] = both[:, size:]


def compose_body(later_ref, first_ref, out_ref):
    heads, size, _ = later_ref.shape
    for h in range(heads):
        both = dot(later_ref[h, :, :size], first_ref[h])
        out_ref[h, :, :size] = both[:, :size].astype(bf16)
        out_ref[h, :, size:] = (both[:, size:] + later_ref[h, :, size:].astype(f32)).astype(bf16)


def compose(later, first):
    return vmem_call(
        compose_body,
        jax.ShapeDtypeStruct(later.shape, bf16),
        (later, first),
        flops=2 * math.prod(later.shape) * later.shape[1],
        moved=6 * math.prod(later.shape),
    )


def back_body(
    order_ref, near_ref, far_ref, raised_ref, output_ref, gate_ref, gain_ref, weight_ref,
    keep_ref, send_ref, normed,
):
    heads, count, size = raised_ref.shape
    slab_count = order_ref.shape[0]
    slab_rows = count // slab_count
    for h in range(heads):
        lanes = slice(h * size, (h + 1) * size)
        state = dot(near_ref[h, :, :size], far_ref[h]) + near_ref[h, :, size:].astype(f32)
        attended = dot(raised_ref[h], state.astype(bf16)) + output_ref[:, lanes]
        power = jnp.sum(attended * attended, -1, keepdims=True) * (1.0 / size)
        normed[:, lanes] = (
            attended * lax.rsqrt(power + 1e-05) * gain_ref[...] * gate_ref[:, lanes]
        ).astype(bf16)
    ordered = jnp.concatenate(
        [
            normed[pl.ds(pl.multiple_of(order_ref[k] * slab_rows, 16), slab_rows), :]
            for k in range(slab_count)
        ],
        axis=0,
    )
    total = dot(ordered, weight_ref[...])
    half = keep_ref.shape[0]
    keep_ref[...] = total[:half]
    send_ref[...] = total[half:].astype(bf16)


def shards(
    hidden_in,
    qkv_weight,
    conv_weight,
    decay_log,
    dt_bias,
    decay_down,
    decay_up,
    beta_weight,
    gate_down,
    gate_up,
    norm_gain,
    out_weight,
):
    heads, size = decay_log.shape[0], norm_gain.shape[0]
    channels = heads * size
    devices, here = lax.axis_size("head"), lax.axis_index("head")
    slabs = slabs_of(hidden_in, "head")
    rim = rim_of(hidden_in, RIM)
    order = jnp.arange(devices, dtype=jnp.int32) ^ here.astype(jnp.int32)
    beta = jnp.pad(beta_weight, ((0, 0), (0, 128 - heads)))
    small = jnp.concatenate([decay_down, gate_down, beta], axis=1)
    taps = conv_weight.astype(f32).reshape(-1, channels)
    rate = jnp.repeat(jnp.exp(decay_log), size)[None]
    pair, solved, attend, start, gate_low = front(
        order,
        rim,
        slabs,
        qkv_weight.transpose(1, 0, 2),
        small,
        taps,
        rate,
        dt_bias[None],
        decay_up,
        heads,
        size,
    )
    count = start.shape[1]
    raised, output_rows, out_gate = vmem_call(
        rows_body,
        (
            jax.ShapeDtypeStruct((heads, count, size), bf16),
            jax.ShapeDtypeStruct((count, channels), f32),
            jax.ShapeDtypeStruct((count, channels), f32),
        ),
        (attend, solved, start, gate_low, gate_up),
        flops=2 * heads * count * count * 2 * size,
        moved=4 * heads * count * count,
    )
    blocks = lax.axis_size("seq")
    near, far = jnp.zeros_like(pair), jnp.zeros((heads, size, size), bf16)
    distance = 1
    while distance < blocks:
        if 2 * distance < blocks:
            arrived = passed_along(pair, "seq", distance)
            near = arrived if distance == 1 else compose(near, arrived)
            pair = compose(pair, arrived)
        else:
            far = passed_along(pair[:, :, size:], "seq", distance)
            if distance == 1:
                near = jnp.concatenate([jnp.zeros_like(far), far], axis=2)
        distance *= 2
    order_out = jnp.asarray(reversed_order(devices), jnp.int32) ^ here.astype(jnp.int32)
    half = count // 2 if devices > 1 else count
    vm = pl.BlockSpec(memory_space=pltpu.VMEM)
    keep, send = vmem_call(
        back_body,
        (
            jax.ShapeDtypeStruct((half, out_weight.shape[1]), f32),
            jax.ShapeDtypeStruct((half, out_weight.shape[1]), bf16),
        ),
        (order_out, near, far, raised, output_rows, out_gate, norm_gain[None], out_weight),
        scratch=[pltpu.VMEM((count, channels), bf16)],
        in_specs=[pl.BlockSpec(memory_space=pltpu.SMEM)] + [vm] * 7,
        flops=2 * count * channels * out_weight.shape[1],
        moved=2 * channels * out_weight.shape[1],
    )
    for bit in bits_of(devices):
        keep = keep + swapped(send, "head", bit).astype(f32)
        if 2 * bit < devices:
            half = keep.shape[0] // 2
            keep, send = keep[:half], keep[half:].astype(bf16)
    return keep.astype(bf16)


def solution(mesh):
    return jax.shard_map(
        shards,
        mesh=mesh,
        in_specs=(
            P(("seq", "head"), None),
            P(None, None, "head"),
            P(None, None, "head"),
            P("head"),
            P("head"),
            P(),
            P(None, "head"),
            P(None, "head"),
            P(),
            P(None, "head"),
            P(),
            P("head", None),
        ),
        out_specs=P(("seq", "head"), None),
        check_vma=False,
    )
```

time: 383 us -> 75.5 us (0.20)
  blocking collectives: 257 us -> 0 us
  matrix products: 57.4 us -> 0 us
  starting transfers between devices: 4.33 us -> 28.1 us
  local copies, waits for them, and re-layouts: 23.6 us -> 5.18 us
  between operations: 13.8 us -> 0.32 us
  Pallas kernels: 0 us -> 12.5 us
  waiting for transfers between devices: 16.1 us -> 25.4 us
  other arithmetic: 7.67 us -> 2.52 us
    all_gather x8 -> x0, blocking collectives: 248 us -> none  [entering(): lax.all_gather(part.astype(kind), axis)]
    dot_general x126 -> x0, matrix products: 57.4 us -> none  [the longest x72 25.7 us: product(): return jnp.einsum('hij,hjk->hik', left, right, precision=exact_precision)]
    ppermute x1 -> x12, starting transfers between devices: 4.29 us -> 28.1 us  [the longest x3 15.6 us: passed_along(): lax.ppermute(block, axis, [(i, i + distance) for i in range(size - distan...]
    ppermute x1 -> x12, waiting for transfers between devices: 3.52 us -> 25.4 us  [the longest x3 13.2 us: passed_along(): lax.ppermute(block, axis, [(i, i + distance) for i in range(size - distan...]
    pallas_call x0 -> x6, Pallas kernels: none -> 12.5 us  [vmem_call(): pl.pallas_call(body, out_shape=out_shape, in_specs=in_specs or [pl.BlockS...]
    all_gather x2 -> x0, waiting for transfers between devices: 11.2 us -> none  [the longest x1 11.2 us: shards(): gathered = lax.all_gather(hidden_in, 'head', axis=0, tiled=True)]
    all_to_all x1 -> x0, blocking collectives: 8.42 us -> none  [shards(): lax.all_to_all(normed, 'head', split_axis=0, concat_axis=1, tiled=True)]
    unnamed x27 -> x21, local copies, waits for them, and re-layouts: 10.1 us -> 4.16 us
  transfers between devices with their start and end apart: 3 -> 12, of which waited for: 2 -> 6; matrix products, arithmetic and copies ran while one was open for 22% -> 4% of each run, Pallas kernels for 0% -> 1%
where the time goes in v1:
time: 75.5 us; the launch traced here: 74 us
  starting transfers between devices  28.1 us (37%)
  waiting for transfers between devices  25.4 us (34%)
  Pallas kernels  12.5 us (17%)
  local copies, waits for them, and re-layouts  5.18 us (7%)
  other arithmetic  2.52 us (3%)
    ppermute x3, starting transfers between devices, passed_along(): lax.ppermute(block, axis, [(i, i + distance) for i in range(size - distan...  15.6 us
    ppermute x3, waiting for transfers between devices, passed_along(): lax.ppermute(block, axis, [(i, i + distance) for i in range(size - distan...  13.2 us
    pallas_call x6, Pallas kernels, vmem_call(): pl.pallas_call(body, out_shape=out_shape, in_specs=in_specs or [pl.BlockS...  12.5 us
    ppermute x5, waiting for transfers between devices, swapped(): lax.ppermute(block, axis, [(i, i ^ bit) for i in range(lax.axis_size(axis...  12.2 us
    ppermute x5, starting transfers between devices, swapped(): lax.ppermute(block, axis, [(i, i ^ bit) for i in range(lax.axis_size(axis...  9.79 us
    unnamed x21, local copies, waits for them, and re-layouts  4.16 us
    ppermute x4, starting transfers between devices, rim_of(): rim = rim + lax.ppermute(tail, ('seq', 'head'), route)  2.65 us
    concatenate x1, other arithmetic, shards(): small = jnp.concatenate([decay_down, gate_down, beta], axis=1)  1.59 us
  transfers between devices with their start and end apart: 12, of which 6 were waited for; matrix products, arithmetic and copies ran while one was open for 4% of the time, Pallas kernels for 1%

profile of v1, /device:TPU:0, one launch (start us, length us, event | category | flops | bytes accessed | tf_op | source)
XLA Modules:
  0.0 74.0 jit_solution(17745165780914471510)
XLA Ops:
  0.0 0.9 %slice.13 = bf16[16,2304]{1,0:T(8,128)(2,1)S(1)} slice(bf16[64,2304]{1,0:T(8,128)(2,1)} %refs_0_.1), slice={[48:64], [0:2304]} | slice | bytes 147456 | tf_op jit(solution)/shard_map/slice | solution.py:52
  0.9 0.7 collective-permute-start.3
  1.6 0.7 collective-permute-start.2
  2.2 0.7 collective-permute-start.1
  2.9 0.7 collective-permute-start
  3.6 3.0 %collective-permute-start.5 = (bf16[64,2304]{1,0:T(8,128)(2,1)}, bf16[64,2304]{1,0:T(8,128)(2,1)S(1)}, u32[]{:S(2)}, u32[]{:S(2)}) collective-permute-start(bf16[64,2304]{1,0:T(8,128)(2,1)} %refs_0_.1), channel_id=1, source_target_pairs={{0,2},{1,3},{2,0},{3,1},{4,6},{5,7},{6,4},{7,5},{8,10},{9,11},{10,... | collective-permute-start | bytes 884744 | tf_op jit(solution)/shard_map/ppermute | solution.py:28
  6.6 1.1 %copy.14 = bf16[2304,4]{1,0:T(8,128)(2,1)S(1)} copy(bf16[2304,4]{0,1:T(4,128)(2,1)} %param.20) | data formatting | bytes 36864 | tf_op args[7]
  7.7 0.0 copy-start.8
  7.7 0.0 copy-start.7
  7.7 0.0 copy-start.2
  7.7 0.0 copy-start.3
  7.7 0.0 copy-start.5
  7.7 1.6 %fusion.1.refs_5_ = bf16[2304,384]{1,0:T(8,128)(2,1)S(1)} fusion(bf16[2304,4]{1,0:T(8,128)(2,1)S(1)} %copy.14, bf16[2304,128]{1,0:T(8,128)(2,1)} %param.21, bf16[2304,128]{1,0:T(8,128)(2,1)} %param.18), kind=kLoop, calls=%fused_computation.2 | loop fusion | flops 7077888 | bytes 2967552 | tf_op jit(solution)/shard_map/concatenate | solution.py:345
  9.3 0.0 copy-done.8
  9.4 0.0 copy-done.7
  9.4 0.0 collective-permute-done.3
  9.4 0.0 copy-done.2
  9.4 4.0 %collective-permute-start.4 = (bf16[64,2304]{1,0:T(8,128)(2,1)S(1)}, bf16[64,2304]{1,0:T(8,128)(2,1)S(1)}, u32[]{:S(2)}, u32[]{:S(2)}) collective-permute-start(bf16[64,2304]{1,0:T(8,128)(2,1)S(1)} %copy-done.2), channel_id=1, source_target_pairs={{0,1},{1,0},{2,3},{3,2},{4,5},{5,4},{6,7},{7,6},{8,9},{9,8},{10,11... | collective-permute-start | bytes 884744 | tf_op jit(solution)/shard_map/ppermute | solution.py:28
  13.4 0.0 collective-permute-done.5.refs_2_
  13.4 2.7 %collective-permute-start.6 = (bf16[64,2304]{1,0:T(8,128)(2,1)S(1)}, bf16[64,2304]{1,0:T(8,128)(2,1)S(1)}, u32[]{:S(2)}, u32[]{:S(2)}) collective-permute-start(bf16[64,2304]{1,0:T(8,128)(2,1)S(1)} %collective-permute-done.5.refs_2_), channel_id=1, source_target_pairs={{0,1},{1,0},{2,3},{3,2},{4,5},{5,4},{6,7},{7,6},{8,9},{9,8},{10,11... | collective-permute-start | bytes 884744 | tf_op jit(solution)/shard_map/ppermute | solution.py:28
  16.1 0.0 collective-permute-done.2
  16.1 0.0 collective-permute-done.1
  16.1 0.0 collective-permute-done
  16.1 0.0 collective-permute-done.4.refs_1_
  16.1 1.2 %collective-permute-done.6.refs_3_ = bf16[64,2304]{1,0:T(8,128)(2,1)S(1)} collective-permute-done((bf16[64,2304]{1,0:T(8,128)(2,1)S(1)}, bf16[64,2304]{1,0:T(8,128)(2,1)S(1)}, u32[]{:S(2)}, u32[]{:S(2)}) %collective-permute-start.6) | collective-permute-done | bytes 294944 | tf_op jit(solution)/shard_map/ppermute | solution.py:28
  17.3 0.1 broadcast_in_dim.9
  17.3 0.0 copy-done.3
  17.3 0.0 copy-done.5
  17.3 0.0 copy-start
  17.3 3.0 %copy-done = bf16[2304,3,512]{2,0,1:T(8,128)(2,1)S(1)} copy-done((bf16[2304,3,512]{2,0,1:T(8,128)(2,1)S(1)}, bf16[2304,3,512]{2,0,1:T(8,128)(2,1)}, u32[]{:S(2)}) %copy-start) | copy-done | bytes 7077912
  20.3 9.6 %shard_map.127 = (bf16[4,128,256]{2,1,0:T(8,128)(2,1)S(1)}, bf16[4,256,256]{2,1,0:T(8,128)(2,1)S(1)}, bf16[4,256,256]{2,1,0:T(8,128)(2,1)S(1)}, f32[4,256,128]{2,1,0:T(8,128)S(1)}, bf16[256,128]{1,0:T(8,128)(2,1)S(1)}) custom-call(s32[4]{0:T(128)S(1)} %iota_xor_fusion.order_ref, bf16[16,2304]{1,0:T(8,128)(2,1)S(1)} %add_add_fusion.rim_ref, ...), custom_call_target="tpu_custom_call" | custom-call | flops 2415919104 | bytes 9437184 | tf_op jit(solution)/shard_map/pallas_call | solution.py:61
  29.9 0.0 copy-start.9
  29.9 0.0 copy-start.4
  30.0 3.2 %collective-permute-start.7 = (bf16[4,128,256]{2,1,0:T(8,128)(2,1)S(1)}, bf16[4,128,256]{2,1,0:T(8,128)(2,1)S(1)}, u32[]{:S(2)}, u32[]{:S(2)}) collective-permute-start(bf16[4,128,256]{2,1,0:T(8,128)(2,1)S(1)} %get-tuple-element.15.later_ref), channel_id=1, source_target_pairs={{0,4},{4,8},{8,12},{12,16},{16,20},{20,24},{24,28},{1,5},{5,9},{9,... | collective-permute-start | bytes 786440 | tf_op jit(solution)/shard_map/ppermute | solution.py:24
  33.1 6.1 %collective-permute-done.7.first_ref.later_ref = bf16[4,128,256]{2,1,0:T(8,128)(2,1)S(1)} collective-permute-done((bf16[4,128,256]{2,1,0:T(8,128)(2,1)S(1)}, bf16[4,128,256]{2,1,0:T(8,128)(2,1)S(1)}, u32[]{:S(2)}, u32[]{:S(2)}) %collective-permute-start.7) | collective-permute-done | bytes 262176 | tf_op jit(solution)/shard_map/ppermute | solution.py:24
  39.2 0.2 shard_map.128.later_ref
  39.4 0.0 copy-start.1
  39.4 0.0 copy-start.6
  39.4 7.1 %collective-permute-start.8 = (bf16[4,128,256]{2,1,0:T(8,128)(2,1)S(1)}, bf16[4,128,256]{2,1,0:T(8,128)(2,1)S(1)}, u32[]{:S(2)}, u32[]{:S(2)}) collective-permute-start(bf16[4,128,256]{2,1,0:T(8,128)(2,1)S(1)} %shard_map.128.later_ref), channel_id=1, source_target_pairs={{0,8},{4,12},{8,16},{12,20},{16,24},{20,28},{1,9},{5,13},{9,17},{1... | collective-permute-start | bytes 786440 | tf_op jit(solution)/shard_map/ppermute | solution.py:24
  46.5 5.3 %collective-permute-done.8.first_ref = bf16[4,128,256]{2,1,0:T(8,128)(2,1)S(1)} collective-permute-done((bf16[4,128,256]{2,1,0:T(8,128)(2,1)S(1)}, bf16[4,128,256]{2,1,0:T(8,128)(2,1)S(1)}, u32[]{:S(2)}, u32[]{:S(2)}) %collective-permute-start.8) | collective-permute-done | bytes 262176 | tf_op jit(solution)/shard_map/ppermute | solution.py:24
  51.8 0.2 shard_map.130
  52.0 5.4 %collective-permute-start.9 = (bf16[4,128,128]{2,1,0:T(8,128)(2,1)S(1)}, bf16[4,128,128]{2,1,0:T(8,128)(2,1)S(1)}, u32[]{:S(2)}, u32[]{:S(2)}) collective-permute-start(bf16[4,128,128]{2,1,0:T(8,128)(2,1)S(1)} %slice.17), channel_id=1, source_target_pairs={{0,16},{4,20},{8,24},{12,28},{1,17},{5,21},{9,25},{13,29},{2,18},{... | collective-permute-start | bytes 393224 | tf_op jit(solution)/shard_map/ppermute | solution.py:24
  57.4 0.0 copy-done.9
  57.4 0.0 copy-done.4
  57.5 0.4 shard_map.131
  57.8 0.2 shard_map.129.near_ref
  58.0 1.9 %collective-permute-done.9.far_ref = bf16[4,128,128]{2,1,0:T(8,128)(2,1)S(1)} collective-permute-done((bf16[4,128,128]{2,1,0:T(8,128)(2,1)S(1)}, bf16[4,128,128]{2,1,0:T(8,128)(2,1)S(1)}, u32[]{:S(2)}, u32[]{:S(2)}) %collective-permute-start.9) | collective-permute-done | bytes 131104 | tf_op jit(solution)/shard_map/ppermute | solution.py:24
  59.9 0.0 copy-done.1
  59.9 0.0 copy-done.6
  59.9 1.9 %shard_map.132 = (f32[128,2304]{1,0:T(8,128)S(1)}, bf16[128,2304]{1,0:T(8,128)(2,1)S(1)}) custom-call(s32[4]{0:T(128)S(1)} %broadcast_xor_fusion.order_ref, bf16[4,128,256]{2,1,0:T(8,128)(2,1)S(1)} %shard_map.129.near_ref, bf16[4,128,128]{2,1,0:T(8,128)(2,1)S(1)} %collective-permute-done.9.far_ref, bf16[4,256,128]{2,1,0:T(8,128)(2,1)S(1)} %get-tuple-element.20.raised_ref, ...), custom_call_target="tpu_custom_call" | custom-call | flops 603979776 | bytes 2359296 | tf_op jit(solution)/shard_map/pallas_call | solution.py:61
  61.9 0.1 collective-permute-start.10
  61.9 2.0 %collective-permute-done.10 = bf16[128,2304]{1,0:T(8,128)(2,1)S(1)} collective-permute-done((bf16[128,2304]{1,0:T(8,128)(2,1)S(1)}, bf16[128,2304]{1,0:T(8,128)(2,1)S(1)}, u32[]{:S(2)}, u32[]{:S(2)}) %collective-permute-start.10) | collective-permute-done | bytes 589856 | tf_op jit(solution)/shard_map/ppermute | solution.py:28
  63.9 0.1 convert_add_fusion
  64.1 0.1 collective-permute-start.11
  64.2 9.0 %collective-permute-done.11 = bf16[64,2304]{1,0:T(8,128)(2,1)S(1)} collective-permute-done((bf16[64,2304]{1,0:T(8,128)(2,1)S(1)}, bf16[64,2304]{1,0:T(8,128)(2,1)S(1)}, u32[]{:S(2)}, u32[]{:S(2)}) %collective-permute-start.11) | collective-permute-done | bytes 294944 | tf_op jit(solution)/shard_map/ppermute | solution.py:28
  73.2 0.8 %fusion.2 = bf16[64,2304]{1,0:T(8,128)(2,1)} fusion(f32[128,2304]{1,0:T(8,128)S(1)} %convert_add_fusion, bf16[64,2304]{1,0:T(8,128)(2,1)S(1)} %collective-permute-done.11), kind=kLoop, calls=%fused_computation.6 | loop fusion | flops 442368 | bytes 1179648 | tf_op jit(solution)/shard_map/convert_element_type | solution.py:406
  (7 shorter events, 0.1 us)
Async XLA Ops:
  0.9 8.5 %collective-permute-start.3 = (bf16[16,2304]{1,0:T(8,128)(2,1)S(1)}, bf16[16,2304]{1,0:T(8,128)(2,1)S(1)}, u32[]{:S(2)}, u32[]{:S(2)}) collective-permute-start(bf16[16,2304]{1,0:T(8,128)(2,1)S(1)} %slice.13), channel_id=1, source_target_pairs={{3,7},{7,11},{11,15},{15,19},{19,23},{23,27},{27,31}} | collective-permute-start | bytes 221192 | tf_op jit(solution)/shard_map/ppermute | solution.py:56
  1.6 14.5 %collective-permute-start.2 = (bf16[16,2304]{1,0:T(8,128)(2,1)S(1)}, bf16[16,2304]{1,0:T(8,128)(2,1)S(1)}, u32[]{:S(2)}, u32[]{:S(2)}) collective-permute-start(bf16[16,2304]{1,0:T(8,128)(2,1)S(1)} %slice.13), channel_id=1, source_target_pairs={{3,6},{7,10},{11,14},{15,18},{19,22},{23,26},{27,30}} | collective-permute-start | bytes 221192 | tf_op jit(solution)/shard_map/ppermute | solution.py:56
  2.2 13.8 %collective-permute-start.1 = (bf16[16,2304]{1,0:T(8,128)(2,1)S(1)}, bf16[16,2304]{1,0:T(8,128)(2,1)S(1)}, u32[]{:S(2)}, u32[]{:S(2)}) collective-permute-start(bf16[16,2304]{1,0:T(8,128)(2,1)S(1)} %slice.13), channel_id=1, source_target_pairs={{3,5},{7,9},{11,13},{15,17},{19,21},{23,25},{27,29}} | collective-permute-start | bytes 221192 | tf_op jit(solution)/shard_map/ppermute | solution.py:56
  2.9 13.2 %collective-permute-start = (bf16[16,2304]{1,0:T(8,128)(2,1)S(1)}, bf16[16,2304]{1,0:T(8,128)(2,1)S(1)}, u32[]{:S(2)}, u32[]{:S(2)}) collective-permute-start(bf16[16,2304]{1,0:T(8,128)(2,1)S(1)} %slice.13), channel_id=1, source_target_pairs={{3,4},{7,8},{11,12},{15,16},{19,20},{23,24},{27,28}} | collective-permute-start | bytes 221192 | tf_op jit(solution)/shard_map/ppermute | solution.py:56
  3.6 9.8 %collective-permute-start.5 = (bf16[64,2304]{1,0:T(8,128)(2,1)}, bf16[64,2304]{1,0:T(8,128)(2,1)S(1)}, u32[]{:S(2)}, u32[]{:S(2)}) collective-permute-start(bf16[64,2304]{1,0:T(8,128)(2,1)} %refs_0_.1), channel_id=1, source_target_pairs={{0,2},{1,3},{2,0},{3,1},{4,6},{5,7},{6,4},{7,5},{8,10},{9,11},{10,... | collective-permute-start | bytes 884744 | tf_op jit(solution)/shard_map/ppermute | solution.py:28
  7.7 1.7 %copy-start.8 = (f32[4]{0:T(128)S(1)}, f32[4]{0:T(128)}, u32[]{:S(2)}) copy-start(f32[4]{0:T(128)} %param.16) | copy-start | bytes 52
  7.7 1.7 %copy-start.7 = (bf16[3,4,512]{2,1,0:T(4,128)(2,1)S(1)}, bf16[3,4,512]{2,1,0:T(4,128)(2,1)}, u32[]{:S(2)}) copy-start(bf16[3,4,512]{2,1,0:T(4,128)(2,1)} %param.15) | copy-start | bytes 36868
  7.7 1.7 %copy-start.2 = (bf16[64,2304]{1,0:T(8,128)(2,1)S(1)}, bf16[64,2304]{1,0:T(8,128)(2,1)}, u32[]{:S(2)}) copy-start(bf16[64,2304]{1,0:T(8,128)(2,1)} %refs_0_.1) | copy-start | bytes 884740
  7.7 9.6 %copy-start.3 = (bf16[128,512]{1,0:T(8,128)(2,1)S(1)}, bf16[128,512]{1,0:T(8,128)(2,1)}, u32[]{:S(2)}) copy-start(bf16[128,512]{1,0:T(8,128)(2,1)} %refs_9_.1) | copy-start | bytes 393220
  7.7 9.6 %copy-start.5 = (f32[512]{0:T(512)S(1)}, f32[512]{0:T(512)}, u32[]{:S(2)}) copy-start(f32[512]{0:T(512)} %param.17) | copy-start | bytes 6148
  9.4 6.7 %collective-permute-start.4 = (bf16[64,2304]{1,0:T(8,128)(2,1)S(1)}, bf16[64,2304]{1,0:T(8,128)(2,1)S(1)}, u32[]{:S(2)}, u32[]{:S(2)}) collective-permute-start(bf16[64,2304]{1,0:T(8,128)(2,1)S(1)} %copy-done.2), channel_id=1, source_target_pairs={{0,1},{1,0},{2,3},{3,2},{4,5},{5,4},{6,7},{7,6},{8,9},{9,8},{10,11... | collective-permute-start | bytes 884744 | tf_op jit(solution)/shard_map/ppermute | solution.py:28
  13.4 3.9 %collective-permute-start.6 = (bf16[64,2304]{1,0:T(8,128)(2,1)S(1)}, bf16[64,2304]{1,0:T(8,128)(2,1)S(1)}, u32[]{:S(2)}, u32[]{:S(2)}) collective-permute-start(bf16[64,2304]{1,0:T(8,128)(2,1)S(1)} %collective-permute-done.5.refs_2_), channel_id=1, source_target_pairs={{0,1},{1,0},{2,3},{3,2},{4,5},{5,4},{6,7},{7,6},{8,9},{9,8},{10,11... | collective-permute-start | bytes 884744 | tf_op jit(solution)/shard_map/ppermute | solution.py:28
  17.3 3.0 %copy-start = (bf16[2304,3,512]{2,0,1:T(8,128)(2,1)S(1)}, bf16[2304,3,512]{2,0,1:T(8,128)(2,1)}, u32[]{:S(2)}) copy-start(bf16[2304,3,512]{2,0,1:T(8,128)(2,1)} %param.14) | copy-start | bytes 21233668
  29.9 27.5 %copy-start.9 = (s32[4]{0:T(128)S(1)}, s32[4]{0:T(128)}, u32[]{:S(2)}) copy-start(s32[4]{0:T(128)} %constant.9.clone) | copy-start | bytes 52
  29.9 27.5 %copy-start.4 = (bf16[128,512]{1,0:T(8,128)(2,1)S(1)}, bf16[128,512]{1,0:T(8,128)(2,1)}, u32[]{:S(2)}) copy-start(bf16[128,512]{1,0:T(8,128)(2,1)} %up_ref.1) | copy-start | bytes 393220
  30.0 9.2 %collective-permute-start.7 = (bf16[4,128,256]{2,1,0:T(8,128)(2,1)S(1)}, bf16[4,128,256]{2,1,0:T(8,128)(2,1)S(1)}, u32[]{:S(2)}, u32[]{:S(2)}) collective-permute-start(bf16[4,128,256]{2,1,0:T(8,128)(2,1)S(1)} %get-tuple-element.15.later_ref), channel_id=1, source_target_pairs={{0,4},{4,8},{8,12},{12,16},{16,20},{20,24},{24,28},{1,5},{5,9},{9,... | collective-permute-start | bytes 786440 | tf_op jit(solution)/shard_map/ppermute | solution.py:24
  39.4 20.5 %copy-start.1 = (bf16[512,2304]{1,0:T(8,128)(2,1)S(1)}, bf16[512,2304]{1,0:T(8,128)(2,1)}, u32[]{:S(2)}) copy-start(bf16[512,2304]{1,0:T(8,128)(2,1)} %weight_ref.1) | copy-start | bytes 7077892
  39.4 20.5 %copy-start.6 = (f32[128]{0:T(128)S(1)}, f32[128]{0:T(128)}, u32[]{:S(2)}) copy-start(f32[128]{0:T(128)} %param.23) | copy-start | bytes 1540
  39.4 12.3 %collective-permute-start.8 = (bf16[4,128,256]{2,1,0:T(8,128)(2,1)S(1)}, bf16[4,128,256]{2,1,0:T(8,128)(2,1)S(1)}, u32[]{:S(2)}, u32[]{:S(2)}) collective-permute-start(bf16[4,128,256]{2,1,0:T(8,128)(2,1)S(1)} %shard_map.128.later_ref), channel_id=1, source_target_pairs={{0,8},{4,12},{8,16},{12,20},{16,24},{20,28},{1,9},{5,13},{9,17},{1... | collective-permute-start | bytes 786440 | tf_op jit(solution)/shard_map/ppermute | solution.py:24
  52.0 7.9 %collective-permute-start.9 = (bf16[4,128,128]{2,1,0:T(8,128)(2,1)S(1)}, bf16[4,128,128]{2,1,0:T(8,128)(2,1)S(1)}, u32[]{:S(2)}, u32[]{:S(2)}) collective-permute-start(bf16[4,128,128]{2,1,0:T(8,128)(2,1)S(1)} %slice.17), channel_id=1, source_target_pairs={{0,16},{4,20},{8,24},{12,28},{1,17},{5,21},{9,25},{13,29},{2,18},{... | collective-permute-start | bytes 393224 | tf_op jit(solution)/shard_map/ppermute | solution.py:24
  61.9 2.1 %collective-permute-start.10 = (bf16[128,2304]{1,0:T(8,128)(2,1)S(1)}, bf16[128,2304]{1,0:T(8,128)(2,1)S(1)}, u32[]{:S(2)}, u32[]{:S(2)}) collective-permute-start(bf16[128,2304]{1,0:T(8,128)(2,1)S(1)} %get-tuple-element.24), channel_id=1, source_target_pairs={{0,1},{1,0},{2,3},{3,2},{4,5},{5,4},{6,7},{7,6},{8,9},{9,8},{10,11... | collective-permute-start | bytes 1769480 | tf_op jit(solution)/shard_map/ppermute | solution.py:28
  64.1 9.1 %collective-permute-start.11 = (bf16[64,2304]{1,0:T(8,128)(2,1)S(1)}, bf16[64,2304]{1,0:T(8,128)(2,1)S(1)}, u32[]{:S(2)}, u32[]{:S(2)}) collective-permute-start(bf16[64,2304]{1,0:T(8,128)(2,1)S(1)} %slice.24), channel_id=1, source_target_pairs={{0,2},{1,3},{2,0},{3,1},{4,6},{5,7},{6,4},{7,5},{8,10},{9,11},{10,... | collective-permute-start | bytes 884744 | tf_op jit(solution)/shard_map/ppermute | solution.py:28

commit v2 on v1

--- a/solution.py
+++ b/solution.py
@@ -10,6 +10,7 @@
 
 RIM = 16
 BASE = 16
+GROUPS = 2
 VMEM_LIMIT = 40 * 1024 * 1024
 f32 = jnp.float32
 bf16 = jnp.bfloat16
@@ -19,11 +20,6 @@
     return lax.dot_general(left, right, (contract, ((), ())), preferred_element_type=f32)
 
 
-def passed_along(block, axis, distance):
-    size = lax.axis_size(axis)
-    return lax.ppermute(block, axis, [(i, i + distance) for i in range(size - distance)])
-
-
 def swapped(block, axis, bit):
     return lax.ppermute(block, axis, [(i, i ^ bit) for i in range(lax.axis_size(axis))])
 
@@ -31,11 +27,6 @@
 def bits_of(size):
     assert size & (size - 1) == 0
     return [1 << i for i in range(size.bit_length() - 1)]
-
-
-def reversed_order(size):
-    width = size.bit_length() - 1
-    return sorted(range(size), key=lambda k: int(f"{k:0{width}b}"[::-1], 2) if width else 0)
 
 
 def slabs_of(own, axis):
@@ -47,21 +38,22 @@
     return [slabs[k] for k in range(size)]
 
 
-def rim_of(own, size_rows):
+def rim_of(own, row_count):
     heads, seqs = lax.axis_size("head"), lax.axis_size("seq")
-    tail = own[own.shape[0] - size_rows :]
+    tail = own[own.shape[0] - row_count :]
     rim = jnp.zeros_like(tail)
-    for k in range(heads):
+    for k in range(min(1, heads - 1), heads, 2):
         route = [(s * heads + heads - 1, (s + 1) * heads + k) for s in range(seqs - 1)]
         rim = rim + lax.ppermute(tail, ("seq", "head"), route)
-    return rim
-
-
-def vmem_call(body, out_shape, args, scratch=(), in_specs=None, flops=0, moved=0):
+    return rim + swapped(rim, "head", 1) if heads > 1 else rim
+
+
+def vmem_call(body, out_shape, args, scratch=(), scalars=0, flops=0, moved=0):
+    spaces = [pltpu.SMEM] * scalars + [pltpu.VMEM] * (len(args) - scalars)
     return pl.pallas_call(
         body,
         out_shape=out_shape,
-        in_specs=in_specs or [pl.BlockSpec(memory_space=pltpu.VMEM)] * len(args),
+        in_specs=[pl.BlockSpec(memory_space=space) for space in spaces],
         out_specs=jax.tree.map(lambda _: pl.BlockSpec(memory_space=pltpu.VMEM), out_shape),
         scratch_shapes=list(scratch),
         compiler_params=pltpu.CompilerParams(vmem_limit_bytes=VMEM_LIMIT),
@@ -78,7 +70,10 @@
     slab_refs = refs[:slab_count]
     (
         weight_ref,
-        small_ref,
+        _,
+        decay_down_ref,
+        gate_down_ref,
+        beta_ref,
         taps_ref,
         rate_ref,
         bias_ref,
@@ -89,13 +84,10 @@
         start_ref,
         gate_ref,
         rows_ref,
-        weights,
         projected,
         mixing,
         inverse,
         inverse_low,
-        row_sem,
-        weight_sem,
     ) = refs[slab_count:]
     slab_rows = slab_refs[0].shape[0]
     heads, size = pair_ref.shape[0], pair_ref.shape[1]
@@ -104,27 +96,17 @@
     chunk = math.gcd(count, 64)
     chunks = count // chunk
 
-    copies = [pltpu.make_async_copy(rim_ref, rows_ref.at[pl.ds(0, RIM)], row_sem.at[slab_count])]
+    rows_ref[:RIM, :] = rim_ref[...]
     for k in range(slab_count):
         begin = pl.multiple_of(RIM + order_ref[k] * slab_rows, 16)
-        copies.append(
-            pltpu.make_async_copy(
-                slab_refs[k], rows_ref.at[pl.ds(begin, slab_rows)], row_sem.at[k]
-            )
-        )
-    loads = [
-        pltpu.make_async_copy(weight_ref.at[c], weights.at[c], weight_sem.at[c]) for c in range(3)
-    ]
-    for copy in copies + loads:
-        copy.start()
-    for copy in copies:
-        copy.wait()
-
-    low = dot(rows_ref[RIM:, :], small_ref[...])
+        rows_ref[pl.ds(begin, slab_rows), :] = slab_refs[k][...]
+
+    here_rows = rows_ref[RIM:, :]
     rank = decay_up_ref.shape[0]
+    low = dot(here_rows, jnp.concatenate([decay_down_ref[...], gate_down_ref[...]], axis=1))
     decay_low = low[:, :rank].astype(bf16)
-    gate_ref[...] = low[:, rank : 2 * rank].astype(bf16)
-    strength = jax.nn.sigmoid(low[:, 2 * rank :])
+    gate_ref[...] = low[:, rank:].astype(bf16)
+    strength = jax.nn.sigmoid(dot(here_rows, beta_ref[...], ((1,), (1,))))
     raw = dot(decay_low, decay_up_ref[...]) + bias_ref[...]
     softplus = jnp.maximum(raw, 0.0) + jnp.log1p(jnp.exp(-jnp.abs(raw)))
     log_decay = -rate_ref[...] * softplus
@@ -136,8 +118,7 @@
 
     convolved = []
     for c in range(3):
-        loads[c].wait()
-        projected[c] = dot(rows_ref[...], weights[c]).astype(bf16).astype(f32)
+        projected[c] = dot(rows_ref[...], weight_ref[c]).astype(bf16).astype(f32)
         total = None
         for i in range(tap_count):
             term = projected[c, pl.ds(RIM - tap_count + 1 + i, count), :] * taps_ref[
@@ -232,14 +213,12 @@
         pair_ref[h, :, size:] = moved[:, size:].astype(bf16)
 
 
-def front(order, rim, slabs, weight, small, taps, rate, bias, decay_up, heads, size):
+def front(order, rim, slabs, weight, ready, downs, taps, rate, bias, decay_up, heads, size):
     slab_count, slab_rows = len(slabs), slabs[0].shape[0]
     count = slab_count * slab_rows
     width = weight.shape[1]
     channels = heads * size
-    vm, anywhere = pl.BlockSpec(memory_space=pltpu.VMEM), pl.BlockSpec(memory_space=pl.ANY)
-    args = (order, rim, *slabs, weight, small, taps, rate, bias, decay_up)
-    specs = [pl.BlockSpec(memory_space=pltpu.SMEM)] + [anywhere] * (slab_count + 2) + [vm] * 5
+    args = (order, rim, *slabs, weight, ready, *downs, taps, rate, bias, decay_up)
     return vmem_call(
         functools.partial(front_body, slab_count),
         (
@@ -252,18 +231,19 @@
         args,
         scratch=[
             pltpu.VMEM((RIM + count, width), bf16),
-            pltpu.VMEM((3, width, channels), bf16),
             pltpu.VMEM((3, RIM + count, channels), f32),
             pltpu.VMEM((heads, count, count), bf16),
             pltpu.VMEM((heads, count, count), f32),
             pltpu.VMEM((heads, count, count), bf16),
-            pltpu.SemaphoreType.DMA((slab_count + 1,)),
-            pltpu.SemaphoreType.DMA((3,)),
         ],
-        in_specs=specs,
+        scalars=1,
         flops=2 * count * width * channels * 4,
         moved=2 * 4 * width * channels,
     )
+
+
+def ready_body(weight_ref, out_ref):
+    out_ref[...] = weight_ref[0, :8, :128].astype(f32)
 
 
 def rows_body(attend_ref, solved_ref, start_ref, low_ref, up_ref, raised_ref, output_ref, gate_ref):
@@ -275,50 +255,130 @@
         output_ref[:, h * size : (h + 1) * size] = both[:, size:]
 
 
-def compose_body(later_ref, first_ref, out_ref):
-    heads, size, _ = later_ref.shape
-    for h in range(heads):
-        both = dot(later_ref[h, :, :size], first_ref[h])
-        out_ref[h, :, :size] = both[:, :size].astype(bf16)
-        out_ref[h, :, size:] = (both[:, size:] + later_ref[h, :, size:].astype(f32)).astype(bf16)
-
-
-def compose(later, first):
+def composed(later, first, size):
+    both = dot(later[:, :size], first)
+    return both[:, :size], both[:, size:] + later[:, size:].astype(f32)
+
+
+def turn_body(first, last, flag_ref, own_ref, far_ref, near_ref, total_ref, out_ref):
+    heads, size, _ = own_ref.shape
+    upper = flag_ref[0] == 1
+
+    def put(ref, h, pair):
+        if ref.shape[2] == size:
+            ref[h] = pair[1].astype(bf16)
+        else:
+            ref[h, :, :size] = pair[0].astype(bf16)
+            ref[h, :, size:] = pair[1].astype(bf16)
+
+    @pl.when(upper)
+    def _():
+        for h in range(heads):
+            put(total_ref, h, composed(own_ref[h], far_ref[h], size))
+        for h in range(heads):
+            if first:
+                out_ref[h] = far_ref[h]
+            else:
+                put(out_ref, h, composed(near_ref[h], far_ref[h], size))
+
+    @pl.when(jnp.logical_not(upper))
+    def _():
+        for h in range(heads):
+            put(total_ref, h, composed(far_ref[h], own_ref[h], size))
+        if first:
+            row = lax.broadcasted_iota(jnp.int32, (size, 2 * size), 0)
+            col = lax.broadcasted_iota(jnp.int32, (size, 2 * size), 1)
+            for h in range(heads):
+                out_ref[h] = jnp.where(row == col, 1.0, 0.0).astype(bf16)
+        else:
+            out_ref[...] = near_ref[...]
+
+
+def turn(flag, own, far, near, first, last):
+    heads, size, width = own.shape
     return vmem_call(
-        compose_body,
-        jax.ShapeDtypeStruct(later.shape, bf16),
-        (later, first),
-        flops=2 * math.prod(later.shape) * later.shape[1],
-        moved=6 * math.prod(later.shape),
-    )
-
-
-def back_body(
-    order_ref, near_ref, far_ref, raised_ref, output_ref, gate_ref, gain_ref, weight_ref,
-    keep_ref, send_ref, normed,
-):
-    heads, count, size = raised_ref.shape
-    slab_count = order_ref.shape[0]
-    slab_rows = count // slab_count
-    for h in range(heads):
-        lanes = slice(h * size, (h + 1) * size)
-        state = dot(near_ref[h, :, :size], far_ref[h]) + near_ref[h, :, size:].astype(f32)
-        attended = dot(raised_ref[h], state.astype(bf16)) + output_ref[:, lanes]
-        power = jnp.sum(attended * attended, -1, keepdims=True) * (1.0 / size)
-        normed[:, lanes] = (
-            attended * lax.rsqrt(power + 1e-05) * gain_ref[...] * gate_ref[:, lanes]
-        ).astype(bf16)
-    ordered = jnp.concatenate(
-        [
-            normed[pl.ds(pl.multiple_of(order_ref[k] * slab_rows, 16), slab_rows), :]
-            for k in range(slab_count)
-        ],
-        axis=0,
-    )
-    total = dot(ordered, weight_ref[...])
-    half = keep_ref.shape[0]
-    keep_ref[...] = total[:half]
-    send_ref[...] = total[half:].astype(bf16)
+        functools.partial(turn_body, first, last),
+        (
+            jax.ShapeDtypeStruct((heads, size, size if last else width), bf16),
+            jax.ShapeDtypeStruct(own.shape, bf16),
+        ),
+        (flag, own, far, near),
+        scalars=1,
+        flops=4 * heads * size * size * width,
+        moved=10 * heads * size * width,
+    )
+
+
+def entry_body(flag_ref, near_ref, far_ref, state_ref):
+    heads, size, _ = near_ref.shape
+    for h in range(heads):
+        moved = dot(near_ref[h, :, :size], far_ref[h])
+        moved = jnp.where(flag_ref[0] == 1, moved, 0.0) + near_ref[h, :, size:].astype(f32)
+        state_ref[h] = moved.astype(bf16)
+
+
+def entry_state(pair):
+    heads, size, width = pair.shape
+    bits = bits_of(lax.axis_size("seq"))
+    here = lax.axis_index("seq").astype(jnp.int32)
+    shift, near = pair, pair
+    for i, bit in enumerate(bits[:-1]):
+        flag = (here & bit != 0).astype(jnp.int32)[None]
+        far = swapped(shift, "seq", bit)
+        shift, near = turn(flag, shift, far, near, i == 0, i == len(bits) - 2)
+    if not bits:
+        return jnp.zeros((heads, size, size), bf16)
+    if len(bits) == 1:
+        shift = pair[:, :, size:]
+        near = jnp.broadcast_to(jnp.eye(size, width, dtype=bf16), pair.shape)
+    flag = (here & bits[-1] != 0).astype(jnp.int32)[None]
+    return vmem_call(
+        entry_body,
+        jax.ShapeDtypeStruct((heads, size, size), bf16),
+        (flag, near, swapped(shift, "seq", bits[-1])),
+        scalars=1,
+        flops=2 * heads * size * size * size,
+        moved=8 * heads * size * size,
+    )
+
+
+def back_body(groups, place_ref, *refs):
+    state_refs = refs[:groups]
+    raised_ref, output_ref, gate_ref, gain_ref, weight_ref, keep_ref, *rest = refs[groups:]
+    normed = rest[-1]
+    size = gain_ref.shape[1]
+    slab_rows = keep_ref.shape[0]
+    group_heads = state_refs[0].shape[0]
+    for k in range(place_ref.shape[0]):
+        rows = pl.ds(pl.multiple_of(place_ref[k] * slab_rows, 16), slab_rows)
+        for h in range(raised_ref.shape[0]):
+            lanes = slice(h * size, (h + 1) * size)
+            state = state_refs[h // group_heads][h % group_heads]
+            attended = dot(raised_ref[h, rows, :], state) + output_ref[rows, lanes]
+            power = jnp.sum(attended * attended, -1, keepdims=True) * (1.0 / size)
+            normed[k * slab_rows : (k + 1) * slab_rows, lanes] = (
+                attended * lax.rsqrt(power + 1e-05) * gain_ref[...] * gate_ref[rows, lanes]
+            ).astype(bf16)
+    total = dot(normed[...], weight_ref[...])
+    keep_ref[...] = total[:slab_rows]
+    if len(rest) > 1:
+        rest[0][...] = total[slab_rows:].astype(bf16)
+
+
+def back(places, states, raised, output_rows, out_gate, gain, weight, slab_rows):
+    slab_count, width = places.shape[0], weight.shape[1]
+    shapes = [jax.ShapeDtypeStruct((slab_rows, width), f32)]
+    if slab_count > 1:
+        shapes.append(jax.ShapeDtypeStruct((slab_rows, width), bf16))
+    return vmem_call(
+        functools.partial(back_body, len(states)),
+        shapes,
+        (places, *states, raised, output_rows, out_gate, gain, weight),
+        scratch=[pltpu.VMEM((slab_count * slab_rows, weight.shape[0]), bf16)],
+        scalars=1,
+        flops=2 * slab_count * slab_rows * weight.shape[0] * width,
+        moved=2 * weight.shape[0] * width,
+    )
 
 
 def shards(
@@ -337,20 +397,23 @@
 ):
     heads, size = decay_log.shape[0], norm_gain.shape[0]
     channels = heads * size
-    devices, here = lax.axis_size("head"), lax.axis_index("head")
+    devices, here = lax.axis_size("head"), lax.axis_index("head").astype(jnp.int32)
+    order = jnp.arange(devices, dtype=jnp.int32) ^ here
+    weight = qkv_weight.transpose(1, 0, 2)
+    ready = vmem_call(
+        ready_body, jax.ShapeDtypeStruct((8, 128), f32), (weight,), moved=2 * weight.size
+    )
     slabs = slabs_of(hidden_in, "head")
     rim = rim_of(hidden_in, RIM)
-    order = jnp.arange(devices, dtype=jnp.int32) ^ here.astype(jnp.int32)
-    beta = jnp.pad(beta_weight, ((0, 0), (0, 128 - heads)))
-    small = jnp.concatenate([decay_down, gate_down, beta], axis=1)
     taps = conv_weight.astype(f32).reshape(-1, channels)
     rate = jnp.repeat(jnp.exp(decay_log), size)[None]
     pair, solved, attend, start, gate_low = front(
         order,
         rim,
         slabs,
-        qkv_weight.transpose(1, 0, 2),
-        small,
+        weight,
+        ready,
+        (decay_down, gate_down, beta_weight.T),
         taps,
         rate,
         dt_bias[None],
@@ -370,40 +433,22 @@
         flops=2 * heads * count * count * 2 * size,
         moved=4 * heads * count * count,
     )
-    blocks = lax.axis_size("seq")
-    near, far = jnp.zeros_like(pair), jnp.zeros((heads, size, size), bf16)
-    distance = 1
-    while distance < blocks:
-        if 2 * distance < blocks:
-            arrived = passed_along(pair, "seq", distance)
-            near = arrived if distance == 1 else compose(near, arrived)
-            pair = compose(pair, arrived)
-        else:
-            far = passed_along(pair[:, :, size:], "seq", distance)
-            if distance == 1:
-                near = jnp.concatenate([jnp.zeros_like(far), far], axis=2)
-        distance *= 2
-    order_out = jnp.asarray(reversed_order(devices), jnp.int32) ^ here.astype(jnp.int32)
-    half = count // 2 if devices > 1 else count
-    vm = pl.BlockSpec(memory_space=pltpu.VMEM)
-    keep, send = vmem_call(
-        back_body,
-        (
-            jax.ShapeDtypeStruct((half, out_weight.shape[1]), f32),
-            jax.ShapeDtypeStruct((half, out_weight.shape[1]), bf16),
-        ),
-        (order_out, near, far, raised, output_rows, out_gate, norm_gain[None], out_weight),
-        scratch=[pltpu.VMEM((count, channels), bf16)],
-        in_specs=[pl.BlockSpec(memory_space=pltpu.SMEM)] + [vm] * 7,
-        flops=2 * count * channels * out_weight.shape[1],
-        moved=2 * channels * out_weight.shape[1],
-    )
-    for bit in bits_of(devices):
-        keep = keep + swapped(send, "head", bit).astype(f32)
-        if 2 * bit < devices:
-            half = keep.shape[0] // 2
-            keep, send = keep[:half], keep[half:].astype(bf16)
-    return keep.astype(bf16)
+    step = max(heads // GROUPS, 1)
+    states = [entry_state(pair[h : h + step]) for h in range(0, heads, step)]
+    slab_rows = count // devices
+    sums = {}
+    for g in reversed(range(max(devices // 2, 1))):
+        places = jnp.asarray([2 * g, 2 * g + 1][:devices], jnp.int32) ^ here
+        keep, *send = back(
+            places, states, raised, output_rows, out_gate, norm_gain[None], out_weight, slab_rows
+        )
+        sums[g] = [keep] + [swapped(part, "head", 1).astype(f32) for part in send]
+    for bit in bits_of(devices)[1:]:
+        for g in sorted(sums):
+            if 2 * g & bit:
+                arrived = swapped(sum(sums.pop(g)).astype(bf16), "head", bit)
+                sums[g ^ bit // 2].append(arrived.astype(f32))
+    return sum(sums[0]).astype(bf16)
 
 
 def solution(mesh):

time: 75.5 us -> 80.7 us (1.069); the launches traced: 74 us -> 80 us
  local copies, waits for them, and re-layouts: 5.18 us -> 22.4 us
  waiting for transfers between devices: 25.4 us -> 19.9 us
  starting transfers between devices: 28.1 us -> 24.8 us
  other arithmetic: 2.52 us -> 0.91 us
    unnamed x21 -> x58, local copies, waits for them, and re-layouts: 4.16 us -> 20.8 us
    ppermute x3 -> x0, starting transfers between devices: 15.6 us -> none  [passed_along(): lax.ppermute(block, axis, [(i, i + distance) for i in range(size - distan...]
    ppermute x5 -> x13, starting transfers between devices: 9.79 us -> 23.5 us  [swapped(): lax.ppermute(block, axis, [(i, i ^ bit) for i in range(lax.axis_size(axis...]
    ppermute x3 -> x0, waiting for transfers between devices: 13.2 us -> none  [passed_along(): lax.ppermute(block, axis, [(i, i + distance) for i in range(size - distan...]
    ppermute x5 -> x13, waiting for transfers between devices: 12.2 us -> 19.9 us  [swapped(): lax.ppermute(block, axis, [(i, i ^ bit) for i in range(lax.axis_size(axis...]
    concatenate x1 -> x0, other arithmetic: 1.59 us -> none  [shards(): small = jnp.concatenate([decay_down, gate_down, beta], axis=1)]
    ppermute x4 -> x2, starting transfers between devices: 2.65 us -> 1.32 us  [rim_of(): rim = rim + lax.ppermute(tail, ('seq', 'head'), route)]
    pallas_call x6 -> x11, Pallas kernels: 12.5 us -> 11.7 us  [vmem_call(): pl.pallas_call(body, out_shape=out_shape, in_specs=[pl.BlockSpec(memory_s...]
  transfers between devices with their start and end apart: 12 -> 15, of which waited for: 6 -> 5; matrix products, arithmetic and copies ran while one was open for 4% -> 2% of each run, Pallas kernels for 1% -> 3%
where the time goes in v2:
time: 80.7 us; the launch traced here: 80 us
  starting transfers between devices  24.8 us (31%)
  local copies, waits for them, and re-layouts  22.4 us (28%)
  waiting for transfers between devices  19.9 us (25%)
  Pallas kernels  11.7 us (14%)
  other arithmetic  0.91 us (1%)
    ppermute x13, starting transfers between devices, swapped(): lax.ppermute(block, axis, [(i, i ^ bit) for i in range(lax.axis_size(axis...  23.5 us
    unnamed x58, local copies, waits for them, and re-layouts  20.8 us
    ppermute x13, waiting for transfers between devices, swapped(): lax.ppermute(block, axis, [(i, i ^ bit) for i in range(lax.axis_size(axis...  19.9 us
    pallas_call x11, Pallas kernels, vmem_call(): pl.pallas_call(body, out_shape=out_shape, in_specs=[pl.BlockSpec(memory_s...  11.7 us
  transfers between devices with their start and end apart: 15, of which 5 were waited for; matrix products, arithmetic and copies ran while one was open for 2% of the time, Pallas kernels for 3%

profile of v2, /device:TPU:0, one launch (start us, length us, event | category | flops | bytes accessed | tf_op | source)
XLA Modules:
  0.0 80.0 jit_solution(12752056744458127645)
XLA Ops:
  0.0 3.0 %collective-permute-start.4 = (bf16[64,2304]{1,0:T(8,128)(2,1)}, bf16[64,2304]{1,0:T(8,128)(2,1)S(1)}, u32[]{:S(2)}, u32[]{:S(2)}) collective-permute-start(bf16[64,2304]{1,0:T(8,128)(2,1)} %refs_0_.1), channel_id=1, source_target_pairs={{0,2},{1,3},{2,0},{3,1},{4,6},{5,7},{6,4},{7,5},{8,10},{9,11},{10,... | collective-permute-start | bytes 884744 | tf_op jit(solution)/shard_map/ppermute | solution.py:24
  3.0 0.0 collective-permute-start.3
  3.0 7.2 %collective-permute-done.4.refs_2_ = bf16[64,2304]{1,0:T(8,128)(2,1)S(1)} collective-permute-done((bf16[64,2304]{1,0:T(8,128)(2,1)}, bf16[64,2304]{1,0:T(8,128)(2,1)S(1)}, u32[]{:S(2)}, u32[]{:S(2)}) %collective-permute-start.4) | collective-permute-done | bytes 294944 | tf_op jit(solution)/shard_map/ppermute | solution.py:24
  10.2 0.0 collective-permute-start.5
  10.2 1.0 %slice.9 = bf16[16,2304]{1,0:T(8,128)(2,1)S(1)} slice(bf16[64,2304]{1,0:T(8,128)(2,1)} %refs_0_.1), slice={[48:64], [0:2304]} | slice | bytes 147456 | tf_op jit(solution)/shard_map/slice | solution.py:43
  11.2 0.7 collective-permute-start
  11.9 0.7 collective-permute-start.1
  12.5 0.0 copy-start
  12.6 3.0 %copy-done = bf16[2304,3,512]{2,0,1:T(8,128)(2,1)S(1)} copy-done((bf16[2304,3,512]{2,0,1:T(8,128)(2,1)S(1)}, bf16[2304,3,512]{2,0,1:T(8,128)(2,1)}, u32[]{:S(2)}) %copy-start) | copy-done | bytes 7077912
  15.6 0.0 copy-start.27
  15.6 0.6 reshape.11.refs_9_
  16.2 0.0 collective-permute-done.1
  16.2 0.5 collective-permute-start.2
  16.7 0.9 %collective-permute-done.2 = bf16[16,2304]{1,0:T(8,128)(2,1)S(1)} collective-permute-done((bf16[16,2304]{1,0:T(8,128)(2,1)S(1)}, bf16[16,2304]{1,0:T(8,128)(2,1)S(1)}, u32[]{:S(2)}, u32[]{:S(2)}) %collective-permute-start.2) | collective-permute-done | bytes 73760 | tf_op jit(solution)/shard_map/ppermute | solution.py:24
  17.7 0.0 collective-permute-done.3.refs_1_
  17.7 0.0 copy-start.14
  17.7 0.7 copy-done.14
  18.4 0.7 copy-done.16
  19.1 0.1 broadcast_in_dim.34
  19.2 0.0 copy-start.1
  19.2 3.0 %copy-done.1 = bf16[2304,3,512]{2,0,1:T(8,128)(2,1)S(1)} copy-done((bf16[2304,3,512]{2,0,1:T(8,128)(2,1)S(1)}, bf16[2304,3,512]{2,0,1:T(8,128)(2,1)}, u32[]{:S(2)}) %copy-start.1) | copy-done | bytes 7077912
  22.2 1.0 %copy-done.11 = bf16[64,2304]{1,0:T(8,128)(2,1)S(1)} copy-done((bf16[64,2304]{1,0:T(8,128)(2,1)S(1)}, bf16[64,2304]{1,0:T(8,128)(2,1)}, u32[]{:S(2)}) %copy-start.11) | copy-done | bytes 294936
  23.2 1.0 %copy-done.13 = bf16[64,2304]{1,0:T(8,128)(2,1)S(1)} copy-done((bf16[64,2304]{1,0:T(8,128)(2,1)S(1)}, bf16[64,2304]{1,0:T(8,128)(2,1)}, u32[]{:S(2)}) %copy-start.13) | copy-done | bytes 294936
  24.2 1.0 %copy-done.15 = bf16[64,2304]{1,0:T(8,128)(2,1)S(1)} copy-done((bf16[64,2304]{1,0:T(8,128)(2,1)S(1)}, bf16[64,2304]{1,0:T(8,128)(2,1)}, u32[]{:S(2)}) %copy-start.15) | copy-done | bytes 294936
  25.1 1.0 %copy-done.17 = bf16[64,2304]{1,0:T(8,128)(2,1)S(1)} copy-done((bf16[64,2304]{1,0:T(8,128)(2,1)S(1)}, bf16[64,2304]{1,0:T(8,128)(2,1)}, u32[]{:S(2)}) %copy-start.17) | copy-done | bytes 294936
  26.1 0.9 %copy-done.18 = bf16[128,512]{1,0:T(8,128)(2,1)S(1)} copy-done((bf16[128,512]{1,0:T(8,128)(2,1)S(1)}, bf16[128,512]{1,0:T(8,128)(2,1)}, u32[]{:S(2)}) %copy-start.18) | copy-done | bytes 131096
  27.0 0.8 copy-done.19
  27.7 0.7 copy-done.23
  28.5 7.8 %shard_map.137 = (bf16[4,128,256]{2,1,0:T(8,128)(2,1)S(1)}, bf16[4,256,256]{2,1,0:T(8,128)(2,1)S(1)}, bf16[4,256,256]{2,1,0:T(8,128)(2,1)S(1)}, f32[4,256,128]{2,1,0:T(8,128)S(1)}, bf16[256,128]{1,0:T(8,128)(2,1)S(1)}) custom-call(s32[4]{0:T(128)S(1)} %iota_xor_fusion.order_ref, bf16[16,2304]{1,0:T(8,128)(2,1)S(1)} %add.16.rim_ref, ...), custom_call_target="tpu_custom_call" | custom-call | flops 2415919104 | bytes 9437184 | tf_op jit(solution)/shard_map/pallas_call | solution.py:53
  36.3 0.8 copy-done.7
  37.0 0.8 copy-done.9
  37.8 0.6 copy-done.21
  38.5 2.8 %collective-permute-start.6 = (bf16[2,128,256]{2,1,0:T(8,128)(2,1)S(1)}, bf16[2,128,256]{2,1,0:T(8,128)(2,1)S(1)}, u32[]{:S(2)}, u32[]{:S(2)}) collective-permute-start(bf16[2,128,256]{2,1,0:T(8,128)(2,1)S(1)} %get-tuple-element.46.own_ref.near_ref), channel_id=1, source_target_pairs={{0,4},{4,0},{8,12},{12,8},{16,20},{20,16},{24,28},{28,24},{1,5},{5... | collective-permute-start | bytes 393224 | tf_op jit(solution)/shard_map/ppermute | solution.py:24
  41.3 0.7 collective-permute-start.9
  42.0 3.6 %collective-permute-done.6.far_ref = bf16[2,128,256]{2,1,0:T(8,128)(2,1)S(1)} collective-permute-done((bf16[2,128,256]{2,1,0:T(8,128)(2,1)S(1)}, bf16[2,128,256]{2,1,0:T(8,128)(2,1)S(1)}, u32[]{:S(2)}, u32[]{:S(2)}) %collective-permute-start.6) | collective-permute-done | bytes 131104 | tf_op jit(solution)/shard_map/ppermute | solution.py:24
  45.7 0.2 shard_map.138
  45.8 3.0 %collective-permute-start.7 = (bf16[2,128,256]{2,1,0:T(8,128)(2,1)S(1)}, bf16[2,128,256]{2,1,0:T(8,128)(2,1)S(1)}, u32[]{:S(2)}, u32[]{:S(2)}) collective-permute-start(bf16[2,128,256]{2,1,0:T(8,128)(2,1)S(1)} %get-tuple-element.26.own_ref), channel_id=1, source_target_pairs={{0,8},{4,12},{8,0},{12,4},{16,24},{20,28},{24,16},{28,20},{1,9},{5... | collective-permute-start | bytes 393224 | tf_op jit(solution)/shard_map/ppermute | solution.py:24
  48.8 0.0 collective-permute-done.9.far_ref
  48.8 0.2 shard_map.141
  49.0 2.1 %collective-permute-start.10 = (bf16[2,128,256]{2,1,0:T(8,128)(2,1)S(1)}, bf16[2,128,256]{2,1,0:T(8,128)(2,1)S(1)}, u32[]{:S(2)}, u32[]{:S(2)}) collective-permute-start(bf16[2,128,256]{2,1,0:T(8,128)(2,1)S(1)} %get-tuple-element.30.own_ref), channel_id=1, source_target_pairs={{0,8},{4,12},{8,0},{12,4},{16,24},{20,28},{24,16},{28,20},{1,9},{5... | collective-permute-start | bytes 393224 | tf_op jit(solution)/shard_map/ppermute | solution.py:24
  51.1 1.0 %collective-permute-done.7.far_ref = bf16[2,128,256]{2,1,0:T(8,128)(2,1)S(1)} collective-permute-done((bf16[2,128,256]{2,1,0:T(8,128)(2,1)S(1)}, bf16[2,128,256]{2,1,0:T(8,128)(2,1)S(1)}, u32[]{:S(2)}, u32[]{:S(2)}) %collective-permute-start.7) | collective-permute-done | bytes 131104 | tf_op jit(solution)/shard_map/ppermute | solution.py:24
  52.1 0.2 shard_map.139
  52.2 3.4 %collective-permute-start.8 = (bf16[2,128,128]{2,1,0:T(8,128)(2,1)S(1)}, bf16[2,128,128]{2,1,0:T(8,128)(2,1)S(1)}, u32[]{:S(2)}, u32[]{:S(2)}) collective-permute-start(bf16[2,128,128]{2,1,0:T(8,128)(2,1)S(1)} %get-tuple-element.29), channel_id=1, source_target_pairs={{0,16},{4,20},{8,24},{12,28},{16,0},{20,4},{24,8},{28,12},{1,17},{... | collective-permute-start | bytes 196616 | tf_op jit(solution)/shard_map/ppermute | solution.py:24
  55.6 0.0 collective-permute-done.10.far_ref
  55.6 0.2 shard_map.142
  55.8 2.7 %collective-permute-start.11 = (bf16[2,128,128]{2,1,0:T(8,128)(2,1)S(1)}, bf16[2,128,128]{2,1,0:T(8,128)(2,1)S(1)}, u32[]{:S(2)}, u32[]{:S(2)}) collective-permute-start(bf16[2,128,128]{2,1,0:T(8,128)(2,1)S(1)} %get-tuple-element.33), channel_id=1, source_target_pairs={{0,16},{4,20},{8,24},{12,28},{16,0},{20,4},{24,8},{28,12},{1,17},{... | collective-permute-start | bytes 196616 | tf_op jit(solution)/shard_map/ppermute | solution.py:24
  58.6 1.0 %copy-done.6 = bf16[4,256,256]{2,1,0:T(8,128)(2,1)S(1)} copy-done((bf16[4,256,256]{2,1,0:T(8,128)(2,1)S(1)}, bf16[4,256,256]{2,1,0:T(8,128)(2,1)}, u32[]{:S(2)}) %copy-start.6) | copy-done | bytes 524312
  59.6 1.0 %copy-done.8 = bf16[4,256,256]{2,1,0:T(8,128)(2,1)S(1)} copy-done((bf16[4,256,256]{2,1,0:T(8,128)(2,1)S(1)}, bf16[4,256,256]{2,1,0:T(8,128)(2,1)}, u32[]{:S(2)}) %copy-start.8) | copy-done | bytes 524312
  60.7 1.0 %copy-done.10 = f32[4,256,128]{2,1,0:T(8,128)S(1)} copy-done((f32[4,256,128]{2,1,0:T(8,128)S(1)}, f32[4,256,128]{2,1,0:T(8,128)}, u32[]{:S(2)}) %copy-start.10) | copy-done | bytes 524312
  61.7 0.9 %copy-done.20 = bf16[128,512]{1,0:T(8,128)(2,1)S(1)} copy-done((bf16[128,512]{1,0:T(8,128)(2,1)S(1)}, bf16[128,512]{1,0:T(8,128)(2,1)}, u32[]{:S(2)}) %copy-start.20) | copy-done | bytes 131096
  62.6 0.8 %copy-done.22 = bf16[256,128]{1,0:T(8,128)(2,1)S(1)} copy-done((bf16[256,128]{1,0:T(8,128)(2,1)S(1)}, bf16[256,128]{1,0:T(8,128)(2,1)}, u32[]{:S(2)}) %copy-start.22) | copy-done | bytes 65560
  63.4 0.4 shard_map.144
  63.8 0.2 shard_map.140.refs_0_
  64.0 0.0 collective-permute-done.11.far_ref
  64.0 0.2 shard_map.143.refs_1_
  64.2 1.3 %shard_map.146 = (f32[64,2304]{1,0:T(8,128)S(1)}, bf16[64,2304]{1,0:T(8,128)(2,1)S(1)}) custom-call(s32[2]{0:T(128)S(1)} %get-tuple-element.48.place_ref, bf16[2,128,128]{2,1,0:T(8,128)(2,1)S(1)} %shard_map.140.refs_0_, bf16[2,128,128]{2,1,0:T(8,128)(2,1)S(1)} %shard_map.143.refs_1_, bf16[4,256,128]{2,1,0:T(8,128)(2,1)S(1)} %get-tuple-element.38.refs_2_, ...), custom_call_target="tpu_custom_call" | custom-call | flops 301989888 | bytes 2359296 | tf_op jit(solution)/shard_map/pallas_call | solution.py:53
  65.4 0.1 collective-permute-start.13
  65.5 1.3 %shard_map.145 = (f32[64,2304]{1,0:T(8,128)S(1)}, bf16[64,2304]{1,0:T(8,128)(2,1)S(1)}) custom-call(s32[2]{0:T(128)S(1)} %get-tuple-element.47.place_ref, bf16[2,128,128]{2,1,0:T(8,128)(2,1)S(1)} %shard_map.140.refs_0_, bf16[2,128,128]{2,1,0:T(8,128)(2,1)S(1)} %shard_map.143.refs_1_, bf16[4,256,128]{2,1,0:T(8,128)(2,1)S(1)} %get-tuple-element.38.refs_2_, ...), custom_call_target="tpu_custom_call" | custom-call | flops 301989888 | bytes 2359296 | tf_op jit(solution)/shard_map/pallas_call | solution.py:53
  66.8 0.6 collective-permute-start.12
  67.3 0.0 collective-permute-done.13
  67.3 0.1 add_convert_fusion.1
  67.4 4.6 %collective-permute-start.14 = (bf16[64,2304]{1,0:T(8,128)(2,1)S(1)}, bf16[64,2304]{1,0:T(8,128)(2,1)S(1)}, u32[]{:S(2)}, u32[]{:S(2)}) collective-permute-start(bf16[64,2304]{1,0:T(8,128)(2,1)S(1)} %add_convert_fusion.1), channel_id=1, source_target_pairs={{0,2},{1,3},{2,0},{3,1},{4,6},{5,7},{6,4},{7,5},{8,10},{9,11},{10,... | collective-permute-start | bytes 884744 | tf_op jit(solution)/shard_map/ppermute | solution.py:24
  72.0 7.2 %collective-permute-done.14 = bf16[64,2304]{1,0:T(8,128)(2,1)S(1)} collective-permute-done((bf16[64,2304]{1,0:T(8,128)(2,1)S(1)}, bf16[64,2304]{1,0:T(8,128)(2,1)S(1)}, u32[]{:S(2)}, u32[]{:S(2)}) %collective-permute-start.14) | collective-permute-done | bytes 294944 | tf_op jit(solution)/shard_map/ppermute | solution.py:24
  79.2 0.8 %add_convert_fusion = bf16[64,2304]{1,0:T(8,128)(2,1)} fusion(bf16[64,2304]{1,0:T(8,128)(2,1)S(1)} %collective-permute-done.14, f32[64,2304]{1,0:T(8,128)S(1)} %get-tuple-element.41, bf16[64,2304]{1,0:T(8,128)(2,1)S(1)} %collective-permute-done.12), kind=kLoop, calls=%fused_computation | loop fusion | flops 737280 | bytes 1474560 | tf_op jit(solution)/shard_map/convert_element_type | solution.py:451
  (46 shorter events, 0.1 us)
Async XLA Ops:
  0.0 15.6 %copy-start.26 = (bf16[3,4,512]{2,1,0:T(4,128)(2,1)S(1)}, bf16[3,4,512]{2,1,0:T(4,128)(2,1)}, u32[]{:S(2)}) copy-start(bf16[3,4,512]{2,1,0:T(4,128)(2,1)} %param.16) | copy-start | bytes 36868
  0.0 16.2 %copy-start.28 = (f32[4]{0:T(128)S(1)}, f32[4]{0:T(128)}, u32[]{:S(2)}) copy-start(f32[4]{0:T(128)} %param.17) | copy-start | bytes 52
  0.0 19.2 %copy-start.25 = (f32[512]{0:T(512)S(1)}, f32[512]{0:T(512)}, u32[]{:S(2)}) copy-start(f32[512]{0:T(512)} %param.18) | copy-start | bytes 6148
  0.0 10.2 %collective-permute-start.4 = (bf16[64,2304]{1,0:T(8,128)(2,1)}, bf16[64,2304]{1,0:T(8,128)(2,1)S(1)}, u32[]{:S(2)}, u32[]{:S(2)}) collective-permute-start(bf16[64,2304]{1,0:T(8,128)(2,1)} %refs_0_.1), channel_id=1, source_target_pairs={{0,2},{1,3},{2,0},{3,1},{4,6},{5,7},{6,4},{7,5},{8,10},{9,11},{10,... | collective-permute-start | bytes 884744 | tf_op jit(solution)/shard_map/ppermute | solution.py:24
  3.0 14.7 %collective-permute-start.3 = (bf16[64,2304]{1,0:T(8,128)(2,1)}, bf16[64,2304]{1,0:T(8,128)(2,1)S(1)}, u32[]{:S(2)}, u32[]{:S(2)}) collective-permute-start(bf16[64,2304]{1,0:T(8,128)(2,1)} %refs_0_.1), channel_id=1, source_target_pairs={{0,1},{1,0},{2,3},{3,2},{4,5},{5,4},{6,7},{7,6},{8,9},{9,8},{10,11... | collective-permute-start | bytes 884744 | tf_op jit(solution)/shard_map/ppermute | solution.py:24
  10.2 9.0 %copy-start.12 = (bf16[64,2304]{1,0:T(8,128)(2,1)}, bf16[64,2304]{1,0:T(8,128)(2,1)S(1)}, u32[]{:S(2)}) copy-start(bf16[64,2304]{1,0:T(8,128)(2,1)S(1)} %collective-permute-done.4.refs_2_) | copy-start | bytes 884740
  10.2 8.2 %collective-permute-start.5 = (bf16[64,2304]{1,0:T(8,128)(2,1)S(1)}, bf16[64,2304]{1,0:T(8,128)(2,1)S(1)}, u32[]{:S(2)}, u32[]{:S(2)}) collective-permute-start(bf16[64,2304]{1,0:T(8,128)(2,1)S(1)} %collective-permute-done.4.refs_2_), channel_id=1, source_target_pairs={{0,1},{1,0},{2,3},{3,2},{4,5},{5,4},{6,7},{7,6},{8,9},{9,8},{10,11... | collective-permute-start | bytes 884744 | tf_op jit(solution)/shard_map/ppermute | solution.py:24
  11.2 5.0 %collective-permute-start = (bf16[16,2304]{1,0:T(8,128)(2,1)S(1)}, bf16[16,2304]{1,0:T(8,128)(2,1)S(1)}, u32[]{:S(2)}, u32[]{:S(2)}) collective-permute-start(bf16[16,2304]{1,0:T(8,128)(2,1)S(1)} %slice.9), channel_id=1, source_target_pairs={{3,5},{7,9},{11,13},{15,17},{19,21},{23,25},{27,29}} | collective-permute-start | bytes 221192 | tf_op jit(solution)/shard_map/ppermute | solution.py:47
  11.9 4.3 %collective-permute-start.1 = (bf16[16,2304]{1,0:T(8,128)(2,1)S(1)}, bf16[16,2304]{1,0:T(8,128)(2,1)S(1)}, u32[]{:S(2)}, u32[]{:S(2)}) collective-permute-start(bf16[16,2304]{1,0:T(8,128)(2,1)S(1)} %slice.9), channel_id=1, source_target_pairs={{3,7},{7,11},{11,15},{15,19},{19,23},{23,27},{27,31}} | collective-permute-start | bytes 221192 | tf_op jit(solution)/shard_map/ppermute | solution.py:47
  12.5 3.0 %copy-start = (bf16[2304,3,512]{2,0,1:T(8,128)(2,1)S(1)}, bf16[2304,3,512]{2,0,1:T(8,128)(2,1)}, u32[]{:S(2)}) copy-start(bf16[2304,3,512]{2,0,1:T(8,128)(2,1)} %param.15) | copy-start | bytes 21233668
  15.6 3.7 %copy-start.3 = (bf16[2304,128]{1,0:T(8,128)(2,1)S(1)}, bf16[2304,128]{1,0:T(8,128)(2,1)}, u32[]{:S(2)}) copy-start(bf16[2304,128]{1,0:T(8,128)(2,1)} %refs_6_.3) | copy-start | bytes 1769476
  15.6 3.7 %copy-start.4 = (bf16[2304,128]{1,0:T(8,128)(2,1)S(1)}, bf16[2304,128]{1,0:T(8,128)(2,1)}, u32[]{:S(2)}) copy-start(bf16[2304,128]{1,0:T(8,128)(2,1)} %refs_7_.1) | copy-start | bytes 1769476
  15.6 43.0 %copy-start.27 = (s32[2]{0:T(128)S(1)}, s32[2]{0:T(128)}, u32[]{:S(2)}) copy-start(s32[2]{0:T(128)} %constant.21.clone) | copy-start | bytes 28
  16.2 1.4 %collective-permute-start.2 = (bf16[16,2304]{1,0:T(8,128)(2,1)S(1)}, bf16[16,2304]{1,0:T(8,128)(2,1)S(1)}, u32[]{:S(2)}, u32[]{:S(2)}) collective-permute-start(bf16[16,2304]{1,0:T(8,128)(2,1)S(1)} %add.15), channel_id=1, source_target_pairs={{0,1},{1,0},{2,3},{3,2},{4,5},{5,4},{6,7},{7,6},{8,9},{9,8},{10,11... | collective-permute-start | bytes 221192 | tf_op jit(solution)/shard_map/ppermute | solution.py:24
  17.7 0.7 copy-start.14
  18.4 0.7 copy-start.16
  19.2 3.0 %copy-start.1 = (bf16[2304,3,512]{2,0,1:T(8,128)(2,1)S(1)}, bf16[2304,3,512]{2,0,1:T(8,128)(2,1)}, u32[]{:S(2)}) copy-start(bf16[2304,3,512]{2,0,1:T(8,128)(2,1)} %param.15) | copy-start | bytes 21233668
  22.2 1.0 %copy-start.11 = (bf16[64,2304]{1,0:T(8,128)(2,1)S(1)}, bf16[64,2304]{1,0:T(8,128)(2,1)}, u32[]{:S(2)}) copy-start(bf16[64,2304]{1,0:T(8,128)(2,1)} %refs_0_.1) | copy-start | bytes 884740
  23.2 1.0 %copy-start.13 = (bf16[64,2304]{1,0:T(8,128)(2,1)S(1)}, bf16[64,2304]{1,0:T(8,128)(2,1)}, u32[]{:S(2)}) copy-start(bf16[64,2304]{1,0:T(8,128)(2,1)} %copy-done.12) | copy-start | bytes 884740
  24.1 1.0 %copy-start.15 = (bf16[64,2304]{1,0:T(8,128)(2,1)S(1)}, bf16[64,2304]{1,0:T(8,128)(2,1)}, u32[]{:S(2)}) copy-start(bf16[64,2304]{1,0:T(8,128)(2,1)} %copy-done.14) | copy-start | bytes 884740
  25.1 1.0 %copy-start.17 = (bf16[64,2304]{1,0:T(8,128)(2,1)S(1)}, bf16[64,2304]{1,0:T(8,128)(2,1)}, u32[]{:S(2)}) copy-start(bf16[64,2304]{1,0:T(8,128)(2,1)} %copy-done.16) | copy-start | bytes 884740
  26.1 0.9 %copy-start.18 = (bf16[128,512]{1,0:T(8,128)(2,1)S(1)}, bf16[128,512]{1,0:T(8,128)(2,1)}, u32[]{:S(2)}) copy-start(bf16[128,512]{1,0:T(8,128)(2,1)} %refs_12_.1) | copy-start | bytes 393220
  27.0 0.8 copy-start.19
  27.7 0.7 copy-start.23
  28.5 35.7 %copy-start.2 = (bf16[512,2304]{1,0:T(8,128)(2,1)S(1)}, bf16[512,2304]{1,0:T(8,128)(2,1)}, u32[]{:S(2)}) copy-start(bf16[512,2304]{1,0:T(8,128)(2,1)} %refs_6_.5) | copy-start | bytes 7077892
  28.5 35.7 %copy-start.24 = (f32[128]{0:T(128)S(1)}, f32[128]{0:T(128)}, u32[]{:S(2)}) copy-start(f32[128]{0:T(128)} %param.24) | copy-start | bytes 1540
  36.3 0.8 copy-start.7
  37.0 0.8 copy-start.9
  37.8 0.6 copy-start.21
  38.5 2.8 %copy-start.5 = (bf16[4,256,256]{2,1,0:T(8,128)(2,1)}, bf16[4,256,256]{2,1,0:T(8,128)(2,1)S(1)}, u32[]{:S(2)}) copy-start(bf16[4,256,256]{2,1,0:T(8,128)(2,1)S(1)} %get-tuple-element.35.solved_ref) | copy-start | bytes 1572868
  38.5 7.2 %collective-permute-start.6 = (bf16[2,128,256]{2,1,0:T(8,128)(2,1)S(1)}, bf16[2,128,256]{2,1,0:T(8,128)(2,1)S(1)}, u32[]{:S(2)}, u32[]{:S(2)}) collective-permute-start(bf16[2,128,256]{2,1,0:T(8,128)(2,1)S(1)} %get-tuple-element.46.own_ref.near_ref), channel_id=1, source_target_pairs={{0,4},{4,0},{8,12},{12,8},{16,20},{20,16},{24,28},{28,24},{1,5},{5... | collective-permute-start | bytes 393224 | tf_op jit(solution)/shard_map/ppermute | solution.py:24
  41.3 7.5 %collective-permute-start.9 = (bf16[2,128,256]{2,1,0:T(8,128)(2,1)S(1)}, bf16[2,128,256]{2,1,0:T(8,128)(2,1)S(1)}, u32[]{:S(2)}, u32[]{:S(2)}) collective-permute-start(bf16[2,128,256]{2,1,0:T(8,128)(2,1)S(1)} %get-tuple-element.45.own_ref.near_ref), channel_id=1, source_target_pairs={{0,4},{4,0},{8,12},{12,8},{16,20},{20,16},{24,28},{28,24},{1,5},{5... | collective-permute-start | bytes 393224 | tf_op jit(solution)/shard_map/ppermute | solution.py:24
  45.8 6.2 %collective-permute-start.7 = (bf16[2,128,256]{2,1,0:T(8,128)(2,1)S(1)}, bf16[2,128,256]{2,1,0:T(8,128)(2,1)S(1)}, u32[]{:S(2)}, u32[]{:S(2)}) collective-permute-start(bf16[2,128,256]{2,1,0:T(8,128)(2,1)S(1)} %get-tuple-element.26.own_ref), channel_id=1, source_target_pairs={{0,8},{4,12},{8,0},{12,4},{16,24},{20,28},{24,16},{28,20},{1,9},{5... | collective-permute-start | bytes 393224 | tf_op jit(solution)/shard_map/ppermute | solution.py:24
  49.0 6.6 %collective-permute-start.10 = (bf16[2,128,256]{2,1,0:T(8,128)(2,1)S(1)}, bf16[2,128,256]{2,1,0:T(8,128)(2,1)S(1)}, u32[]{:S(2)}, u32[]{:S(2)}) collective-permute-start(bf16[2,128,256]{2,1,0:T(8,128)(2,1)S(1)} %get-tuple-element.30.own_ref), channel_id=1, source_target_pairs={{0,8},{4,12},{8,0},{12,4},{16,24},{20,28},{24,16},{28,20},{1,9},{5... | collective-permute-start | bytes 393224 | tf_op jit(solution)/shard_map/ppermute | solution.py:24
  52.2 11.6 %collective-permute-start.8 = (bf16[2,128,128]{2,1,0:T(8,128)(2,1)S(1)}, bf16[2,128,128]{2,1,0:T(8,128)(2,1)S(1)}, u32[]{:S(2)}, u32[]{:S(2)}) collective-permute-start(bf16[2,128,128]{2,1,0:T(8,128)(2,1)S(1)} %get-tuple-element.29), channel_id=1, source_target_pairs={{0,16},{4,20},{8,24},{12,28},{16,0},{20,4},{24,8},{28,12},{1,17},{... | collective-permute-start | bytes 196616 | tf_op jit(solution)/shard_map/ppermute | solution.py:24
  55.8 8.2 %collective-permute-start.11 = (bf16[2,128,128]{2,1,0:T(8,128)(2,1)S(1)}, bf16[2,128,128]{2,1,0:T(8,128)(2,1)S(1)}, u32[]{:S(2)}, u32[]{:S(2)}) collective-permute-start(bf16[2,128,128]{2,1,0:T(8,128)(2,1)S(1)} %get-tuple-element.33), channel_id=1, source_target_pairs={{0,16},{4,20},{8,24},{12,28},{16,0},{20,4},{24,8},{28,12},{1,17},{... | collective-permute-start | bytes 196616 | tf_op jit(solution)/shard_map/ppermute | solution.py:24
  58.6 1.0 %copy-start.6 = (bf16[4,256,256]{2,1,0:T(8,128)(2,1)S(1)}, bf16[4,256,256]{2,1,0:T(8,128)(2,1)}, u32[]{:S(2)}) copy-start(bf16[4,256,256]{2,1,0:T(8,128)(2,1)} %copy-done.5) | copy-start | bytes 1572868
  59.6 1.0 %copy-start.8 = (bf16[4,256,256]{2,1,0:T(8,128)(2,1)S(1)}, bf16[4,256,256]{2,1,0:T(8,128)(2,1)}, u32[]{:S(2)}) copy-start(bf16[4,256,256]{2,1,0:T(8,128)(2,1)} %copy-done.7) | copy-start | bytes 1572868
  60.7 1.0 %copy-start.10 = (f32[4,256,128]{2,1,0:T(8,128)S(1)}, f32[4,256,128]{2,1,0:T(8,128)}, u32[]{:S(2)}) copy-start(f32[4,256,128]{2,1,0:T(8,128)} %copy-done.9) | copy-start | bytes 1572868
  61.7 0.9 %copy-start.20 = (bf16[128,512]{1,0:T(8,128)(2,1)S(1)}, bf16[128,512]{1,0:T(8,128)(2,1)}, u32[]{:S(2)}) copy-start(bf16[128,512]{1,0:T(8,128)(2,1)} %up_ref.1) | copy-start | bytes 393220
  62.6 0.8 %copy-start.22 = (bf16[256,128]{1,0:T(8,128)(2,1)S(1)}, bf16[256,128]{1,0:T(8,128)(2,1)}, u32[]{:S(2)}) copy-start(bf16[256,128]{1,0:T(8,128)(2,1)} %copy-done.21) | copy-start | bytes 196612
  65.4 1.9 %collective-permute-start.13 = (bf16[64,2304]{1,0:T(8,128)(2,1)S(1)}, bf16[64,2304]{1,0:T(8,128)(2,1)S(1)}, u32[]{:S(2)}, u32[]{:S(2)}) collective-permute-start(bf16[64,2304]{1,0:T(8,128)(2,1)S(1)} %get-tuple-element.44), channel_id=1, source_target_pairs={{0,1},{1,0},{2,3},{3,2},{4,5},{5,4},{6,7},{7,6},{8,9},{9,8},{10,11... | collective-permute-start | bytes 884744 | tf_op jit(solution)/shard_map/ppermute | solution.py:24
  66.8 5.2 %collective-permute-start.12 = (bf16[64,2304]{1,0:T(8,128)(2,1)S(1)}, bf16[64,2304]{1,0:T(8,128)(2,1)S(1)}, u32[]{:S(2)}, u32[]{:S(2)}) collective-permute-start(bf16[64,2304]{1,0:T(8,128)(2,1)S(1)} %get-tuple-element.42), channel_id=1, source_target_pairs={{0,1},{1,0},{2,3},{3,2},{4,5},{5,4},{6,7},{7,6},{8,9},{9,8},{10,11... | collective-permute-start | bytes 884744 | tf_op jit(solution)/shard_map/ppermute | solution.py:24
  67.4 11.8 %collective-permute-start.14 = (bf16[64,2304]{1,0:T(8,128)(2,1)S(1)}, bf16[64,2304]{1,0:T(8,128)(2,1)S(1)}, u32[]{:S(2)}, u32[]{:S(2)}) collective-permute-start(bf16[64,2304]{1,0:T(8,128)(2,1)S(1)} %add_convert_fusion.1), channel_id=1, source_target_pairs={{0,2},{1,3},{2,0},{3,1},{4,6},{5,7},{6,4},{7,5},{8,10},{9,11},{10,... | collective-permute-start | bytes 884744 | tf_op jit(solution)/shard_map/ppermute | solution.py:24

commit v3 on v2

v3 whole, which is shorter than its diff:
```python
import functools
import math

import jax
import jax.numpy as jnp
from jax import lax
from jax.experimental import pallas as pl
from jax.experimental.pallas import tpu as pltpu
from jax.sharding import PartitionSpec as P

RIM = 16
BASE = 16
MIB = 1024 * 1024
f32 = jnp.float32
bf16 = jnp.bfloat16


def dot(left, right, contract=((1,), (0,))):
    return lax.dot_general(left, right, (contract, ((), ())), preferred_element_type=f32)


def swapped(block, axis, bit):
    return lax.ppermute(block, axis, [(i, i ^ bit) for i in range(lax.axis_size(axis))])


def bits_of(size):
    assert size & (size - 1) == 0
    return [1 << i for i in range(size.bit_length() - 1)]


def gathered(own, row_count):
    heads, seqs = lax.axis_size("head"), lax.axis_size("seq")
    slabs = {0: own}
    for bit in reversed(bits_of(heads)[1:]):
        for k in sorted(slabs):
            slabs[k ^ bit] = swapped(slabs[k], "head", bit)
    tail = own[own.shape[0] - row_count :]
    rim = jnp.zeros_like(tail)
    for k in range(min(1, heads - 1), heads, 2):
        route = [(s * heads + heads - 1, (s + 1) * heads + k) for s in range(seqs - 1)]
        rim = rim + lax.ppermute(tail, ("seq", "head"), route)
    if heads > 1:
        slabs[1] = swapped(own, "head", 1)
        arrived = [k for k in sorted(slabs) if k > 1]
        moved, rim = lax.optimization_barrier(([slabs[k] for k in arrived], rim))
        for k, slab in zip(arrived, moved):
            slabs[k], slabs[k ^ 1] = slab, swapped(slab, "head", 1)
        rim = rim + swapped(rim, "head", 1)
    return [slabs[k] for k in range(heads)], rim


def vmem_call(body, out_shape, args, scratch=(), hbm=0, grant=4, flops=0, moved=0):
    here = len(args) - hbm
    args = [pltpu.with_memory_space_constraint(a, pltpu.HBM) if i >= here else a for i, a in enumerate(args)]
    spaces = [pltpu.VMEM] * here + [pltpu.HBM] * hbm
    return pl.pallas_call(
        body,
        out_shape=out_shape,
        in_specs=[pl.BlockSpec(memory_space=space) for space in spaces],
        out_specs=jax.tree.map(lambda _: pl.BlockSpec(memory_space=pltpu.VMEM), out_shape),
        scratch_shapes=list(scratch),
        compiler_params=pltpu.CompilerParams(vmem_limit_bytes=grant * MIB),
        cost_estimate=pl.CostEstimate(flops=flops, bytes_accessed=moved, transcendentals=0),
    )(*args)


def place(axis, bit=None):
    here = lax.axis_index(axis)
    return here if bit is None else here // bit % 2


def front_body(slab_count, *refs):
    arrived_refs, refs = refs[:slab_count], refs[slab_count:]
    hbm_refs, refs = refs[:9], refs[9:]
    (own_ref, other_ref, solved_ref, attend_ref, start_ref, gate_ref), refs = refs[:6], refs[6:]
    loaded, refs = refs[:8], refs[8:]
    rows_ref, projected, mixing, inverse, inverse_low, sems = refs
    rates, decay_down_ref, gate_down_ref, beta_ref, decay_up_ref, bias_ref, conv_ref, weights = loaded
    hidden_ref, weight_ref = hbm_refs[0], hbm_refs[-1]
    rim_ref, *slab_refs = arrived_refs
    slab_rows = hidden_ref.shape[0]
    heads, count, size = start_ref.shape
    tap_count = conv_ref.shape[1]
    chunk = math.gcd(count, 64)
    chunks = count // chunk
    here = place("head")

    def rows_of(k):
        return pl.ds(pl.multiple_of(RIM + (here ^ k) * slab_rows, 16), slab_rows)

    firsts = [pltpu.make_async_copy(hidden_ref, rows_ref.at[rows_of(0)], sems.at[0])]
    for i in range(7):
        firsts.append(pltpu.make_async_copy(hbm_refs[1 + i], loaded[i], sems.at[1 + i]))
    pieces = [slice(i, i + 2 * size) for i in range(0, heads * size, 2 * size)]
    loads = {}
    for c in range(3):
        for piece in pieces:
            loads[c, piece.start] = pltpu.make_async_copy(
                weight_ref.at[c, :, piece], weights.at[c, :, piece], sems.at[8 + len(loads)]
            )
    for copy in firsts + list(loads.values()):
        copy.start()
    rows_ref[:RIM, :] = rim_ref[...]
    for k, ref in enumerate(slab_refs):
        rows_ref[rows_of(k + 1), :] = ref[...]
    for copy in firsts:
        copy.wait()

    here_rows = rows_ref[RIM:, :]
    rank = decay_up_ref.shape[0]
    low = dot(here_rows, jnp.concatenate([decay_down_ref[...], gate_down_ref[...]], axis=1))
    decay_low = low[:, :rank].astype(bf16)
    gate_ref[...] = low[:, rank:].astype(bf16)
    strength = jax.nn.sigmoid(dot(here_rows, beta_ref[...], ((1,), (1,))))
    raw = dot(decay_low, decay_up_ref[...]) + bias_ref[...]
    rate = jnp.concatenate(
        [jnp.exp(jnp.full((1, size), rates[h], f32)) for h in range(heads)], axis=1
    )
    softplus = jnp.maximum(raw, 0.0) + jnp.log1p(jnp.exp(-jnp.abs(raw)))
    log_decay = -rate * softplus
    row = lax.broadcasted_iota(jnp.int32, (count, count), 0)
    col = lax.broadcasted_iota(jnp.int32, (count, count), 1)
    lower = jnp.where(row >= col, 1.0, 0.0).astype(bf16)
    high = log_decay.astype(bf16)
    cumulative = dot(lower, high) + dot(lower, (log_decay - high.astype(f32)).astype(bf16))

    convolved = []
    for c in range(3):
        parts = []
        taps = conv_ref[c].astype(f32)
        for piece in pieces:
            loads[c, piece.start].wait()
            projected[c, :, piece] = (
                dot(rows_ref[...], weights[c, :, piece]).astype(bf16).astype(f32)
            )
            total = None
            for i in range(tap_count):
                shifted = projected[c, pl.ds(RIM - tap_count + 1 + i, count), piece]
                term = shifted * taps[i : i + 1, piece]
                total = term if total is None else total + term
            parts.append((total / (1.0 + jnp.exp(-total))).astype(bf16).astype(f32))
        convolved.append(jnp.concatenate(parts, axis=1))

    def by_chunk(rows):
        return jnp.concatenate([jnp.broadcast_to(r, (chunk, size)) for r in rows], axis=0)

    eye = row == col
    stops, sides = [], []
    for h in range(heads):
        lanes = slice(h * size, (h + 1) * size)
        queries, keys, values = (part[:, lanes] for part in convolved)
        queries = queries * lax.rsqrt(jnp.sum(queries * queries, -1, keepdims=True) + 1e-06)
        queries = queries * size ** (-0.5)
        keys = keys * lax.rsqrt(jnp.sum(keys * keys, -1, keepdims=True) + 1e-06)
        running = cumulative[:, lanes]
        middles = [running[a * chunk + chunk // 2 : a * chunk + chunk // 2 + 1] for a in range(chunks)]
        middle = by_chunk(middles)
        rise = jnp.exp(running - middle)
        key_rise, query_rise = keys * rise, queries * rise
        key_fall = keys * strength[:, h : h + 1] * jnp.exp(middle - running)
        last = running[count - 1 :]
        stops.append(
            ((key_fall * by_chunk([jnp.exp(last - m) for m in middles])).astype(bf16), jnp.exp(last))
        )
        entry = by_chunk([jnp.exp(m) for m in middles])
        start_ref[h] = query_rise * entry
        sides.append(
            jnp.concatenate([(key_rise * entry).astype(bf16), values.astype(bf16)], axis=1)
        )
        for a in range(chunks):
            here = slice(a * chunk, (a + 1) * chunk)
            left = jnp.concatenate([key_rise[here], query_rise[here]], axis=0).astype(bf16)
            falls = []
            for b in range(chunks):
                there = slice(b * chunk, (b + 1) * chunk)
                if b < a:
                    falls.append(key_fall[there] * jnp.exp(middles[a] - middles[b]))
                elif b == a:
                    falls.append(key_fall[there])
                else:
                    falls.append(jnp.zeros((chunk, size), f32))
            right = jnp.concatenate(falls, axis=0).astype(bf16)
            scores = dot(left, right, ((1,), (1,)))
            mixing[h, here, :] = jnp.where(row[here] > col[here], scores[:chunk], 0.0).astype(bf16)
            attend_ref[h, here, :] = jnp.where(row[here] >= col[here], scores[chunk:], 0.0).astype(
                bf16
            )

    base = math.gcd(count, BASE)
    same = row // base == col // base
    powers = [None] * heads
    for h in range(heads):
        nilpotent = jnp.where(same, -mixing[h].astype(f32), 0.0)
        powers[h] = nilpotent.astype(bf16)
        inverse[h] = jnp.where(eye, 1.0, nilpotent)
    for _ in range(1, (base - 1).bit_length()):
        for h in range(heads):
            powers[h] = dot(powers[h], powers[h]).astype(bf16)
        for h in range(heads):
            inverse[h] = inverse[h] + dot(inverse[h].astype(bf16), powers[h])
    for h in range(heads):
        inverse_low[h] = inverse[h].astype(bf16)
    width = base
    while width < count:
        odd = [slice(i, i + width) for i in range(width, count, 2 * width)]
        pair_mask = jnp.where(
            (row // width % 2 == 1) & (col // width == row // width - 1), 1.0, 0.0
        ).astype(bf16)
        halves = []
        for h in range(heads):
            chosen = jnp.concatenate([inverse_low[h, rows, :] for rows in odd], axis=0)
            halves.append(dot(chosen, mixing[h] * pair_mask).astype(bf16))
        for h in range(heads):
            change = dot(halves[h], inverse_low[h])
            for i, rows in enumerate(odd):
                new = inverse_low[h, rows, :].astype(f32) - change[i * width : (i + 1) * width]
                inverse_low[h, rows, :] = new.astype(bf16)
        width *= 2

    pairs = []
    for h in range(heads):
        solved = dot(inverse_low[h], sides[h]).astype(bf16)
        solved_ref[h] = solved
        stop, fade = stops[h]
        moved = dot(stop, solved, ((0,), (0,)))
        diagonal = jnp.where(eye[:size, :size], jnp.broadcast_to(fade, (size, size)), 0.0)
        pairs.append(jnp.concatenate([diagonal - moved[:, :size], moved[:, size:]], axis=1))
    upper = place("seq", 1) == 1
    for h in range(heads // 2):
        low, high = pairs[h], pairs[heads // 2 + h]
        own_ref[h] = jnp.where(upper, high, low).astype(bf16)
        other_ref[h] = jnp.where(upper, low, high).astype(bf16)


def front(rim, slabs, loaded, weight, size):
    slab_count, slab_rows = len(slabs), slabs[0].shape[0]
    count = slab_count * slab_rows
    _, width, channels = weight.shape
    heads = channels // size
    rank = loaded[1].shape[1]
    buffers = [pltpu.SMEM(loaded[0].shape, f32)]
    buffers += [pltpu.VMEM(part.shape, part.dtype) for part in (*loaded[1:], weight)]
    return vmem_call(
        functools.partial(front_body, slab_count),
        (
            jax.ShapeDtypeStruct((heads // 2, size, 2 * size), bf16),
            jax.ShapeDtypeStruct((heads // 2, size, 2 * size), bf16),
            jax.ShapeDtypeStruct((heads, count, 2 * size), bf16),
            jax.ShapeDtypeStruct((heads, count, count), bf16),
            jax.ShapeDtypeStruct((heads, count, size), f32),
            jax.ShapeDtypeStruct((count, rank), bf16),
        ),
        (rim, *slabs[1:], slabs[0], *loaded, weight),
        scratch=[
            *buffers,
            pltpu.VMEM((RIM + count, width), bf16),
            pltpu.VMEM((3, RIM + count, channels), f32),
            pltpu.VMEM((heads, count, count), bf16),
            pltpu.VMEM((heads, count, count), f32),
            pltpu.VMEM((heads, count, count), bf16),
            pltpu.SemaphoreType.DMA((8 + 3 * pl.cdiv(heads, 2),)),
        ],
        hbm=2 + len(loaded),
        grant=24,
        flops=2 * count * width * channels * 4,
        moved=2 * 4 * width * channels,
    )


def rows_body(attend_ref, solved_ref, start_ref, low_ref, up_ref, raised_ref, output_ref, gate_ref):
    heads, _, size = start_ref.shape
    gate_ref[...] = jax.nn.sigmoid(dot(low_ref[...], up_ref[...]))
    for h in range(heads):
        both = dot(attend_ref[h], solved_ref[h])
        raised_ref[h] = (start_ref[h] - both[:, :size]).astype(bf16)
        output_ref[:, h * size : (h + 1) * size] = both[:, size:]


def composed(later, first, size):
    both = dot(later[:, :size], first)
    return both[:, :size], both[:, size:] + later[:, size:].astype(f32)


def put(ref, h, pair):
    size = ref.shape[1]
    if ref.shape[2] > size:
        ref[h, :, :size] = pair[0].astype(bf16)
    ref[h, :, ref.shape[2] - size :] = pair[1].astype(bf16)


def join_body(bit, own_ref, far_ref, total_ref):
    heads, size, _ = own_ref.shape
    for h in range(heads):
        own, far = own_ref[h], far_ref[h]
        upper = place("seq", bit) == 1
        later, first = jnp.where(upper, own, far), jnp.where(upper, far, own)
        put(total_ref, h, composed(later, first, size))


def join(bit, own, far, last):
    heads, size, width = own.shape
    return vmem_call(
        functools.partial(join_body, bit),
        jax.ShapeDtypeStruct((heads, size, size if last else width), bf16),
        (own, far),
        flops=2 * heads * size * size * width,
        moved=6 * heads * size * width,
    )


def before_body(bit, near_ref, far_ref, out_ref):
    heads, size, _ = near_ref.shape
    for h in range(heads):
        near = near_ref[h]
        pair = jnp.concatenate(composed(near, far_ref[h], size), axis=1)
        out_ref[h] = jnp.where(place("seq", bit) == 1, pair, near.astype(f32)).astype(bf16)


def before(bit, near, far):
    return vmem_call(
        functools.partial(before_body, bit),
        jax.ShapeDtypeStruct(near.shape, bf16),
        (near, far),
        flops=2 * math.prod(near.shape) * near.shape[1],
        moved=6 * math.prod(near.shape),
    )


def entry_body(bit, near_ref, far_ref, own_ref, partner_ref, keep_ref, send_ref):
    heads, size, _ = near_ref.shape
    arrived, upper = place("seq", bit) == 1, place("seq", 1) == 1
    for h in range(heads):
        state = dot(near_ref[h, :, :size], far_ref[h])
        state = jnp.where(arrived, state, 0.0) + near_ref[h, :, size:].astype(f32)
        first = jnp.where(upper, partner_ref[h], own_ref[h])
        state = state.astype(bf16)
        later = dot(first[:, :size], state) + first[:, size:].astype(f32)
        later = later.astype(bf16)
        keep_ref[h] = jnp.where(upper, later, state)
        send_ref[h] = jnp.where(upper, state, later)


def entry_states(own, other):
    heads, size, width = own.shape
    bits = bits_of(lax.axis_size("seq"))
    partner = swapped(other, "seq", 1)
    total = join(1, own, partner, len(bits) == 2)
    near = jnp.broadcast_to(jnp.eye(size, width, dtype=bf16), own.shape)
    for bit in bits[1:-1]:
        far = swapped(total, "seq", bit)
        total = join(bit, total, far, 2 * bit == bits[-1])
        near = before(bit, near, far)
    far = swapped(total, "seq", bits[-1])
    state = jax.ShapeDtypeStruct((heads, size, size), bf16)
    keep, send = vmem_call(
        functools.partial(entry_body, bits[-1]),
        (state, state),
        (near, far, own, partner),
        flops=4 * heads * size * size * size,
        moved=14 * heads * size * size,
    )
    return keep, swapped(send, "seq", 1)


def back_body(
    places, own_ref, other_ref, raised_ref, output_ref, gate_ref, gain_ref, weight_ref, keep_ref,
    *rest,
):
    normed = rest[-1]
    size = gain_ref.shape[1]
    slab_rows = keep_ref.shape[0]
    half = own_ref.shape[0]
    upper = place("seq", 1) == 1
    for k, away in enumerate(places):
        rows = pl.ds(pl.multiple_of((place("head") ^ away) * slab_rows, 16), slab_rows)
        for h in range(raised_ref.shape[0]):
            lanes = slice(h * size, (h + 1) * size)
            own, other = own_ref[h % half], other_ref[h % half]
            state = jnp.where(upper, other, own) if h < half else jnp.where(upper, own, other)
            attended = dot(raised_ref[h, rows, :], state) + output_ref[rows, lanes]
            power = jnp.sum(attended * attended, -1, keepdims=True) * (1.0 / size)
            normed[k * slab_rows : (k + 1) * slab_rows, lanes] = (
                attended * lax.rsqrt(power + 1e-05) * gain_ref[...] * gate_ref[rows, lanes]
            ).astype(bf16)
    total = dot(normed[...], weight_ref[...])
    keep_ref[...] = total[:slab_rows]
    if len(rest) > 1:
        rest[0][...] = total[slab_rows:].astype(bf16)


def back(places, states, raised, output_rows, out_gate, gain, weight, slab_rows):
    slab_count, width = len(places), weight.shape[1]
    shapes = [jax.ShapeDtypeStruct((slab_rows, width), f32)]
    if slab_count > 1:
        shapes.append(jax.ShapeDtypeStruct((slab_rows, width), bf16))
    return vmem_call(
        functools.partial(back_body, places),
        shapes,
        (*states, raised, output_rows, out_gate, gain, weight),
        scratch=[pltpu.VMEM((slab_count * slab_rows, weight.shape[0]), bf16)],
        grant=10,
        flops=2 * slab_count * slab_rows * weight.shape[0] * width,
        moved=2 * weight.shape[0] * width,
    )


def shards(
    hidden_in,
    qkv_weight,
    conv_weight,
    decay_log,
    dt_bias,
    decay_down,
    decay_up,
    beta_weight,
    gate_down,
    gate_up,
    norm_gain,
    out_weight,
):
    heads, size = decay_log.shape[0], norm_gain.shape[0]
    channels = heads * size
    devices = lax.axis_size("head")
    slabs, rim = gathered(hidden_in, RIM)
    own, other, solved, attend, start, gate_low = front(
        rim,
        slabs,
        (decay_log, decay_down, gate_down, beta_weight.T, decay_up, dt_bias[None], conv_weight),
        qkv_weight.transpose(1, 0, 2),
        size,
    )
    count = start.shape[1]
    raised, output_rows, out_gate = vmem_call(
        rows_body,
        (
            jax.ShapeDtypeStruct((heads, count, size), bf16),
            jax.ShapeDtypeStruct((count, channels), f32),
            jax.ShapeDtypeStruct((count, channels), f32),
        ),
        (attend, solved, start, gate_low, gate_up),
        grant=8,
        flops=2 * heads * count * count * 2 * size,
        moved=4 * heads * count * count,
    )
    states = entry_states(own, other)
    slab_rows = count // devices
    sums = {}
    for g in reversed(range(max(devices // 2, 1))):
        places = [2 * g, 2 * g + 1][:devices]
        keep, *send = back(
            places, states, raised, output_rows, out_gate, norm_gain[None], out_weight, slab_rows
        )
        sums[g] = [keep] + [swapped(part, "head", 1).astype(f32) for part in send]
    for bit in bits_of(devices)[1:]:
        for g in sorted(sums):
            if 2 * g & bit:
                arrived = swapped(sum(sums.pop(g)).astype(bf16), "head", bit)
                sums[g ^ bit // 2].append(arrived.astype(f32))
    return sum(sums[0]).astype(bf16)


def solution(mesh):
    return jax.shard_map(
        shards,
        mesh=mesh,
        in_specs=(
            P(("seq", "head"), None),
            P(None, None, "head"),
            P(None, None, "head"),
            P("head"),
            P("head"),
            P(),
            P(None, "head"),
            P(None, "head"),
            P(),
            P(None, "head"),
            P(),
            P("head", None),
        ),
        out_specs=P(("seq", "head"), None),
        check_vma=False,
    )
```

time: 80.7 us -> 59.3 us (0.73)
  local copies, waits for them, and re-layouts: 22.4 us -> 0.94 us
  starting transfers between devices: 24.8 us -> 15.8 us
  waiting for transfers between devices: 19.9 us -> 26.6 us
  Pallas kernels: 11.7 us -> 14.6 us
    unnamed x58 -> x6, local copies, waits for them, and re-layouts: 20.8 us -> 0.01 us
    ppermute x13 -> x11, starting transfers between devices: 23.5 us -> 14.5 us  [swapped(): lax.ppermute(block, axis, [(i, i ^ bit) for i in range(lax.axis_size(axis...]
    ppermute x13 -> x11, waiting for transfers between devices: 19.9 us -> 26.6 us  [swapped(): lax.ppermute(block, axis, [(i, i ^ bit) for i in range(lax.axis_size(axis...]
    pallas_call x11 -> x8, Pallas kernels: 11.7 us -> 14.6 us  [vmem_call(): pl.pallas_call(body, out_shape=out_shape, in_specs=[pl.BlockSpec(memory_s...]
  transfers between devices with their start and end apart: 15 -> 13, of which waited for: 5 -> 8; matrix products, arithmetic and copies ran while one was open for 2% -> 2% of each run, Pallas kernels for 3% -> 2%
where the time goes in v3:
time: 59.3 us; the launch traced here: 59.1 us
  waiting for transfers between devices  26.6 us (45%)
  starting transfers between devices  15.8 us (27%)
  Pallas kernels  14.6 us (25%)
  local copies, waits for them, and re-layouts  0.94 us (2%)
  other arithmetic  0.91 us (2%)
    ppermute x11, waiting for transfers between devices, swapped(): lax.ppermute(block, axis, [(i, i ^ bit) for i in range(lax.axis_size(axis...  26.6 us
    pallas_call x8, Pallas kernels, vmem_call(): pl.pallas_call(body, out_shape=out_shape, in_specs=[pl.BlockSpec(memory_s...  14.6 us
    ppermute x11, starting transfers between devices, swapped(): lax.ppermute(block, axis, [(i, i ^ bit) for i in range(lax.axis_size(axis...  14.5 us
    ppermute x2, starting transfers between devices, gathered(): rim = rim + lax.ppermute(tail, ('seq', 'head'), route)  1.32 us
  transfers between devices with their start and end apart: 13, of which 8 were waited for; matrix products, arithmetic and copies ran while one was open for 2% of the time, Pallas kernels for 2%

profile of v3, /device:TPU:0, one launch (start us, length us, event | category | flops | bytes accessed | tf_op | source)
XLA Modules:
  0.0 59.1 jit_solution(5777210685791767873)
XLA Ops:
  0.0 0.0 copy-start.1
  0.0 0.0 copy-start.2
  0.0 0.0 copy-start
  0.0 3.0 %collective-permute-start = (bf16[64,2304]{1,0:T(8,128)(2,1)}, bf16[64,2304]{1,0:T(8,128)(2,1)S(1)}, u32[]{:S(2)}, u32[]{:S(2)}) collective-permute-start(bf16[64,2304]{1,0:T(8,128)(2,1)} %refs_4_.1), channel_id=1, source_target_pairs={{0,2},{1,3},{2,0},{3,1},{4,6},{5,7},{6,4},{7,5},{8,10},{9,11},{10,... | collective-permute-start | bytes 884744 | tf_op jit(solution)/shard_map/ppermute | solution.py:23
  3.0 0.9 %slice.3 = bf16[16,2304]{1,0:T(8,128)(2,1)S(1)} slice(bf16[64,2304]{1,0:T(8,128)(2,1)} %refs_4_.1), slice={[48:64], [0:2304]} | slice | bytes 147456 | tf_op jit(solution)/shard_map/slice | solution.py:37
  3.9 0.7 %collective-permute-start.1 = (bf16[16,2304]{1,0:T(8,128)(2,1)S(1)}, bf16[16,2304]{1,0:T(8,128)(2,1)S(1)}, u32[]{:S(2)}, u32[]{:S(2)}) collective-permute-start(bf16[16,2304]{1,0:T(8,128)(2,1)S(1)} %slice.3), channel_id=1, source_target_pairs={{3,5},{7,9},{11,13},{15,17},{19,21},{23,25},{27,29}} | collective-permute-start | bytes 221192 | tf_op jit(solution)/shard_map/ppermute | solution.py:41
  4.6 0.7 %collective-permute-start.2 = (bf16[16,2304]{1,0:T(8,128)(2,1)S(1)}, bf16[16,2304]{1,0:T(8,128)(2,1)S(1)}, u32[]{:S(2)}, u32[]{:S(2)}) collective-permute-start(bf16[16,2304]{1,0:T(8,128)(2,1)S(1)} %slice.3), channel_id=1, source_target_pairs={{3,7},{7,11},{11,15},{15,19},{19,23},{23,27},{27,31}} | collective-permute-start | bytes 221192 | tf_op jit(solution)/shard_map/ppermute | solution.py:41
  5.3 0.1 collective-permute-start.4
  5.4 0.0 collective-permute-done.1
  5.4 0.0 collective-permute-done.2
  5.4 5.6 %collective-permute-done.refs_2_ = bf16[64,2304]{1,0:T(8,128)(2,1)S(1)} collective-permute-done((bf16[64,2304]{1,0:T(8,128)(2,1)}, bf16[64,2304]{1,0:T(8,128)(2,1)S(1)}, u32[]{:S(2)}, u32[]{:S(2)}) %collective-permute-start) | collective-permute-done | bytes 294944 | tf_op jit(solution)/shard_map/ppermute | solution.py:23
  11.0 0.0 collective-permute-start.5
  11.0 0.5 collective-permute-start.3
  11.5 1.2 %collective-permute-done.3 = bf16[16,2304]{1,0:T(8,128)(2,1)S(1)} collective-permute-done((bf16[16,2304]{1,0:T(8,128)(2,1)S(1)}, bf16[16,2304]{1,0:T(8,128)(2,1)S(1)}, u32[]{:S(2)}, u32[]{:S(2)}) %collective-permute-start.3) | collective-permute-done | bytes 73760 | tf_op jit(solution)/shard_map/ppermute | solution.py:23
  12.7 0.0 collective-permute-done.4.refs_1_
  12.7 0.0 collective-permute-done.5.refs_3_
  12.8 11.9 %shard_map.118 = (bf16[2,128,256]{2,1,0:T(8,128)(2,1)S(1)}, bf16[2,128,256]{2,1,0:T(8,128)(2,1)S(1)}, bf16[4,256,256]{2,1,0:T(8,128)(2,1)S(1)}, bf16[4,256,256]{...) custom-call(bf16[16,2304]{1,0:T(8,128)(2,1)S(1)} %add.16.refs_0_, ...), custom_call_target="tpu_custom_call" | custom-call | flops 2415919104 | bytes 9437184 | tf_op jit(solution)/shard_map/pallas_call | solution.py:56
  24.7 1.1 %collective-permute-start.6 = (bf16[2,128,256]{2,1,0:T(8,128)(2,1)S(1)}, bf16[2,128,256]{2,1,0:T(8,128)(2,1)S(1)}, u32[]{:S(2)}, u32[]{:S(2)}) collective-permute-start(bf16[2,128,256]{2,1,0:T(8,128)(2,1)S(1)} %get-tuple-element.25), channel_id=1, source_target_pairs={{0,4},{4,0},{8,12},{12,8},{16,20},{20,16},{24,28},{28,24},{1,5},{5... | collective-permute-start | bytes 393224 | tf_op jit(solution)/shard_map/ppermute | solution.py:23
  25.8 4.5 %collective-permute-done.6.far_ref.partner_ref = bf16[2,128,256]{2,1,0:T(8,128)(2,1)S(1)} collective-permute-done((bf16[2,128,256]{2,1,0:T(8,128)(2,1)S(1)}, bf16[2,128,256]{2,1,0:T(8,128)(2,1)S(1)}, u32[]{:S(2)}, u32[]{:S(2)}) %collective-permute-start.6) | collective-permute-done | bytes 131104 | tf_op jit(solution)/shard_map/ppermute | solution.py:23
  30.3 0.2 shard_map.119.own_ref
  30.5 1.9 %collective-permute-start.7 = (bf16[2,128,256]{2,1,0:T(8,128)(2,1)S(1)}, bf16[2,128,256]{2,1,0:T(8,128)(2,1)S(1)}, u32[]{:S(2)}, u32[]{:S(2)}) collective-permute-start(bf16[2,128,256]{2,1,0:T(8,128)(2,1)S(1)} %shard_map.119.own_ref), channel_id=1, source_target_pairs={{0,8},{4,12},{8,0},{12,4},{16,24},{20,28},{24,16},{28,20},{1,9},{5... | collective-permute-start | bytes 393224 | tf_op jit(solution)/shard_map/ppermute | solution.py:23
  32.4 3.1 %collective-permute-done.7.far_ref = bf16[2,128,256]{2,1,0:T(8,128)(2,1)S(1)} collective-permute-done((bf16[2,128,256]{2,1,0:T(8,128)(2,1)S(1)}, bf16[2,128,256]{2,1,0:T(8,128)(2,1)S(1)}, u32[]{:S(2)}, u32[]{:S(2)}) %collective-permute-start.7) | collective-permute-done | bytes 131104 | tf_op jit(solution)/shard_map/ppermute | solution.py:23
  35.5 0.2 shard_map.121
  35.7 2.9 %collective-permute-start.8 = (bf16[2,128,128]{2,1,0:T(8,128)(2,1)S(1)}, bf16[2,128,128]{2,1,0:T(8,128)(2,1)S(1)}, u32[]{:S(2)}, u32[]{:S(2)}) collective-permute-start(bf16[2,128,128]{2,1,0:T(8,128)(2,1)S(1)} %shard_map.121), channel_id=1, source_target_pairs={{0,16},{4,20},{8,24},{12,28},{16,0},{20,4},{24,8},{28,12},{1,17},{... | collective-permute-start | bytes 196616 | tf_op jit(solution)/shard_map/ppermute | solution.py:23
  38.7 0.2 shard_map.120.near_ref
  38.8 2.1 %collective-permute-done.8.far_ref = bf16[2,128,128]{2,1,0:T(8,128)(2,1)S(1)} collective-permute-done((bf16[2,128,128]{2,1,0:T(8,128)(2,1)S(1)}, bf16[2,128,128]{2,1,0:T(8,128)(2,1)S(1)}, u32[]{:S(2)}, u32[]{:S(2)}) %collective-permute-start.8) | collective-permute-done | bytes 65568 | tf_op jit(solution)/shard_map/ppermute | solution.py:23
  40.9 0.3 shard_map.122
  41.3 1.5 %collective-permute-start.9 = (bf16[2,128,128]{2,1,0:T(8,128)(2,1)S(1)}, bf16[2,128,128]{2,1,0:T(8,128)(2,1)S(1)}, u32[]{:S(2)}, u32[]{:S(2)}) collective-permute-start(bf16[2,128,128]{2,1,0:T(8,128)(2,1)S(1)} %get-tuple-element.27), channel_id=1, source_target_pairs={{0,4},{4,0},{8,12},{12,8},{16,20},{20,16},{24,28},{28,24},{1,5},{5... | collective-permute-start | bytes 196616 | tf_op jit(solution)/shard_map/ppermute | solution.py:23
  42.8 0.0 copy-done.1
  42.8 0.4 shard_map.123
  43.1 2.5 %collective-permute-done.9.other_ref = bf16[2,128,128]{2,1,0:T(8,128)(2,1)S(1)} collective-permute-done((bf16[2,128,128]{2,1,0:T(8,128)(2,1)S(1)}, bf16[2,128,128]{2,1,0:T(8,128)(2,1)S(1)}, u32[]{:S(2)}, u32[]{:S(2)}) %collective-permute-start.9) | collective-permute-done | bytes 65568 | tf_op jit(solution)/shard_map/ppermute | solution.py:23
  45.6 0.0 copy-done.2
  45.6 0.0 copy-done
  45.6 0.7 %shard_map.125 = (f32[64,2304]{1,0:T(8,128)S(1)}, bf16[64,2304]{1,0:T(8,128)(2,1)S(1)}) custom-call(bf16[2,128,128]{2,1,0:T(8,128)(2,1)S(1)} %get-tuple-element.26.own_ref, bf16[2,128,128]{2,1,0:T(8,128)(2,1)S(1)} %collective-permute-done.9.other_ref, bf16[4,256,128]{2,1,0:T(8,128)(2,1)S(1)} %get-tuple-element.32.raised_ref, ...), custom_call_target="tpu_custom_call" | custom-call | flops 301989888 | bytes 2359296 | tf_op jit(solution)/shard_map/pallas_call | solution.py:56
  46.3 0.1 collective-permute-start.11
  46.4 0.7 %shard_map.124 = (f32[64,2304]{1,0:T(8,128)S(1)}, bf16[64,2304]{1,0:T(8,128)(2,1)S(1)}) custom-call(bf16[2,128,128]{2,1,0:T(8,128)(2,1)S(1)} %get-tuple-element.26.own_ref, bf16[2,128,128]{2,1,0:T(8,128)(2,1)S(1)} %collective-permute-done.9.other_ref, bf16[4,256,128]{2,1,0:T(8,128)(2,1)S(1)} %get-tuple-element.32.raised_ref, ...), custom_call_target="tpu_custom_call" | custom-call | flops 301989888 | bytes 2359296 | tf_op jit(solution)/shard_map/pallas_call | solution.py:56
  47.2 0.6 collective-permute-start.10
  47.7 0.3 collective-permute-done.11
  48.0 0.1 add_convert_fusion.1
  48.0 2.9 %collective-permute-start.12 = (bf16[64,2304]{1,0:T(8,128)(2,1)S(1)}, bf16[64,2304]{1,0:T(8,128)(2,1)S(1)}, u32[]{:S(2)}, u32[]{:S(2)}) collective-permute-start(bf16[64,2304]{1,0:T(8,128)(2,1)S(1)} %add_convert_fusion.1), channel_id=1, source_target_pairs={{0,2},{1,3},{2,0},{3,1},{4,6},{5,7},{6,4},{7,5},{8,10},{9,11},{10,... | collective-permute-start | bytes 884744 | tf_op jit(solution)/shard_map/ppermute | solution.py:23
  51.0 0.0 collective-permute-done.10
  51.0 7.3 %collective-permute-done.12 = bf16[64,2304]{1,0:T(8,128)(2,1)S(1)} collective-permute-done((bf16[64,2304]{1,0:T(8,128)(2,1)S(1)}, bf16[64,2304]{1,0:T(8,128)(2,1)S(1)}, u32[]{:S(2)}, u32[]{:S(2)}) %collective-permute-start.12) | collective-permute-done | bytes 294944 | tf_op jit(solution)/shard_map/ppermute | solution.py:23
  58.3 0.8 %add_convert_fusion = bf16[64,2304]{1,0:T(8,128)(2,1)} fusion(bf16[64,2304]{1,0:T(8,128)(2,1)S(1)} %collective-permute-done.12, f32[64,2304]{1,0:T(8,128)S(1)} %get-tuple-element.35, bf16[64,2304]{1,0:T(8,128)(2,1)S(1)} %collective-permute-done.10), kind=kLoop, calls=%fused_computation | loop fusion | flops 737280 | bytes 1474560 | tf_op jit(solution)/shard_map/convert_element_type | solution.py:459
  (4 shorter events, 0.1 us)
Async XLA Ops:
  0.0 42.8 %copy-start.1 = (bf16[128,512]{1,0:T(8,128)(2,1)S(1)}, bf16[128,512]{1,0:T(8,128)(2,1)}, u32[]{:S(2)}) copy-start(bf16[128,512]{1,0:T(8,128)(2,1)} %up_ref.1) | copy-start | bytes 393220
  0.0 45.6 %copy-start.2 = (f32[128]{0:T(128)S(1)}, f32[128]{0:T(128)}, u32[]{:S(2)}) copy-start(f32[128]{0:T(128)} %param.22) | copy-start | bytes 1540
  0.0 45.6 %copy-start = (bf16[512,2304]{1,0:T(8,128)(2,1)S(1)}, bf16[512,2304]{1,0:T(8,128)(2,1)}, u32[]{:S(2)}) copy-start(bf16[512,2304]{1,0:T(8,128)(2,1)} %weight_ref.3) | copy-start | bytes 7077892
  0.0 11.0 %collective-permute-start = (bf16[64,2304]{1,0:T(8,128)(2,1)}, bf16[64,2304]{1,0:T(8,128)(2,1)S(1)}, u32[]{:S(2)}, u32[]{:S(2)}) collective-permute-start(bf16[64,2304]{1,0:T(8,128)(2,1)} %refs_4_.1), channel_id=1, source_target_pairs={{0,2},{1,3},{2,0},{3,1},{4,6},{5,7},{6,4},{7,5},{8,10},{9,11},{10,... | collective-permute-start | bytes 884744 | tf_op jit(solution)/shard_map/ppermute | solution.py:23
  3.9 1.4 %collective-permute-start.1 = (bf16[16,2304]{1,0:T(8,128)(2,1)S(1)}, bf16[16,2304]{1,0:T(8,128)(2,1)S(1)}, u32[]{:S(2)}, u32[]{:S(2)}) collective-permute-start(bf16[16,2304]{1,0:T(8,128)(2,1)S(1)} %slice.3), channel_id=1, source_target_pairs={{3,5},{7,9},{11,13},{15,17},{19,21},{23,25},{27,29}} | collective-permute-start | bytes 221192 | tf_op jit(solution)/shard_map/ppermute | solution.py:41
  4.6 0.8 %collective-permute-start.2 = (bf16[16,2304]{1,0:T(8,128)(2,1)S(1)}, bf16[16,2304]{1,0:T(8,128)(2,1)S(1)}, u32[]{:S(2)}, u32[]{:S(2)}) collective-permute-start(bf16[16,2304]{1,0:T(8,128)(2,1)S(1)} %slice.3), channel_id=1, source_target_pairs={{3,7},{7,11},{11,15},{15,19},{19,23},{23,27},{27,31}} | collective-permute-start | bytes 221192 | tf_op jit(solution)/shard_map/ppermute | solution.py:41
  5.3 7.5 %collective-permute-start.4 = (bf16[64,2304]{1,0:T(8,128)(2,1)}, bf16[64,2304]{1,0:T(8,128)(2,1)S(1)}, u32[]{:S(2)}, u32[]{:S(2)}) collective-permute-start(bf16[64,2304]{1,0:T(8,128)(2,1)} %refs_4_.1), channel_id=1, source_target_pairs={{0,1},{1,0},{2,3},{3,2},{4,5},{5,4},{6,7},{7,6},{8,9},{9,8},{10,11... | collective-permute-start | bytes 884744 | tf_op jit(solution)/shard_map/ppermute | solution.py:23
  11.0 1.7 %collective-permute-start.5 = (bf16[64,2304]{1,0:T(8,128)(2,1)S(1)}, bf16[64,2304]{1,0:T(8,128)(2,1)S(1)}, u32[]{:S(2)}, u32[]{:S(2)}) collective-permute-start(bf16[64,2304]{1,0:T(8,128)(2,1)S(1)} %collective-permute-done.refs_2_), channel_id=1, source_target_pairs={{0,1},{1,0},{2,3},{3,2},{4,5},{5,4},{6,7},{7,6},{8,9},{9,8},{10,11... | collective-permute-start | bytes 884744 | tf_op jit(solution)/shard_map/ppermute | solution.py:23
  11.0 1.7 %collective-permute-start.3 = (bf16[16,2304]{1,0:T(8,128)(2,1)S(1)}, bf16[16,2304]{1,0:T(8,128)(2,1)S(1)}, u32[]{:S(2)}, u32[]{:S(2)}) collective-permute-start(bf16[16,2304]{1,0:T(8,128)(2,1)S(1)} %add.15), channel_id=1, source_target_pairs={{0,1},{1,0},{2,3},{3,2},{4,5},{5,4},{6,7},{7,6},{8,9},{9,8},{10,11... | collective-permute-start | bytes 221192 | tf_op jit(solution)/shard_map/ppermute | solution.py:23
  24.7 5.6 %collective-permute-start.6 = (bf16[2,128,256]{2,1,0:T(8,128)(2,1)S(1)}, bf16[2,128,256]{2,1,0:T(8,128)(2,1)S(1)}, u32[]{:S(2)}, u32[]{:S(2)}) collective-permute-start(bf16[2,128,256]{2,1,0:T(8,128)(2,1)S(1)} %get-tuple-element.25), channel_id=1, source_target_pairs={{0,4},{4,0},{8,12},{12,8},{16,20},{20,16},{24,28},{28,24},{1,5},{5... | collective-permute-start | bytes 393224 | tf_op jit(solution)/shard_map/ppermute | solution.py:23
  30.5 5.0 %collective-permute-start.7 = (bf16[2,128,256]{2,1,0:T(8,128)(2,1)S(1)}, bf16[2,128,256]{2,1,0:T(8,128)(2,1)S(1)}, u32[]{:S(2)}, u32[]{:S(2)}) collective-permute-start(bf16[2,128,256]{2,1,0:T(8,128)(2,1)S(1)} %shard_map.119.own_ref), channel_id=1, source_target_pairs={{0,8},{4,12},{8,0},{12,4},{16,24},{20,28},{24,16},{28,20},{1,9},{5... | collective-permute-start | bytes 393224 | tf_op jit(solution)/shard_map/ppermute | solution.py:23
  35.7 5.2 %collective-permute-start.8 = (bf16[2,128,128]{2,1,0:T(8,128)(2,1)S(1)}, bf16[2,128,128]{2,1,0:T(8,128)(2,1)S(1)}, u32[]{:S(2)}, u32[]{:S(2)}) collective-permute-start(bf16[2,128,128]{2,1,0:T(8,128)(2,1)S(1)} %shard_map.121), channel_id=1, source_target_pairs={{0,16},{4,20},{8,24},{12,28},{16,0},{20,4},{24,8},{28,12},{1,17},{... | collective-permute-start | bytes 196616 | tf_op jit(solution)/shard_map/ppermute | solution.py:23
  41.3 4.3 %collective-permute-start.9 = (bf16[2,128,128]{2,1,0:T(8,128)(2,1)S(1)}, bf16[2,128,128]{2,1,0:T(8,128)(2,1)S(1)}, u32[]{:S(2)}, u32[]{:S(2)}) collective-permute-start(bf16[2,128,128]{2,1,0:T(8,128)(2,1)S(1)} %get-tuple-element.27), channel_id=1, source_target_pairs={{0,4},{4,0},{8,12},{12,8},{16,20},{20,16},{24,28},{28,24},{1,5},{5... | collective-permute-start | bytes 196616 | tf_op jit(solution)/shard_map/ppermute | solution.py:23
  46.3 1.6 %collective-permute-start.11 = (bf16[64,2304]{1,0:T(8,128)(2,1)S(1)}, bf16[64,2304]{1,0:T(8,128)(2,1)S(1)}, u32[]{:S(2)}, u32[]{:S(2)}) collective-permute-start(bf16[64,2304]{1,0:T(8,128)(2,1)S(1)} %get-tuple-element.38), channel_id=1, source_target_pairs={{0,1},{1,0},{2,3},{3,2},{4,5},{5,4},{6,7},{7,6},{8,9},{9,8},{10,11... | collective-permute-start | bytes 884744 | tf_op jit(solution)/shard_map/ppermute | solution.py:23
  47.2 3.8 %collective-permute-start.10 = (bf16[64,2304]{1,0:T(8,128)(2,1)S(1)}, bf16[64,2304]{1,0:T(8,128)(2,1)S(1)}, u32[]{:S(2)}, u32[]{:S(2)}) collective-permute-start(bf16[64,2304]{1,0:T(8,128)(2,1)S(1)} %get-tuple-element.36), channel_id=1, source_target_pairs={{0,1},{1,0},{2,3},{3,2},{4,5},{5,4},{6,7},{7,6},{8,9},{9,8},{10,11... | collective-permute-start | bytes 884744 | tf_op jit(solution)/shard_map/ppermute | solution.py:23
  48.0 10.2 %collective-permute-start.12 = (bf16[64,2304]{1,0:T(8,128)(2,1)S(1)}, bf16[64,2304]{1,0:T(8,128)(2,1)S(1)}, u32[]{:S(2)}, u32[]{:S(2)}) collective-permute-start(bf16[64,2304]{1,0:T(8,128)(2,1)S(1)} %add_convert_fusion.1), channel_id=1, source_target_pairs={{0,2},{1,3},{2,0},{3,1},{4,6},{5,7},{6,4},{7,5},{8,10},{9,11},{10,... | collective-permute-start | bytes 884744 | tf_op jit(solution)/shard_map/ppermute | solution.py:23

commit v4 on v3

--- a/solution.py
+++ b/solution.py
@@ -28,25 +28,44 @@
     return [1 << i for i in range(size.bit_length() - 1)]
 
 
-def gathered(own, row_count):
+def tail_body(own_ref, tail_ref):
+    tail_ref[...] = own_ref[own_ref.shape[0] - tail_ref.shape[0] :, :]
+
+
+def tail_of(own, row_count):
+    return vmem_call(tail_body, jax.ShapeDtypeStruct((row_count, own.shape[1]), own.dtype), (own,))
+
+
+def rim_at_last(tail):
     heads, seqs = lax.axis_size("head"), lax.axis_size("seq")
+    swaps = []
+    for parity in range(2):
+        route = []
+        for s in range(parity, seqs - 1, 2):
+            one, two = s * heads + heads - 1, (s + 1) * heads + heads - 1
+            route += [(one, two), (two, one)]
+        swaps.append(lax.ppermute(tail, ("seq", "head"), route))
+    return jnp.where(lax.axis_index("seq") % 2 == 1, swaps[0], swaps[1])
+
+
+def gathered(own, row_count, early):
+    bits = bits_of(lax.axis_size("head"))
+    assert bits
     slabs = {0: own}
-    for bit in reversed(bits_of(heads)[1:]):
+    for bit in reversed(bits[1:]):
         for k in sorted(slabs):
             slabs[k ^ bit] = swapped(slabs[k], "head", bit)
-    tail = own[own.shape[0] - row_count :]
-    rim = jnp.zeros_like(tail)
-    for k in range(min(1, heads - 1), heads, 2):
-        route = [(s * heads + heads - 1, (s + 1) * heads + k) for s in range(seqs - 1)]
-        rim = rim + lax.ppermute(tail, ("seq", "head"), route)
-    if heads > 1:
-        slabs[1] = swapped(own, "head", 1)
-        arrived = [k for k in sorted(slabs) if k > 1]
-        moved, rim = lax.optimization_barrier(([slabs[k] for k in arrived], rim))
-        for k, slab in zip(arrived, moved):
-            slabs[k], slabs[k ^ 1] = slab, swapped(slab, "head", 1)
-        rim = rim + swapped(rim, "head", 1)
-    return [slabs[k] for k in range(heads)], rim
+    rim = rim_at_last(tail_of(own, row_count))
+    slabs[1] = swapped(own, "head", 1)
+    arrived = [k for k in sorted(slabs) if k > 1]
+    moved, rim, done = lax.optimization_barrier(
+        ([slabs[k] for k in arrived], rim, early(slabs[0], slabs[1]))
+    )
+    for k, slab in zip(arrived, moved):
+        slabs[k], slabs[k ^ 1] = slab, swapped(slab, "head", 1)
+    for bit in reversed(bits):
+        rim = rim + swapped(rim, "head", bit)
+    return [slabs[k] for k in range(2, 2 ** len(bits))], rim, done
 
 
 def vmem_call(body, out_shape, args, scratch=(), hbm=0, grant=4, flops=0, moved=0):
@@ -69,49 +88,110 @@
     return here if bit is None else here // bit % 2
 
 
+def column_pieces(width):
+    step = math.gcd(width, 256)
+    return [slice(i, i + step) for i in range(0, width, step)]
+
+
+def early_body(
+    near_ref, hidden_ref, decay_down_ref, gate_down_ref, beta_ref, weight_ref,
+    weights, downs, betas, projected_ref, low_ref, strength_ref, rows_ref, sems,
+):
+    slab_rows, rank = hidden_ref.shape[0], decay_down_ref.shape[1]
+    firsts = [
+        pltpu.make_async_copy(hidden_ref, rows_ref.at[pl.ds(0, slab_rows)], sems.at[0]),
+        pltpu.make_async_copy(decay_down_ref, downs.at[:, pl.ds(0, rank)], sems.at[1]),
+        pltpu.make_async_copy(gate_down_ref, downs.at[:, pl.ds(rank, rank)], sems.at[2]),
+        pltpu.make_async_copy(beta_ref, betas, sems.at[3]),
+    ]
+    pieces = column_pieces(weight_ref.shape[2])
+    loads = {}
+    for c in range(3):
+        for piece in pieces:
+            loads[c, piece.start] = pltpu.make_async_copy(
+                weight_ref.at[c, :, piece], weights.at[c, :, piece], sems.at[4 + len(loads)]
+            )
+    for copy in firsts + list(loads.values()):
+        copy.start()
+    rows_ref[slab_rows:, :] = near_ref[...]
+    for copy in firsts:
+        copy.wait()
+    low_ref[...] = dot(rows_ref[...], downs[...]).astype(bf16)
+    strength_ref[...] = dot(rows_ref[...], betas[...], ((1,), (1,)))
+    for c in range(3):
+        for piece in pieces:
+            loads[c, piece.start].wait()
+            projected_ref[c, :, piece] = dot(rows_ref[...], weights[c, :, piece]).astype(bf16)
+
+
+def early(own, near, decay_down, gate_down, beta, weight):
+    slab_rows, width = own.shape
+    channels, rank, count = weight.shape[2], decay_down.shape[1], 2 * slab_rows
+    return vmem_call(
+        early_body,
+        (
+            jax.ShapeDtypeStruct(weight.shape, bf16),
+            jax.ShapeDtypeStruct((width, 2 * rank), bf16),
+            jax.ShapeDtypeStruct(beta.shape, bf16),
+            jax.ShapeDtypeStruct((3, count, channels), bf16),
+            jax.ShapeDtypeStruct((count, 2 * rank), bf16),
+            jax.ShapeDtypeStruct((count, beta.shape[0]), f32),
+        ),
+        (near, own, decay_down, gate_down, beta, weight),
+        scratch=[
+            pltpu.VMEM((count, width), bf16),
+            pltpu.SemaphoreType.DMA((4 + 3 * len(column_pieces(channels)),)),
+        ],
+        hbm=5,
+        grant=14,
+        flops=1024,
+        moved=1024,
+    )
+
+
 def front_body(slab_count, *refs):
-    arrived_refs, refs = refs[:slab_count], refs[slab_count:]
-    hbm_refs, refs = refs[:9], refs[9:]
+    rim_ref, slab_refs, refs = refs[0], refs[1 : slab_count - 1], refs[slab_count - 1 :]
+    (weights, downs, betas, pair_ref, pair_low_ref, pair_strength_ref), refs = refs[:6], refs[6:]
+    hbm_refs, refs = refs[:4], refs[4:]
     (own_ref, other_ref, solved_ref, attend_ref, start_ref, gate_ref), refs = refs[:6], refs[6:]
-    loaded, refs = refs[:8], refs[8:]
-    rows_ref, projected, mixing, inverse, inverse_low, sems = refs
-    rates, decay_down_ref, gate_down_ref, beta_ref, decay_up_ref, bias_ref, conv_ref, weights = loaded
-    hidden_ref, weight_ref = hbm_refs[0], hbm_refs[-1]
-    rim_ref, *slab_refs = arrived_refs
-    slab_rows = hidden_ref.shape[0]
+    loaded, refs = refs[:4], refs[4:]
+    rows_ref, projected, low_ref, strength_ref, mixing, inverse, inverse_low, sems = refs
+    rates, decay_up_ref, bias_ref, conv_ref = loaded
     heads, count, size = start_ref.shape
+    slab_rows = count // slab_count
     tap_count = conv_ref.shape[1]
     chunk = math.gcd(count, 64)
     chunks = count // chunk
     here = place("head")
-
-    def rows_of(k):
-        return pl.ds(pl.multiple_of(RIM + (here ^ k) * slab_rows, 16), slab_rows)
-
-    firsts = [pltpu.make_async_copy(hidden_ref, rows_ref.at[rows_of(0)], sems.at[0])]
-    for i in range(7):
-        firsts.append(pltpu.make_async_copy(hbm_refs[1 + i], loaded[i], sems.at[1 + i]))
-    pieces = [slice(i, i + 2 * size) for i in range(0, heads * size, 2 * size)]
-    loads = {}
-    for c in range(3):
-        for piece in pieces:
-            loads[c, piece.start] = pltpu.make_async_copy(
-                weight_ref.at[c, :, piece], weights.at[c, :, piece], sems.at[8 + len(loads)]
-            )
-    for copy in firsts + list(loads.values()):
+    copies = [pltpu.make_async_copy(hbm_refs[i], loaded[i], sems.at[i]) for i in range(4)]
+    for copy in copies:
         copy.start()
+
+    def rows_of(k, above=0):
+        return pl.ds(pl.multiple_of(above + (here ^ k) * slab_rows, 16), slab_rows)
+
     rows_ref[:RIM, :] = rim_ref[...]
     for k, ref in enumerate(slab_refs):
-        rows_ref[rows_of(k + 1), :] = ref[...]
-    for copy in firsts:
+        rows_ref[RIM + k * slab_rows : RIM + (k + 1) * slab_rows, :] = ref[...]
+    for k in range(2):
+        part = slice(k * slab_rows, (k + 1) * slab_rows)
+        low_ref[rows_of(k), :] = pair_low_ref[part, :]
+        strength_ref[rows_of(k), :] = pair_strength_ref[part, :]
+        for c in range(3):
+            projected[c, rows_of(k, RIM), :] = pair_ref[c, part, :].astype(f32)
+    far_low = dot(rows_ref[RIM:, :], downs[...]).astype(bf16)
+    far_strength = dot(rows_ref[RIM:, :], betas[...], ((1,), (1,)))
+    for k in range(2, slab_count):
+        part = slice((k - 2) * slab_rows, (k - 1) * slab_rows)
+        low_ref[rows_of(k), :] = far_low[part]
+        strength_ref[rows_of(k), :] = far_strength[part]
+    for copy in copies:
         copy.wait()
-
-    here_rows = rows_ref[RIM:, :]
     rank = decay_up_ref.shape[0]
-    low = dot(here_rows, jnp.concatenate([decay_down_ref[...], gate_down_ref[...]], axis=1))
-    decay_low = low[:, :rank].astype(bf16)
-    gate_ref[...] = low[:, rank:].astype(bf16)
-    strength = jax.nn.sigmoid(dot(here_rows, beta_ref[...], ((1,), (1,))))
+    low = low_ref[...]
+    decay_low = low[:, :rank]
+    gate_ref[...] = low[:, rank:]
+    strength = jax.nn.sigmoid(strength_ref[...])
     raw = dot(decay_low, decay_up_ref[...]) + bias_ref[...]
     rate = jnp.concatenate(
         [jnp.exp(jnp.full((1, size), rates[h], f32)) for h in range(heads)], axis=1
@@ -128,11 +208,12 @@
     for c in range(3):
         parts = []
         taps = conv_ref[c].astype(f32)
-        for piece in pieces:
-            loads[c, piece.start].wait()
-            projected[c, :, piece] = (
-                dot(rows_ref[...], weights[c, :, piece]).astype(bf16).astype(f32)
-            )
+        for piece in column_pieces(heads * size):
+            part = dot(rows_ref[...], weights[c, :, piece]).astype(bf16).astype(f32)
+            projected[c, :RIM, piece] = part[:RIM]
+            for k in range(2, slab_count):
+                begin = RIM + (k - 2) * slab_rows
+                projected[c, rows_of(k, RIM), piece] = part[begin : begin + slab_rows]
             total = None
             for i in range(tap_count):
                 shifted = projected[c, pl.ds(RIM - tap_count + 1 + i, count), piece]
@@ -232,14 +313,14 @@
         other_ref[h] = jnp.where(upper, low, high).astype(bf16)
 
 
-def front(rim, slabs, loaded, weight, size):
-    slab_count, slab_rows = len(slabs), slabs[0].shape[0]
+def front(rim, slabs, fetched, loaded, size):
+    weight, downs = fetched[:2]
+    slab_count, slab_rows = 2 + len(slabs), fetched[3].shape[1] // 2
     count = slab_count * slab_rows
     _, width, channels = weight.shape
     heads = channels // size
-    rank = loaded[1].shape[1]
     buffers = [pltpu.SMEM(loaded[0].shape, f32)]
-    buffers += [pltpu.VMEM(part.shape, part.dtype) for part in (*loaded[1:], weight)]
+    buffers += [pltpu.VMEM(part.shape, part.dtype) for part in loaded[1:]]
     return vmem_call(
         functools.partial(front_body, slab_count),
         (
@@ -248,19 +329,21 @@
             jax.ShapeDtypeStruct((heads, count, 2 * size), bf16),
             jax.ShapeDtypeStruct((heads, count, count), bf16),
             jax.ShapeDtypeStruct((heads, count, size), f32),
-            jax.ShapeDtypeStruct((count, rank), bf16),
+            jax.ShapeDtypeStruct((count, downs.shape[1] // 2), bf16),
         ),
-        (rim, *slabs[1:], slabs[0], *loaded, weight),
+        (rim, *slabs, *fetched, *loaded),
         scratch=[
             *buffers,
-            pltpu.VMEM((RIM + count, width), bf16),
+            pltpu.VMEM((RIM + count - 2 * slab_rows, width), bf16),
             pltpu.VMEM((3, RIM + count, channels), f32),
+            pltpu.VMEM((count, downs.shape[1]), bf16),
+            pltpu.VMEM((count, heads), f32),
             pltpu.VMEM((heads, count, count), bf16),
             pltpu.VMEM((heads, count, count), f32),
             pltpu.VMEM((heads, count, count), bf16),
-            pltpu.SemaphoreType.DMA((8 + 3 * pl.cdiv(heads, 2),)),
+            pltpu.SemaphoreType.DMA((len(loaded),)),
         ],
-        hbm=2 + len(loaded),
+        hbm=len(loaded),
         grant=24,
         flops=2 * count * width * channels * 4,
         moved=2 * 4 * width * channels,
@@ -421,13 +504,14 @@
     heads, size = decay_log.shape[0], norm_gain.shape[0]
     channels = heads * size
     devices = lax.axis_size("head")
-    slabs, rim = gathered(hidden_in, RIM)
+    weight = qkv_weight.transpose(1, 0, 2)
+    slabs, rim, fetched = gathered(
+        hidden_in,
+        RIM,
+        lambda one, two: early(one, two, decay_down, gate_down, beta_weight.T, weight),
+    )
     own, other, solved, attend, start, gate_low = front(
-        rim,
-        slabs,
-        (decay_log, decay_down, gate_down, beta_weight.T, decay_up, dt_bias[None], conv_weight),
-        qkv_weight.transpose(1, 0, 2),
-        size,
+        rim, slabs, fetched, (decay_log, decay_up, dt_bias[None], conv_weight), size
     )
     count = start.shape[1]
     raised, output_rows, out_gate = vmem_call(

time: 59.3 us -> 64.5 us (1.088)
  starting transfers between devices: 15.8 us -> 21 us
  Pallas kernels: 14.6 us -> 15.7 us
  local copies, waits for them, and re-layouts: 0.94 us -> 0.03 us
    ppermute x11 -> x12, starting transfers between devices: 14.5 us -> 19.6 us  [swapped(): lax.ppermute(block, axis, [(i, i ^ bit) for i in range(lax.axis_size(axis...]
    pallas_call x8 -> x10, Pallas kernels: 14.6 us -> 15.7 us  [vmem_call(): pl.pallas_call(body, out_shape=out_shape, in_specs=[pl.BlockSpec(memory_s...]
    slice x1 -> x0, local copies, waits for them, and re-layouts: 0.92 us -> none  [gathered(): tail = own[own.shape[0] - row_count:]]
    ppermute x11 -> x12, waiting for transfers between devices: 26.6 us -> 26.5 us  [swapped(): lax.ppermute(block, axis, [(i, i ^ bit) for i in range(lax.axis_size(axis...]
  transfers between devices with their start and end apart: 13 -> 14, of which waited for: 8 -> 9; matrix products, arithmetic and copies ran while one was open for 2% -> 0% of each run, Pallas kernels for 2% -> 9%
where the time goes in v4:
time: 64.5 us; the launch traced here: 64.3 us
  waiting for transfers between devices  26.5 us (41%)
  starting transfers between devices  21 us (33%)
  Pallas kernels  15.7 us (24%)
  other arithmetic  0.92 us (1%)
    ppermute x12, waiting for transfers between devices, swapped(): lax.ppermute(block, axis, [(i, i ^ bit) for i in range(lax.axis_size(axis...  26.5 us
    ppermute x12, starting transfers between devices, swapped(): lax.ppermute(block, axis, [(i, i ^ bit) for i in range(lax.axis_size(axis...  19.6 us
    pallas_call x10, Pallas kernels, vmem_call(): pl.pallas_call(body, out_shape=out_shape, in_specs=[pl.BlockSpec(memory_s...  15.7 us
    ppermute x2, starting transfers between devices, rim_at_last(): swaps.append(lax.ppermute(tail, ('seq', 'head'), route))  1.32 us
  transfers between devices with their start and end apart: 14, of which 9 were waited for; matrix products, arithmetic and copies ran while one was open for 0% of the time, Pallas kernels for 9%

profile of v4, /device:TPU:0, one launch (start us, length us, event | category | flops | bytes accessed | tf_op | source)
XLA Modules:
  0.0 64.3 jit_solution(13000663015314407727)
XLA Ops:
  0.0 1.0 %shard_map.118 = bf16[16,2304]{1,0:T(8,128)(2,1)S(1)} custom-call(bf16[64,2304]{1,0:T(8,128)(2,1)} %hidden_ref.1), custom_call_target="tpu_custom_call" | custom-call | tf_op jit(solution)/shard_map/pallas_call | solution.py:75
  1.0 0.7 %collective-permute-start.1 = (bf16[16,2304]{1,0:T(8,128)(2,1)S(1)}, bf16[16,2304]{1,0:T(8,128)(2,1)S(1)}, u32[]{:S(2)}, u32[]{:S(2)}) collective-permute-start(bf16[16,2304]{1,0:T(8,128)(2,1)S(1)} %shard_map.118), channel_id=1, source_target_pairs={{3,7},{7,3},{11,15},{15,11},{19,23},{23,19},{27,31},{31,27}} | collective-permute-start | bytes 221192 | tf_op jit(solution)/shard_map/ppermute | solution.py:47
  1.6 0.7 %collective-permute-start.2 = (bf16[16,2304]{1,0:T(8,128)(2,1)S(1)}, bf16[16,2304]{1,0:T(8,128)(2,1)S(1)}, u32[]{:S(2)}, u32[]{:S(2)}) collective-permute-start(bf16[16,2304]{1,0:T(8,128)(2,1)S(1)} %shard_map.118), channel_id=1, source_target_pairs={{7,11},{11,7},{15,19},{19,15},{23,27},{27,23}} | collective-permute-start | bytes 221192 | tf_op jit(solution)/shard_map/ppermute | solution.py:47
  2.3 0.5 collective-permute-start.3
  2.8 4.8 %collective-permute-start = (bf16[64,2304]{1,0:T(8,128)(2,1)}, bf16[64,2304]{1,0:T(8,128)(2,1)S(1)}, u32[]{:S(2)}, u32[]{:S(2)}) collective-permute-start(bf16[64,2304]{1,0:T(8,128)(2,1)} %hidden_ref.1), channel_id=1, source_target_pairs={{0,2},{1,3},{2,0},{3,1},{4,6},{5,7},{6,4},{7,5},{8,10},{9,11},{10,... | collective-permute-start | bytes 884744 | tf_op jit(solution)/shard_map/ppermute | solution.py:23
  7.6 0.0 collective-permute-done.1
  7.6 0.0 collective-permute-done.2
  7.6 0.0 collective-permute-done.3.near_ref
  7.7 4.6 %shard_map.119 = (bf16[3,2304,512]{2,1,0:T(8,128)(2,1)S(1)}, bf16[2304,256]{1,0:T(8,128)(2,1)S(1)}, bf16[4,2304]{1,0:T(4,128)(2,1)S(1)}, bf16[3,128,512]{2,1,0:T...) custom-call(bf16[64,2304]{1,0:T(8,128)(2,1)S(1)} %collective-permute-done.3.near_ref, ...), custom_call_target="tpu_custom_call" | custom-call | flops 1024 | bytes 1024 | tf_op jit(solution)/shard_map/pallas_call | solution.py:75
  12.3 0.0 copy-start.1
  12.3 0.0 copy-start
  12.3 0.0 copy-start.2
  12.3 2.8 %collective-permute-done.refs_1_ = bf16[64,2304]{1,0:T(8,128)(2,1)S(1)} collective-permute-done((bf16[64,2304]{1,0:T(8,128)(2,1)}, bf16[64,2304]{1,0:T(8,128)(2,1)S(1)}, u32[]{:S(2)}, u32[]{:S(2)}) %collective-permute-start) | collective-permute-done | bytes 294944 | tf_op jit(solution)/shard_map/ppermute | solution.py:23
  15.1 0.0 collective-permute-start.6
  15.1 1.7 %collective-permute-start.4 = (bf16[16,2304]{1,0:T(8,128)(2,1)S(1)}, bf16[16,2304]{1,0:T(8,128)(2,1)S(1)}, u32[]{:S(2)}, u32[]{:S(2)}) collective-permute-start(bf16[16,2304]{1,0:T(8,128)(2,1)S(1)} %broadcast_select_fusion), channel_id=1, source_target_pairs={{0,2},{1,3},{2,0},{3,1},{4,6},{5,7},{6,4},{7,5},{8,10},{9,11},{10,... | collective-permute-start | bytes 221192 | tf_op jit(solution)/shard_map/ppermute | solution.py:23
  16.8 2.9 %collective-permute-done.4 = bf16[16,2304]{1,0:T(8,128)(2,1)S(1)} collective-permute-done((bf16[16,2304]{1,0:T(8,128)(2,1)S(1)}, bf16[16,2304]{1,0:T(8,128)(2,1)S(1)}, u32[]{:S(2)}, u32[]{:S(2)}) %collective-permute-start.4) | collective-permute-done | bytes 73760 | tf_op jit(solution)/shard_map/ppermute | solution.py:23
  19.8 0.1 collective-permute-start.5
  19.9 1.3 %collective-permute-done.5 = bf16[16,2304]{1,0:T(8,128)(2,1)S(1)} collective-permute-done((bf16[16,2304]{1,0:T(8,128)(2,1)S(1)}, bf16[16,2304]{1,0:T(8,128)(2,1)S(1)}, u32[]{:S(2)}, u32[]{:S(2)}) %collective-permute-start.5) | collective-permute-done | bytes 73760 | tf_op jit(solution)/shard_map/ppermute | solution.py:23
  21.2 0.0 collective-permute-done.6.refs_2_
  21.2 7.5 %shard_map.120 = (bf16[2,128,256]{2,1,0:T(8,128)(2,1)S(1)}, bf16[2,128,256]{2,1,0:T(8,128)(2,1)S(1)}, bf16[4,256,256]{2,1,0:T(8,128)(2,1)S(1)}, bf16[4,256,256]{...) custom-call(bf16[16,2304]{1,0:T(8,128)(2,1)S(1)} %add.21.refs_0_, ...), custom_call_target="tpu_custom_call" | custom-call | flops 2415919104 | bytes 9437184 | tf_op jit(solution)/shard_map/pallas_call | solution.py:75
  28.6 4.1 %collective-permute-start.7 = (bf16[2,128,256]{2,1,0:T(8,128)(2,1)S(1)}, bf16[2,128,256]{2,1,0:T(8,128)(2,1)S(1)}, u32[]{:S(2)}, u32[]{:S(2)}) collective-permute-start(bf16[2,128,256]{2,1,0:T(8,128)(2,1)S(1)} %get-tuple-element.49), channel_id=1, source_target_pairs={{0,4},{4,0},{8,12},{12,8},{16,20},{20,16},{24,28},{28,24},{1,5},{5... | collective-permute-start | bytes 393224 | tf_op jit(solution)/shard_map/ppermute | solution.py:23
  32.7 3.8 %collective-permute-done.7.far_ref.partner_ref = bf16[2,128,256]{2,1,0:T(8,128)(2,1)S(1)} collective-permute-done((bf16[2,128,256]{2,1,0:T(8,128)(2,1)S(1)}, bf16[2,128,256]{2,1,0:T(8,128)(2,1)S(1)}, u32[]{:S(2)}, u32[]{:S(2)}) %collective-permute-start.7) | collective-permute-done | bytes 131104 | tf_op jit(solution)/shard_map/ppermute | solution.py:23
  36.5 0.2 shard_map.121.own_ref
  36.7 1.6 %collective-permute-start.8 = (bf16[2,128,256]{2,1,0:T(8,128)(2,1)S(1)}, bf16[2,128,256]{2,1,0:T(8,128)(2,1)S(1)}, u32[]{:S(2)}, u32[]{:S(2)}) collective-permute-start(bf16[2,128,256]{2,1,0:T(8,128)(2,1)S(1)} %shard_map.121.own_ref), channel_id=1, source_target_pairs={{0,8},{4,12},{8,0},{12,4},{16,24},{20,28},{24,16},{28,20},{1,9},{5... | collective-permute-start | bytes 393224 | tf_op jit(solution)/shard_map/ppermute | solution.py:23
  38.3 3.5 %collective-permute-done.8.far_ref = bf16[2,128,256]{2,1,0:T(8,128)(2,1)S(1)} collective-permute-done((bf16[2,128,256]{2,1,0:T(8,128)(2,1)S(1)}, bf16[2,128,256]{2,1,0:T(8,128)(2,1)S(1)}, u32[]{:S(2)}, u32[]{:S(2)}) %collective-permute-start.8) | collective-permute-done | bytes 131104 | tf_op jit(solution)/shard_map/ppermute | solution.py:23
  41.8 0.2 shard_map.123
  42.0 2.6 %collective-permute-start.9 = (bf16[2,128,128]{2,1,0:T(8,128)(2,1)S(1)}, bf16[2,128,128]{2,1,0:T(8,128)(2,1)S(1)}, u32[]{:S(2)}, u32[]{:S(2)}) collective-permute-start(bf16[2,128,128]{2,1,0:T(8,128)(2,1)S(1)} %shard_map.123), channel_id=1, source_target_pairs={{0,16},{4,20},{8,24},{12,28},{16,0},{20,4},{24,8},{28,12},{1,17},{... | collective-permute-start | bytes 196616 | tf_op jit(solution)/shard_map/ppermute | solution.py:23
  44.7 0.2 shard_map.122.near_ref
  44.9 2.4 %collective-permute-done.9.far_ref = bf16[2,128,128]{2,1,0:T(8,128)(2,1)S(1)} collective-permute-done((bf16[2,128,128]{2,1,0:T(8,128)(2,1)S(1)}, bf16[2,128,128]{2,1,0:T(8,128)(2,1)S(1)}, u32[]{:S(2)}, u32[]{:S(2)}) %collective-permute-start.9) | collective-permute-done | bytes 65568 | tf_op jit(solution)/shard_map/ppermute | solution.py:23
  47.2 0.3 shard_map.124
  47.6 1.7 %collective-permute-start.10 = (bf16[2,128,128]{2,1,0:T(8,128)(2,1)S(1)}, bf16[2,128,128]{2,1,0:T(8,128)(2,1)S(1)}, u32[]{:S(2)}, u32[]{:S(2)}) collective-permute-start(bf16[2,128,128]{2,1,0:T(8,128)(2,1)S(1)} %get-tuple-element.51), channel_id=1, source_target_pairs={{0,4},{4,0},{8,12},{12,8},{16,20},{20,16},{24,28},{28,24},{1,5},{5... | collective-permute-start | bytes 196616 | tf_op jit(solution)/shard_map/ppermute | solution.py:23
  49.3 0.0 copy-done.1
  49.3 0.4 shard_map.125
  49.6 2.2 %collective-permute-done.10.other_ref = bf16[2,128,128]{2,1,0:T(8,128)(2,1)S(1)} collective-permute-done((bf16[2,128,128]{2,1,0:T(8,128)(2,1)S(1)}, bf16[2,128,128]{2,1,0:T(8,128)(2,1)S(1)}, u32[]{:S(2)}, u32[]{:S(2)}) %collective-permute-start.10) | collective-permute-done | bytes 65568 | tf_op jit(solution)/shard_map/ppermute | solution.py:23
  51.9 0.0 copy-done
  51.9 0.0 copy-done.2
  51.9 0.7 %shard_map.127 = (f32[64,2304]{1,0:T(8,128)S(1)}, bf16[64,2304]{1,0:T(8,128)(2,1)S(1)}) custom-call(bf16[2,128,128]{2,1,0:T(8,128)(2,1)S(1)} %get-tuple-element.50.own_ref, bf16[2,128,128]{2,1,0:T(8,128)(2,1)S(1)} %collective-permute-done.10.other_ref, bf16[4,256,128]{2,1,0:T(8,128)(2,1)S(1)} %get-tuple-element.56.raised_ref, ...), custom_call_target="tpu_custom_call" | custom-call | flops 301989888 | bytes 2359296 | tf_op jit(solution)/shard_map/pallas_call | solution.py:75
  52.6 0.1 collective-permute-start.12
  52.7 0.7 %shard_map.126 = (f32[64,2304]{1,0:T(8,128)S(1)}, bf16[64,2304]{1,0:T(8,128)(2,1)S(1)}) custom-call(bf16[2,128,128]{2,1,0:T(8,128)(2,1)S(1)} %get-tuple-element.50.own_ref, bf16[2,128,128]{2,1,0:T(8,128)(2,1)S(1)} %collective-permute-done.10.other_ref, bf16[4,256,128]{2,1,0:T(8,128)(2,1)S(1)} %get-tuple-element.56.raised_ref, ...), custom_call_target="tpu_custom_call" | custom-call | flops 301989888 | bytes 2359296 | tf_op jit(solution)/shard_map/pallas_call | solution.py:75
  53.5 0.6 collective-permute-start.11
  54.0 0.3 collective-permute-done.12
  54.3 0.1 add_convert_fusion.1
  54.3 1.8 %collective-permute-start.13 = (bf16[64,2304]{1,0:T(8,128)(2,1)S(1)}, bf16[64,2304]{1,0:T(8,128)(2,1)S(1)}, u32[]{:S(2)}, u32[]{:S(2)}) collective-permute-start(bf16[64,2304]{1,0:T(8,128)(2,1)S(1)} %add_convert_fusion.1), channel_id=1, source_target_pairs={{0,2},{1,3},{2,0},{3,1},{4,6},{5,7},{6,4},{7,5},{8,10},{9,11},{10,... | collective-permute-start | bytes 884744 | tf_op jit(solution)/shard_map/ppermute | solution.py:23
  56.2 0.0 collective-permute-done.11
  56.2 7.3 %collective-permute-done.13 = bf16[64,2304]{1,0:T(8,128)(2,1)S(1)} collective-permute-done((bf16[64,2304]{1,0:T(8,128)(2,1)S(1)}, bf16[64,2304]{1,0:T(8,128)(2,1)S(1)}, u32[]{:S(2)}, u32[]{:S(2)}) %collective-permute-start.13) | collective-permute-done | bytes 294944 | tf_op jit(solution)/shard_map/ppermute | solution.py:23
  63.5 0.8 %add_convert_fusion = bf16[64,2304]{1,0:T(8,128)(2,1)} fusion(bf16[64,2304]{1,0:T(8,128)(2,1)S(1)} %collective-permute-done.13, f32[64,2304]{1,0:T(8,128)S(1)} %get-tuple-element.59, bf16[64,2304]{1,0:T(8,128)(2,1)S(1)} %collective-permute-done.11), kind=kLoop, calls=%fused_computation | loop fusion | flops 737280 | bytes 1474560 | tf_op jit(solution)/shard_map/convert_element_type | solution.py:543
  (5 shorter events, 0.1 us)
Async XLA Ops:
  1.0 6.7 %collective-permute-start.1 = (bf16[16,2304]{1,0:T(8,128)(2,1)S(1)}, bf16[16,2304]{1,0:T(8,128)(2,1)S(1)}, u32[]{:S(2)}, u32[]{:S(2)}) collective-permute-start(bf16[16,2304]{1,0:T(8,128)(2,1)S(1)} %shard_map.118), channel_id=1, source_target_pairs={{3,7},{7,3},{11,15},{15,11},{19,23},{23,19},{27,31},{31,27}} | collective-permute-start | bytes 221192 | tf_op jit(solution)/shard_map/ppermute | solution.py:47
  1.6 6.0 %collective-permute-start.2 = (bf16[16,2304]{1,0:T(8,128)(2,1)S(1)}, bf16[16,2304]{1,0:T(8,128)(2,1)S(1)}, u32[]{:S(2)}, u32[]{:S(2)}) collective-permute-start(bf16[16,2304]{1,0:T(8,128)(2,1)S(1)} %shard_map.118), channel_id=1, source_target_pairs={{7,11},{11,7},{15,19},{19,15},{23,27},{27,23}} | collective-permute-start | bytes 221192 | tf_op jit(solution)/shard_map/ppermute | solution.py:47
  2.3 5.3 %collective-permute-start.3 = (bf16[64,2304]{1,0:T(8,128)(2,1)}, bf16[64,2304]{1,0:T(8,128)(2,1)S(1)}, u32[]{:S(2)}, u32[]{:S(2)}) collective-permute-start(bf16[64,2304]{1,0:T(8,128)(2,1)} %hidden_ref.1), channel_id=1, source_target_pairs={{0,1},{1,0},{2,3},{3,2},{4,5},{5,4},{6,7},{7,6},{8,9},{9,8},{10,11... | collective-permute-start | bytes 884744 | tf_op jit(solution)/shard_map/ppermute | solution.py:23
  2.8 12.3 %collective-permute-start = (bf16[64,2304]{1,0:T(8,128)(2,1)}, bf16[64,2304]{1,0:T(8,128)(2,1)S(1)}, u32[]{:S(2)}, u32[]{:S(2)}) collective-permute-start(bf16[64,2304]{1,0:T(8,128)(2,1)} %hidden_ref.1), channel_id=1, source_target_pairs={{0,2},{1,3},{2,0},{3,1},{4,6},{5,7},{6,4},{7,5},{8,10},{9,11},{10,... | collective-permute-start | bytes 884744 | tf_op jit(solution)/shard_map/ppermute | solution.py:23
  12.3 37.0 %copy-start.1 = (bf16[128,512]{1,0:T(8,128)(2,1)S(1)}, bf16[128,512]{1,0:T(8,128)(2,1)}, u32[]{:S(2)}) copy-start(bf16[128,512]{1,0:T(8,128)(2,1)} %up_ref.1) | copy-start | bytes 393220
  12.3 39.6 %copy-start = (bf16[512,2304]{1,0:T(8,128)(2,1)S(1)}, bf16[512,2304]{1,0:T(8,128)(2,1)}, u32[]{:S(2)}) copy-start(bf16[512,2304]{1,0:T(8,128)(2,1)} %weight_ref.3) | copy-start | bytes 7077892
  12.3 39.6 %copy-start.2 = (f32[128]{0:T(128)S(1)}, f32[128]{0:T(128)}, u32[]{:S(2)}) copy-start(f32[128]{0:T(128)} %param.22) | copy-start | bytes 1540
  15.1 6.1 %collective-permute-start.6 = (bf16[64,2304]{1,0:T(8,128)(2,1)S(1)}, bf16[64,2304]{1,0:T(8,128)(2,1)S(1)}, u32[]{:S(2)}, u32[]{:S(2)}) collective-permute-start(bf16[64,2304]{1,0:T(8,128)(2,1)S(1)} %collective-permute-done.refs_1_), channel_id=1, source_target_pairs={{0,1},{1,0},{2,3},{3,2},{4,5},{5,4},{6,7},{7,6},{8,9},{9,8},{10,11... | collective-permute-start | bytes 884744 | tf_op jit(solution)/shard_map/ppermute | solution.py:23
  15.1 4.7 %collective-permute-start.4 = (bf16[16,2304]{1,0:T(8,128)(2,1)S(1)}, bf16[16,2304]{1,0:T(8,128)(2,1)S(1)}, u32[]{:S(2)}, u32[]{:S(2)}) collective-permute-start(bf16[16,2304]{1,0:T(8,128)(2,1)S(1)} %broadcast_select_fusion), channel_id=1, source_target_pairs={{0,2},{1,3},{2,0},{3,1},{4,6},{5,7},{6,4},{7,5},{8,10},{9,11},{10,... | collective-permute-start | bytes 221192 | tf_op jit(solution)/shard_map/ppermute | solution.py:23
  19.8 1.3 %collective-permute-start.5 = (bf16[16,2304]{1,0:T(8,128)(2,1)S(1)}, bf16[16,2304]{1,0:T(8,128)(2,1)S(1)}, u32[]{:S(2)}, u32[]{:S(2)}) collective-permute-start(bf16[16,2304]{1,0:T(8,128)(2,1)S(1)} %add.20), channel_id=1, source_target_pairs={{0,1},{1,0},{2,3},{3,2},{4,5},{5,4},{6,7},{7,6},{8,9},{9,8},{10,11... | collective-permute-start | bytes 221192 | tf_op jit(solution)/shard_map/ppermute | solution.py:23
  28.6 7.9 %collective-permute-start.7 = (bf16[2,128,256]{2,1,0:T(8,128)(2,1)S(1)}, bf16[2,128,256]{2,1,0:T(8,128)(2,1)S(1)}, u32[]{:S(2)}, u32[]{:S(2)}) collective-permute-start(bf16[2,128,256]{2,1,0:T(8,128)(2,1)S(1)} %get-tuple-element.49), channel_id=1, source_target_pairs={{0,4},{4,0},{8,12},{12,8},{16,20},{20,16},{24,28},{28,24},{1,5},{5... | collective-permute-start | bytes 393224 | tf_op jit(solution)/shard_map/ppermute | solution.py:23
  36.7 5.1 %collective-permute-start.8 = (bf16[2,128,256]{2,1,0:T(8,128)(2,1)S(1)}, bf16[2,128,256]{2,1,0:T(8,128)(2,1)S(1)}, u32[]{:S(2)}, u32[]{:S(2)}) collective-permute-start(bf16[2,128,256]{2,1,0:T(8,128)(2,1)S(1)} %shard_map.121.own_ref), channel_id=1, source_target_pairs={{0,8},{4,12},{8,0},{12,4},{16,24},{20,28},{24,16},{28,20},{1,9},{5... | collective-permute-start | bytes 393224 | tf_op jit(solution)/shard_map/ppermute | solution.py:23
  42.0 5.2 %collective-permute-start.9 = (bf16[2,128,128]{2,1,0:T(8,128)(2,1)S(1)}, bf16[2,128,128]{2,1,0:T(8,128)(2,1)S(1)}, u32[]{:S(2)}, u32[]{:S(2)}) collective-permute-start(bf16[2,128,128]{2,1,0:T(8,128)(2,1)S(1)} %shard_map.123), channel_id=1, source_target_pairs={{0,16},{4,20},{8,24},{12,28},{16,0},{20,4},{24,8},{28,12},{1,17},{... | collective-permute-start | bytes 196616 | tf_op jit(solution)/shard_map/ppermute | solution.py:23
  47.6 4.3 %collective-permute-start.10 = (bf16[2,128,128]{2,1,0:T(8,128)(2,1)S(1)}, bf16[2,128,128]{2,1,0:T(8,128)(2,1)S(1)}, u32[]{:S(2)}, u32[]{:S(2)}) collective-permute-start(bf16[2,128,128]{2,1,0:T(8,128)(2,1)S(1)} %get-tuple-element.51), channel_id=1, source_target_pairs={{0,4},{4,0},{8,12},{12,8},{16,20},{20,16},{24,28},{28,24},{1,5},{5... | collective-permute-start | bytes 196616 | tf_op jit(solution)/shard_map/ppermute | solution.py:23
  52.6 1.6 %collective-permute-start.12 = (bf16[64,2304]{1,0:T(8,128)(2,1)S(1)}, bf16[64,2304]{1,0:T(8,128)(2,1)S(1)}, u32[]{:S(2)}, u32[]{:S(2)}) collective-permute-start(bf16[64,2304]{1,0:T(8,128)(2,1)S(1)} %get-tuple-element.62), channel_id=1, source_target_pairs={{0,1},{1,0},{2,3},{3,2},{4,5},{5,4},{6,7},{7,6},{8,9},{9,8},{10,11... | collective-permute-start | bytes 884744 | tf_op jit(solution)/shard_map/ppermute | solution.py:23
  53.5 2.7 %collective-permute-start.11 = (bf16[64,2304]{1,0:T(8,128)(2,1)S(1)}, bf16[64,2304]{1,0:T(8,128)(2,1)S(1)}, u32[]{:S(2)}, u32[]{:S(2)}) collective-permute-start(bf16[64,2304]{1,0:T(8,128)(2,1)S(1)} %get-tuple-element.60), channel_id=1, source_target_pairs={{0,1},{1,0},{2,3},{3,2},{4,5},{5,4},{6,7},{7,6},{8,9},{9,8},{10,11... | collective-permute-start | bytes 884744 | tf_op jit(solution)/shard_map/ppermute | solution.py:23
  54.3 9.1 %collective-permute-start.13 = (bf16[64,2304]{1,0:T(8,128)(2,1)S(1)}, bf16[64,2304]{1,0:T(8,128)(2,1)S(1)}, u32[]{:S(2)}, u32[]{:S(2)}) collective-permute-start(bf16[64,2304]{1,0:T(8,128)(2,1)S(1)} %add_convert_fusion.1), channel_id=1, source_target_pairs={{0,2},{1,3},{2,0},{3,1},{4,6},{5,7},{6,4},{7,5},{8,10},{9,11},{10,... | collective-permute-start | bytes 884744 | tf_op jit(solution)/shard_map/ppermute | solution.py:23

commit v5 on v3

--- a/solution.py
+++ b/solution.py
@@ -28,24 +28,31 @@
     return [1 << i for i in range(size.bit_length() - 1)]
 
 
-def gathered(own, row_count):
+def rim_route(target):
     heads, seqs = lax.axis_size("head"), lax.axis_size("seq")
+    pairs = [(s * heads + heads - 1, (s + 1) * heads + target) for s in range(seqs - 1)]
+    return pairs + [(two, one) for one, two in pairs]
+
+
+def gathered(own, tail):
+    bits = bits_of(lax.axis_size("head"))
+    assert bits
+    heads, here = lax.axis_size("head"), lax.axis_index("head")
     slabs = {0: own}
-    for bit in reversed(bits_of(heads)[1:]):
+    for bit in reversed(bits[1:]):
         for k in sorted(slabs):
             slabs[k ^ bit] = swapped(slabs[k], "head", bit)
-    tail = own[own.shape[0] - row_count :]
+    targets = [first if first == heads - 2 else first + 1 for first in range(0, heads, 2)]
+    tails = [lax.ppermute(tail, ("seq", "head"), rim_route(target)) for target in targets]
+    slabs[1] = swapped(own, "head", 1)
+    arrived = [k for k in sorted(slabs) if k > 1]
+    moved, tails = lax.optimization_barrier(([slabs[k] for k in arrived], tails))
     rim = jnp.zeros_like(tail)
-    for k in range(min(1, heads - 1), heads, 2):
-        route = [(s * heads + heads - 1, (s + 1) * heads + k) for s in range(seqs - 1)]
-        rim = rim + lax.ppermute(tail, ("seq", "head"), route)
-    if heads > 1:
-        slabs[1] = swapped(own, "head", 1)
-        arrived = [k for k in sorted(slabs) if k > 1]
-        moved, rim = lax.optimization_barrier(([slabs[k] for k in arrived], rim))
-        for k, slab in zip(arrived, moved):
-            slabs[k], slabs[k ^ 1] = slab, swapped(slab, "head", 1)
-        rim = rim + swapped(rim, "head", 1)
+    for target, received in zip(targets, tails):
+        rim = jnp.where(here == target, received, rim)
+    for k, slab in zip(arrived, moved):
+        slabs[k], slabs[k ^ 1] = slab, swapped(slab, "head", 1)
+    rim = rim + swapped(rim, "head", 1)
     return [slabs[k] for k in range(heads)], rim
 
 
@@ -69,109 +76,162 @@
     return here if bit is None else here // bit % 2
 
 
+def column_pieces(width):
+    step = math.gcd(width, 256)
+    return [slice(i, i + step) for i in range(0, width, step)]
+
+
+def load_body(
+    hidden_ref, decay_down_ref, gate_down_ref, beta_ref, weight_ref,
+    tail_ref, weights, downs, betas, sems,
+):
+    first, rank = hidden_ref.shape[0] - tail_ref.shape[0], decay_down_ref.shape[1]
+    copies = [
+        pltpu.make_async_copy(hidden_ref.at[pl.ds(first, tail_ref.shape[0])], tail_ref, sems.at[0]),
+        pltpu.make_async_copy(decay_down_ref, downs.at[:, pl.ds(0, rank)], sems.at[1]),
+        pltpu.make_async_copy(gate_down_ref, downs.at[:, pl.ds(rank, rank)], sems.at[2]),
+        pltpu.make_async_copy(beta_ref, betas, sems.at[3]),
+    ]
+    for c in range(2):
+        copies.append(pltpu.make_async_copy(weight_ref.at[c], weights.at[c], sems.at[4 + c]))
+    for copy in copies:
+        copy.start()
+    for copy in copies:
+        copy.wait()
+
+
+def load(own, decay_down, gate_down, beta, weight):
+    width, rank = decay_down.shape
+    return vmem_call(
+        load_body,
+        (
+            jax.ShapeDtypeStruct((RIM, width), bf16),
+            jax.ShapeDtypeStruct((2, *weight.shape[1:]), bf16),
+            jax.ShapeDtypeStruct((width, 2 * rank), bf16),
+            jax.ShapeDtypeStruct(beta.shape, bf16),
+        ),
+        (own, decay_down, gate_down, beta, weight),
+        scratch=[pltpu.SemaphoreType.DMA((6,))],
+        hbm=5,
+        grant=8,
+    )
+
+
 def front_body(slab_count, *refs):
-    arrived_refs, refs = refs[:slab_count], refs[slab_count:]
-    hbm_refs, refs = refs[:9], refs[9:]
+    (rim_ref, *slab_refs), refs = refs[:slab_count], refs[slab_count:]
+    (weights, downs, betas), refs = refs[:3], refs[3:]
+    hbm_refs, refs = refs[:6], refs[6:]
     (own_ref, other_ref, solved_ref, attend_ref, start_ref, gate_ref), refs = refs[:6], refs[6:]
-    loaded, refs = refs[:8], refs[8:]
-    rows_ref, projected, mixing, inverse, inverse_low, sems = refs
-    rates, decay_down_ref, gate_down_ref, beta_ref, decay_up_ref, bias_ref, conv_ref, weights = loaded
+    loaded, refs = refs[:5], refs[5:]
+    rows_ref, projected, mixing, inverse, sems = refs
+    rates, decay_up_ref, bias_ref, conv_ref, value_weight = loaded
     hidden_ref, weight_ref = hbm_refs[0], hbm_refs[-1]
-    rim_ref, *slab_refs = arrived_refs
-    slab_rows = hidden_ref.shape[0]
     heads, count, size = start_ref.shape
+    slab_rows = count // slab_count
     tap_count = conv_ref.shape[1]
+    rank = decay_up_ref.shape[0]
     chunk = math.gcd(count, 64)
     chunks = count // chunk
+    block = math.gcd(count, 128)
+    blocks = count // block
     here = place("head")
 
     def rows_of(k):
         return pl.ds(pl.multiple_of(RIM + (here ^ k) * slab_rows, 16), slab_rows)
 
-    firsts = [pltpu.make_async_copy(hidden_ref, rows_ref.at[rows_of(0)], sems.at[0])]
-    for i in range(7):
-        firsts.append(pltpu.make_async_copy(hbm_refs[1 + i], loaded[i], sems.at[1 + i]))
-    pieces = [slice(i, i + 2 * size) for i in range(0, heads * size, 2 * size)]
-    loads = {}
-    for c in range(3):
-        for piece in pieces:
-            loads[c, piece.start] = pltpu.make_async_copy(
-                weight_ref.at[c, :, piece], weights.at[c, :, piece], sems.at[8 + len(loads)]
+    fetch = pltpu.make_async_copy(hidden_ref, rows_ref.at[rows_of(0)], sems.at[0])
+    small = [pltpu.make_async_copy(hbm_refs[1 + i], loaded[i], sems.at[1 + i]) for i in range(4)]
+    pieces = column_pieces(heads * size)
+    streams = []
+    for i, piece in enumerate(pieces):
+        streams.append(
+            pltpu.make_async_copy(
+                weight_ref.at[2, :, piece], value_weight.at[:, piece], sems.at[5 + i]
             )
-    for copy in firsts + list(loads.values()):
+        )
+    for copy in [fetch] + small + streams:
         copy.start()
     rows_ref[:RIM, :] = rim_ref[...]
     for k, ref in enumerate(slab_refs):
         rows_ref[rows_of(k + 1), :] = ref[...]
-    for copy in firsts:
+    fetch.wait()
+    for c in range(2):
+        for piece in pieces:
+            projected[c, :, piece] = dot(rows_ref[...], weights[c, :, piece])
+    low = dot(rows_ref[RIM:, :], downs[...]).astype(bf16)
+    gate_ref[...] = low[:, rank:]
+    strength = jax.nn.sigmoid(dot(rows_ref[RIM:, :], betas[...], ((1,), (1,))))
+    for copy in small:
         copy.wait()
-
-    here_rows = rows_ref[RIM:, :]
-    rank = decay_up_ref.shape[0]
-    low = dot(here_rows, jnp.concatenate([decay_down_ref[...], gate_down_ref[...]], axis=1))
-    decay_low = low[:, :rank].astype(bf16)
-    gate_ref[...] = low[:, rank:].astype(bf16)
-    strength = jax.nn.sigmoid(dot(here_rows, beta_ref[...], ((1,), (1,))))
-    raw = dot(decay_low, decay_up_ref[...]) + bias_ref[...]
+    raw = dot(low[:, :rank], decay_up_ref[...]) + bias_ref[...]
+    softplus = jnp.maximum(raw, 0.0) + jnp.log(1.0 + jnp.exp(-jnp.abs(raw)))
     rate = jnp.concatenate(
         [jnp.exp(jnp.full((1, size), rates[h], f32)) for h in range(heads)], axis=1
     )
-    softplus = jnp.maximum(raw, 0.0) + jnp.log1p(jnp.exp(-jnp.abs(raw)))
     log_decay = -rate * softplus
     row = lax.broadcasted_iota(jnp.int32, (count, count), 0)
     col = lax.broadcasted_iota(jnp.int32, (count, count), 1)
     lower = jnp.where(row >= col, 1.0, 0.0).astype(bf16)
-    high = log_decay.astype(bf16)
-    cumulative = dot(lower, high) + dot(lower, (log_decay - high.astype(f32)).astype(bf16))
-
-    convolved = []
-    for c in range(3):
-        parts = []
+
+    def exact(left, right):
+        high = right.astype(bf16)
+        return dot(left, high) + dot(left, (right - high.astype(f32)).astype(bf16))
+
+    cumulative = exact(lower, log_decay)
+    spread = lax.broadcasted_iota(jnp.int32, (heads, heads * size), 1) // size
+    spread = spread == lax.broadcasted_iota(jnp.int32, (heads, heads * size), 0)
+    spread = jnp.where(spread, 1.0, 0.0).astype(bf16)
+    high = strength.astype(bf16)
+    strengths = dot(high, spread) + dot((strength - high.astype(f32)).astype(bf16), spread)
+    for i, piece in enumerate(pieces):
+        streams[i].wait()
+        projected[2, :, piece] = dot(rows_ref[...], value_weight[:, piece])
+
+    def convolved(c, lanes):
         taps = conv_ref[c].astype(f32)
-        for piece in pieces:
-            loads[c, piece.start].wait()
-            projected[c, :, piece] = (
-                dot(rows_ref[...], weights[c, :, piece]).astype(bf16).astype(f32)
-            )
-            total = None
-            for i in range(tap_count):
-                shifted = projected[c, pl.ds(RIM - tap_count + 1 + i, count), piece]
-                term = shifted * taps[i : i + 1, piece]
-                total = term if total is None else total + term
-            parts.append((total / (1.0 + jnp.exp(-total))).astype(bf16).astype(f32))
-        convolved.append(jnp.concatenate(parts, axis=1))
+        total = None
+        for i in range(tap_count):
+            shifted = projected[c, pl.ds(RIM - tap_count + 1 + i, count), lanes]
+            term = shifted * taps[i : i + 1, lanes]
+            total = term if total is None else total + term
+        half = 0.5 * total
+        return half + half * jnp.tanh(half)
 
     def by_chunk(rows):
         return jnp.concatenate([jnp.broadcast_to(r, (chunk, size)) for r in rows], axis=0)
 
-    eye = row == col
+    ones = jnp.full((size, size), 1.0, bf16)
+    scaled = jnp.full((size, size), float(size), bf16)
     stops, sides = [], []
     for h in range(heads):
         lanes = slice(h * size, (h + 1) * size)
-        queries, keys, values = (part[:, lanes] for part in convolved)
-        queries = queries * lax.rsqrt(jnp.sum(queries * queries, -1, keepdims=True) + 1e-06)
-        queries = queries * size ** (-0.5)
-        keys = keys * lax.rsqrt(jnp.sum(keys * keys, -1, keepdims=True) + 1e-06)
+        queries, keys, values = (convolved(c, lanes) for c in range(3))
+        power = dot((queries * queries).astype(bf16), scaled)
+        queries = queries * lax.rsqrt(power + size * 1e-06)
+        power = dot((keys * keys).astype(bf16), ones)
+        keys = keys * lax.rsqrt(power + 1e-06)
         running = cumulative[:, lanes]
         middles = [running[a * chunk + chunk // 2 : a * chunk + chunk // 2 + 1] for a in range(chunks)]
-        middle = by_chunk(middles)
-        rise = jnp.exp(running - middle)
+        above = running - by_chunk(middles)
+        rise = jnp.exp(above)
         key_rise, query_rise = keys * rise, queries * rise
-        key_fall = keys * strength[:, h : h + 1] * jnp.exp(middle - running)
+        key_fall = keys * strengths[:, lanes] * jnp.exp(-above)
         last = running[count - 1 :]
         stops.append(
             ((key_fall * by_chunk([jnp.exp(last - m) for m in middles])).astype(bf16), jnp.exp(last))
         )
         entry = by_chunk([jnp.exp(m) for m in middles])
-        start_ref[h] = query_rise * entry
+        start_ref[h] = (query_rise * entry).astype(bf16)
         sides.append(
             jnp.concatenate([(key_rise * entry).astype(bf16), values.astype(bf16)], axis=1)
         )
+        key_rise, query_rise = key_rise.astype(bf16), query_rise.astype(bf16)
         for a in range(chunks):
-            here = slice(a * chunk, (a + 1) * chunk)
-            left = jnp.concatenate([key_rise[here], query_rise[here]], axis=0).astype(bf16)
+            rows = slice(a * chunk, (a + 1) * chunk)
+            left = jnp.concatenate([key_rise[rows], query_rise[rows]], axis=0)
+            reach = (a * chunk // block + 1) * block
             falls = []
-            for b in range(chunks):
+            for b in range(reach // chunk):
                 there = slice(b * chunk, (b + 1) * chunk)
                 if b < a:
                     falls.append(key_fall[there] * jnp.exp(middles[a] - middles[b]))
@@ -181,49 +241,59 @@
                     falls.append(jnp.zeros((chunk, size), f32))
             right = jnp.concatenate(falls, axis=0).astype(bf16)
             scores = dot(left, right, ((1,), (1,)))
-            mixing[h, here, :] = jnp.where(row[here] > col[here], scores[:chunk], 0.0).astype(bf16)
-            attend_ref[h, here, :] = jnp.where(row[here] >= col[here], scores[chunk:], 0.0).astype(
-                bf16
-            )
-
-    base = math.gcd(count, BASE)
-    same = row // base == col // base
-    powers = [None] * heads
+            inside = slice(reach - block, reach)
+            if reach > block:
+                before = slice(0, reach - block)
+                mixing[h, rows, before] = scores[:chunk, before].astype(bf16)
+                attend_ref[h, rows, before] = scores[chunk:, before].astype(bf16)
+            at, to = row[rows, inside], col[rows, inside]
+            mixing[h, rows, inside] = jnp.where(at > to, scores[:chunk, inside], 0.0).astype(bf16)
+            attend_ref[h, rows, inside] = jnp.where(
+                at >= to, scores[chunk:, inside], 0.0
+            ).astype(bf16)
+
+    at, to = row[:block, :block], col[:block, :block]
+    eye = jnp.where(at == to, 1.0, 0.0).astype(bf16)
+    base = math.gcd(block, BASE)
+    near = jnp.where(at // base == to // base, -1.0, 0.0).astype(bf16)
+    corners = [(h, slice(d * block, (d + 1) * block)) for h in range(heads) for d in range(blocks)]
+    powers = [mixing[h, d, d] * near for h, d in corners]
+    totals = [power + eye for power in powers]
+    for _ in range(1, (base - 1).bit_length()):
+        powers = [dot(power, power).astype(bf16) for power in powers]
+        totals = [dot(t, power + eye).astype(bf16) for t, power in zip(totals, powers)]
+    for (h, d), total in zip(corners, totals):
+        inverse[h, d, :] = total
+    width = base
+    while width < block:
+        odd = range(width, block, 2 * width)
+        pair_mask = (at // width % 2 == 1) & (to // width == at // width - 1)
+        pair_mask = jnp.where(pair_mask, 1.0, 0.0).astype(bf16)
+        halves = []
+        for h, d in corners:
+            parts = [inverse[h, d.start + i : d.start + i + width, :] for i in odd]
+            chosen = jnp.concatenate(parts, axis=0)
+            halves.append((chosen, dot(chosen, mixing[h, d, d] * pair_mask).astype(bf16)))
+        for (h, d), (chosen, half) in zip(corners, halves):
+            new = (chosen.astype(f32) - dot(half, inverse[h, d, :])).astype(bf16)
+            for n, i in enumerate(odd):
+                inverse[h, d.start + i : d.start + i + width, :] = new[n * width : (n + 1) * width]
+        width *= 2
+
+    for d in range(blocks):
+        rows = slice(d * block, (d + 1) * block)
+        for h in range(heads):
+            side = sides[h][rows]
+            if d:
+                done = solved_ref[h, : d * block, :]
+                side = (side.astype(f32) - dot(mixing[h, rows, : d * block], done)).astype(bf16)
+            solved_ref[h, rows, :] = dot(inverse[h, rows, :], side).astype(bf16)
+    pairs = []
+    unit = row[:size, :size] == col[:size, :size]
     for h in range(heads):
-        nilpotent = jnp.where(same, -mixing[h].astype(f32), 0.0)
-        powers[h] = nilpotent.astype(bf16)
-        inverse[h] = jnp.where(eye, 1.0, nilpotent)
-    for _ in range(1, (base - 1).bit_length()):
-        for h in range(heads):
-            powers[h] = dot(powers[h], powers[h]).astype(bf16)
-        for h in range(heads):
-            inverse[h] = inverse[h] + dot(inverse[h].astype(bf16), powers[h])
-    for h in range(heads):
-        inverse_low[h] = inverse[h].astype(bf16)
-    width = base
-    while width < count:
-        odd = [slice(i, i + width) for i in range(width, count, 2 * width)]
-        pair_mask = jnp.where(
-            (row // width % 2 == 1) & (col // width == row // width - 1), 1.0, 0.0
-        ).astype(bf16)
-        halves = []
-        for h in range(heads):
-            chosen = jnp.concatenate([inverse_low[h, rows, :] for rows in odd], axis=0)
-            halves.append(dot(chosen, mixing[h] * pair_mask).astype(bf16))
-        for h in range(heads):
-            change = dot(halves[h], inverse_low[h])
-            for i, rows in enumerate(odd):
-                new = inverse_low[h, rows, :].astype(f32) - change[i * width : (i + 1) * width]
-                inverse_low[h, rows, :] = new.astype(bf16)
-        width *= 2
-
-    pairs = []
-    for h in range(heads):
-        solved = dot(inverse_low[h], sides[h]).astype(bf16)
-        solved_ref[h] = solved
         stop, fade = stops[h]
-        moved = dot(stop, solved, ((0,), (0,)))
-        diagonal = jnp.where(eye[:size, :size], jnp.broadcast_to(fade, (size, size)), 0.0)
+        moved = dot(stop, solved_ref[h], ((0,), (0,)))
+        diagonal = jnp.where(unit, jnp.broadcast_to(fade, (size, size)), 0.0)
         pairs.append(jnp.concatenate([diagonal - moved[:, :size], moved[:, size:]], axis=1))
     upper = place("seq", 1) == 1
     for h in range(heads // 2):
@@ -232,14 +302,13 @@
         other_ref[h] = jnp.where(upper, low, high).astype(bf16)
 
 
-def front(rim, slabs, loaded, weight, size):
+def front(rim, slabs, fetched, loaded, weight, size):
     slab_count, slab_rows = len(slabs), slabs[0].shape[0]
     count = slab_count * slab_rows
     _, width, channels = weight.shape
-    heads = channels // size
-    rank = loaded[1].shape[1]
+    heads, block = channels // size, math.gcd(count, 128)
     buffers = [pltpu.SMEM(loaded[0].shape, f32)]
-    buffers += [pltpu.VMEM(part.shape, part.dtype) for part in (*loaded[1:], weight)]
+    buffers += [pltpu.VMEM(part.shape, part.dtype) for part in loaded[1:]]
     return vmem_call(
         functools.partial(front_body, slab_count),
         (
@@ -247,18 +316,18 @@
             jax.ShapeDtypeStruct((heads // 2, size, 2 * size), bf16),
             jax.ShapeDtypeStruct((heads, count, 2 * size), bf16),
             jax.ShapeDtypeStruct((heads, count, count), bf16),
-            jax.ShapeDtypeStruct((heads, count, size), f32),
-            jax.ShapeDtypeStruct((count, rank), bf16),
+            jax.ShapeDtypeStruct((heads, count, size), bf16),
+            jax.ShapeDtypeStruct((count, fetched[1].shape[1] // 2), bf16),
         ),
-        (rim, *slabs[1:], slabs[0], *loaded, weight),
+        (rim, *slabs[1:], *fetched, slabs[0], *loaded, weight),
         scratch=[
             *buffers,
+            pltpu.VMEM((width, channels), bf16),
             pltpu.VMEM((RIM + count, width), bf16),
             pltpu.VMEM((3, RIM + count, channels), f32),
             pltpu.VMEM((heads, count, count), bf16),
-            pltpu.VMEM((heads, count, count), f32),
-            pltpu.VMEM((heads, count, count), bf16),
-            pltpu.SemaphoreType.DMA((8 + 3 * pl.cdiv(heads, 2),)),
+            pltpu.VMEM((heads, count, block), bf16),
+            pltpu.SemaphoreType.DMA((5 + len(column_pieces(channels)),)),
         ],
         hbm=2 + len(loaded),
         grant=24,
@@ -270,10 +339,14 @@
 def rows_body(attend_ref, solved_ref, start_ref, low_ref, up_ref, raised_ref, output_ref, gate_ref):
     heads, _, size = start_ref.shape
     gate_ref[...] = jax.nn.sigmoid(dot(low_ref[...], up_ref[...]))
+    count = attend_ref.shape[1]
+    block = math.gcd(count, 128)
     for h in range(heads):
-        both = dot(attend_ref[h], solved_ref[h])
-        raised_ref[h] = (start_ref[h] - both[:, :size]).astype(bf16)
-        output_ref[:, h * size : (h + 1) * size] = both[:, size:]
+        for begin in range(0, count, block):
+            rows, reach = slice(begin, begin + block), slice(0, begin + block)
+            both = dot(attend_ref[h, rows, reach], solved_ref[h, reach, :])
+            raised_ref[h, rows, :] = (start_ref[h, rows, :].astype(f32) - both[:, :size]).astype(bf16)
+            output_ref[rows, h * size : (h + 1) * size] = both[:, size:]
 
 
 def composed(later, first, size):
@@ -421,13 +494,11 @@
     heads, size = decay_log.shape[0], norm_gain.shape[0]
     channels = heads * size
     devices = lax.axis_size("head")
-    slabs, rim = gathered(hidden_in, RIM)
+    weight = qkv_weight.transpose(1, 0, 2)
+    tail, *fetched = load(hidden_in, decay_down, gate_down, beta_weight.T, weight)
+    slabs, rim = gathered(hidden_in, tail)
     own, other, solved, attend, start, gate_low = front(
-        rim,
-        slabs,
-        (decay_log, decay_down, gate_down, beta_weight.T, decay_up, dt_bias[None], conv_weight),
-        qkv_weight.transpose(1, 0, 2),
-        size,
+        rim, slabs, fetched, (decay_log, decay_up, dt_bias[None], conv_weight), weight, size
     )
     count = start.shape[1]
     raised, output_rows, out_gate = vmem_call(

time: 59.3 us -> 64 us (1.079)
  starting transfers between devices: 15.8 us -> 21.1 us
  waiting for transfers between devices: 26.6 us -> 22 us
  local copies, waits for them, and re-layouts: 0.94 us -> 4.49 us
    ppermute x11, starting transfers between devices: 14.5 us -> 19.8 us  [swapped(): lax.ppermute(block, axis, [(i, i ^ bit) for i in range(lax.axis_size(axis...]
    ppermute x11, waiting for transfers between devices: 26.6 us -> 22 us  [swapped(): lax.ppermute(block, axis, [(i, i ^ bit) for i in range(lax.axis_size(axis...]
    unnamed x6 -> x12, local copies, waits for them, and re-layouts: 0.01 us -> 4.48 us
    slice x1 -> x0, local copies, waits for them, and re-layouts: 0.92 us -> none  [gathered(): tail = own[own.shape[0] - row_count:]]
    pallas_call x8 -> x9, Pallas kernels: 14.6 us -> 15.2 us  [vmem_call(): pl.pallas_call(body, out_shape=out_shape, in_specs=[pl.BlockSpec(memory_s...]
  transfers between devices with their start and end apart: 13 -> 13, of which waited for: 8 -> 8; matrix products, arithmetic and copies ran while one was open for 2% -> 0% of each run, Pallas kernels for 2% -> 6%
where the time goes in v5:
time: 64 us; the launch traced here: 63.9 us
  waiting for transfers between devices  22 us (34%)
  starting transfers between devices  21.1 us (33%)
  Pallas kernels  15.2 us (24%)
  local copies, waits for them, and re-layouts  4.49 us (7%)
  other arithmetic  0.9 us (1%)
    ppermute x11, waiting for transfers between devices, swapped(): lax.ppermute(block, axis, [(i, i ^ bit) for i in range(lax.axis_size(axis...  22 us
    ppermute x11, starting transfers between devices, swapped(): lax.ppermute(block, axis, [(i, i ^ bit) for i in range(lax.axis_size(axis...  19.8 us
    pallas_call x9, Pallas kernels, vmem_call(): pl.pallas_call(body, out_shape=out_shape, in_specs=[pl.BlockSpec(memory_s...  15.2 us
    unnamed x12, local copies, waits for them, and re-layouts  4.48 us
    ppermute x2, starting transfers between devices, gathered(): lax.ppermute(tail, ('seq', 'head'), rim_route(target))  1.32 us
  transfers between devices with their start and end apart: 13, of which 8 were waited for; matrix products, arithmetic and copies ran while one was open for 0% of the time, Pallas kernels for 6%

profile of v5, /device:TPU:0, one launch (start us, length us, event | category | flops | bytes accessed | tf_op | source)
XLA Modules:
  0.0 63.9 jit_solution(17252765296788191940)
XLA Ops:
  0.0 0.0 copy-start.5
  0.0 2.9 %collective-permute-start = (bf16[64,2304]{1,0:T(8,128)(2,1)}, bf16[64,2304]{1,0:T(8,128)(2,1)S(1)}, u32[]{:S(2)}, u32[]{:S(2)}) collective-permute-start(bf16[64,2304]{1,0:T(8,128)(2,1)} %refs_7_.1), channel_id=1, source_target_pairs={{0,2},{1,3},{2,0},{3,1},{4,6},{5,7},{6,4},{7,5},{8,10},{9,11},{10,... | collective-permute-start | bytes 884744 | tf_op jit(solution)/shard_map/ppermute | solution.py:23
  2.9 2.9 %shard_map.118 = (bf16[16,2304]{1,0:T(8,128)(2,1)S(1)}, bf16[2,2304,512]{2,1,0:T(8,128)(2,1)S(1)}, bf16[2304,256]{1,0:T(8,128)(2,1)S(1)}, bf16[4,2304]{1,0:T(4,128)(2,1)S(1)}) custom-call(bf16[64,2304]{1,0:T(8,128)(2,1)} %refs_7_.1, bf16[2304,128]{1,0:T(8,128)(2,1)} %decay_down_ref.1, bf16[2304,128]{1,0:T(8,128)(2,1)} %gate_down_ref.1, ...), custom_call_target="tpu_custom_call" | custom-call | tf_op jit(solution)/shard_map/pallas_call | solution.py:63
  5.8 0.0 copy-start.1
  5.8 2.1 %copy-done.1 = bf16[2,2304,512]{2,1,0:T(8,128)(2,1)} copy-done((bf16[2,2304,512]{2,1,0:T(8,128)(2,1)}, bf16[2,2304,512]{2,1,0:T(8,128)(2,1)S(1)}, u32[]{:S(2)}) %copy-start.1) | copy-done | bytes 4718616
  7.9 0.7 %collective-permute-start.1 = (bf16[16,2304]{1,0:T(8,128)(2,1)S(1)}, bf16[16,2304]{1,0:T(8,128)(2,1)S(1)}, u32[]{:S(2)}, u32[]{:S(2)}) collective-permute-start(bf16[16,2304]{1,0:T(8,128)(2,1)S(1)} %get-tuple-element.27), channel_id=1, source_target_pairs={{3,5},{7,9},{11,13},{15,17},{19,21},{23,25},{27,29},{5,3},{9,7},{1... | collective-permute-start | bytes 221192 | tf_op jit(solution)/shard_map/ppermute | solution.py:46
  8.6 0.7 %collective-permute-start.2 = (bf16[16,2304]{1,0:T(8,128)(2,1)S(1)}, bf16[16,2304]{1,0:T(8,128)(2,1)S(1)}, u32[]{:S(2)}, u32[]{:S(2)}) collective-permute-start(bf16[16,2304]{1,0:T(8,128)(2,1)S(1)} %get-tuple-element.27), channel_id=1, source_target_pairs={{3,6},{7,10},{11,14},{15,18},{19,22},{23,26},{27,30},{6,3},{10,7},... | collective-permute-start | bytes 221192 | tf_op jit(solution)/shard_map/ppermute | solution.py:46
  9.3 0.0 copy-done.5
  9.3 0.1 collective-permute-start.4
  9.4 0.0 collective-permute-done.1
  9.4 0.0 collective-permute-done.2
  9.4 0.8 %collective-permute-done.refs_2_ = bf16[64,2304]{1,0:T(8,128)(2,1)S(1)} collective-permute-done((bf16[64,2304]{1,0:T(8,128)(2,1)}, bf16[64,2304]{1,0:T(8,128)(2,1)S(1)}, u32[]{:S(2)}, u32[]{:S(2)}) %collective-permute-start) | collective-permute-done | bytes 294944 | tf_op jit(solution)/shard_map/ppermute | solution.py:23
  10.2 0.0 collective-permute-start.5
  10.2 0.6 collective-permute-start.3
  10.8 1.1 %collective-permute-done.3 = bf16[16,2304]{1,0:T(8,128)(2,1)S(1)} collective-permute-done((bf16[16,2304]{1,0:T(8,128)(2,1)S(1)}, bf16[16,2304]{1,0:T(8,128)(2,1)S(1)}, u32[]{:S(2)}, u32[]{:S(2)}) %collective-permute-start.3) | collective-permute-done | bytes 73760 | tf_op jit(solution)/shard_map/ppermute | solution.py:23
  11.9 0.0 collective-permute-done.4.refs_1_
  12.0 0.0 collective-permute-done.5.refs_3_
  12.0 0.0 copy-start.2
  12.0 2.3 %copy-done.2 = bf16[2,2304,512]{2,1,0:T(8,128)(2,1)S(1)} copy-done((bf16[2,2304,512]{2,1,0:T(8,128)(2,1)S(1)}, bf16[2,2304,512]{2,1,0:T(8,128)(2,1)}, u32[]{:S(2)}) %copy-start.2) | copy-done | bytes 4718616
  14.3 0.0 copy-start.3
  14.3 0.0 copy-start.4
  14.3 9.6 %shard_map.119 = (bf16[2,128,256]{2,1,0:T(8,128)(2,1)S(1)}, bf16[2,128,256]{2,1,0:T(8,128)(2,1)S(1)}, bf16[4,256,256]{2,1,0:T(8,128)(2,1)S(1)}, bf16[4,256,256]{...) custom-call(bf16[16,2304]{1,0:T(8,128)(2,1)S(1)} %add.12.refs_0_, ...), custom_call_target="tpu_custom_call" | custom-call | flops 2415919104 | bytes 9437184 | tf_op jit(solution)/shard_map/pallas_call | solution.py:63
  23.9 0.0 copy-start
  24.0 4.5 %collective-permute-start.6 = (bf16[2,128,256]{2,1,0:T(8,128)(2,1)S(1)}, bf16[2,128,256]{2,1,0:T(8,128)(2,1)S(1)}, u32[]{:S(2)}, u32[]{:S(2)}) collective-permute-start(bf16[2,128,256]{2,1,0:T(8,128)(2,1)S(1)} %get-tuple-element.35), channel_id=1, source_target_pairs={{0,4},{4,0},{8,12},{12,8},{16,20},{20,16},{24,28},{28,24},{1,5},{5... | collective-permute-start | bytes 393224 | tf_op jit(solution)/shard_map/ppermute | solution.py:23
  28.4 4.0 %collective-permute-done.6.far_ref.partner_ref = bf16[2,128,256]{2,1,0:T(8,128)(2,1)S(1)} collective-permute-done((bf16[2,128,256]{2,1,0:T(8,128)(2,1)S(1)}, bf16[2,128,256]{2,1,0:T(8,128)(2,1)S(1)}, u32[]{:S(2)}, u32[]{:S(2)}) %collective-permute-start.6) | collective-permute-done | bytes 131104 | tf_op jit(solution)/shard_map/ppermute | solution.py:23
  32.5 0.2 shard_map.120.own_ref
  32.7 2.8 %collective-permute-start.7 = (bf16[2,128,256]{2,1,0:T(8,128)(2,1)S(1)}, bf16[2,128,256]{2,1,0:T(8,128)(2,1)S(1)}, u32[]{:S(2)}, u32[]{:S(2)}) collective-permute-start(bf16[2,128,256]{2,1,0:T(8,128)(2,1)S(1)} %shard_map.120.own_ref), channel_id=1, source_target_pairs={{0,8},{4,12},{8,0},{12,4},{16,24},{20,28},{24,16},{28,20},{1,9},{5... | collective-permute-start | bytes 393224 | tf_op jit(solution)/shard_map/ppermute | solution.py:23
  35.4 3.2 %collective-permute-done.7.far_ref = bf16[2,128,256]{2,1,0:T(8,128)(2,1)S(1)} collective-permute-done((bf16[2,128,256]{2,1,0:T(8,128)(2,1)S(1)}, bf16[2,128,256]{2,1,0:T(8,128)(2,1)S(1)}, u32[]{:S(2)}, u32[]{:S(2)}) %collective-permute-start.7) | collective-permute-done | bytes 131104 | tf_op jit(solution)/shard_map/ppermute | solution.py:23
  38.6 0.2 shard_map.122
  38.8 2.8 %collective-permute-start.8 = (bf16[2,128,128]{2,1,0:T(8,128)(2,1)S(1)}, bf16[2,128,128]{2,1,0:T(8,128)(2,1)S(1)}, u32[]{:S(2)}, u32[]{:S(2)}) collective-permute-start(bf16[2,128,128]{2,1,0:T(8,128)(2,1)S(1)} %shard_map.122), channel_id=1, source_target_pairs={{0,16},{4,20},{8,24},{12,28},{16,0},{20,4},{24,8},{28,12},{1,17},{... | collective-permute-start | bytes 196616 | tf_op jit(solution)/shard_map/ppermute | solution.py:23
  41.7 0.2 shard_map.121.near_ref
  41.9 2.2 %collective-permute-done.8.far_ref = bf16[2,128,128]{2,1,0:T(8,128)(2,1)S(1)} collective-permute-done((bf16[2,128,128]{2,1,0:T(8,128)(2,1)S(1)}, bf16[2,128,128]{2,1,0:T(8,128)(2,1)S(1)}, u32[]{:S(2)}, u32[]{:S(2)}) %collective-permute-start.8) | collective-permute-done | bytes 65568 | tf_op jit(solution)/shard_map/ppermute | solution.py:23
  44.0 0.3 shard_map.123
  44.4 0.9 %collective-permute-start.9 = (bf16[2,128,128]{2,1,0:T(8,128)(2,1)S(1)}, bf16[2,128,128]{2,1,0:T(8,128)(2,1)S(1)}, u32[]{:S(2)}, u32[]{:S(2)}) collective-permute-start(bf16[2,128,128]{2,1,0:T(8,128)(2,1)S(1)} %get-tuple-element.37), channel_id=1, source_target_pairs={{0,4},{4,0},{8,12},{12,8},{16,20},{20,16},{24,28},{28,24},{1,5},{5... | collective-permute-start | bytes 196616 | tf_op jit(solution)/shard_map/ppermute | solution.py:23
  45.2 0.0 copy-done.3
  45.2 0.4 shard_map.124
  45.6 3.1 %collective-permute-done.9.other_ref = bf16[2,128,128]{2,1,0:T(8,128)(2,1)S(1)} collective-permute-done((bf16[2,128,128]{2,1,0:T(8,128)(2,1)S(1)}, bf16[2,128,128]{2,1,0:T(8,128)(2,1)S(1)}, u32[]{:S(2)}, u32[]{:S(2)}) %collective-permute-start.9) | collective-permute-done | bytes 65568 | tf_op jit(solution)/shard_map/ppermute | solution.py:23
  48.7 0.0 copy-done.4
  48.7 0.0 copy-done
  48.7 0.7 %shard_map.126 = (f32[64,2304]{1,0:T(8,128)S(1)}, bf16[64,2304]{1,0:T(8,128)(2,1)S(1)}) custom-call(bf16[2,128,128]{2,1,0:T(8,128)(2,1)S(1)} %get-tuple-element.36.own_ref, bf16[2,128,128]{2,1,0:T(8,128)(2,1)S(1)} %collective-permute-done.9.other_ref, bf16[4,256,128]{2,1,0:T(8,128)(2,1)S(1)} %get-tuple-element.42.raised_ref, ...), custom_call_target="tpu_custom_call" | custom-call | flops 301989888 | bytes 2359296 | tf_op jit(solution)/shard_map/pallas_call | solution.py:63
  49.4 0.1 collective-permute-start.11
  49.5 0.7 %shard_map.125 = (f32[64,2304]{1,0:T(8,128)S(1)}, bf16[64,2304]{1,0:T(8,128)(2,1)S(1)}) custom-call(bf16[2,128,128]{2,1,0:T(8,128)(2,1)S(1)} %get-tuple-element.36.own_ref, bf16[2,128,128]{2,1,0:T(8,128)(2,1)S(1)} %collective-permute-done.9.other_ref, bf16[4,256,128]{2,1,0:T(8,128)(2,1)S(1)} %get-tuple-element.42.raised_ref, ...), custom_call_target="tpu_custom_call" | custom-call | flops 301989888 | bytes 2359296 | tf_op jit(solution)/shard_map/pallas_call | solution.py:63
  50.3 0.6 collective-permute-start.10
  50.8 0.3 collective-permute-done.11
  51.1 0.1 add_convert_fusion.1
  51.1 4.6 %collective-permute-start.12 = (bf16[64,2304]{1,0:T(8,128)(2,1)S(1)}, bf16[64,2304]{1,0:T(8,128)(2,1)S(1)}, u32[]{:S(2)}, u32[]{:S(2)}) collective-permute-start(bf16[64,2304]{1,0:T(8,128)(2,1)S(1)} %add_convert_fusion.1), channel_id=1, source_target_pairs={{0,2},{1,3},{2,0},{3,1},{4,6},{5,7},{6,4},{7,5},{8,10},{9,11},{10,... | collective-permute-start | bytes 884744 | tf_op jit(solution)/shard_map/ppermute | solution.py:23
  55.8 0.0 collective-permute-done.10
  55.8 7.3 %collective-permute-done.12 = bf16[64,2304]{1,0:T(8,128)(2,1)S(1)} collective-permute-done((bf16[64,2304]{1,0:T(8,128)(2,1)S(1)}, bf16[64,2304]{1,0:T(8,128)(2,1)S(1)}, u32[]{:S(2)}, u32[]{:S(2)}) %collective-permute-start.12) | collective-permute-done | bytes 294944 | tf_op jit(solution)/shard_map/ppermute | solution.py:23
  63.1 0.8 %add_convert_fusion = bf16[64,2304]{1,0:T(8,128)(2,1)} fusion(bf16[64,2304]{1,0:T(8,128)(2,1)S(1)} %collective-permute-done.12, f32[64,2304]{1,0:T(8,128)S(1)} %get-tuple-element.45, bf16[64,2304]{1,0:T(8,128)(2,1)S(1)} %collective-permute-done.10), kind=kLoop, calls=%fused_computation | loop fusion | flops 737280 | bytes 1474560 | tf_op jit(solution)/shard_map/convert_element_type | solution.py:530
  (4 shorter events, 0.1 us)
Async XLA Ops:
  0.0 9.3 %copy-start.5 = (bf16[64,2304]{1,0:T(8,128)(2,1)S(1)}, bf16[64,2304]{1,0:T(8,128)(2,1)}, u32[]{:S(2)}) copy-start(bf16[64,2304]{1,0:T(8,128)(2,1)} %refs_7_.1) | copy-start | bytes 884740
  0.0 10.2 %collective-permute-start = (bf16[64,2304]{1,0:T(8,128)(2,1)}, bf16[64,2304]{1,0:T(8,128)(2,1)S(1)}, u32[]{:S(2)}, u32[]{:S(2)}) collective-permute-start(bf16[64,2304]{1,0:T(8,128)(2,1)} %refs_7_.1), channel_id=1, source_target_pairs={{0,2},{1,3},{2,0},{3,1},{4,6},{5,7},{6,4},{7,5},{8,10},{9,11},{10,... | collective-permute-start | bytes 884744 | tf_op jit(solution)/shard_map/ppermute | solution.py:23
  5.8 2.1 %copy-start.1 = (bf16[2,2304,512]{2,1,0:T(8,128)(2,1)}, bf16[2,2304,512]{2,1,0:T(8,128)(2,1)S(1)}, u32[]{:S(2)}) copy-start(bf16[2,2304,512]{2,1,0:T(8,128)(2,1)S(1)} %get-tuple-element.31.refs_4_) | copy-start | bytes 14155780
  7.9 1.4 %collective-permute-start.1 = (bf16[16,2304]{1,0:T(8,128)(2,1)S(1)}, bf16[16,2304]{1,0:T(8,128)(2,1)S(1)}, u32[]{:S(2)}, u32[]{:S(2)}) collective-permute-start(bf16[16,2304]{1,0:T(8,128)(2,1)S(1)} %get-tuple-element.27), channel_id=1, source_target_pairs={{3,5},{7,9},{11,13},{15,17},{19,21},{23,25},{27,29},{5,3},{9,7},{1... | collective-permute-start | bytes 221192 | tf_op jit(solution)/shard_map/ppermute | solution.py:46
  8.6 0.8 %collective-permute-start.2 = (bf16[16,2304]{1,0:T(8,128)(2,1)S(1)}, bf16[16,2304]{1,0:T(8,128)(2,1)S(1)}, u32[]{:S(2)}, u32[]{:S(2)}) collective-permute-start(bf16[16,2304]{1,0:T(8,128)(2,1)S(1)} %get-tuple-element.27), channel_id=1, source_target_pairs={{3,6},{7,10},{11,14},{15,18},{19,22},{23,26},{27,30},{6,3},{10,7},... | collective-permute-start | bytes 221192 | tf_op jit(solution)/shard_map/ppermute | solution.py:46
  9.3 2.7 %collective-permute-start.4 = (bf16[64,2304]{1,0:T(8,128)(2,1)S(1)}, bf16[64,2304]{1,0:T(8,128)(2,1)S(1)}, u32[]{:S(2)}, u32[]{:S(2)}) collective-permute-start(bf16[64,2304]{1,0:T(8,128)(2,1)S(1)} %copy-done.5), channel_id=1, source_target_pairs={{0,1},{1,0},{2,3},{3,2},{4,5},{5,4},{6,7},{7,6},{8,9},{9,8},{10,11... | collective-permute-start | bytes 884744 | tf_op jit(solution)/shard_map/ppermute | solution.py:23
  10.2 1.7 %collective-permute-start.5 = (bf16[64,2304]{1,0:T(8,128)(2,1)S(1)}, bf16[64,2304]{1,0:T(8,128)(2,1)S(1)}, u32[]{:S(2)}, u32[]{:S(2)}) collective-permute-start(bf16[64,2304]{1,0:T(8,128)(2,1)S(1)} %collective-permute-done.refs_2_), channel_id=1, source_target_pairs={{0,1},{1,0},{2,3},{3,2},{4,5},{5,4},{6,7},{7,6},{8,9},{9,8},{10,11... | collective-permute-start | bytes 884744 | tf_op jit(solution)/shard_map/ppermute | solution.py:23
  10.2 1.7 %collective-permute-start.3 = (bf16[16,2304]{1,0:T(8,128)(2,1)S(1)}, bf16[16,2304]{1,0:T(8,128)(2,1)S(1)}, u32[]{:S(2)}, u32[]{:S(2)}) collective-permute-start(bf16[16,2304]{1,0:T(8,128)(2,1)S(1)} %select_select_fusion), channel_id=1, source_target_pairs={{0,1},{1,0},{2,3},{3,2},{4,5},{5,4},{6,7},{7,6},{8,9},{9,8},{10,11... | collective-permute-start | bytes 221192 | tf_op jit(solution)/shard_map/ppermute | solution.py:23
  12.0 2.3 %copy-start.2 = (bf16[2,2304,512]{2,1,0:T(8,128)(2,1)S(1)}, bf16[2,2304,512]{2,1,0:T(8,128)(2,1)}, u32[]{:S(2)}) copy-start(bf16[2,2304,512]{2,1,0:T(8,128)(2,1)} %copy-done.1) | copy-start | bytes 14155780
  14.3 30.9 %copy-start.3 = (bf16[128,512]{1,0:T(8,128)(2,1)S(1)}, bf16[128,512]{1,0:T(8,128)(2,1)}, u32[]{:S(2)}) copy-start(bf16[128,512]{1,0:T(8,128)(2,1)} %up_ref.1) | copy-start | bytes 393220
  14.3 34.4 %copy-start.4 = (f32[128]{0:T(128)S(1)}, f32[128]{0:T(128)}, u32[]{:S(2)}) copy-start(f32[128]{0:T(128)} %param.22) | copy-start | bytes 1540
  23.9 24.7 %copy-start = (bf16[512,2304]{1,0:T(8,128)(2,1)S(1)}, bf16[512,2304]{1,0:T(8,128)(2,1)}, u32[]{:S(2)}) copy-start(bf16[512,2304]{1,0:T(8,128)(2,1)} %weight_ref.3) | copy-start | bytes 7077892
  24.0 8.5 %collective-permute-start.6 = (bf16[2,128,256]{2,1,0:T(8,128)(2,1)S(1)}, bf16[2,128,256]{2,1,0:T(8,128)(2,1)S(1)}, u32[]{:S(2)}, u32[]{:S(2)}) collective-permute-start(bf16[2,128,256]{2,1,0:T(8,128)(2,1)S(1)} %get-tuple-element.35), channel_id=1, source_target_pairs={{0,4},{4,0},{8,12},{12,8},{16,20},{20,16},{24,28},{28,24},{1,5},{5... | collective-permute-start | bytes 393224 | tf_op jit(solution)/shard_map/ppermute | solution.py:23
  32.7 6.0 %collective-permute-start.7 = (bf16[2,128,256]{2,1,0:T(8,128)(2,1)S(1)}, bf16[2,128,256]{2,1,0:T(8,128)(2,1)S(1)}, u32[]{:S(2)}, u32[]{:S(2)}) collective-permute-start(bf16[2,128,256]{2,1,0:T(8,128)(2,1)S(1)} %shard_map.120.own_ref), channel_id=1, source_target_pairs={{0,8},{4,12},{8,0},{12,4},{16,24},{20,28},{24,16},{28,20},{1,9},{5... | collective-permute-start | bytes 393224 | tf_op jit(solution)/shard_map/ppermute | solution.py:23
  38.8 5.2 %collective-permute-start.8 = (bf16[2,128,128]{2,1,0:T(8,128)(2,1)S(1)}, bf16[2,128,128]{2,1,0:T(8,128)(2,1)S(1)}, u32[]{:S(2)}, u32[]{:S(2)}) collective-permute-start(bf16[2,128,128]{2,1,0:T(8,128)(2,1)S(1)} %shard_map.122), channel_id=1, source_target_pairs={{0,16},{4,20},{8,24},{12,28},{16,0},{20,4},{24,8},{28,12},{1,17},{... | collective-permute-start | bytes 196616 | tf_op jit(solution)/shard_map/ppermute | solution.py:23
  44.4 4.3 %collective-permute-start.9 = (bf16[2,128,128]{2,1,0:T(8,128)(2,1)S(1)}, bf16[2,128,128]{2,1,0:T(8,128)(2,1)S(1)}, u32[]{:S(2)}, u32[]{:S(2)}) collective-permute-start(bf16[2,128,128]{2,1,0:T(8,128)(2,1)S(1)} %get-tuple-element.37), channel_id=1, source_target_pairs={{0,4},{4,0},{8,12},{12,8},{16,20},{20,16},{24,28},{28,24},{1,5},{5... | collective-permute-start | bytes 196616 | tf_op jit(solution)/shard_map/ppermute | solution.py:23
  49.4 1.6 %collective-permute-start.11 = (bf16[64,2304]{1,0:T(8,128)(2,1)S(1)}, bf16[64,2304]{1,0:T(8,128)(2,1)S(1)}, u32[]{:S(2)}, u32[]{:S(2)}) collective-permute-start(bf16[64,2304]{1,0:T(8,128)(2,1)S(1)} %get-tuple-element.48), channel_id=1, source_target_pairs={{0,1},{1,0},{2,3},{3,2},{4,5},{5,4},{6,7},{7,6},{8,9},{9,8},{10,11... | collective-permute-start | bytes 884744 | tf_op jit(solution)/shard_map/ppermute | solution.py:23
  50.3 5.5 %collective-permute-start.10 = (bf16[64,2304]{1,0:T(8,128)(2,1)S(1)}, bf16[64,2304]{1,0:T(8,128)(2,1)S(1)}, u32[]{:S(2)}, u32[]{:S(2)}) collective-permute-start(bf16[64,2304]{1,0:T(8,128)(2,1)S(1)} %get-tuple-element.46), channel_id=1, source_target_pairs={{0,1},{1,0},{2,3},{3,2},{4,5},{5,4},{6,7},{7,6},{8,9},{9,8},{10,11... | collective-permute-start | bytes 884744 | tf_op jit(solution)/shard_map/ppermute | solution.py:23
  51.1 11.9 %collective-permute-start.12 = (bf16[64,2304]{1,0:T(8,128)(2,1)S(1)}, bf16[64,2304]{1,0:T(8,128)(2,1)S(1)}, u32[]{:S(2)}, u32[]{:S(2)}) collective-permute-start(bf16[64,2304]{1,0:T(8,128)(2,1)S(1)} %add_convert_fusion.1), channel_id=1, source_target_pairs={{0,2},{1,3},{2,0},{3,1},{4,6},{5,7},{6,4},{7,5},{8,10},{9,11},{10,... | collective-permute-start | bytes 884744 | tf_op jit(solution)/shard_map/ppermute | solution.py:23

commit v6 on v5

--- a/solution.py
+++ b/solution.py
@@ -30,30 +30,39 @@
 
 def rim_route(target):
     heads, seqs = lax.axis_size("head"), lax.axis_size("seq")
-    pairs = [(s * heads + heads - 1, (s + 1) * heads + target) for s in range(seqs - 1)]
-    return pairs + [(two, one) for one, two in pairs]
-
-
-def gathered(own, tail):
-    bits = bits_of(lax.axis_size("head"))
+    return [(s * heads + heads - 1, (s + 1) * heads + target) for s in range(seqs - 1)]
+
+
+def pick_body(targets, *refs):
+    *tail_refs, rim_ref = refs
+    rim = jnp.zeros(rim_ref.shape, f32)
+    for target, ref in zip(targets, tail_refs):
+        rim = jnp.where(place("head") == target, ref[...].astype(f32), rim)
+    rim_ref[...] = rim.astype(rim_ref.dtype)
+
+
+def gathered(own, loaded):
+    heads = lax.axis_size("head")
+    bits = bits_of(heads)
     assert bits
-    heads, here = lax.axis_size("head"), lax.axis_index("head")
     slabs = {0: own}
     for bit in reversed(bits[1:]):
         for k in sorted(slabs):
             slabs[k ^ bit] = swapped(slabs[k], "head", bit)
+    tail = own[own.shape[0] - RIM :]
     targets = [first if first == heads - 2 else first + 1 for first in range(0, heads, 2)]
     tails = [lax.ppermute(tail, ("seq", "head"), rim_route(target)) for target in targets]
     slabs[1] = swapped(own, "head", 1)
     arrived = [k for k in sorted(slabs) if k > 1]
-    moved, tails = lax.optimization_barrier(([slabs[k] for k in arrived], tails))
-    rim = jnp.zeros_like(tail)
-    for target, received in zip(targets, tails):
-        rim = jnp.where(here == target, received, rim)
+    moved, tails, loaded = lax.optimization_barrier(
+        ([slabs[k] for k in arrived], tails, loaded)
+    )
     for k, slab in zip(arrived, moved):
         slabs[k], slabs[k ^ 1] = slab, swapped(slab, "head", 1)
-    rim = rim + swapped(rim, "head", 1)
-    return [slabs[k] for k in range(heads)], rim
+    rim = vmem_call(
+        functools.partial(pick_body, targets), jax.ShapeDtypeStruct(tail.shape, bf16), tails
+    )
+    return [slabs[k] for k in range(1, heads)], [rim, swapped(rim, "head", 1)], loaded
 
 
 def vmem_call(body, out_shape, args, scratch=(), hbm=0, grant=4, flops=0, moved=0):
@@ -83,11 +92,11 @@
 
 def load_body(
     hidden_ref, decay_down_ref, gate_down_ref, beta_ref, weight_ref,
-    tail_ref, weights, downs, betas, sems,
+    own_ref, weights, downs, betas, sems,
 ):
-    first, rank = hidden_ref.shape[0] - tail_ref.shape[0], decay_down_ref.shape[1]
+    rank = decay_down_ref.shape[1]
     copies = [
-        pltpu.make_async_copy(hidden_ref.at[pl.ds(first, tail_ref.shape[0])], tail_ref, sems.at[0]),
+        pltpu.make_async_copy(hidden_ref, own_ref, sems.at[0]),
         pltpu.make_async_copy(decay_down_ref, downs.at[:, pl.ds(0, rank)], sems.at[1]),
         pltpu.make_async_copy(gate_down_ref, downs.at[:, pl.ds(rank, rank)], sems.at[2]),
         pltpu.make_async_copy(beta_ref, betas, sems.at[3]),
@@ -105,7 +114,7 @@
     return vmem_call(
         load_body,
         (
-            jax.ShapeDtypeStruct((RIM, width), bf16),
+            jax.ShapeDtypeStruct(own.shape, bf16),
             jax.ShapeDtypeStruct((2, *weight.shape[1:]), bf16),
             jax.ShapeDtypeStruct((width, 2 * rank), bf16),
             jax.ShapeDtypeStruct(beta.shape, bf16),
@@ -118,14 +127,14 @@
 
 
 def front_body(slab_count, *refs):
-    (rim_ref, *slab_refs), refs = refs[:slab_count], refs[slab_count:]
-    (weights, downs, betas), refs = refs[:3], refs[3:]
-    hbm_refs, refs = refs[:6], refs[6:]
+    (one_ref, two_ref, *slab_refs), refs = refs[: slab_count + 1], refs[slab_count + 1 :]
+    (own_rows_ref, weights, downs, betas), refs = refs[:4], refs[4:]
+    hbm_refs, refs = refs[:5], refs[5:]
     (own_ref, other_ref, solved_ref, attend_ref, start_ref, gate_ref), refs = refs[:6], refs[6:]
     loaded, refs = refs[:5], refs[5:]
-    rows_ref, projected, mixing, inverse, sems = refs
+    rows_ref, projected, mixing, inverse, sides, sems = refs
     rates, decay_up_ref, bias_ref, conv_ref, value_weight = loaded
-    hidden_ref, weight_ref = hbm_refs[0], hbm_refs[-1]
+    weight_ref = hbm_refs[-1]
     heads, count, size = start_ref.shape
     slab_rows = count // slab_count
     tap_count = conv_ref.shape[1]
@@ -139,22 +148,20 @@
     def rows_of(k):
         return pl.ds(pl.multiple_of(RIM + (here ^ k) * slab_rows, 16), slab_rows)
 
-    fetch = pltpu.make_async_copy(hidden_ref, rows_ref.at[rows_of(0)], sems.at[0])
-    small = [pltpu.make_async_copy(hbm_refs[1 + i], loaded[i], sems.at[1 + i]) for i in range(4)]
+    small = [pltpu.make_async_copy(hbm_refs[i], loaded[i], sems.at[i]) for i in range(4)]
     pieces = column_pieces(heads * size)
     streams = []
     for i, piece in enumerate(pieces):
         streams.append(
             pltpu.make_async_copy(
-                weight_ref.at[2, :, piece], value_weight.at[:, piece], sems.at[5 + i]
+                weight_ref.at[2, :, piece], value_weight.at[:, piece], sems.at[4 + i]
             )
         )
-    for copy in [fetch] + small + streams:
+    for copy in small + streams:
         copy.start()
-    rows_ref[:RIM, :] = rim_ref[...]
-    for k, ref in enumerate(slab_refs):
-        rows_ref[rows_of(k + 1), :] = ref[...]
-    fetch.wait()
+    rows_ref[:RIM, :] = (one_ref[...].astype(f32) + two_ref[...].astype(f32)).astype(bf16)
+    for k, ref in enumerate([own_rows_ref, *slab_refs]):
+        rows_ref[rows_of(k), :] = ref[...]
     for c in range(2):
         for piece in pieces:
             projected[c, :, piece] = dot(rows_ref[...], weights[c, :, piece])
@@ -183,9 +190,6 @@
     spread = jnp.where(spread, 1.0, 0.0).astype(bf16)
     high = strength.astype(bf16)
     strengths = dot(high, spread) + dot((strength - high.astype(f32)).astype(bf16), spread)
-    for i, piece in enumerate(pieces):
-        streams[i].wait()
-        projected[2, :, piece] = dot(rows_ref[...], value_weight[:, piece])
 
     def convolved(c, lanes):
         taps = conv_ref[c].astype(f32)
@@ -202,10 +206,10 @@
 
     ones = jnp.full((size, size), 1.0, bf16)
     scaled = jnp.full((size, size), float(size), bf16)
-    stops, sides = [], []
+    stops = []
     for h in range(heads):
         lanes = slice(h * size, (h + 1) * size)
-        queries, keys, values = (convolved(c, lanes) for c in range(3))
+        queries, keys = convolved(0, lanes), convolved(1, lanes)
         power = dot((queries * queries).astype(bf16), scaled)
         queries = queries * lax.rsqrt(power + size * 1e-06)
         power = dot((keys * keys).astype(bf16), ones)
@@ -222,9 +226,7 @@
         )
         entry = by_chunk([jnp.exp(m) for m in middles])
         start_ref[h] = (query_rise * entry).astype(bf16)
-        sides.append(
-            jnp.concatenate([(key_rise * entry).astype(bf16), values.astype(bf16)], axis=1)
-        )
+        sides[h, :, :size] = (key_rise * entry).astype(bf16)
         key_rise, query_rise = key_rise.astype(bf16), query_rise.astype(bf16)
         for a in range(chunks):
             rows = slice(a * chunk, (a + 1) * chunk)
@@ -251,6 +253,10 @@
             attend_ref[h, rows, inside] = jnp.where(
                 at >= to, scores[chunk:, inside], 0.0
             ).astype(bf16)
+
+    for i, piece in enumerate(pieces):
+        streams[i].wait()
+        projected[2, :, piece] = dot(rows_ref[...], value_weight[:, piece])
 
     at, to = row[:block, :block], col[:block, :block]
     eye = jnp.where(at == to, 1.0, 0.0).astype(bf16)
@@ -280,10 +286,12 @@
                 inverse[h, d.start + i : d.start + i + width, :] = new[n * width : (n + 1) * width]
         width *= 2
 
+    for h in range(heads):
+        sides[h, :, size:] = convolved(2, slice(h * size, (h + 1) * size)).astype(bf16)
     for d in range(blocks):
         rows = slice(d * block, (d + 1) * block)
         for h in range(heads):
-            side = sides[h][rows]
+            side = sides[h, rows, :]
             if d:
                 done = solved_ref[h, : d * block, :]
                 side = (side.astype(f32) - dot(mixing[h, rows, : d * block], done)).astype(bf16)
@@ -302,8 +310,8 @@
         other_ref[h] = jnp.where(upper, low, high).astype(bf16)
 
 
-def front(rim, slabs, fetched, loaded, weight, size):
-    slab_count, slab_rows = len(slabs), slabs[0].shape[0]
+def front(rims, slabs, fetched, loaded, weight, size):
+    slab_count, slab_rows = 1 + len(slabs), slabs[0].shape[0]
     count = slab_count * slab_rows
     _, width, channels = weight.shape
     heads, block = channels // size, math.gcd(count, 128)
@@ -317,9 +325,9 @@
             jax.ShapeDtypeStruct((heads, count, 2 * size), bf16),
             jax.ShapeDtypeStruct((heads, count, count), bf16),
             jax.ShapeDtypeStruct((heads, count, size), bf16),
-            jax.ShapeDtypeStruct((count, fetched[1].shape[1] // 2), bf16),
+            jax.ShapeDtypeStruct((count, fetched[2].shape[1] // 2), bf16),
         ),
-        (rim, *slabs[1:], *fetched, slabs[0], *loaded, weight),
+        (*rims, *slabs, *fetched, *loaded, weight),
         scratch=[
             *buffers,
             pltpu.VMEM((width, channels), bf16),
@@ -327,9 +335,10 @@
             pltpu.VMEM((3, RIM + count, channels), f32),
             pltpu.VMEM((heads, count, count), bf16),
             pltpu.VMEM((heads, count, block), bf16),
-            pltpu.SemaphoreType.DMA((5 + len(column_pieces(channels)),)),
+            pltpu.VMEM((heads, count, 2 * size), bf16),
+            pltpu.SemaphoreType.DMA((4 + len(column_pieces(channels)),)),
         ],
-        hbm=2 + len(loaded),
+        hbm=1 + len(loaded),
         grant=24,
         flops=2 * count * width * channels * 4,
         moved=2 * 4 * width * channels,
@@ -381,21 +390,28 @@
     )
 
 
-def before_body(bit, near_ref, far_ref, out_ref):
-    heads, size, _ = near_ref.shape
-    for h in range(heads):
-        near = near_ref[h]
-        pair = jnp.concatenate(composed(near, far_ref[h], size), axis=1)
-        out_ref[h] = jnp.where(place("seq", bit) == 1, pair, near.astype(f32)).astype(bf16)
+def before_body(bit, far_ref, *refs):
+    *near_refs, out_ref = refs
+    heads, size, width = far_ref.shape
+    row = lax.broadcasted_iota(jnp.int32, (size, width), 0)
+    col = lax.broadcasted_iota(jnp.int32, (size, width), 1)
+    for h in range(heads):
+        if near_refs:
+            near = near_refs[0][h]
+            pair = jnp.concatenate(composed(near, far_ref[h], size), axis=1)
+            near = near.astype(f32)
+        else:
+            near, pair = jnp.where(row == col, 1.0, 0.0), far_ref[h].astype(f32)
+        out_ref[h] = jnp.where(place("seq", bit) == 1, pair, near).astype(bf16)
 
 
 def before(bit, near, far):
     return vmem_call(
         functools.partial(before_body, bit),
-        jax.ShapeDtypeStruct(near.shape, bf16),
-        (near, far),
-        flops=2 * math.prod(near.shape) * near.shape[1],
-        moved=6 * math.prod(near.shape),
+        jax.ShapeDtypeStruct(far.shape, bf16),
+        (far, *near),
+        flops=2 * math.prod(far.shape) * far.shape[1],
+        moved=6 * math.prod(far.shape),
     )
 
 
@@ -418,17 +434,18 @@
     bits = bits_of(lax.axis_size("seq"))
     partner = swapped(other, "seq", 1)
     total = join(1, own, partner, len(bits) == 2)
-    near = jnp.broadcast_to(jnp.eye(size, width, dtype=bf16), own.shape)
+    near = ()
+    assert len(bits) > 2
     for bit in bits[1:-1]:
         far = swapped(total, "seq", bit)
         total = join(bit, total, far, 2 * bit == bits[-1])
-        near = before(bit, near, far)
+        near = (before(bit, near, far),)
     far = swapped(total, "seq", bits[-1])
     state = jax.ShapeDtypeStruct((heads, size, size), bf16)
     keep, send = vmem_call(
         functools.partial(entry_body, bits[-1]),
         (state, state),
-        (near, far, own, partner),
+        (*near, far, own, partner),
         flops=4 * heads * size * size * size,
         moved=14 * heads * size * size,
     )
@@ -495,10 +512,10 @@
     channels = heads * size
     devices = lax.axis_size("head")
     weight = qkv_weight.transpose(1, 0, 2)
-    tail, *fetched = load(hidden_in, decay_down, gate_down, beta_weight.T, weight)
-    slabs, rim = gathered(hidden_in, tail)
+    fetched = load(hidden_in, decay_down, gate_down, beta_weight.T, weight)
+    slabs, rims, fetched = gathered(hidden_in, fetched)
     own, other, solved, attend, start, gate_low = front(
-        rim, slabs, fetched, (decay_log, decay_up, dt_bias[None], conv_weight), weight, size
+        rims, slabs, fetched, (decay_log, decay_up, dt_bias[None], conv_weight), weight, size
     )
     count = start.shape[1]
     raised, output_rows, out_gate = vmem_call(

time: 64 us -> 56 us (0.88)
  starting transfers between devices: 21.1 us -> 15.4 us
  local copies, waits for them, and re-layouts: 4.49 us -> 0.93 us
  waiting for transfers between devices: 22 us -> 23.4 us
    ppermute x11, starting transfers between devices: 19.8 us -> 14.1 us  [swapped(): lax.ppermute(block, axis, [(i, i ^ bit) for i in range(lax.axis_size(axis...]
    unnamed x12 -> x6, local copies, waits for them, and re-layouts: 4.48 us -> 0.01 us
    ppermute x11, waiting for transfers between devices: 22 us -> 23.4 us  [swapped(): lax.ppermute(block, axis, [(i, i ^ bit) for i in range(lax.axis_size(axis...]
    slice x0 -> x1, local copies, waits for them, and re-layouts: none -> 0.92 us  [gathered(): tail = own[own.shape[0] - RIM:]]
    pallas_call x9 -> x10, Pallas kernels: 15.2 us -> 15.1 us  [vmem_call(): pl.pallas_call(body, out_shape=out_shape, in_specs=[pl.BlockSpec(memory_s...]
  transfers between devices with their start and end apart: 13 -> 13, of which waited for: 8 -> 8; matrix products, arithmetic and copies ran while one was open for 0% -> 2% of each run, Pallas kernels for 6% -> 7%
where the time goes in v6:
time: 56 us; the launch traced here: 55.8 us
  waiting for transfers between devices  23.4 us (42%)
  starting transfers between devices  15.4 us (28%)
  Pallas kernels  15.1 us (27%)
  local copies, waits for them, and re-layouts  0.93 us (2%)
  other arithmetic  0.85 us (2%)
    ppermute x11, waiting for transfers between devices, swapped(): lax.ppermute(block, axis, [(i, i ^ bit) for i in range(lax.axis_size(axis...  23.4 us
    pallas_call x10, Pallas kernels, vmem_call(): pl.pallas_call(body, out_shape=out_shape, in_specs=[pl.BlockSpec(memory_s...  15.1 us
    ppermute x11, starting transfers between devices, swapped(): lax.ppermute(block, axis, [(i, i ^ bit) for i in range(lax.axis_size(axis...  14.1 us
    ppermute x2, starting transfers between devices, gathered(): lax.ppermute(tail, ('seq', 'head'), rim_route(target))  1.32 us
  transfers between devices with their start and end apart: 13, of which 8 were waited for; matrix products, arithmetic and copies ran while one was open for 2% of the time, Pallas kernels for 7%

profile of v6, /device:TPU:0, one launch (start us, length us, event | category | flops | bytes accessed | tf_op | source)
XLA Modules:
  0.0 55.8 jit_solution(3260278636685587854)
XLA Ops:
  0.0 2.9 %collective-permute-start = (bf16[64,2304]{1,0:T(8,128)(2,1)}, bf16[64,2304]{1,0:T(8,128)(2,1)S(1)}, u32[]{:S(2)}, u32[]{:S(2)}) collective-permute-start(bf16[64,2304]{1,0:T(8,128)(2,1)} %hidden_ref.1), channel_id=1, source_target_pairs={{0,2},{1,3},{2,0},{3,1},{4,6},{5,7},{6,4},{7,5},{8,10},{9,11},{10,... | collective-permute-start | bytes 884744 | tf_op jit(solution)/shard_map/ppermute | solution.py:23
  2.9 0.9 %slice.3 = bf16[16,2304]{1,0:T(8,128)(2,1)S(1)} slice(bf16[64,2304]{1,0:T(8,128)(2,1)} %hidden_ref.1), slice={[48:64], [0:2304]} | slice | bytes 147456 | tf_op jit(solution)/shard_map/slice | solution.py:52
  3.9 0.7 %collective-permute-start.2 = (bf16[16,2304]{1,0:T(8,128)(2,1)S(1)}, bf16[16,2304]{1,0:T(8,128)(2,1)S(1)}, u32[]{:S(2)}, u32[]{:S(2)}) collective-permute-start(bf16[16,2304]{1,0:T(8,128)(2,1)S(1)} %slice.3), channel_id=1, source_target_pairs={{3,6},{7,10},{11,14},{15,18},{19,22},{23,26},{27,30}} | collective-permute-start | bytes 221192 | tf_op jit(solution)/shard_map/ppermute | solution.py:54
  4.5 0.7 %collective-permute-start.1 = (bf16[16,2304]{1,0:T(8,128)(2,1)S(1)}, bf16[16,2304]{1,0:T(8,128)(2,1)S(1)}, u32[]{:S(2)}, u32[]{:S(2)}) collective-permute-start(bf16[16,2304]{1,0:T(8,128)(2,1)S(1)} %slice.3), channel_id=1, source_target_pairs={{3,5},{7,9},{11,13},{15,17},{19,21},{23,25},{27,29}} | collective-permute-start | bytes 221192 | tf_op jit(solution)/shard_map/ppermute | solution.py:54
  5.2 0.1 collective-permute-start.4
  5.3 2.9 %shard_map.118 = (bf16[64,2304]{1,0:T(8,128)(2,1)S(1)}, bf16[2,2304,512]{2,1,0:T(8,128)(2,1)S(1)}, bf16[2304,256]{1,0:T(8,128)(2,1)S(1)}, bf16[4,2304]{1,0:T(4,128)(2,1)S(1)}) custom-call(bf16[64,2304]{1,0:T(8,128)(2,1)} %hidden_ref.1, bf16[2304,128]{1,0:T(8,128)(2,1)} %decay_down_ref.1, bf16[2304,128]{1,0:T(8,128)(2,1)} %gate_down_ref.1, ...), custom_call_target="tpu_custom_call" | custom-call | tf_op jit(solution)/shard_map/pallas_call | solution.py:72
  8.2 0.0 collective-permute-done.2.refs_1_
  8.2 0.0 collective-permute-done.1.refs_0_
  8.2 2.0 %collective-permute-done.refs_3_ = bf16[64,2304]{1,0:T(8,128)(2,1)S(1)} collective-permute-done((bf16[64,2304]{1,0:T(8,128)(2,1)}, bf16[64,2304]{1,0:T(8,128)(2,1)S(1)}, u32[]{:S(2)}, u32[]{:S(2)}) %collective-permute-start) | collective-permute-done | bytes 294944 | tf_op jit(solution)/shard_map/ppermute | solution.py:23
  10.2 0.0 collective-permute-start.5
  10.2 0.6 %collective-permute-start.3 = (bf16[16,2304]{1,0:T(8,128)(2,1)S(1)}, bf16[16,2304]{1,0:T(8,128)(2,1)S(1)}, u32[]{:S(2)}, u32[]{:S(2)}) collective-permute-start(bf16[16,2304]{1,0:T(8,128)(2,1)S(1)} %shard_map.119.refs_0_), channel_id=1, source_target_pairs={{0,1},{1,0},{2,3},{3,2},{4,5},{5,4},{6,7},{7,6},{8,9},{9,8},{10,11... | collective-permute-start | bytes 221192 | tf_op jit(solution)/shard_map/ppermute | solution.py:23
  10.8 0.0 collective-permute-done.4.refs_2_
  10.8 1.1 %collective-permute-done.3.refs_1_ = bf16[16,2304]{1,0:T(8,128)(2,1)S(1)} collective-permute-done((bf16[16,2304]{1,0:T(8,128)(2,1)S(1)}, bf16[16,2304]{1,0:T(8,128)(2,1)S(1)}, u32[]{:S(2)}, u32[]{:S(2)}) %collective-permute-start.3) | collective-permute-done | bytes 73760 | tf_op jit(solution)/shard_map/ppermute | solution.py:23
  11.9 0.0 collective-permute-done.5.refs_4_
  11.9 0.0 copy-start.1
  11.9 0.0 copy-start
  11.9 0.0 copy-start.2
  11.9 9.6 %shard_map.120 = (bf16[2,128,256]{2,1,0:T(8,128)(2,1)S(1)}, bf16[2,128,256]{2,1,0:T(8,128)(2,1)S(1)}, bf16[4,256,256]{2,1,0:T(8,128)(2,1)S(1)}, bf16[4,256,256]{...) custom-call(bf16[16,2304]{1,0:T(8,128)(2,1)S(1)} %shard_map.119.refs_0_, ...), custom_call_target="tpu_custom_call" | custom-call | flops 2415919104 | bytes 9437184 | tf_op jit(solution)/shard_map/pallas_call | solution.py:72
  21.5 1.8 %collective-permute-start.6 = (bf16[2,128,256]{2,1,0:T(8,128)(2,1)S(1)}, bf16[2,128,256]{2,1,0:T(8,128)(2,1)S(1)}, u32[]{:S(2)}, u32[]{:S(2)}) collective-permute-start(bf16[2,128,256]{2,1,0:T(8,128)(2,1)S(1)} %get-tuple-element.43), channel_id=1, source_target_pairs={{0,4},{4,0},{8,12},{12,8},{16,20},{20,16},{24,28},{28,24},{1,5},{5... | collective-permute-start | bytes 393224 | tf_op jit(solution)/shard_map/ppermute | solution.py:23
  23.3 4.0 %collective-permute-done.6.far_ref.partner_ref = bf16[2,128,256]{2,1,0:T(8,128)(2,1)S(1)} collective-permute-done((bf16[2,128,256]{2,1,0:T(8,128)(2,1)S(1)}, bf16[2,128,256]{2,1,0:T(8,128)(2,1)S(1)}, u32[]{:S(2)}, u32[]{:S(2)}) %collective-permute-start.6) | collective-permute-done | bytes 131104 | tf_op jit(solution)/shard_map/ppermute | solution.py:23
  27.2 0.2 shard_map.121.own_ref
  27.4 2.8 %collective-permute-start.7 = (bf16[2,128,256]{2,1,0:T(8,128)(2,1)S(1)}, bf16[2,128,256]{2,1,0:T(8,128)(2,1)S(1)}, u32[]{:S(2)}, u32[]{:S(2)}) collective-permute-start(bf16[2,128,256]{2,1,0:T(8,128)(2,1)S(1)} %shard_map.121.own_ref), channel_id=1, source_target_pairs={{0,8},{4,12},{8,0},{12,4},{16,24},{20,28},{24,16},{28,20},{1,9},{5... | collective-permute-start | bytes 393224 | tf_op jit(solution)/shard_map/ppermute | solution.py:23
  30.2 3.2 %collective-permute-done.7.far_ref = bf16[2,128,256]{2,1,0:T(8,128)(2,1)S(1)} collective-permute-done((bf16[2,128,256]{2,1,0:T(8,128)(2,1)S(1)}, bf16[2,128,256]{2,1,0:T(8,128)(2,1)S(1)}, u32[]{:S(2)}, u32[]{:S(2)}) %collective-permute-start.7) | collective-permute-done | bytes 131104 | tf_op jit(solution)/shard_map/ppermute | solution.py:23
  33.4 0.2 shard_map.123
  33.6 2.9 %collective-permute-start.8 = (bf16[2,128,128]{2,1,0:T(8,128)(2,1)S(1)}, bf16[2,128,128]{2,1,0:T(8,128)(2,1)S(1)}, u32[]{:S(2)}, u32[]{:S(2)}) collective-permute-start(bf16[2,128,128]{2,1,0:T(8,128)(2,1)S(1)} %shard_map.123), channel_id=1, source_target_pairs={{0,16},{4,20},{8,24},{12,28},{16,0},{20,4},{24,8},{28,12},{1,17},{... | collective-permute-start | bytes 196616 | tf_op jit(solution)/shard_map/ppermute | solution.py:23
  36.5 2.3 %collective-permute-done.8.far_ref = bf16[2,128,128]{2,1,0:T(8,128)(2,1)S(1)} collective-permute-done((bf16[2,128,128]{2,1,0:T(8,128)(2,1)S(1)}, bf16[2,128,128]{2,1,0:T(8,128)(2,1)S(1)}, u32[]{:S(2)}, u32[]{:S(2)}) %collective-permute-start.8) | collective-permute-done | bytes 65568 | tf_op jit(solution)/shard_map/ppermute | solution.py:23
  38.8 0.3 shard_map.124
  39.1 1.2 %collective-permute-start.9 = (bf16[2,128,128]{2,1,0:T(8,128)(2,1)S(1)}, bf16[2,128,128]{2,1,0:T(8,128)(2,1)S(1)}, u32[]{:S(2)}, u32[]{:S(2)}) collective-permute-start(bf16[2,128,128]{2,1,0:T(8,128)(2,1)S(1)} %get-tuple-element.45), channel_id=1, source_target_pairs={{0,4},{4,0},{8,12},{12,8},{16,20},{20,16},{24,28},{28,24},{1,5},{5... | collective-permute-start | bytes 196616 | tf_op jit(solution)/shard_map/ppermute | solution.py:23
  40.4 0.0 copy-done.1
  40.4 0.4 shard_map.125
  40.7 2.7 %collective-permute-done.9.other_ref = bf16[2,128,128]{2,1,0:T(8,128)(2,1)S(1)} collective-permute-done((bf16[2,128,128]{2,1,0:T(8,128)(2,1)S(1)}, bf16[2,128,128]{2,1,0:T(8,128)(2,1)S(1)}, u32[]{:S(2)}, u32[]{:S(2)}) %collective-permute-start.9) | collective-permute-done | bytes 65568 | tf_op jit(solution)/shard_map/ppermute | solution.py:23
  43.4 0.0 copy-done
  43.4 0.0 copy-done.2
  43.5 0.7 %shard_map.127 = (f32[64,2304]{1,0:T(8,128)S(1)}, bf16[64,2304]{1,0:T(8,128)(2,1)S(1)}) custom-call(bf16[2,128,128]{2,1,0:T(8,128)(2,1)S(1)} %get-tuple-element.44.own_ref, bf16[2,128,128]{2,1,0:T(8,128)(2,1)S(1)} %collective-permute-done.9.other_ref, bf16[4,256,128]{2,1,0:T(8,128)(2,1)S(1)} %get-tuple-element.50.raised_ref, ...), custom_call_target="tpu_custom_call" | custom-call | flops 301989888 | bytes 2359296 | tf_op jit(solution)/shard_map/pallas_call | solution.py:72
  44.2 0.1 collective-permute-start.11
  44.3 0.7 %shard_map.126 = (f32[64,2304]{1,0:T(8,128)S(1)}, bf16[64,2304]{1,0:T(8,128)(2,1)S(1)}) custom-call(bf16[2,128,128]{2,1,0:T(8,128)(2,1)S(1)} %get-tuple-element.44.own_ref, bf16[2,128,128]{2,1,0:T(8,128)(2,1)S(1)} %collective-permute-done.9.other_ref, bf16[4,256,128]{2,1,0:T(8,128)(2,1)S(1)} %get-tuple-element.50.raised_ref, ...), custom_call_target="tpu_custom_call" | custom-call | flops 301989888 | bytes 2359296 | tf_op jit(solution)/shard_map/pallas_call | solution.py:72
  45.0 0.6 collective-permute-start.10
  45.6 0.3 collective-permute-done.11
  45.8 0.1 add_convert_fusion.1
  45.9 1.2 %collective-permute-start.12 = (bf16[64,2304]{1,0:T(8,128)(2,1)S(1)}, bf16[64,2304]{1,0:T(8,128)(2,1)S(1)}, u32[]{:S(2)}, u32[]{:S(2)}) collective-permute-start(bf16[64,2304]{1,0:T(8,128)(2,1)S(1)} %add_convert_fusion.1), channel_id=1, source_target_pairs={{0,2},{1,3},{2,0},{3,1},{4,6},{5,7},{6,4},{7,5},{8,10},{9,11},{10,... | collective-permute-start | bytes 884744 | tf_op jit(solution)/shard_map/ppermute | solution.py:23
  47.1 0.0 collective-permute-done.10
  47.1 8.0 %collective-permute-done.12 = bf16[64,2304]{1,0:T(8,128)(2,1)S(1)} collective-permute-done((bf16[64,2304]{1,0:T(8,128)(2,1)S(1)}, bf16[64,2304]{1,0:T(8,128)(2,1)S(1)}, u32[]{:S(2)}, u32[]{:S(2)}) %collective-permute-start.12) | collective-permute-done | bytes 294944 | tf_op jit(solution)/shard_map/ppermute | solution.py:23
  55.0 0.8 %add_convert_fusion = bf16[64,2304]{1,0:T(8,128)(2,1)} fusion(bf16[64,2304]{1,0:T(8,128)(2,1)S(1)} %collective-permute-done.12, f32[64,2304]{1,0:T(8,128)S(1)} %get-tuple-element.53, bf16[64,2304]{1,0:T(8,128)(2,1)S(1)} %collective-permute-done.10), kind=kLoop, calls=%fused_computation | loop fusion | flops 737280 | bytes 1474560 | tf_op jit(solution)/shard_map/convert_element_type | solution.py:547
  (2 shorter events, 0.1 us)
Async XLA Ops:
  0.0 10.2 %collective-permute-start = (bf16[64,2304]{1,0:T(8,128)(2,1)}, bf16[64,2304]{1,0:T(8,128)(2,1)S(1)}, u32[]{:S(2)}, u32[]{:S(2)}) collective-permute-start(bf16[64,2304]{1,0:T(8,128)(2,1)} %hidden_ref.1), channel_id=1, source_target_pairs={{0,2},{1,3},{2,0},{3,1},{4,6},{5,7},{6,4},{7,5},{8,10},{9,11},{10,... | collective-permute-start | bytes 884744 | tf_op jit(solution)/shard_map/ppermute | solution.py:23
  3.9 4.3 %collective-permute-start.2 = (bf16[16,2304]{1,0:T(8,128)(2,1)S(1)}, bf16[16,2304]{1,0:T(8,128)(2,1)S(1)}, u32[]{:S(2)}, u32[]{:S(2)}) collective-permute-start(bf16[16,2304]{1,0:T(8,128)(2,1)S(1)} %slice.3), channel_id=1, source_target_pairs={{3,6},{7,10},{11,14},{15,18},{19,22},{23,26},{27,30}} | collective-permute-start | bytes 221192 | tf_op jit(solution)/shard_map/ppermute | solution.py:54
  4.5 3.7 %collective-permute-start.1 = (bf16[16,2304]{1,0:T(8,128)(2,1)S(1)}, bf16[16,2304]{1,0:T(8,128)(2,1)S(1)}, u32[]{:S(2)}, u32[]{:S(2)}) collective-permute-start(bf16[16,2304]{1,0:T(8,128)(2,1)S(1)} %slice.3), channel_id=1, source_target_pairs={{3,5},{7,9},{11,13},{15,17},{19,21},{23,25},{27,29}} | collective-permute-start | bytes 221192 | tf_op jit(solution)/shard_map/ppermute | solution.py:54
  5.2 5.6 %collective-permute-start.4 = (bf16[64,2304]{1,0:T(8,128)(2,1)}, bf16[64,2304]{1,0:T(8,128)(2,1)S(1)}, u32[]{:S(2)}, u32[]{:S(2)}) collective-permute-start(bf16[64,2304]{1,0:T(8,128)(2,1)} %hidden_ref.1), channel_id=1, source_target_pairs={{0,1},{1,0},{2,3},{3,2},{4,5},{5,4},{6,7},{7,6},{8,9},{9,8},{10,11... | collective-permute-start | bytes 884744 | tf_op jit(solution)/shard_map/ppermute | solution.py:23
  10.2 1.7 %collective-permute-start.5 = (bf16[64,2304]{1,0:T(8,128)(2,1)S(1)}, bf16[64,2304]{1,0:T(8,128)(2,1)S(1)}, u32[]{:S(2)}, u32[]{:S(2)}) collective-permute-start(bf16[64,2304]{1,0:T(8,128)(2,1)S(1)} %collective-permute-done.refs_3_), channel_id=1, source_target_pairs={{0,1},{1,0},{2,3},{3,2},{4,5},{5,4},{6,7},{7,6},{8,9},{9,8},{10,11... | collective-permute-start | bytes 884744 | tf_op jit(solution)/shard_map/ppermute | solution.py:23
  10.2 1.7 %collective-permute-start.3 = (bf16[16,2304]{1,0:T(8,128)(2,1)S(1)}, bf16[16,2304]{1,0:T(8,128)(2,1)S(1)}, u32[]{:S(2)}, u32[]{:S(2)}) collective-permute-start(bf16[16,2304]{1,0:T(8,128)(2,1)S(1)} %shard_map.119.refs_0_), channel_id=1, source_target_pairs={{0,1},{1,0},{2,3},{3,2},{4,5},{5,4},{6,7},{7,6},{8,9},{9,8},{10,11... | collective-permute-start | bytes 221192 | tf_op jit(solution)/shard_map/ppermute | solution.py:23
  11.9 28.5 %copy-start.1 = (bf16[128,512]{1,0:T(8,128)(2,1)S(1)}, bf16[128,512]{1,0:T(8,128)(2,1)}, u32[]{:S(2)}) copy-start(bf16[128,512]{1,0:T(8,128)(2,1)} %up_ref.1) | copy-start | bytes 393220
  11.9 31.6 %copy-start = (bf16[512,2304]{1,0:T(8,128)(2,1)S(1)}, bf16[512,2304]{1,0:T(8,128)(2,1)}, u32[]{:S(2)}) copy-start(bf16[512,2304]{1,0:T(8,128)(2,1)} %weight_ref.3) | copy-start | bytes 7077892
  11.9 31.6 %copy-start.2 = (f32[128]{0:T(128)S(1)}, f32[128]{0:T(128)}, u32[]{:S(2)}) copy-start(f32[128]{0:T(128)} %param.22) | copy-start | bytes 1540
  21.5 5.8 %collective-permute-start.6 = (bf16[2,128,256]{2,1,0:T(8,128)(2,1)S(1)}, bf16[2,128,256]{2,1,0:T(8,128)(2,1)S(1)}, u32[]{:S(2)}, u32[]{:S(2)}) collective-permute-start(bf16[2,128,256]{2,1,0:T(8,128)(2,1)S(1)} %get-tuple-element.43), channel_id=1, source_target_pairs={{0,4},{4,0},{8,12},{12,8},{16,20},{20,16},{24,28},{28,24},{1,5},{5... | collective-permute-start | bytes 393224 | tf_op jit(solution)/shard_map/ppermute | solution.py:23
  27.4 6.0 %collective-permute-start.7 = (bf16[2,128,256]{2,1,0:T(8,128)(2,1)S(1)}, bf16[2,128,256]{2,1,0:T(8,128)(2,1)S(1)}, u32[]{:S(2)}, u32[]{:S(2)}) collective-permute-start(bf16[2,128,256]{2,1,0:T(8,128)(2,1)S(1)} %shard_map.121.own_ref), channel_id=1, source_target_pairs={{0,8},{4,12},{8,0},{12,4},{16,24},{20,28},{24,16},{28,20},{1,9},{5... | collective-permute-start | bytes 393224 | tf_op jit(solution)/shard_map/ppermute | solution.py:23
  33.6 5.2 %collective-permute-start.8 = (bf16[2,128,128]{2,1,0:T(8,128)(2,1)S(1)}, bf16[2,128,128]{2,1,0:T(8,128)(2,1)S(1)}, u32[]{:S(2)}, u32[]{:S(2)}) collective-permute-start(bf16[2,128,128]{2,1,0:T(8,128)(2,1)S(1)} %shard_map.123), channel_id=1, source_target_pairs={{0,16},{4,20},{8,24},{12,28},{16,0},{20,4},{24,8},{28,12},{1,17},{... | collective-permute-start | bytes 196616 | tf_op jit(solution)/shard_map/ppermute | solution.py:23
  39.1 4.3 %collective-permute-start.9 = (bf16[2,128,128]{2,1,0:T(8,128)(2,1)S(1)}, bf16[2,128,128]{2,1,0:T(8,128)(2,1)S(1)}, u32[]{:S(2)}, u32[]{:S(2)}) collective-permute-start(bf16[2,128,128]{2,1,0:T(8,128)(2,1)S(1)} %get-tuple-element.45), channel_id=1, source_target_pairs={{0,4},{4,0},{8,12},{12,8},{16,20},{20,16},{24,28},{28,24},{1,5},{5... | collective-permute-start | bytes 196616 | tf_op jit(solution)/shard_map/ppermute | solution.py:23
  44.2 1.6 %collective-permute-start.11 = (bf16[64,2304]{1,0:T(8,128)(2,1)S(1)}, bf16[64,2304]{1,0:T(8,128)(2,1)S(1)}, u32[]{:S(2)}, u32[]{:S(2)}) collective-permute-start(bf16[64,2304]{1,0:T(8,128)(2,1)S(1)} %get-tuple-element.56), channel_id=1, source_target_pairs={{0,1},{1,0},{2,3},{3,2},{4,5},{5,4},{6,7},{7,6},{8,9},{9,8},{10,11... | collective-permute-start | bytes 884744 | tf_op jit(solution)/shard_map/ppermute | solution.py:23
  45.0 2.0 %collective-permute-start.10 = (bf16[64,2304]{1,0:T(8,128)(2,1)S(1)}, bf16[64,2304]{1,0:T(8,128)(2,1)S(1)}, u32[]{:S(2)}, u32[]{:S(2)}) collective-permute-start(bf16[64,2304]{1,0:T(8,128)(2,1)S(1)} %get-tuple-element.54), channel_id=1, source_target_pairs={{0,1},{1,0},{2,3},{3,2},{4,5},{5,4},{6,7},{7,6},{8,9},{9,8},{10,11... | collective-permute-start | bytes 884744 | tf_op jit(solution)/shard_map/ppermute | solution.py:23
  45.9 9.1 %collective-permute-start.12 = (bf16[64,2304]{1,0:T(8,128)(2,1)S(1)}, bf16[64,2304]{1,0:T(8,128)(2,1)S(1)}, u32[]{:S(2)}, u32[]{:S(2)}) collective-permute-start(bf16[64,2304]{1,0:T(8,128)(2,1)S(1)} %add_convert_fusion.1), channel_id=1, source_target_pairs={{0,2},{1,3},{2,0},{3,1},{4,6},{5,7},{6,4},{7,5},{8,10},{9,11},{10,... | collective-permute-start | bytes 884744 | tf_op jit(solution)/shard_map/ppermute | solution.py:23

commit v7 on v6

--- a/solution.py
+++ b/solution.py
@@ -132,7 +132,7 @@
     hbm_refs, refs = refs[:5], refs[5:]
     (own_ref, other_ref, solved_ref, attend_ref, start_ref, gate_ref), refs = refs[:6], refs[6:]
     loaded, refs = refs[:5], refs[5:]
-    rows_ref, projected, mixing, inverse, sides, sems = refs
+    rows_ref, projected, running_ref, parts_ref, mixing, inverse, sides, sems = refs
     rates, decay_up_ref, bias_ref, conv_ref, value_weight = loaded
     weight_ref = hbm_refs[-1]
     heads, count, size = start_ref.shape
@@ -170,79 +170,72 @@
     strength = jax.nn.sigmoid(dot(rows_ref[RIM:, :], betas[...], ((1,), (1,))))
     for copy in small:
         copy.wait()
-    raw = dot(low[:, :rank], decay_up_ref[...]) + bias_ref[...]
-    softplus = jnp.maximum(raw, 0.0) + jnp.log(1.0 + jnp.exp(-jnp.abs(raw)))
-    rate = jnp.concatenate(
-        [jnp.exp(jnp.full((1, size), rates[h], f32)) for h in range(heads)], axis=1
-    )
-    log_decay = -rate * softplus
+    running_ref[...] = dot(low[:, :rank], decay_up_ref[...])
+    tiles = [slice(a * chunk, (a + 1) * chunk) for a in range(chunks)]
+    for h in range(heads):
+        lanes = slice(h * size, (h + 1) * size)
+        rate = jnp.exp(jnp.full((1, size), rates[h], f32))
+        for rows in tiles:
+            raw = running_ref[rows, lanes] + bias_ref[:, lanes]
+            softplus = jnp.maximum(raw, 0.0) + jnp.log(1.0 + jnp.exp(-jnp.abs(raw)))
+            log_decay = -rate * softplus
+            high = log_decay.astype(bf16)
+            parts_ref[rows, lanes] = high
+            rest = (log_decay - high.astype(f32)).astype(bf16)
+            parts_ref[count + rows.start : count + rows.stop, lanes] = rest
     row = lax.broadcasted_iota(jnp.int32, (count, count), 0)
     col = lax.broadcasted_iota(jnp.int32, (count, count), 1)
     lower = jnp.where(row >= col, 1.0, 0.0).astype(bf16)
-
-    def exact(left, right):
-        high = right.astype(bf16)
-        return dot(left, high) + dot(left, (right - high.astype(f32)).astype(bf16))
-
-    cumulative = exact(lower, log_decay)
-    spread = lax.broadcasted_iota(jnp.int32, (heads, heads * size), 1) // size
-    spread = spread == lax.broadcasted_iota(jnp.int32, (heads, heads * size), 0)
-    spread = jnp.where(spread, 1.0, 0.0).astype(bf16)
-    high = strength.astype(bf16)
-    strengths = dot(high, spread) + dot((strength - high.astype(f32)).astype(bf16), spread)
-
-    def convolved(c, lanes):
+    running_ref[...] = dot(jnp.concatenate([lower, lower], axis=1), parts_ref[...])
+
+    def convolved(c, rows, lanes):
         taps = conv_ref[c].astype(f32)
         total = None
         for i in range(tap_count):
-            shifted = projected[c, pl.ds(RIM - tap_count + 1 + i, count), lanes]
-            term = shifted * taps[i : i + 1, lanes]
+            first = RIM - tap_count + 1 + i + rows.start
+            term = projected[c, pl.ds(first, chunk), lanes] * taps[i : i + 1, lanes]
             total = term if total is None else total + term
         half = 0.5 * total
         return half + half * jnp.tanh(half)
 
-    def by_chunk(rows):
-        return jnp.concatenate([jnp.broadcast_to(r, (chunk, size)) for r in rows], axis=0)
-
-    ones = jnp.full((size, size), 1.0, bf16)
-    scaled = jnp.full((size, size), float(size), bf16)
     stops = []
     for h in range(heads):
         lanes = slice(h * size, (h + 1) * size)
-        queries, keys = convolved(0, lanes), convolved(1, lanes)
-        power = dot((queries * queries).astype(bf16), scaled)
-        queries = queries * lax.rsqrt(power + size * 1e-06)
-        power = dot((keys * keys).astype(bf16), ones)
-        keys = keys * lax.rsqrt(power + 1e-06)
-        running = cumulative[:, lanes]
-        middles = [running[a * chunk + chunk // 2 : a * chunk + chunk // 2 + 1] for a in range(chunks)]
-        above = running - by_chunk(middles)
-        rise = jnp.exp(above)
-        key_rise, query_rise = keys * rise, queries * rise
-        key_fall = keys * strengths[:, lanes] * jnp.exp(-above)
-        last = running[count - 1 :]
-        stops.append(
-            ((key_fall * by_chunk([jnp.exp(last - m) for m in middles])).astype(bf16), jnp.exp(last))
-        )
-        entry = by_chunk([jnp.exp(m) for m in middles])
-        start_ref[h] = (query_rise * entry).astype(bf16)
-        sides[h, :, :size] = (key_rise * entry).astype(bf16)
-        key_rise, query_rise = key_rise.astype(bf16), query_rise.astype(bf16)
+        last = running_ref[count - 1 : count, lanes]
+        middles, key_falls, stop, lefts = [], [], [], []
+        for rows in tiles:
+            running = running_ref[rows, lanes]
+            middle = running[chunk // 2 : chunk // 2 + 1]
+            above = running - middle
+            rise, entry = jnp.exp(above), jnp.exp(middle)
+            queries = convolved(0, rows, lanes)
+            power = jnp.sum(queries * queries, -1, keepdims=True)
+            queries = queries * (lax.rsqrt(power + 1e-06) * size ** (-0.5)) * rise
+            start_ref[h, rows, :] = (queries * entry).astype(bf16)
+            keys = convolved(1, rows, lanes)
+            power = jnp.sum(keys * keys, -1, keepdims=True)
+            keys = keys * lax.rsqrt(power + 1e-06)
+            key_fall = keys * strength[rows, h : h + 1] * jnp.exp(-above)
+            keys = keys * rise
+            sides[h, rows, :size] = (keys * entry).astype(bf16)
+            stop.append((key_fall * jnp.exp(last - middle)).astype(bf16))
+            middles.append(middle)
+            key_falls.append(key_fall)
+            lefts.append(jnp.concatenate([keys.astype(bf16), queries.astype(bf16)], axis=0))
+        stops.append((jnp.concatenate(stop, axis=0), jnp.exp(last)))
         for a in range(chunks):
-            rows = slice(a * chunk, (a + 1) * chunk)
-            left = jnp.concatenate([key_rise[rows], query_rise[rows]], axis=0)
+            rows = tiles[a]
             reach = (a * chunk // block + 1) * block
             falls = []
             for b in range(reach // chunk):
-                there = slice(b * chunk, (b + 1) * chunk)
                 if b < a:
-                    falls.append(key_fall[there] * jnp.exp(middles[a] - middles[b]))
+                    falls.append(key_falls[b] * jnp.exp(middles[a] - middles[b]))
                 elif b == a:
-                    falls.append(key_fall[there])
+                    falls.append(key_falls[b])
                 else:
                     falls.append(jnp.zeros((chunk, size), f32))
             right = jnp.concatenate(falls, axis=0).astype(bf16)
-            scores = dot(left, right, ((1,), (1,)))
+            scores = dot(lefts[a], right, ((1,), (1,)))
             inside = slice(reach - block, reach)
             if reach > block:
                 before = slice(0, reach - block)
@@ -265,9 +258,18 @@
     corners = [(h, slice(d * block, (d + 1) * block)) for h in range(heads) for d in range(blocks)]
     powers = [mixing[h, d, d] * near for h, d in corners]
     totals = [power + eye for power in powers]
-    for _ in range(1, (base - 1).bit_length()):
+    steps = (base - 1).bit_length() - 1
+    if steps:
         powers = [dot(power, power).astype(bf16) for power in powers]
-        totals = [dot(t, power + eye).astype(bf16) for t, power in zip(totals, powers)]
+    for step in range(steps):
+        for n in range(len(corners)):
+            power, total = powers[n], totals[n]
+            if step < steps - 1:
+                both = dot(jnp.concatenate([power, total], axis=0), power)
+                powers[n], more = both[:block].astype(bf16), both[block:]
+            else:
+                more = dot(total, power)
+            totals[n] = (total.astype(f32) + more).astype(bf16)
     for (h, d), total in zip(corners, totals):
         inverse[h, d, :] = total
     width = base
@@ -287,7 +289,9 @@
         width *= 2
 
     for h in range(heads):
-        sides[h, :, size:] = convolved(2, slice(h * size, (h + 1) * size)).astype(bf16)
+        for rows in tiles:
+            lanes = slice(h * size, (h + 1) * size)
+            sides[h, rows, size:] = convolved(2, rows, lanes).astype(bf16)
     for d in range(blocks):
         rows = slice(d * block, (d + 1) * block)
         for h in range(heads):
@@ -333,6 +337,8 @@
             pltpu.VMEM((width, channels), bf16),
             pltpu.VMEM((RIM + count, width), bf16),
             pltpu.VMEM((3, RIM + count, channels), f32),
+            pltpu.VMEM((count, channels), f32),
+            pltpu.VMEM((2 * count, channels), bf16),
             pltpu.VMEM((heads, count, count), bf16),
             pltpu.VMEM((heads, count, block), bf16),
             pltpu.VMEM((heads, count, 2 * size), bf16),

time: 56 us -> 55.8 us (level)
  no operation moved by 1% of the time
where the time goes in v7:
time: 55.8 us; the launch traced here: 55.6 us
  waiting for transfers between devices  23.5 us (42%)
  starting transfers between devices  15.4 us (28%)
  Pallas kernels  14.8 us (27%)
  local copies, waits for them, and re-layouts  0.93 us (2%)
  other arithmetic  0.85 us (2%)
    ppermute x11, waiting for transfers between devices, swapped(): lax.ppermute(block, axis, [(i, i ^ bit) for i in range(lax.axis_size(axis...  23.5 us
    pallas_call x10, Pallas kernels, vmem_call(): pl.pallas_call(body, out_shape=out_shape, in_specs=[pl.BlockSpec(memory_s...  14.8 us
    ppermute x11, starting transfers between devices, swapped(): lax.ppermute(block, axis, [(i, i ^ bit) for i in range(lax.axis_size(axis...  14 us
    ppermute x2, starting transfers between devices, gathered(): lax.ppermute(tail, ('seq', 'head'), rim_route(target))  1.32 us
  transfers between devices with their start and end apart: 13, of which 8 were waited for; matrix products, arithmetic and copies ran while one was open for 2% of the time, Pallas kernels for 7%

profile of v7, /device:TPU:0, one launch (start us, length us, event | category | flops | bytes accessed | tf_op | source)
XLA Modules:
  0.0 55.6 jit_solution(18296528481416057538)
XLA Ops:
  0.0 2.9 %collective-permute-start = (bf16[64,2304]{1,0:T(8,128)(2,1)}, bf16[64,2304]{1,0:T(8,128)(2,1)S(1)}, u32[]{:S(2)}, u32[]{:S(2)}) collective-permute-start(bf16[64,2304]{1,0:T(8,128)(2,1)} %hidden_ref.1), channel_id=1, source_target_pairs={{0,2},{1,3},{2,0},{3,1},{4,6},{5,7},{6,4},{7,5},{8,10},{9,11},{10,... | collective-permute-start | bytes 884744 | tf_op jit(solution)/shard_map/ppermute | solution.py:23
  2.9 0.9 %slice.3 = bf16[16,2304]{1,0:T(8,128)(2,1)S(1)} slice(bf16[64,2304]{1,0:T(8,128)(2,1)} %hidden_ref.1), slice={[48:64], [0:2304]} | slice | bytes 147456 | tf_op jit(solution)/shard_map/slice | solution.py:52
  3.9 0.7 %collective-permute-start.2 = (bf16[16,2304]{1,0:T(8,128)(2,1)S(1)}, bf16[16,2304]{1,0:T(8,128)(2,1)S(1)}, u32[]{:S(2)}, u32[]{:S(2)}) collective-permute-start(bf16[16,2304]{1,0:T(8,128)(2,1)S(1)} %slice.3), channel_id=1, source_target_pairs={{3,6},{7,10},{11,14},{15,18},{19,22},{23,26},{27,30}} | collective-permute-start | bytes 221192 | tf_op jit(solution)/shard_map/ppermute | solution.py:54
  4.5 0.7 %collective-permute-start.1 = (bf16[16,2304]{1,0:T(8,128)(2,1)S(1)}, bf16[16,2304]{1,0:T(8,128)(2,1)S(1)}, u32[]{:S(2)}, u32[]{:S(2)}) collective-permute-start(bf16[16,2304]{1,0:T(8,128)(2,1)S(1)} %slice.3), channel_id=1, source_target_pairs={{3,5},{7,9},{11,13},{15,17},{19,21},{23,25},{27,29}} | collective-permute-start | bytes 221192 | tf_op jit(solution)/shard_map/ppermute | solution.py:54
  5.2 0.1 collective-permute-start.4
  5.3 2.9 %shard_map.118 = (bf16[64,2304]{1,0:T(8,128)(2,1)S(1)}, bf16[2,2304,512]{2,1,0:T(8,128)(2,1)S(1)}, bf16[2304,256]{1,0:T(8,128)(2,1)S(1)}, bf16[4,2304]{1,0:T(4,128)(2,1)S(1)}) custom-call(bf16[64,2304]{1,0:T(8,128)(2,1)} %hidden_ref.1, bf16[2304,128]{1,0:T(8,128)(2,1)} %decay_down_ref.1, bf16[2304,128]{1,0:T(8,128)(2,1)} %gate_down_ref.1, ...), custom_call_target="tpu_custom_call" | custom-call | tf_op jit(solution)/shard_map/pallas_call | solution.py:72
  8.2 0.0 collective-permute-done.2.refs_1_
  8.2 0.0 collective-permute-done.1.refs_0_
  8.2 2.0 %collective-permute-done.refs_3_ = bf16[64,2304]{1,0:T(8,128)(2,1)S(1)} collective-permute-done((bf16[64,2304]{1,0:T(8,128)(2,1)}, bf16[64,2304]{1,0:T(8,128)(2,1)S(1)}, u32[]{:S(2)}, u32[]{:S(2)}) %collective-permute-start) | collective-permute-done | bytes 294944 | tf_op jit(solution)/shard_map/ppermute | solution.py:23
  10.2 0.0 collective-permute-start.5
  10.2 0.6 %collective-permute-start.3 = (bf16[16,2304]{1,0:T(8,128)(2,1)S(1)}, bf16[16,2304]{1,0:T(8,128)(2,1)S(1)}, u32[]{:S(2)}, u32[]{:S(2)}) collective-permute-start(bf16[16,2304]{1,0:T(8,128)(2,1)S(1)} %shard_map.119.refs_0_), channel_id=1, source_target_pairs={{0,1},{1,0},{2,3},{3,2},{4,5},{5,4},{6,7},{7,6},{8,9},{9,8},{10,11... | collective-permute-start | bytes 221192 | tf_op jit(solution)/shard_map/ppermute | solution.py:23
  10.8 0.0 collective-permute-done.4.refs_2_
  10.8 1.1 %collective-permute-done.3.refs_1_ = bf16[16,2304]{1,0:T(8,128)(2,1)S(1)} collective-permute-done((bf16[16,2304]{1,0:T(8,128)(2,1)S(1)}, bf16[16,2304]{1,0:T(8,128)(2,1)S(1)}, u32[]{:S(2)}, u32[]{:S(2)}) %collective-permute-start.3) | collective-permute-done | bytes 73760 | tf_op jit(solution)/shard_map/ppermute | solution.py:23
  11.9 0.0 collective-permute-done.5.refs_4_
  11.9 0.0 copy-start.1
  11.9 0.0 copy-start
  11.9 0.0 copy-start.2
  11.9 9.3 %shard_map.120 = (bf16[2,128,256]{2,1,0:T(8,128)(2,1)S(1)}, bf16[2,128,256]{2,1,0:T(8,128)(2,1)S(1)}, bf16[4,256,256]{2,1,0:T(8,128)(2,1)S(1)}, bf16[4,256,256]{...) custom-call(bf16[16,2304]{1,0:T(8,128)(2,1)S(1)} %shard_map.119.refs_0_, ...), custom_call_target="tpu_custom_call" | custom-call | flops 2415919104 | bytes 9437184 | tf_op jit(solution)/shard_map/pallas_call | solution.py:72
  21.2 1.8 %collective-permute-start.6 = (bf16[2,128,256]{2,1,0:T(8,128)(2,1)S(1)}, bf16[2,128,256]{2,1,0:T(8,128)(2,1)S(1)}, u32[]{:S(2)}, u32[]{:S(2)}) collective-permute-start(bf16[2,128,256]{2,1,0:T(8,128)(2,1)S(1)} %get-tuple-element.43), channel_id=1, source_target_pairs={{0,4},{4,0},{8,12},{12,8},{16,20},{20,16},{24,28},{28,24},{1,5},{5... | collective-permute-start | bytes 393224 | tf_op jit(solution)/shard_map/ppermute | solution.py:23
  23.0 4.0 %collective-permute-done.6.far_ref.partner_ref = bf16[2,128,256]{2,1,0:T(8,128)(2,1)S(1)} collective-permute-done((bf16[2,128,256]{2,1,0:T(8,128)(2,1)S(1)}, bf16[2,128,256]{2,1,0:T(8,128)(2,1)S(1)}, u32[]{:S(2)}, u32[]{:S(2)}) %collective-permute-start.6) | collective-permute-done | bytes 131104 | tf_op jit(solution)/shard_map/ppermute | solution.py:23
  27.0 0.2 shard_map.121.own_ref
  27.2 2.8 %collective-permute-start.7 = (bf16[2,128,256]{2,1,0:T(8,128)(2,1)S(1)}, bf16[2,128,256]{2,1,0:T(8,128)(2,1)S(1)}, u32[]{:S(2)}, u32[]{:S(2)}) collective-permute-start(bf16[2,128,256]{2,1,0:T(8,128)(2,1)S(1)} %shard_map.121.own_ref), channel_id=1, source_target_pairs={{0,8},{4,12},{8,0},{12,4},{16,24},{20,28},{24,16},{28,20},{1,9},{5... | collective-permute-start | bytes 393224 | tf_op jit(solution)/shard_map/ppermute | solution.py:23
  30.0 3.2 %collective-permute-done.7.far_ref = bf16[2,128,256]{2,1,0:T(8,128)(2,1)S(1)} collective-permute-done((bf16[2,128,256]{2,1,0:T(8,128)(2,1)S(1)}, bf16[2,128,256]{2,1,0:T(8,128)(2,1)S(1)}, u32[]{:S(2)}, u32[]{:S(2)}) %collective-permute-start.7) | collective-permute-done | bytes 131104 | tf_op jit(solution)/shard_map/ppermute | solution.py:23
  33.2 0.2 shard_map.123
  33.4 2.9 %collective-permute-start.8 = (bf16[2,128,128]{2,1,0:T(8,128)(2,1)S(1)}, bf16[2,128,128]{2,1,0:T(8,128)(2,1)S(1)}, u32[]{:S(2)}, u32[]{:S(2)}) collective-permute-start(bf16[2,128,128]{2,1,0:T(8,128)(2,1)S(1)} %shard_map.123), channel_id=1, source_target_pairs={{0,16},{4,20},{8,24},{12,28},{16,0},{20,4},{24,8},{28,12},{1,17},{... | collective-permute-start | bytes 196616 | tf_op jit(solution)/shard_map/ppermute | solution.py:23
  36.3 2.3 %collective-permute-done.8.far_ref = bf16[2,128,128]{2,1,0:T(8,128)(2,1)S(1)} collective-permute-done((bf16[2,128,128]{2,1,0:T(8,128)(2,1)S(1)}, bf16[2,128,128]{2,1,0:T(8,128)(2,1)S(1)}, u32[]{:S(2)}, u32[]{:S(2)}) %collective-permute-start.8) | collective-permute-done | bytes 65568 | tf_op jit(solution)/shard_map/ppermute | solution.py:23
  38.6 0.3 shard_map.124
  38.9 1.2 %collective-permute-start.9 = (bf16[2,128,128]{2,1,0:T(8,128)(2,1)S(1)}, bf16[2,128,128]{2,1,0:T(8,128)(2,1)S(1)}, u32[]{:S(2)}, u32[]{:S(2)}) collective-permute-start(bf16[2,128,128]{2,1,0:T(8,128)(2,1)S(1)} %get-tuple-element.45), channel_id=1, source_target_pairs={{0,4},{4,0},{8,12},{12,8},{16,20},{20,16},{24,28},{28,24},{1,5},{5... | collective-permute-start | bytes 196616 | tf_op jit(solution)/shard_map/ppermute | solution.py:23
  40.1 0.0 copy-done.1
  40.1 0.4 shard_map.125
  40.5 2.7 %collective-permute-done.9.other_ref = bf16[2,128,128]{2,1,0:T(8,128)(2,1)S(1)} collective-permute-done((bf16[2,128,128]{2,1,0:T(8,128)(2,1)S(1)}, bf16[2,128,128]{2,1,0:T(8,128)(2,1)S(1)}, u32[]{:S(2)}, u32[]{:S(2)}) %collective-permute-start.9) | collective-permute-done | bytes 65568 | tf_op jit(solution)/shard_map/ppermute | solution.py:23
  43.2 0.0 copy-done
  43.2 0.0 copy-done.2
  43.2 0.7 %shard_map.127 = (f32[64,2304]{1,0:T(8,128)S(1)}, bf16[64,2304]{1,0:T(8,128)(2,1)S(1)}) custom-call(bf16[2,128,128]{2,1,0:T(8,128)(2,1)S(1)} %get-tuple-element.44.own_ref, bf16[2,128,128]{2,1,0:T(8,128)(2,1)S(1)} %collective-permute-done.9.other_ref, bf16[4,256,128]{2,1,0:T(8,128)(2,1)S(1)} %get-tuple-element.50.raised_ref, ...), custom_call_target="tpu_custom_call" | custom-call | flops 301989888 | bytes 2359296 | tf_op jit(solution)/shard_map/pallas_call | solution.py:72
  44.0 0.1 collective-permute-start.11
  44.1 0.7 %shard_map.126 = (f32[64,2304]{1,0:T(8,128)S(1)}, bf16[64,2304]{1,0:T(8,128)(2,1)S(1)}) custom-call(bf16[2,128,128]{2,1,0:T(8,128)(2,1)S(1)} %get-tuple-element.44.own_ref, bf16[2,128,128]{2,1,0:T(8,128)(2,1)S(1)} %collective-permute-done.9.other_ref, bf16[4,256,128]{2,1,0:T(8,128)(2,1)S(1)} %get-tuple-element.50.raised_ref, ...), custom_call_target="tpu_custom_call" | custom-call | flops 301989888 | bytes 2359296 | tf_op jit(solution)/shard_map/pallas_call | solution.py:72
  44.8 0.6 collective-permute-start.10
  45.4 0.3 collective-permute-done.11
  45.6 0.1 add_convert_fusion.1
  45.7 1.2 %collective-permute-start.12 = (bf16[64,2304]{1,0:T(8,128)(2,1)S(1)}, bf16[64,2304]{1,0:T(8,128)(2,1)S(1)}, u32[]{:S(2)}, u32[]{:S(2)}) collective-permute-start(bf16[64,2304]{1,0:T(8,128)(2,1)S(1)} %add_convert_fusion.1), channel_id=1, source_target_pairs={{0,2},{1,3},{2,0},{3,1},{4,6},{5,7},{6,4},{7,5},{8,10},{9,11},{10,... | collective-permute-start | bytes 884744 | tf_op jit(solution)/shard_map/ppermute | solution.py:23
  46.8 0.0 collective-permute-done.10
  46.8 8.0 %collective-permute-done.12 = bf16[64,2304]{1,0:T(8,128)(2,1)S(1)} collective-permute-done((bf16[64,2304]{1,0:T(8,128)(2,1)S(1)}, bf16[64,2304]{1,0:T(8,128)(2,1)S(1)}, u32[]{:S(2)}, u32[]{:S(2)}) %collective-permute-start.12) | collective-permute-done | bytes 294944 | tf_op jit(solution)/shard_map/ppermute | solution.py:23
  54.8 0.8 %add_convert_fusion = bf16[64,2304]{1,0:T(8,128)(2,1)} fusion(bf16[64,2304]{1,0:T(8,128)(2,1)S(1)} %collective-permute-done.12, f32[64,2304]{1,0:T(8,128)S(1)} %get-tuple-element.53, bf16[64,2304]{1,0:T(8,128)(2,1)S(1)} %collective-permute-done.10), kind=kLoop, calls=%fused_computation | loop fusion | flops 737280 | bytes 1474560 | tf_op jit(solution)/shard_map/convert_element_type | solution.py:553
  (2 shorter events, 0.1 us)
Async XLA Ops:
  0.0 10.2 %collective-permute-start = (bf16[64,2304]{1,0:T(8,128)(2,1)}, bf16[64,2304]{1,0:T(8,128)(2,1)S(1)}, u32[]{:S(2)}, u32[]{:S(2)}) collective-permute-start(bf16[64,2304]{1,0:T(8,128)(2,1)} %hidden_ref.1), channel_id=1, source_target_pairs={{0,2},{1,3},{2,0},{3,1},{4,6},{5,7},{6,4},{7,5},{8,10},{9,11},{10,... | collective-permute-start | bytes 884744 | tf_op jit(solution)/shard_map/ppermute | solution.py:23
  3.9 4.3 %collective-permute-start.2 = (bf16[16,2304]{1,0:T(8,128)(2,1)S(1)}, bf16[16,2304]{1,0:T(8,128)(2,1)S(1)}, u32[]{:S(2)}, u32[]{:S(2)}) collective-permute-start(bf16[16,2304]{1,0:T(8,128)(2,1)S(1)} %slice.3), channel_id=1, source_target_pairs={{3,6},{7,10},{11,14},{15,18},{19,22},{23,26},{27,30}} | collective-permute-start | bytes 221192 | tf_op jit(solution)/shard_map/ppermute | solution.py:54
  4.5 3.7 %collective-permute-start.1 = (bf16[16,2304]{1,0:T(8,128)(2,1)S(1)}, bf16[16,2304]{1,0:T(8,128)(2,1)S(1)}, u32[]{:S(2)}, u32[]{:S(2)}) collective-permute-start(bf16[16,2304]{1,0:T(8,128)(2,1)S(1)} %slice.3), channel_id=1, source_target_pairs={{3,5},{7,9},{11,13},{15,17},{19,21},{23,25},{27,29}} | collective-permute-start | bytes 221192 | tf_op jit(solution)/shard_map/ppermute | solution.py:54
  5.2 5.6 %collective-permute-start.4 = (bf16[64,2304]{1,0:T(8,128)(2,1)}, bf16[64,2304]{1,0:T(8,128)(2,1)S(1)}, u32[]{:S(2)}, u32[]{:S(2)}) collective-permute-start(bf16[64,2304]{1,0:T(8,128)(2,1)} %hidden_ref.1), channel_id=1, source_target_pairs={{0,1},{1,0},{2,3},{3,2},{4,5},{5,4},{6,7},{7,6},{8,9},{9,8},{10,11... | collective-permute-start | bytes 884744 | tf_op jit(solution)/shard_map/ppermute | solution.py:23
  10.2 1.7 %collective-permute-start.5 = (bf16[64,2304]{1,0:T(8,128)(2,1)S(1)}, bf16[64,2304]{1,0:T(8,128)(2,1)S(1)}, u32[]{:S(2)}, u32[]{:S(2)}) collective-permute-start(bf16[64,2304]{1,0:T(8,128)(2,1)S(1)} %collective-permute-done.refs_3_), channel_id=1, source_target_pairs={{0,1},{1,0},{2,3},{3,2},{4,5},{5,4},{6,7},{7,6},{8,9},{9,8},{10,11... | collective-permute-start | bytes 884744 | tf_op jit(solution)/shard_map/ppermute | solution.py:23
  10.2 1.7 %collective-permute-start.3 = (bf16[16,2304]{1,0:T(8,128)(2,1)S(1)}, bf16[16,2304]{1,0:T(8,128)(2,1)S(1)}, u32[]{:S(2)}, u32[]{:S(2)}) collective-permute-start(bf16[16,2304]{1,0:T(8,128)(2,1)S(1)} %shard_map.119.refs_0_), channel_id=1, source_target_pairs={{0,1},{1,0},{2,3},{3,2},{4,5},{5,4},{6,7},{7,6},{8,9},{9,8},{10,11... | collective-permute-start | bytes 221192 | tf_op jit(solution)/shard_map/ppermute | solution.py:23
  11.9 28.2 %copy-start.1 = (bf16[128,512]{1,0:T(8,128)(2,1)S(1)}, bf16[128,512]{1,0:T(8,128)(2,1)}, u32[]{:S(2)}) copy-start(bf16[128,512]{1,0:T(8,128)(2,1)} %up_ref.1) | copy-start | bytes 393220
  11.9 31.4 %copy-start = (bf16[512,2304]{1,0:T(8,128)(2,1)S(1)}, bf16[512,2304]{1,0:T(8,128)(2,1)}, u32[]{:S(2)}) copy-start(bf16[512,2304]{1,0:T(8,128)(2,1)} %weight_ref.3) | copy-start | bytes 7077892
  11.9 31.4 %copy-start.2 = (f32[128]{0:T(128)S(1)}, f32[128]{0:T(128)}, u32[]{:S(2)}) copy-start(f32[128]{0:T(128)} %param.22) | copy-start | bytes 1540
  21.2 5.8 %collective-permute-start.6 = (bf16[2,128,256]{2,1,0:T(8,128)(2,1)S(1)}, bf16[2,128,256]{2,1,0:T(8,128)(2,1)S(1)}, u32[]{:S(2)}, u32[]{:S(2)}) collective-permute-start(bf16[2,128,256]{2,1,0:T(8,128)(2,1)S(1)} %get-tuple-element.43), channel_id=1, source_target_pairs={{0,4},{4,0},{8,12},{12,8},{16,20},{20,16},{24,28},{28,24},{1,5},{5... | collective-permute-start | bytes 393224 | tf_op jit(solution)/shard_map/ppermute | solution.py:23
  27.2 5.9 %collective-permute-start.7 = (bf16[2,128,256]{2,1,0:T(8,128)(2,1)S(1)}, bf16[2,128,256]{2,1,0:T(8,128)(2,1)S(1)}, u32[]{:S(2)}, u32[]{:S(2)}) collective-permute-start(bf16[2,128,256]{2,1,0:T(8,128)(2,1)S(1)} %shard_map.121.own_ref), channel_id=1, source_target_pairs={{0,8},{4,12},{8,0},{12,4},{16,24},{20,28},{24,16},{28,20},{1,9},{5... | collective-permute-start | bytes 393224 | tf_op jit(solution)/shard_map/ppermute | solution.py:23
  33.4 5.2 %collective-permute-start.8 = (bf16[2,128,128]{2,1,0:T(8,128)(2,1)S(1)}, bf16[2,128,128]{2,1,0:T(8,128)(2,1)S(1)}, u32[]{:S(2)}, u32[]{:S(2)}) collective-permute-start(bf16[2,128,128]{2,1,0:T(8,128)(2,1)S(1)} %shard_map.123), channel_id=1, source_target_pairs={{0,16},{4,20},{8,24},{12,28},{16,0},{20,4},{24,8},{28,12},{1,17},{... | collective-permute-start | bytes 196616 | tf_op jit(solution)/shard_map/ppermute | solution.py:23
  38.9 4.3 %collective-permute-start.9 = (bf16[2,128,128]{2,1,0:T(8,128)(2,1)S(1)}, bf16[2,128,128]{2,1,0:T(8,128)(2,1)S(1)}, u32[]{:S(2)}, u32[]{:S(2)}) collective-permute-start(bf16[2,128,128]{2,1,0:T(8,128)(2,1)S(1)} %get-tuple-element.45), channel_id=1, source_target_pairs={{0,4},{4,0},{8,12},{12,8},{16,20},{20,16},{24,28},{28,24},{1,5},{5... | collective-permute-start | bytes 196616 | tf_op jit(solution)/shard_map/ppermute | solution.py:23
  44.0 1.6 %collective-permute-start.11 = (bf16[64,2304]{1,0:T(8,128)(2,1)S(1)}, bf16[64,2304]{1,0:T(8,128)(2,1)S(1)}, u32[]{:S(2)}, u32[]{:S(2)}) collective-permute-start(bf16[64,2304]{1,0:T(8,128)(2,1)S(1)} %get-tuple-element.56), channel_id=1, source_target_pairs={{0,1},{1,0},{2,3},{3,2},{4,5},{5,4},{6,7},{7,6},{8,9},{9,8},{10,11... | collective-permute-start | bytes 884744 | tf_op jit(solution)/shard_map/ppermute | solution.py:23
  44.8 2.0 %collective-permute-start.10 = (bf16[64,2304]{1,0:T(8,128)(2,1)S(1)}, bf16[64,2304]{1,0:T(8,128)(2,1)S(1)}, u32[]{:S(2)}, u32[]{:S(2)}) collective-permute-start(bf16[64,2304]{1,0:T(8,128)(2,1)S(1)} %get-tuple-element.54), channel_id=1, source_target_pairs={{0,1},{1,0},{2,3},{3,2},{4,5},{5,4},{6,7},{7,6},{8,9},{9,8},{10,11... | collective-permute-start | bytes 884744 | tf_op jit(solution)/shard_map/ppermute | solution.py:23
  45.7 9.1 %collective-permute-start.12 = (bf16[64,2304]{1,0:T(8,128)(2,1)S(1)}, bf16[64,2304]{1,0:T(8,128)(2,1)S(1)}, u32[]{:S(2)}, u32[]{:S(2)}) collective-permute-start(bf16[64,2304]{1,0:T(8,128)(2,1)S(1)} %add_convert_fusion.1), channel_id=1, source_target_pairs={{0,2},{1,3},{2,0},{3,1},{4,6},{5,7},{6,4},{7,5},{8,10},{9,11},{10,... | collective-permute-start | bytes 884744 | tf_op jit(solution)/shard_map/ppermute | solution.py:23

commit v8 on v7

--- a/solution.py
+++ b/solution.py
@@ -10,6 +10,7 @@
 
 RIM = 16
 BASE = 16
+GROUPS = 2
 MIB = 1024 * 1024
 f32 = jnp.float32
 bf16 = jnp.bfloat16
@@ -50,7 +51,7 @@
         for k in sorted(slabs):
             slabs[k ^ bit] = swapped(slabs[k], "head", bit)
     tail = own[own.shape[0] - RIM :]
-    targets = [first if first == heads - 2 else first + 1 for first in range(0, heads, 2)]
+    targets = [first if first == heads - 2 else first + 1 for first in range(0, heads, 2)][::-1]
     tails = [lax.ppermute(tail, ("seq", "head"), rim_route(target)) for target in targets]
     slabs[1] = swapped(own, "head", 1)
     arrived = [k for k in sorted(slabs) if k > 1]
@@ -130,7 +131,8 @@
     (one_ref, two_ref, *slab_refs), refs = refs[: slab_count + 1], refs[slab_count + 1 :]
     (own_rows_ref, weights, downs, betas), refs = refs[:4], refs[4:]
     hbm_refs, refs = refs[:5], refs[5:]
-    (own_ref, other_ref, solved_ref, attend_ref, start_ref, gate_ref), refs = refs[:6], refs[6:]
+    (own_refs, other_refs), refs = (refs[:GROUPS], refs[GROUPS : 2 * GROUPS]), refs[2 * GROUPS :]
+    (solved_ref, attend_ref, start_ref, gate_ref), refs = refs[:4], refs[4:]
     loaded, refs = refs[:5], refs[5:]
     rows_ref, projected, running_ref, parts_ref, mixing, inverse, sides, sems = refs
     rates, decay_up_ref, bias_ref, conv_ref, value_weight = loaded
@@ -162,9 +164,16 @@
     rows_ref[:RIM, :] = (one_ref[...].astype(f32) + two_ref[...].astype(f32)).astype(bf16)
     for k, ref in enumerate([own_rows_ref, *slab_refs]):
         rows_ref[rows_of(k), :] = ref[...]
+
+    def project(c, piece, weight):
+        result = dot(rows_ref[...], weight)
+        for begin in range(piece.start, piece.stop, size):
+            at = begin - piece.start
+            projected[c * heads + begin // size] = result[:, at : at + size]
+
     for c in range(2):
         for piece in pieces:
-            projected[c, :, piece] = dot(rows_ref[...], weights[c, :, piece])
+            project(c, piece, weights[c, :, piece])
     low = dot(rows_ref[RIM:, :], downs[...]).astype(bf16)
     gate_ref[...] = low[:, rank:]
     strength = jax.nn.sigmoid(dot(rows_ref[RIM:, :], betas[...], ((1,), (1,))))
@@ -188,12 +197,12 @@
     lower = jnp.where(row >= col, 1.0, 0.0).astype(bf16)
     running_ref[...] = dot(jnp.concatenate([lower, lower], axis=1), parts_ref[...])
 
-    def convolved(c, rows, lanes):
-        taps = conv_ref[c].astype(f32)
+    def convolved(c, rows, h):
+        taps = conv_ref[c].astype(f32)[:, h * size : (h + 1) * size]
         total = None
         for i in range(tap_count):
             first = RIM - tap_count + 1 + i + rows.start
-            term = projected[c, pl.ds(first, chunk), lanes] * taps[i : i + 1, lanes]
+            term = projected[c * heads + h, pl.ds(first, chunk), :] * taps[i : i + 1]
             total = term if total is None else total + term
         half = 0.5 * total
         return half + half * jnp.tanh(half)
@@ -208,11 +217,11 @@
             middle = running[chunk // 2 : chunk // 2 + 1]
             above = running - middle
             rise, entry = jnp.exp(above), jnp.exp(middle)
-            queries = convolved(0, rows, lanes)
+            queries = convolved(0, rows, h)
             power = jnp.sum(queries * queries, -1, keepdims=True)
             queries = queries * (lax.rsqrt(power + 1e-06) * size ** (-0.5)) * rise
             start_ref[h, rows, :] = (queries * entry).astype(bf16)
-            keys = convolved(1, rows, lanes)
+            keys = convolved(1, rows, h)
             power = jnp.sum(keys * keys, -1, keepdims=True)
             keys = keys * lax.rsqrt(power + 1e-06)
             key_fall = keys * strength[rows, h : h + 1] * jnp.exp(-above)
@@ -249,7 +258,7 @@
 
     for i, piece in enumerate(pieces):
         streams[i].wait()
-        projected[2, :, piece] = dot(rows_ref[...], value_weight[:, piece])
+        project(2, piece, value_weight[:, piece])
 
     at, to = row[:block, :block], col[:block, :block]
     eye = jnp.where(at == to, 1.0, 0.0).astype(bf16)
@@ -290,8 +299,7 @@
 
     for h in range(heads):
         for rows in tiles:
-            lanes = slice(h * size, (h + 1) * size)
-            sides[h, rows, size:] = convolved(2, rows, lanes).astype(bf16)
+            sides[h, rows, size:] = convolved(2, rows, h).astype(bf16)
     for d in range(blocks):
         rows = slice(d * block, (d + 1) * block)
         for h in range(heads):
@@ -310,8 +318,9 @@
     upper = place("seq", 1) == 1
     for h in range(heads // 2):
         low, high = pairs[h], pairs[heads // 2 + h]
-        own_ref[h] = jnp.where(upper, high, low).astype(bf16)
-        other_ref[h] = jnp.where(upper, low, high).astype(bf16)
+        group, at = divmod(h, own_refs[0].shape[0])
+        own_refs[group][at] = jnp.where(upper, high, low).astype(bf16)
+        other_refs[group][at] = jnp.where(upper, low, high).astype(bf16)
 
 
 def front(rims, slabs, fetched, loaded, weight, size):
@@ -324,8 +333,7 @@
     return vmem_call(
         functools.partial(front_body, slab_count),
         (
-            jax.ShapeDtypeStruct((heads // 2, size, 2 * size), bf16),
-            jax.ShapeDtypeStruct((heads // 2, size, 2 * size), bf16),
+            *[jax.ShapeDtypeStruct((heads // 2 // GROUPS, size, 2 * size), bf16)] * (2 * GROUPS),
             jax.ShapeDtypeStruct((heads, count, 2 * size), bf16),
             jax.ShapeDtypeStruct((heads, count, count), bf16),
             jax.ShapeDtypeStruct((heads, count, size), bf16),
@@ -336,7 +344,7 @@
             *buffers,
             pltpu.VMEM((width, channels), bf16),
             pltpu.VMEM((RIM + count, width), bf16),
-            pltpu.VMEM((3, RIM + count, channels), f32),
+            pltpu.VMEM((3 * heads, RIM + count, size), f32),
             pltpu.VMEM((count, channels), f32),
             pltpu.VMEM((2 * count, channels), bf16),
             pltpu.VMEM((heads, count, count), bf16),
@@ -458,20 +466,21 @@
     return keep, swapped(send, "seq", 1)
 
 
-def back_body(
-    places, own_ref, other_ref, raised_ref, output_ref, gate_ref, gain_ref, weight_ref, keep_ref,
-    *rest,
-):
+def back_body(places, *refs):
+    own_refs, other_refs, refs = refs[:GROUPS], refs[GROUPS : 2 * GROUPS], refs[2 * GROUPS :]
+    raised_ref, output_ref, gate_ref, gain_ref, weight_ref, keep_ref, *rest = refs
     normed = rest[-1]
     size = gain_ref.shape[1]
     slab_rows = keep_ref.shape[0]
-    half = own_ref.shape[0]
+    share = own_refs[0].shape[0]
+    half = GROUPS * share
     upper = place("seq", 1) == 1
     for k, away in enumerate(places):
         rows = pl.ds(pl.multiple_of((place("head") ^ away) * slab_rows, 16), slab_rows)
         for h in range(raised_ref.shape[0]):
             lanes = slice(h * size, (h + 1) * size)
-            own, other = own_ref[h % half], other_ref[h % half]
+            group, at = divmod(h % half, share)
+            own, other = own_refs[group][at], other_refs[group][at]
             state = jnp.where(upper, other, own) if h < half else jnp.where(upper, own, other)
             attended = dot(raised_ref[h, rows, :], state) + output_ref[rows, lanes]
             power = jnp.sum(attended * attended, -1, keepdims=True) * (1.0 / size)
@@ -520,7 +529,7 @@
     weight = qkv_weight.transpose(1, 0, 2)
     fetched = load(hidden_in, decay_down, gate_down, beta_weight.T, weight)
     slabs, rims, fetched = gathered(hidden_in, fetched)
-    own, other, solved, attend, start, gate_low = front(
+    *pairs, solved, attend, start, gate_low = front(
         rims, slabs, fetched, (decay_log, decay_up, dt_bias[None], conv_weight), weight, size
     )
     count = start.shape[1]
@@ -536,7 +545,8 @@
         flops=2 * heads * count * count * 2 * size,
         moved=4 * heads * count * count,
     )
-    states = entry_states(own, other)
+    states = [entry_states(*both) for both in zip(pairs[:GROUPS], pairs[GROUPS:])]
+    states = [own for own, _ in states] + [other for _, other in states]
     slab_rows = count // devices
     sums = {}
     for g in reversed(range(max(devices // 2, 1))):

time: 55.8 us -> 54.9 us (0.984)
  waiting for transfers between devices: 23.5 us -> 19.5 us
  starting transfers between devices: 15.4 us -> 19.1 us
  Pallas kernels: 14.8 us -> 14.2 us
    ppermute x11 -> x15, waiting for transfers between devices: 23.5 us -> 19.5 us  [swapped(): lax.ppermute(block, axis, [(i, i ^ bit) for i in range(lax.axis_size(axis...]
    ppermute x11 -> x15, starting transfers between devices: 14 us -> 17.8 us  [swapped(): lax.ppermute(block, axis, [(i, i ^ bit) for i in range(lax.axis_size(axis...]
    pallas_call x10 -> x14, Pallas kernels: 14.8 us -> 14.2 us  [vmem_call(): pl.pallas_call(body, out_shape=out_shape, in_specs=[pl.BlockSpec(memory_s...]
  transfers between devices with their start and end apart: 13 -> 17, of which waited for: 8 -> 9; matrix products, arithmetic and copies ran while one was open for 2% -> 2% of each run, Pallas kernels for 7% -> 10%
where the time goes in v8:
time: 54.9 us; the launch traced here: 54.7 us
  waiting for transfers between devices  19.5 us (36%)
  starting transfers between devices  19.1 us (35%)
  Pallas kernels  14.2 us (26%)
  local copies, waits for them, and re-layouts  0.93 us (2%)
  other arithmetic  0.85 us (2%)
    ppermute x15, waiting for transfers between devices, swapped(): lax.ppermute(block, axis, [(i, i ^ bit) for i in range(lax.axis_size(axis...  19.5 us
    ppermute x15, starting transfers between devices, swapped(): lax.ppermute(block, axis, [(i, i ^ bit) for i in range(lax.axis_size(axis...  17.8 us
    pallas_call x14, Pallas kernels, vmem_call(): pl.pallas_call(body, out_shape=out_shape, in_specs=[pl.BlockSpec(memory_s...  14.2 us
    ppermute x2, starting transfers between devices, gathered(): lax.ppermute(tail, ('seq', 'head'), rim_route(target))  1.32 us
  transfers between devices with their start and end apart: 17, of which 9 were waited for; matrix products, arithmetic and copies ran while one was open for 2% of the time, Pallas kernels for 10%

profile of v8, /device:TPU:0, one launch (start us, length us, event | category | flops | bytes accessed | tf_op | source)
XLA Modules:
  0.0 54.7 jit_solution(5484245364981149797)
XLA Ops:
  0.0 2.9 %collective-permute-start = (bf16[64,2304]{1,0:T(8,128)(2,1)}, bf16[64,2304]{1,0:T(8,128)(2,1)S(1)}, u32[]{:S(2)}, u32[]{:S(2)}) collective-permute-start(bf16[64,2304]{1,0:T(8,128)(2,1)} %hidden_ref.1), channel_id=1, source_target_pairs={{0,2},{1,3},{2,0},{3,1},{4,6},{5,7},{6,4},{7,5},{8,10},{9,11},{10,... | collective-permute-start | bytes 884744 | tf_op jit(solution)/shard_map/ppermute | solution.py:24
  2.9 0.9 %slice.3 = bf16[16,2304]{1,0:T(8,128)(2,1)S(1)} slice(bf16[64,2304]{1,0:T(8,128)(2,1)} %hidden_ref.1), slice={[48:64], [0:2304]} | slice | bytes 147456 | tf_op jit(solution)/shard_map/slice | solution.py:53
  3.9 0.7 %collective-permute-start.2 = (bf16[16,2304]{1,0:T(8,128)(2,1)S(1)}, bf16[16,2304]{1,0:T(8,128)(2,1)S(1)}, u32[]{:S(2)}, u32[]{:S(2)}) collective-permute-start(bf16[16,2304]{1,0:T(8,128)(2,1)S(1)} %slice.3), channel_id=1, source_target_pairs={{3,5},{7,9},{11,13},{15,17},{19,21},{23,25},{27,29}} | collective-permute-start | bytes 221192 | tf_op jit(solution)/shard_map/ppermute | solution.py:55
  4.5 0.7 %collective-permute-start.1 = (bf16[16,2304]{1,0:T(8,128)(2,1)S(1)}, bf16[16,2304]{1,0:T(8,128)(2,1)S(1)}, u32[]{:S(2)}, u32[]{:S(2)}) collective-permute-start(bf16[16,2304]{1,0:T(8,128)(2,1)S(1)} %slice.3), channel_id=1, source_target_pairs={{3,6},{7,10},{11,14},{15,18},{19,22},{23,26},{27,30}} | collective-permute-start | bytes 221192 | tf_op jit(solution)/shard_map/ppermute | solution.py:55
  5.2 0.1 collective-permute-start.4
  5.3 2.9 %shard_map.118 = (bf16[64,2304]{1,0:T(8,128)(2,1)S(1)}, bf16[2,2304,512]{2,1,0:T(8,128)(2,1)S(1)}, bf16[2304,256]{1,0:T(8,128)(2,1)S(1)}, bf16[4,2304]{1,0:T(4,128)(2,1)S(1)}) custom-call(bf16[64,2304]{1,0:T(8,128)(2,1)} %hidden_ref.1, bf16[2304,128]{1,0:T(8,128)(2,1)} %decay_down_ref.1, bf16[2304,128]{1,0:T(8,128)(2,1)} %gate_down_ref.1, ...), custom_call_target="tpu_custom_call" | custom-call | tf_op jit(solution)/shard_map/pallas_call | solution.py:73
  8.2 0.0 collective-permute-done.2.refs_1_
  8.2 0.0 collective-permute-done.1.refs_0_
  8.2 2.7 %collective-permute-done.refs_3_ = bf16[64,2304]{1,0:T(8,128)(2,1)S(1)} collective-permute-done((bf16[64,2304]{1,0:T(8,128)(2,1)}, bf16[64,2304]{1,0:T(8,128)(2,1)S(1)}, u32[]{:S(2)}, u32[]{:S(2)}) %collective-permute-start) | collective-permute-done | bytes 294944 | tf_op jit(solution)/shard_map/ppermute | solution.py:24
  10.9 0.0 collective-permute-start.5
  11.0 0.6 %collective-permute-start.3 = (bf16[16,2304]{1,0:T(8,128)(2,1)S(1)}, bf16[16,2304]{1,0:T(8,128)(2,1)S(1)}, u32[]{:S(2)}, u32[]{:S(2)}) collective-permute-start(bf16[16,2304]{1,0:T(8,128)(2,1)S(1)} %shard_map.119.refs_0_), channel_id=1, source_target_pairs={{0,1},{1,0},{2,3},{3,2},{4,5},{5,4},{6,7},{7,6},{8,9},{9,8},{10,11... | collective-permute-start | bytes 221192 | tf_op jit(solution)/shard_map/ppermute | solution.py:24
  11.6 0.0 collective-permute-done.4.refs_2_
  11.6 1.1 %collective-permute-done.3.refs_1_ = bf16[16,2304]{1,0:T(8,128)(2,1)S(1)} collective-permute-done((bf16[16,2304]{1,0:T(8,128)(2,1)S(1)}, bf16[16,2304]{1,0:T(8,128)(2,1)S(1)}, u32[]{:S(2)}, u32[]{:S(2)}) %collective-permute-start.3) | collective-permute-done | bytes 73760 | tf_op jit(solution)/shard_map/ppermute | solution.py:24
  12.6 0.0 collective-permute-done.5.refs_4_
  12.6 0.0 copy-start.1
  12.6 0.0 copy-start
  12.6 0.0 copy-start.2
  12.6 8.1 %shard_map.120 = (bf16[1,128,256]{2,1,0:T(8,128)(2,1)S(1)}, bf16[1,128,256]{2,1,0:T(8,128)(2,1)S(1)}, bf16[1,128,256]{2,1,0:T(8,128)(2,1)S(1)}, bf16[1,128,256]{...) custom-call(bf16[16,2304]{1,0:T(8,128)(2,1)S(1)} %shard_map.119.refs, ...), custom_call_target="tpu_custom_call" | custom-call | flops 2415919104 | bytes 9437184 | tf_op jit(solution)/shard_map/pallas_call | solution.py:73
  20.8 1.0 %collective-permute-start.6 = (bf16[1,128,256]{2,1,0:T(8,128)(2,1)S(1)}, bf16[1,128,256]{2,1,0:T(8,128)(2,1)S(1)}, u32[]{:S(2)}, u32[]{:S(2)}) collective-permute-start(bf16[1,128,256]{2,1,0:T(8,128)(2,1)S(1)} %get-tuple-element.47), channel_id=1, source_target_pairs={{0,4},{4,0},{8,12},{12,8},{16,20},{20,16},{24,28},{28,24},{1,5},{5... | collective-permute-start | bytes 196616 | tf_op jit(solution)/shard_map/ppermute | solution.py:24
  21.8 1.0 %collective-permute-start.9 = (bf16[1,128,256]{2,1,0:T(8,128)(2,1)S(1)}, bf16[1,128,256]{2,1,0:T(8,128)(2,1)S(1)}, u32[]{:S(2)}, u32[]{:S(2)}) collective-permute-start(bf16[1,128,256]{2,1,0:T(8,128)(2,1)S(1)} %get-tuple-element.50), channel_id=1, source_target_pairs={{0,4},{4,0},{8,12},{12,8},{16,20},{20,16},{24,28},{28,24},{1,5},{5... | collective-permute-start | bytes 196616 | tf_op jit(solution)/shard_map/ppermute | solution.py:24
  22.9 2.9 %collective-permute-done.6.far_ref.partner_ref = bf16[1,128,256]{2,1,0:T(8,128)(2,1)S(1)} collective-permute-done((bf16[1,128,256]{2,1,0:T(8,128)(2,1)S(1)}, bf16[1,128,256]{2,1,0:T(8,128)(2,1)S(1)}, u32[]{:S(2)}, u32[]{:S(2)}) %collective-permute-start.6) | collective-permute-done | bytes 65568 | tf_op jit(solution)/shard_map/ppermute | solution.py:24
  25.8 0.2 shard_map.121.own_ref
  26.0 1.5 %collective-permute-start.7 = (bf16[1,128,256]{2,1,0:T(8,128)(2,1)S(1)}, bf16[1,128,256]{2,1,0:T(8,128)(2,1)S(1)}, u32[]{:S(2)}, u32[]{:S(2)}) collective-permute-start(bf16[1,128,256]{2,1,0:T(8,128)(2,1)S(1)} %shard_map.121.own_ref), channel_id=1, source_target_pairs={{0,8},{4,12},{8,0},{12,4},{16,24},{20,28},{24,16},{28,20},{1,9},{5... | collective-permute-start | bytes 196616 | tf_op jit(solution)/shard_map/ppermute | solution.py:24
  27.5 0.0 collective-permute-done.9.far_ref.partner_ref
  27.5 0.2 shard_map.125.own_ref
  27.7 1.0 %collective-permute-start.10 = (bf16[1,128,256]{2,1,0:T(8,128)(2,1)S(1)}, bf16[1,128,256]{2,1,0:T(8,128)(2,1)S(1)}, u32[]{:S(2)}, u32[]{:S(2)}) collective-permute-start(bf16[1,128,256]{2,1,0:T(8,128)(2,1)S(1)} %shard_map.125.own_ref), channel_id=1, source_target_pairs={{0,8},{4,12},{8,0},{12,4},{16,24},{20,28},{24,16},{28,20},{1,9},{5... | collective-permute-start | bytes 196616 | tf_op jit(solution)/shard_map/ppermute | solution.py:24
  28.7 1.6 %collective-permute-done.7.far_ref = bf16[1,128,256]{2,1,0:T(8,128)(2,1)S(1)} collective-permute-done((bf16[1,128,256]{2,1,0:T(8,128)(2,1)S(1)}, bf16[1,128,256]{2,1,0:T(8,128)(2,1)S(1)}, u32[]{:S(2)}, u32[]{:S(2)}) %collective-permute-start.7) | collective-permute-done | bytes 65568 | tf_op jit(solution)/shard_map/ppermute | solution.py:24
  30.3 0.1 shard_map.123
  30.5 2.5 %collective-permute-start.8 = (bf16[1,128,128]{2,1,0:T(8,128)(2,1)S(1)}, bf16[1,128,128]{2,1,0:T(8,128)(2,1)S(1)}, u32[]{:S(2)}, u32[]{:S(2)}) collective-permute-start(bf16[1,128,128]{2,1,0:T(8,128)(2,1)S(1)} %shard_map.123), channel_id=1, source_target_pairs={{0,16},{4,20},{8,24},{12,28},{16,0},{20,4},{24,8},{28,12},{1,17},{... | collective-permute-start | bytes 98312 | tf_op jit(solution)/shard_map/ppermute | solution.py:24
  33.0 0.0 collective-permute-done.10.far_ref
  33.0 0.2 shard_map.127
  33.2 1.6 %collective-permute-start.11 = (bf16[1,128,128]{2,1,0:T(8,128)(2,1)S(1)}, bf16[1,128,128]{2,1,0:T(8,128)(2,1)S(1)}, u32[]{:S(2)}, u32[]{:S(2)}) collective-permute-start(bf16[1,128,128]{2,1,0:T(8,128)(2,1)S(1)} %shard_map.127), channel_id=1, source_target_pairs={{0,16},{4,20},{8,24},{12,28},{16,0},{20,4},{24,8},{28,12},{1,17},{... | collective-permute-start | bytes 98312 | tf_op jit(solution)/shard_map/ppermute | solution.py:24
  34.9 0.8 %collective-permute-done.8.far_ref = bf16[1,128,128]{2,1,0:T(8,128)(2,1)S(1)} collective-permute-done((bf16[1,128,128]{2,1,0:T(8,128)(2,1)S(1)}, bf16[1,128,128]{2,1,0:T(8,128)(2,1)S(1)}, u32[]{:S(2)}, u32[]{:S(2)}) %collective-permute-start.8) | collective-permute-done | bytes 32800 | tf_op jit(solution)/shard_map/ppermute | solution.py:24
  35.7 0.3 shard_map.124
  36.0 1.5 %collective-permute-start.12 = (bf16[1,128,128]{2,1,0:T(8,128)(2,1)S(1)}, bf16[1,128,128]{2,1,0:T(8,128)(2,1)S(1)}, u32[]{:S(2)}, u32[]{:S(2)}) collective-permute-start(bf16[1,128,128]{2,1,0:T(8,128)(2,1)S(1)} %get-tuple-element.52), channel_id=1, source_target_pairs={{0,4},{4,0},{8,12},{12,8},{16,20},{20,16},{24,28},{28,24},{1,5},{5... | collective-permute-start | bytes 98312 | tf_op jit(solution)/shard_map/ppermute | solution.py:24
  37.5 0.5 %collective-permute-done.11.far_ref = bf16[1,128,128]{2,1,0:T(8,128)(2,1)S(1)} collective-permute-done((bf16[1,128,128]{2,1,0:T(8,128)(2,1)S(1)}, bf16[1,128,128]{2,1,0:T(8,128)(2,1)S(1)}, u32[]{:S(2)}, u32[]{:S(2)}) %collective-permute-start.11) | collective-permute-done | bytes 32800 | tf_op jit(solution)/shard_map/ppermute | solution.py:24
  38.1 0.3 shard_map.128
  38.3 2.0 %collective-permute-start.13 = (bf16[1,128,128]{2,1,0:T(8,128)(2,1)S(1)}, bf16[1,128,128]{2,1,0:T(8,128)(2,1)S(1)}, u32[]{:S(2)}, u32[]{:S(2)}) collective-permute-start(bf16[1,128,128]{2,1,0:T(8,128)(2,1)S(1)} %get-tuple-element.53), channel_id=1, source_target_pairs={{0,4},{4,0},{8,12},{12,8},{16,20},{20,16},{24,28},{28,24},{1,5},{5... | collective-permute-start | bytes 98312 | tf_op jit(solution)/shard_map/ppermute | solution.py:24
  40.3 0.0 copy-done.1
  40.3 0.4 shard_map.129
  40.7 0.0 collective-permute-done.12.refs_2_
  40.7 1.6 %collective-permute-done.13.refs_3_ = bf16[1,128,128]{2,1,0:T(8,128)(2,1)S(1)} collective-permute-done((bf16[1,128,128]{2,1,0:T(8,128)(2,1)S(1)}, bf16[1,128,128]{2,1,0:T(8,128)(2,1)S(1)}, u32[]{:S(2)}, u32[]{:S(2)}) %collective-permute-start.13) | collective-permute-done | bytes 32800 | tf_op jit(solution)/shard_map/ppermute | solution.py:24
  42.3 0.0 copy-done
  42.3 0.0 copy-done.2
  42.3 0.7 %shard_map.131 = (f32[64,2304]{1,0:T(8,128)S(1)}, bf16[64,2304]{1,0:T(8,128)(2,1)S(1)}) custom-call(bf16[1,128,128]{2,1,0:T(8,128)(2,1)S(1)} %get-tuple-element.48.refs_0_, bf16[1,128,128]{2,1,0:T(8,128)(2,1)S(1)} %get-tuple-element.51.refs_1_, bf16[1,128,128]{2,1,0:T(8,128)(2,1)S(1)} %collective-permute-done.12.refs_2_, ...), custom_call_target="tpu_custom_call" | custom-call | flops 301989888 | bytes 2359296 | tf_op jit(solution)/shard_map/pallas_call | solution.py:73
  43.1 0.1 collective-permute-start.15
  43.2 0.7 %shard_map.130 = (f32[64,2304]{1,0:T(8,128)S(1)}, bf16[64,2304]{1,0:T(8,128)(2,1)S(1)}) custom-call(bf16[1,128,128]{2,1,0:T(8,128)(2,1)S(1)} %get-tuple-element.48.refs_0_, bf16[1,128,128]{2,1,0:T(8,128)(2,1)S(1)} %get-tuple-element.51.refs_1_, bf16[1,128,128]{2,1,0:T(8,128)(2,1)S(1)} %collective-permute-done.12.refs_2_, ...), custom_call_target="tpu_custom_call" | custom-call | flops 301989888 | bytes 2359296 | tf_op jit(solution)/shard_map/pallas_call | solution.py:73
  43.9 0.5 %collective-permute-start.14 = (bf16[64,2304]{1,0:T(8,128)(2,1)S(1)}, bf16[64,2304]{1,0:T(8,128)(2,1)S(1)}, u32[]{:S(2)}, u32[]{:S(2)}) collective-permute-start(bf16[64,2304]{1,0:T(8,128)(2,1)S(1)} %get-tuple-element.62), channel_id=1, source_target_pairs={{0,1},{1,0},{2,3},{3,2},{4,5},{5,4},{6,7},{7,6},{8,9},{9,8},{10,11... | collective-permute-start | bytes 884744 | tf_op jit(solution)/shard_map/ppermute | solution.py:24
  44.5 0.3 collective-permute-done.15
  44.7 0.1 add_convert_fusion.1
  44.8 1.3 %collective-permute-start.16 = (bf16[64,2304]{1,0:T(8,128)(2,1)S(1)}, bf16[64,2304]{1,0:T(8,128)(2,1)S(1)}, u32[]{:S(2)}, u32[]{:S(2)}) collective-permute-start(bf16[64,2304]{1,0:T(8,128)(2,1)S(1)} %add_convert_fusion.1), channel_id=1, source_target_pairs={{0,2},{1,3},{2,0},{3,1},{4,6},{5,7},{6,4},{7,5},{8,10},{9,11},{10,... | collective-permute-start | bytes 884744 | tf_op jit(solution)/shard_map/ppermute | solution.py:24
  46.1 0.0 collective-permute-done.14
  46.1 7.8 %collective-permute-done.16 = bf16[64,2304]{1,0:T(8,128)(2,1)S(1)} collective-permute-done((bf16[64,2304]{1,0:T(8,128)(2,1)S(1)}, bf16[64,2304]{1,0:T(8,128)(2,1)S(1)}, u32[]{:S(2)}, u32[]{:S(2)}) %collective-permute-start.16) | collective-permute-done | bytes 294944 | tf_op jit(solution)/shard_map/ppermute | solution.py:24
  53.9 0.8 %add_convert_fusion = bf16[64,2304]{1,0:T(8,128)(2,1)} fusion(bf16[64,2304]{1,0:T(8,128)(2,1)S(1)} %collective-permute-done.16, f32[64,2304]{1,0:T(8,128)S(1)} %get-tuple-element.61, bf16[64,2304]{1,0:T(8,128)(2,1)S(1)} %collective-permute-done.14), kind=kLoop, calls=%fused_computation | loop fusion | flops 737280 | bytes 1474560 | tf_op jit(solution)/shard_map/convert_element_type | solution.py:563
  (3 shorter events, 0.1 us)
Async XLA Ops:
  0.0 10.9 %collective-permute-start = (bf16[64,2304]{1,0:T(8,128)(2,1)}, bf16[64,2304]{1,0:T(8,128)(2,1)S(1)}, u32[]{:S(2)}, u32[]{:S(2)}) collective-permute-start(bf16[64,2304]{1,0:T(8,128)(2,1)} %hidden_ref.1), channel_id=1, source_target_pairs={{0,2},{1,3},{2,0},{3,1},{4,6},{5,7},{6,4},{7,5},{8,10},{9,11},{10,... | collective-permute-start | bytes 884744 | tf_op jit(solution)/shard_map/ppermute | solution.py:24
  3.9 4.3 %collective-permute-start.2 = (bf16[16,2304]{1,0:T(8,128)(2,1)S(1)}, bf16[16,2304]{1,0:T(8,128)(2,1)S(1)}, u32[]{:S(2)}, u32[]{:S(2)}) collective-permute-start(bf16[16,2304]{1,0:T(8,128)(2,1)S(1)} %slice.3), channel_id=1, source_target_pairs={{3,5},{7,9},{11,13},{15,17},{19,21},{23,25},{27,29}} | collective-permute-start | bytes 221192 | tf_op jit(solution)/shard_map/ppermute | solution.py:55
  4.5 3.7 %collective-permute-start.1 = (bf16[16,2304]{1,0:T(8,128)(2,1)S(1)}, bf16[16,2304]{1,0:T(8,128)(2,1)S(1)}, u32[]{:S(2)}, u32[]{:S(2)}) collective-permute-start(bf16[16,2304]{1,0:T(8,128)(2,1)S(1)} %slice.3), channel_id=1, source_target_pairs={{3,6},{7,10},{11,14},{15,18},{19,22},{23,26},{27,30}} | collective-permute-start | bytes 221192 | tf_op jit(solution)/shard_map/ppermute | solution.py:55
  5.2 6.4 %collective-permute-start.4 = (bf16[64,2304]{1,0:T(8,128)(2,1)}, bf16[64,2304]{1,0:T(8,128)(2,1)S(1)}, u32[]{:S(2)}, u32[]{:S(2)}) collective-permute-start(bf16[64,2304]{1,0:T(8,128)(2,1)} %hidden_ref.1), channel_id=1, source_target_pairs={{0,1},{1,0},{2,3},{3,2},{4,5},{5,4},{6,7},{7,6},{8,9},{9,8},{10,11... | collective-permute-start | bytes 884744 | tf_op jit(solution)/shard_map/ppermute | solution.py:24
  10.9 1.7 %collective-permute-start.5 = (bf16[64,2304]{1,0:T(8,128)(2,1)S(1)}, bf16[64,2304]{1,0:T(8,128)(2,1)S(1)}, u32[]{:S(2)}, u32[]{:S(2)}) collective-permute-start(bf16[64,2304]{1,0:T(8,128)(2,1)S(1)} %collective-permute-done.refs_3_), channel_id=1, source_target_pairs={{0,1},{1,0},{2,3},{3,2},{4,5},{5,4},{6,7},{7,6},{8,9},{9,8},{10,11... | collective-permute-start | bytes 884744 | tf_op jit(solution)/shard_map/ppermute | solution.py:24
  11.0 1.7 %collective-permute-start.3 = (bf16[16,2304]{1,0:T(8,128)(2,1)S(1)}, bf16[16,2304]{1,0:T(8,128)(2,1)S(1)}, u32[]{:S(2)}, u32[]{:S(2)}) collective-permute-start(bf16[16,2304]{1,0:T(8,128)(2,1)S(1)} %shard_map.119.refs_0_), channel_id=1, source_target_pairs={{0,1},{1,0},{2,3},{3,2},{4,5},{5,4},{6,7},{7,6},{8,9},{9,8},{10,11... | collective-permute-start | bytes 221192 | tf_op jit(solution)/shard_map/ppermute | solution.py:24
  12.6 27.7 %copy-start.1 = (bf16[128,512]{1,0:T(8,128)(2,1)S(1)}, bf16[128,512]{1,0:T(8,128)(2,1)}, u32[]{:S(2)}) copy-start(bf16[128,512]{1,0:T(8,128)(2,1)} %up_ref.1) | copy-start | bytes 393220
  12.6 29.7 %copy-start = (bf16[512,2304]{1,0:T(8,128)(2,1)S(1)}, bf16[512,2304]{1,0:T(8,128)(2,1)}, u32[]{:S(2)}) copy-start(bf16[512,2304]{1,0:T(8,128)(2,1)} %refs_8_.3) | copy-start | bytes 7077892
  12.6 29.7 %copy-start.2 = (f32[128]{0:T(128)S(1)}, f32[128]{0:T(128)}, u32[]{:S(2)}) copy-start(f32[128]{0:T(128)} %param.22) | copy-start | bytes 1540
  20.8 5.0 %collective-permute-start.6 = (bf16[1,128,256]{2,1,0:T(8,128)(2,1)S(1)}, bf16[1,128,256]{2,1,0:T(8,128)(2,1)S(1)}, u32[]{:S(2)}, u32[]{:S(2)}) collective-permute-start(bf16[1,128,256]{2,1,0:T(8,128)(2,1)S(1)} %get-tuple-element.47), channel_id=1, source_target_pairs={{0,4},{4,0},{8,12},{12,8},{16,20},{20,16},{24,28},{28,24},{1,5},{5... | collective-permute-start | bytes 196616 | tf_op jit(solution)/shard_map/ppermute | solution.py:24
  21.8 5.7 %collective-permute-start.9 = (bf16[1,128,256]{2,1,0:T(8,128)(2,1)S(1)}, bf16[1,128,256]{2,1,0:T(8,128)(2,1)S(1)}, u32[]{:S(2)}, u32[]{:S(2)}) collective-permute-start(bf16[1,128,256]{2,1,0:T(8,128)(2,1)S(1)} %get-tuple-element.50), channel_id=1, source_target_pairs={{0,4},{4,0},{8,12},{12,8},{16,20},{20,16},{24,28},{28,24},{1,5},{5... | collective-permute-start | bytes 196616 | tf_op jit(solution)/shard_map/ppermute | solution.py:24
  26.0 4.3 %collective-permute-start.7 = (bf16[1,128,256]{2,1,0:T(8,128)(2,1)S(1)}, bf16[1,128,256]{2,1,0:T(8,128)(2,1)S(1)}, u32[]{:S(2)}, u32[]{:S(2)}) collective-permute-start(bf16[1,128,256]{2,1,0:T(8,128)(2,1)S(1)} %shard_map.121.own_ref), channel_id=1, source_target_pairs={{0,8},{4,12},{8,0},{12,4},{16,24},{20,28},{24,16},{28,20},{1,9},{5... | collective-permute-start | bytes 196616 | tf_op jit(solution)/shard_map/ppermute | solution.py:24
  27.7 5.3 %collective-permute-start.10 = (bf16[1,128,256]{2,1,0:T(8,128)(2,1)S(1)}, bf16[1,128,256]{2,1,0:T(8,128)(2,1)S(1)}, u32[]{:S(2)}, u32[]{:S(2)}) collective-permute-start(bf16[1,128,256]{2,1,0:T(8,128)(2,1)S(1)} %shard_map.125.own_ref), channel_id=1, source_target_pairs={{0,8},{4,12},{8,0},{12,4},{16,24},{20,28},{24,16},{28,20},{1,9},{5... | collective-permute-start | bytes 196616 | tf_op jit(solution)/shard_map/ppermute | solution.py:24
  30.5 5.2 %collective-permute-start.8 = (bf16[1,128,128]{2,1,0:T(8,128)(2,1)S(1)}, bf16[1,128,128]{2,1,0:T(8,128)(2,1)S(1)}, u32[]{:S(2)}, u32[]{:S(2)}) collective-permute-start(bf16[1,128,128]{2,1,0:T(8,128)(2,1)S(1)} %shard_map.123), channel_id=1, source_target_pairs={{0,16},{4,20},{8,24},{12,28},{16,0},{20,4},{24,8},{28,12},{1,17},{... | collective-permute-start | bytes 98312 | tf_op jit(solution)/shard_map/ppermute | solution.py:24
  33.2 4.9 %collective-permute-start.11 = (bf16[1,128,128]{2,1,0:T(8,128)(2,1)S(1)}, bf16[1,128,128]{2,1,0:T(8,128)(2,1)S(1)}, u32[]{:S(2)}, u32[]{:S(2)}) collective-permute-start(bf16[1,128,128]{2,1,0:T(8,128)(2,1)S(1)} %shard_map.127), channel_id=1, source_target_pairs={{0,16},{4,20},{8,24},{12,28},{16,0},{20,4},{24,8},{28,12},{1,17},{... | collective-permute-start | bytes 98312 | tf_op jit(solution)/shard_map/ppermute | solution.py:24
  36.0 4.7 %collective-permute-start.12 = (bf16[1,128,128]{2,1,0:T(8,128)(2,1)S(1)}, bf16[1,128,128]{2,1,0:T(8,128)(2,1)S(1)}, u32[]{:S(2)}, u32[]{:S(2)}) collective-permute-start(bf16[1,128,128]{2,1,0:T(8,128)(2,1)S(1)} %get-tuple-element.52), channel_id=1, source_target_pairs={{0,4},{4,0},{8,12},{12,8},{16,20},{20,16},{24,28},{28,24},{1,5},{5... | collective-permute-start | bytes 98312 | tf_op jit(solution)/shard_map/ppermute | solution.py:24
  38.3 4.0 %collective-permute-start.13 = (bf16[1,128,128]{2,1,0:T(8,128)(2,1)S(1)}, bf16[1,128,128]{2,1,0:T(8,128)(2,1)S(1)}, u32[]{:S(2)}, u32[]{:S(2)}) collective-permute-start(bf16[1,128,128]{2,1,0:T(8,128)(2,1)S(1)} %get-tuple-element.53), channel_id=1, source_target_pairs={{0,4},{4,0},{8,12},{12,8},{16,20},{20,16},{24,28},{28,24},{1,5},{5... | collective-permute-start | bytes 98312 | tf_op jit(solution)/shard_map/ppermute | solution.py:24
  43.1 1.6 %collective-permute-start.15 = (bf16[64,2304]{1,0:T(8,128)(2,1)S(1)}, bf16[64,2304]{1,0:T(8,128)(2,1)S(1)}, u32[]{:S(2)}, u32[]{:S(2)}) collective-permute-start(bf16[64,2304]{1,0:T(8,128)(2,1)S(1)} %get-tuple-element.64), channel_id=1, source_target_pairs={{0,1},{1,0},{2,3},{3,2},{4,5},{5,4},{6,7},{7,6},{8,9},{9,8},{10,11... | collective-permute-start | bytes 884744 | tf_op jit(solution)/shard_map/ppermute | solution.py:24
  43.9 2.1 %collective-permute-start.14 = (bf16[64,2304]{1,0:T(8,128)(2,1)S(1)}, bf16[64,2304]{1,0:T(8,128)(2,1)S(1)}, u32[]{:S(2)}, u32[]{:S(2)}) collective-permute-start(bf16[64,2304]{1,0:T(8,128)(2,1)S(1)} %get-tuple-element.62), channel_id=1, source_target_pairs={{0,1},{1,0},{2,3},{3,2},{4,5},{5,4},{6,7},{7,6},{8,9},{9,8},{10,11... | collective-permute-start | bytes 884744 | tf_op jit(solution)/shard_map/ppermute | solution.py:24
  44.8 9.1 %collective-permute-start.16 = (bf16[64,2304]{1,0:T(8,128)(2,1)S(1)}, bf16[64,2304]{1,0:T(8,128)(2,1)S(1)}, u32[]{:S(2)}, u32[]{:S(2)}) collective-permute-start(bf16[64,2304]{1,0:T(8,128)(2,1)S(1)} %add_convert_fusion.1), channel_id=1, source_target_pairs={{0,2},{1,3},{2,0},{3,1},{4,6},{5,7},{6,4},{7,5},{8,10},{9,11},{10,... | collective-permute-start | bytes 884744 | tf_op jit(solution)/shard_map/ppermute | solution.py:24

commit v9 on v8

--- a/solution.py
+++ b/solution.py
@@ -206,6 +206,10 @@
             total = term if total is None else total + term
         half = 0.5 * total
         return half + half * jnp.tanh(half)
+
+    for i, piece in enumerate(pieces):
+        streams[i].wait()
+        project(2, piece, value_weight[:, piece])
 
     stops = []
     for h in range(heads):
@@ -256,10 +260,6 @@
                 at >= to, scores[chunk:, inside], 0.0
             ).astype(bf16)
 
-    for i, piece in enumerate(pieces):
-        streams[i].wait()
-        project(2, piece, value_weight[:, piece])
-
     at, to = row[:block, :block], col[:block, :block]
     eye = jnp.where(at == to, 1.0, 0.0).astype(bf16)
     base = math.gcd(block, BASE)
@@ -554,7 +554,8 @@
         keep, *send = back(
             places, states, raised, output_rows, out_gate, norm_gain[None], out_weight, slab_rows
         )
-        sums[g] = [keep] + [swapped(part, "head", 1).astype(f32) for part in send]
+        near = [swapped(part, "head", 1).astype(f32) for part in send]
+        sums[g] = [lax.optimization_barrier(sum([keep] + near))]
     for bit in bits_of(devices)[1:]:
         for g in sorted(sums):
             if 2 * g & bit:

time: 54.9 us -> 54.6 us (level)
  no operation moved by 1% of the time
where the time goes in v9:
time: 54.6 us; the launch traced here: 54.4 us
  waiting for transfers between devices  19.5 us (36%)
  starting transfers between devices  19.1 us (35%)
  Pallas kernels  13.9 us (25%)
  local copies, waits for them, and re-layouts  0.93 us (2%)
  other arithmetic  0.86 us (2%)
    ppermute x15, waiting for transfers between devices, swapped(): lax.ppermute(block, axis, [(i, i ^ bit) for i in range(lax.axis_size(axis...  19.5 us
    ppermute x15, starting transfers between devices, swapped(): lax.ppermute(block, axis, [(i, i ^ bit) for i in range(lax.axis_size(axis...  17.7 us
    pallas_call x14, Pallas kernels, vmem_call(): pl.pallas_call(body, out_shape=out_shape, in_specs=[pl.BlockSpec(memory_s...  13.9 us
    ppermute x2, starting transfers between devices, gathered(): lax.ppermute(tail, ('seq', 'head'), rim_route(target))  1.32 us
  transfers between devices with their start and end apart: 17, of which 9 were waited for; matrix products, arithmetic and copies ran while one was open for 2% of the time, Pallas kernels for 10%

profile of v9, /device:TPU:0, one launch (start us, length us, event | category | flops | bytes accessed | tf_op | source)
XLA Modules:
  0.0 54.4 jit_solution(16336978305416304796)
XLA Ops:
  0.0 2.9 %collective-permute-start = (bf16[64,2304]{1,0:T(8,128)(2,1)}, bf16[64,2304]{1,0:T(8,128)(2,1)S(1)}, u32[]{:S(2)}, u32[]{:S(2)}) collective-permute-start(bf16[64,2304]{1,0:T(8,128)(2,1)} %hidden_ref.1), channel_id=1, source_target_pairs={{0,2},{1,3},{2,0},{3,1},{4,6},{5,7},{6,4},{7,5},{8,10},{9,11},{10,... | collective-permute-start | bytes 884744 | tf_op jit(solution)/shard_map/ppermute | solution.py:24
  2.9 0.9 %slice.3 = bf16[16,2304]{1,0:T(8,128)(2,1)S(1)} slice(bf16[64,2304]{1,0:T(8,128)(2,1)} %hidden_ref.1), slice={[48:64], [0:2304]} | slice | bytes 147456 | tf_op jit(solution)/shard_map/slice | solution.py:53
  3.9 0.7 %collective-permute-start.2 = (bf16[16,2304]{1,0:T(8,128)(2,1)S(1)}, bf16[16,2304]{1,0:T(8,128)(2,1)S(1)}, u32[]{:S(2)}, u32[]{:S(2)}) collective-permute-start(bf16[16,2304]{1,0:T(8,128)(2,1)S(1)} %slice.3), channel_id=1, source_target_pairs={{3,5},{7,9},{11,13},{15,17},{19,21},{23,25},{27,29}} | collective-permute-start | bytes 221192 | tf_op jit(solution)/shard_map/ppermute | solution.py:55
  4.5 0.7 %collective-permute-start.1 = (bf16[16,2304]{1,0:T(8,128)(2,1)S(1)}, bf16[16,2304]{1,0:T(8,128)(2,1)S(1)}, u32[]{:S(2)}, u32[]{:S(2)}) collective-permute-start(bf16[16,2304]{1,0:T(8,128)(2,1)S(1)} %slice.3), channel_id=1, source_target_pairs={{3,6},{7,10},{11,14},{15,18},{19,22},{23,26},{27,30}} | collective-permute-start | bytes 221192 | tf_op jit(solution)/shard_map/ppermute | solution.py:55
  5.2 0.1 collective-permute-start.4
  5.3 2.9 %shard_map.118 = (bf16[64,2304]{1,0:T(8,128)(2,1)S(1)}, bf16[2,2304,512]{2,1,0:T(8,128)(2,1)S(1)}, bf16[2304,256]{1,0:T(8,128)(2,1)S(1)}, bf16[4,2304]{1,0:T(4,128)(2,1)S(1)}) custom-call(bf16[64,2304]{1,0:T(8,128)(2,1)} %hidden_ref.1, bf16[2304,128]{1,0:T(8,128)(2,1)} %decay_down_ref.1, bf16[2304,128]{1,0:T(8,128)(2,1)} %gate_down_ref.1, ...), custom_call_target="tpu_custom_call" | custom-call | tf_op jit(solution)/shard_map/pallas_call | solution.py:73
  8.2 0.0 collective-permute-done.2.refs_1_
  8.2 0.0 collective-permute-done.1.refs_0_
  8.2 2.7 %collective-permute-done.refs_3_ = bf16[64,2304]{1,0:T(8,128)(2,1)S(1)} collective-permute-done((bf16[64,2304]{1,0:T(8,128)(2,1)}, bf16[64,2304]{1,0:T(8,128)(2,1)S(1)}, u32[]{:S(2)}, u32[]{:S(2)}) %collective-permute-start) | collective-permute-done | bytes 294944 | tf_op jit(solution)/shard_map/ppermute | solution.py:24
  10.9 0.0 collective-permute-start.5
  11.0 0.6 %collective-permute-start.3 = (bf16[16,2304]{1,0:T(8,128)(2,1)S(1)}, bf16[16,2304]{1,0:T(8,128)(2,1)S(1)}, u32[]{:S(2)}, u32[]{:S(2)}) collective-permute-start(bf16[16,2304]{1,0:T(8,128)(2,1)S(1)} %shard_map.119.refs_0_), channel_id=1, source_target_pairs={{0,1},{1,0},{2,3},{3,2},{4,5},{5,4},{6,7},{7,6},{8,9},{9,8},{10,11... | collective-permute-start | bytes 221192 | tf_op jit(solution)/shard_map/ppermute | solution.py:24
  11.6 0.0 collective-permute-done.4.refs_2_
  11.6 1.1 %collective-permute-done.3.refs_1_ = bf16[16,2304]{1,0:T(8,128)(2,1)S(1)} collective-permute-done((bf16[16,2304]{1,0:T(8,128)(2,1)S(1)}, bf16[16,2304]{1,0:T(8,128)(2,1)S(1)}, u32[]{:S(2)}, u32[]{:S(2)}) %collective-permute-start.3) | collective-permute-done | bytes 73760 | tf_op jit(solution)/shard_map/ppermute | solution.py:24
  12.6 0.0 collective-permute-done.5.refs_4_
  12.6 0.0 copy-start.1
  12.6 0.0 copy-start
  12.6 0.0 copy-start.2
  12.6 7.9 %shard_map.120 = (bf16[1,128,256]{2,1,0:T(8,128)(2,1)S(1)}, bf16[1,128,256]{2,1,0:T(8,128)(2,1)S(1)}, bf16[1,128,256]{2,1,0:T(8,128)(2,1)S(1)}, bf16[1,128,256]{...) custom-call(bf16[16,2304]{1,0:T(8,128)(2,1)S(1)} %shard_map.119.refs, ...), custom_call_target="tpu_custom_call" | custom-call | flops 2415919104 | bytes 9437184 | tf_op jit(solution)/shard_map/pallas_call | solution.py:73
  20.5 1.0 %collective-permute-start.6 = (bf16[1,128,256]{2,1,0:T(8,128)(2,1)S(1)}, bf16[1,128,256]{2,1,0:T(8,128)(2,1)S(1)}, u32[]{:S(2)}, u32[]{:S(2)}) collective-permute-start(bf16[1,128,256]{2,1,0:T(8,128)(2,1)S(1)} %get-tuple-element.47), channel_id=1, source_target_pairs={{0,4},{4,0},{8,12},{12,8},{16,20},{20,16},{24,28},{28,24},{1,5},{5... | collective-permute-start | bytes 196616 | tf_op jit(solution)/shard_map/ppermute | solution.py:24
  21.6 1.0 %collective-permute-start.9 = (bf16[1,128,256]{2,1,0:T(8,128)(2,1)S(1)}, bf16[1,128,256]{2,1,0:T(8,128)(2,1)S(1)}, u32[]{:S(2)}, u32[]{:S(2)}) collective-permute-start(bf16[1,128,256]{2,1,0:T(8,128)(2,1)S(1)} %get-tuple-element.50), channel_id=1, source_target_pairs={{0,4},{4,0},{8,12},{12,8},{16,20},{20,16},{24,28},{28,24},{1,5},{5... | collective-permute-start | bytes 196616 | tf_op jit(solution)/shard_map/ppermute | solution.py:24
  22.6 2.9 %collective-permute-done.6.far_ref.partner_ref = bf16[1,128,256]{2,1,0:T(8,128)(2,1)S(1)} collective-permute-done((bf16[1,128,256]{2,1,0:T(8,128)(2,1)S(1)}, bf16[1,128,256]{2,1,0:T(8,128)(2,1)S(1)}, u32[]{:S(2)}, u32[]{:S(2)}) %collective-permute-start.6) | collective-permute-done | bytes 65568 | tf_op jit(solution)/shard_map/ppermute | solution.py:24
  25.5 0.2 shard_map.121.own_ref
  25.7 1.5 %collective-permute-start.7 = (bf16[1,128,256]{2,1,0:T(8,128)(2,1)S(1)}, bf16[1,128,256]{2,1,0:T(8,128)(2,1)S(1)}, u32[]{:S(2)}, u32[]{:S(2)}) collective-permute-start(bf16[1,128,256]{2,1,0:T(8,128)(2,1)S(1)} %shard_map.121.own_ref), channel_id=1, source_target_pairs={{0,8},{4,12},{8,0},{12,4},{16,24},{20,28},{24,16},{28,20},{1,9},{5... | collective-permute-start | bytes 196616 | tf_op jit(solution)/shard_map/ppermute | solution.py:24
  27.2 0.0 collective-permute-done.9.far_ref.partner_ref
  27.2 0.2 shard_map.125.own_ref
  27.4 1.0 %collective-permute-start.10 = (bf16[1,128,256]{2,1,0:T(8,128)(2,1)S(1)}, bf16[1,128,256]{2,1,0:T(8,128)(2,1)S(1)}, u32[]{:S(2)}, u32[]{:S(2)}) collective-permute-start(bf16[1,128,256]{2,1,0:T(8,128)(2,1)S(1)} %shard_map.125.own_ref), channel_id=1, source_target_pairs={{0,8},{4,12},{8,0},{12,4},{16,24},{20,28},{24,16},{28,20},{1,9},{5... | collective-permute-start | bytes 196616 | tf_op jit(solution)/shard_map/ppermute | solution.py:24
  28.4 1.6 %collective-permute-done.7.far_ref = bf16[1,128,256]{2,1,0:T(8,128)(2,1)S(1)} collective-permute-done((bf16[1,128,256]{2,1,0:T(8,128)(2,1)S(1)}, bf16[1,128,256]{2,1,0:T(8,128)(2,1)S(1)}, u32[]{:S(2)}, u32[]{:S(2)}) %collective-permute-start.7) | collective-permute-done | bytes 65568 | tf_op jit(solution)/shard_map/ppermute | solution.py:24
  30.0 0.1 shard_map.123
  30.2 2.5 %collective-permute-start.8 = (bf16[1,128,128]{2,1,0:T(8,128)(2,1)S(1)}, bf16[1,128,128]{2,1,0:T(8,128)(2,1)S(1)}, u32[]{:S(2)}, u32[]{:S(2)}) collective-permute-start(bf16[1,128,128]{2,1,0:T(8,128)(2,1)S(1)} %shard_map.123), channel_id=1, source_target_pairs={{0,16},{4,20},{8,24},{12,28},{16,0},{20,4},{24,8},{28,12},{1,17},{... | collective-permute-start | bytes 98312 | tf_op jit(solution)/shard_map/ppermute | solution.py:24
  32.7 0.0 collective-permute-done.10.far_ref
  32.7 0.2 shard_map.127
  32.9 1.6 %collective-permute-start.11 = (bf16[1,128,128]{2,1,0:T(8,128)(2,1)S(1)}, bf16[1,128,128]{2,1,0:T(8,128)(2,1)S(1)}, u32[]{:S(2)}, u32[]{:S(2)}) collective-permute-start(bf16[1,128,128]{2,1,0:T(8,128)(2,1)S(1)} %shard_map.127), channel_id=1, source_target_pairs={{0,16},{4,20},{8,24},{12,28},{16,0},{20,4},{24,8},{28,12},{1,17},{... | collective-permute-start | bytes 98312 | tf_op jit(solution)/shard_map/ppermute | solution.py:24
  34.6 0.8 %collective-permute-done.8.far_ref = bf16[1,128,128]{2,1,0:T(8,128)(2,1)S(1)} collective-permute-done((bf16[1,128,128]{2,1,0:T(8,128)(2,1)S(1)}, bf16[1,128,128]{2,1,0:T(8,128)(2,1)S(1)}, u32[]{:S(2)}, u32[]{:S(2)}) %collective-permute-start.8) | collective-permute-done | bytes 32800 | tf_op jit(solution)/shard_map/ppermute | solution.py:24
  35.4 0.3 shard_map.124
  35.7 1.5 %collective-permute-start.12 = (bf16[1,128,128]{2,1,0:T(8,128)(2,1)S(1)}, bf16[1,128,128]{2,1,0:T(8,128)(2,1)S(1)}, u32[]{:S(2)}, u32[]{:S(2)}) collective-permute-start(bf16[1,128,128]{2,1,0:T(8,128)(2,1)S(1)} %get-tuple-element.52), channel_id=1, source_target_pairs={{0,4},{4,0},{8,12},{12,8},{16,20},{20,16},{24,28},{28,24},{1,5},{5... | collective-permute-start | bytes 98312 | tf_op jit(solution)/shard_map/ppermute | solution.py:24
  37.2 0.6 %collective-permute-done.11.far_ref = bf16[1,128,128]{2,1,0:T(8,128)(2,1)S(1)} collective-permute-done((bf16[1,128,128]{2,1,0:T(8,128)(2,1)S(1)}, bf16[1,128,128]{2,1,0:T(8,128)(2,1)S(1)}, u32[]{:S(2)}, u32[]{:S(2)}) %collective-permute-start.11) | collective-permute-done | bytes 32800 | tf_op jit(solution)/shard_map/ppermute | solution.py:24
  37.8 0.3 shard_map.128
  38.1 2.0 %collective-permute-start.13 = (bf16[1,128,128]{2,1,0:T(8,128)(2,1)S(1)}, bf16[1,128,128]{2,1,0:T(8,128)(2,1)S(1)}, u32[]{:S(2)}, u32[]{:S(2)}) collective-permute-start(bf16[1,128,128]{2,1,0:T(8,128)(2,1)S(1)} %get-tuple-element.53), channel_id=1, source_target_pairs={{0,4},{4,0},{8,12},{12,8},{16,20},{20,16},{24,28},{28,24},{1,5},{5... | collective-permute-start | bytes 98312 | tf_op jit(solution)/shard_map/ppermute | solution.py:24
  40.0 0.0 copy-done.1
  40.0 0.4 shard_map.129
  40.4 0.0 collective-permute-done.12.refs_2_
  40.4 1.7 %collective-permute-done.13.refs_3_ = bf16[1,128,128]{2,1,0:T(8,128)(2,1)S(1)} collective-permute-done((bf16[1,128,128]{2,1,0:T(8,128)(2,1)S(1)}, bf16[1,128,128]{2,1,0:T(8,128)(2,1)S(1)}, u32[]{:S(2)}, u32[]{:S(2)}) %collective-permute-start.13) | collective-permute-done | bytes 32800 | tf_op jit(solution)/shard_map/ppermute | solution.py:24
  42.0 0.0 copy-done
  42.0 0.0 copy-done.2
  42.1 0.7 %shard_map.131 = (f32[64,2304]{1,0:T(8,128)S(1)}, bf16[64,2304]{1,0:T(8,128)(2,1)S(1)}) custom-call(bf16[1,128,128]{2,1,0:T(8,128)(2,1)S(1)} %get-tuple-element.48.refs_0_, bf16[1,128,128]{2,1,0:T(8,128)(2,1)S(1)} %get-tuple-element.51.refs_1_, bf16[1,128,128]{2,1,0:T(8,128)(2,1)S(1)} %collective-permute-done.12.refs_2_, ...), custom_call_target="tpu_custom_call" | custom-call | flops 301989888 | bytes 2359296 | tf_op jit(solution)/shard_map/pallas_call | solution.py:73
  42.8 0.1 collective-permute-start.15
  42.9 0.7 %shard_map.130 = (f32[64,2304]{1,0:T(8,128)S(1)}, bf16[64,2304]{1,0:T(8,128)(2,1)S(1)}) custom-call(bf16[1,128,128]{2,1,0:T(8,128)(2,1)S(1)} %get-tuple-element.48.refs_0_, bf16[1,128,128]{2,1,0:T(8,128)(2,1)S(1)} %get-tuple-element.51.refs_1_, bf16[1,128,128]{2,1,0:T(8,128)(2,1)S(1)} %collective-permute-done.12.refs_2_, ...), custom_call_target="tpu_custom_call" | custom-call | flops 301989888 | bytes 2359296 | tf_op jit(solution)/shard_map/pallas_call | solution.py:73
  43.6 0.5 %collective-permute-start.14 = (bf16[64,2304]{1,0:T(8,128)(2,1)S(1)}, bf16[64,2304]{1,0:T(8,128)(2,1)S(1)}, u32[]{:S(2)}, u32[]{:S(2)}) collective-permute-start(bf16[64,2304]{1,0:T(8,128)(2,1)S(1)} %get-tuple-element.62), channel_id=1, source_target_pairs={{0,1},{1,0},{2,3},{3,2},{4,5},{5,4},{6,7},{7,6},{8,9},{9,8},{10,11... | collective-permute-start | bytes 884744 | tf_op jit(solution)/shard_map/ppermute | solution.py:24
  44.2 0.3 collective-permute-done.15
  44.4 0.1 convert_add_fusion
  44.5 1.3 %collective-permute-start.16 = (bf16[64,2304]{1,0:T(8,128)(2,1)S(1)}, bf16[64,2304]{1,0:T(8,128)(2,1)S(1)}, u32[]{:S(2)}, u32[]{:S(2)}) collective-permute-start(bf16[64,2304]{1,0:T(8,128)(2,1)S(1)} %convert_add_fusion), channel_id=1, source_target_pairs={{0,2},{1,3},{2,0},{3,1},{4,6},{5,7},{6,4},{7,5},{8,10},{9,11},{10,... | collective-permute-start | bytes 884744 | tf_op jit(solution)/shard_map/ppermute | solution.py:24
  45.8 0.0 collective-permute-done.14
  45.8 0.1 convert_add_fusion.1
  45.8 7.8 %collective-permute-done.16 = bf16[64,2304]{1,0:T(8,128)(2,1)S(1)} collective-permute-done((bf16[64,2304]{1,0:T(8,128)(2,1)S(1)}, bf16[64,2304]{1,0:T(8,128)(2,1)S(1)}, u32[]{:S(2)}, u32[]{:S(2)}) %collective-permute-start.16) | collective-permute-done | bytes 294944 | tf_op jit(solution)/shard_map/ppermute | solution.py:24
  53.6 0.8 %add_convert_fusion = bf16[64,2304]{1,0:T(8,128)(2,1)} fusion(f32[64,2304]{1,0:T(8,128)S(1)} %convert_add_fusion.1, bf16[64,2304]{1,0:T(8,128)(2,1)S(1)} %collective-permute-done.16), kind=kLoop, calls=%fused_computation | loop fusion | flops 442368 | bytes 1179648 | tf_op jit(solution)/shard_map/convert_element_type | solution.py:564
  (3 shorter events, 0.1 us)
Async XLA Ops:
  0.0 10.9 %collective-permute-start = (bf16[64,2304]{1,0:T(8,128)(2,1)}, bf16[64,2304]{1,0:T(8,128)(2,1)S(1)}, u32[]{:S(2)}, u32[]{:S(2)}) collective-permute-start(bf16[64,2304]{1,0:T(8,128)(2,1)} %hidden_ref.1), channel_id=1, source_target_pairs={{0,2},{1,3},{2,0},{3,1},{4,6},{5,7},{6,4},{7,5},{8,10},{9,11},{10,... | collective-permute-start | bytes 884744 | tf_op jit(solution)/shard_map/ppermute | solution.py:24
  3.9 4.3 %collective-permute-start.2 = (bf16[16,2304]{1,0:T(8,128)(2,1)S(1)}, bf16[16,2304]{1,0:T(8,128)(2,1)S(1)}, u32[]{:S(2)}, u32[]{:S(2)}) collective-permute-start(bf16[16,2304]{1,0:T(8,128)(2,1)S(1)} %slice.3), channel_id=1, source_target_pairs={{3,5},{7,9},{11,13},{15,17},{19,21},{23,25},{27,29}} | collective-permute-start | bytes 221192 | tf_op jit(solution)/shard_map/ppermute | solution.py:55
  4.5 3.7 %collective-permute-start.1 = (bf16[16,2304]{1,0:T(8,128)(2,1)S(1)}, bf16[16,2304]{1,0:T(8,128)(2,1)S(1)}, u32[]{:S(2)}, u32[]{:S(2)}) collective-permute-start(bf16[16,2304]{1,0:T(8,128)(2,1)S(1)} %slice.3), channel_id=1, source_target_pairs={{3,6},{7,10},{11,14},{15,18},{19,22},{23,26},{27,30}} | collective-permute-start | bytes 221192 | tf_op jit(solution)/shard_map/ppermute | solution.py:55
  5.2 6.4 %collective-permute-start.4 = (bf16[64,2304]{1,0:T(8,128)(2,1)}, bf16[64,2304]{1,0:T(8,128)(2,1)S(1)}, u32[]{:S(2)}, u32[]{:S(2)}) collective-permute-start(bf16[64,2304]{1,0:T(8,128)(2,1)} %hidden_ref.1), channel_id=1, source_target_pairs={{0,1},{1,0},{2,3},{3,2},{4,5},{5,4},{6,7},{7,6},{8,9},{9,8},{10,11... | collective-permute-start | bytes 884744 | tf_op jit(solution)/shard_map/ppermute | solution.py:24
  10.9 1.7 %collective-permute-start.5 = (bf16[64,2304]{1,0:T(8,128)(2,1)S(1)}, bf16[64,2304]{1,0:T(8,128)(2,1)S(1)}, u32[]{:S(2)}, u32[]{:S(2)}) collective-permute-start(bf16[64,2304]{1,0:T(8,128)(2,1)S(1)} %collective-permute-done.refs_3_), channel_id=1, source_target_pairs={{0,1},{1,0},{2,3},{3,2},{4,5},{5,4},{6,7},{7,6},{8,9},{9,8},{10,11... | collective-permute-start | bytes 884744 | tf_op jit(solution)/shard_map/ppermute | solution.py:24
  11.0 1.7 %collective-permute-start.3 = (bf16[16,2304]{1,0:T(8,128)(2,1)S(1)}, bf16[16,2304]{1,0:T(8,128)(2,1)S(1)}, u32[]{:S(2)}, u32[]{:S(2)}) collective-permute-start(bf16[16,2304]{1,0:T(8,128)(2,1)S(1)} %shard_map.119.refs_0_), channel_id=1, source_target_pairs={{0,1},{1,0},{2,3},{3,2},{4,5},{5,4},{6,7},{7,6},{8,9},{9,8},{10,11... | collective-permute-start | bytes 221192 | tf_op jit(solution)/shard_map/ppermute | solution.py:24
  12.6 27.4 %copy-start.1 = (bf16[128,512]{1,0:T(8,128)(2,1)S(1)}, bf16[128,512]{1,0:T(8,128)(2,1)}, u32[]{:S(2)}) copy-start(bf16[128,512]{1,0:T(8,128)(2,1)} %up_ref.1) | copy-start | bytes 393220
  12.6 29.4 %copy-start = (bf16[512,2304]{1,0:T(8,128)(2,1)S(1)}, bf16[512,2304]{1,0:T(8,128)(2,1)}, u32[]{:S(2)}) copy-start(bf16[512,2304]{1,0:T(8,128)(2,1)} %refs_8_.3) | copy-start | bytes 7077892
  12.6 29.4 %copy-start.2 = (f32[128]{0:T(128)S(1)}, f32[128]{0:T(128)}, u32[]{:S(2)}) copy-start(f32[128]{0:T(128)} %param.22) | copy-start | bytes 1540
  20.5 5.0 %collective-permute-start.6 = (bf16[1,128,256]{2,1,0:T(8,128)(2,1)S(1)}, bf16[1,128,256]{2,1,0:T(8,128)(2,1)S(1)}, u32[]{:S(2)}, u32[]{:S(2)}) collective-permute-start(bf16[1,128,256]{2,1,0:T(8,128)(2,1)S(1)} %get-tuple-element.47), channel_id=1, source_target_pairs={{0,4},{4,0},{8,12},{12,8},{16,20},{20,16},{24,28},{28,24},{1,5},{5... | collective-permute-start | bytes 196616 | tf_op jit(solution)/shard_map/ppermute | solution.py:24
  21.6 5.7 %collective-permute-start.9 = (bf16[1,128,256]{2,1,0:T(8,128)(2,1)S(1)}, bf16[1,128,256]{2,1,0:T(8,128)(2,1)S(1)}, u32[]{:S(2)}, u32[]{:S(2)}) collective-permute-start(bf16[1,128,256]{2,1,0:T(8,128)(2,1)S(1)} %get-tuple-element.50), channel_id=1, source_target_pairs={{0,4},{4,0},{8,12},{12,8},{16,20},{20,16},{24,28},{28,24},{1,5},{5... | collective-permute-start | bytes 196616 | tf_op jit(solution)/shard_map/ppermute | solution.py:24
  25.7 4.3 %collective-permute-start.7 = (bf16[1,128,256]{2,1,0:T(8,128)(2,1)S(1)}, bf16[1,128,256]{2,1,0:T(8,128)(2,1)S(1)}, u32[]{:S(2)}, u32[]{:S(2)}) collective-permute-start(bf16[1,128,256]{2,1,0:T(8,128)(2,1)S(1)} %shard_map.121.own_ref), channel_id=1, source_target_pairs={{0,8},{4,12},{8,0},{12,4},{16,24},{20,28},{24,16},{28,20},{1,9},{5... | collective-permute-start | bytes 196616 | tf_op jit(solution)/shard_map/ppermute | solution.py:24
  27.4 5.3 %collective-permute-start.10 = (bf16[1,128,256]{2,1,0:T(8,128)(2,1)S(1)}, bf16[1,128,256]{2,1,0:T(8,128)(2,1)S(1)}, u32[]{:S(2)}, u32[]{:S(2)}) collective-permute-start(bf16[1,128,256]{2,1,0:T(8,128)(2,1)S(1)} %shard_map.125.own_ref), channel_id=1, source_target_pairs={{0,8},{4,12},{8,0},{12,4},{16,24},{20,28},{24,16},{28,20},{1,9},{5... | collective-permute-start | bytes 196616 | tf_op jit(solution)/shard_map/ppermute | solution.py:24
  30.2 5.2 %collective-permute-start.8 = (bf16[1,128,128]{2,1,0:T(8,128)(2,1)S(1)}, bf16[1,128,128]{2,1,0:T(8,128)(2,1)S(1)}, u32[]{:S(2)}, u32[]{:S(2)}) collective-permute-start(bf16[1,128,128]{2,1,0:T(8,128)(2,1)S(1)} %shard_map.123), channel_id=1, source_target_pairs={{0,16},{4,20},{8,24},{12,28},{16,0},{20,4},{24,8},{28,12},{1,17},{... | collective-permute-start | bytes 98312 | tf_op jit(solution)/shard_map/ppermute | solution.py:24
  32.9 4.9 %collective-permute-start.11 = (bf16[1,128,128]{2,1,0:T(8,128)(2,1)S(1)}, bf16[1,128,128]{2,1,0:T(8,128)(2,1)S(1)}, u32[]{:S(2)}, u32[]{:S(2)}) collective-permute-start(bf16[1,128,128]{2,1,0:T(8,128)(2,1)S(1)} %shard_map.127), channel_id=1, source_target_pairs={{0,16},{4,20},{8,24},{12,28},{16,0},{20,4},{24,8},{28,12},{1,17},{... | collective-permute-start | bytes 98312 | tf_op jit(solution)/shard_map/ppermute | solution.py:24
  35.7 4.7 %collective-permute-start.12 = (bf16[1,128,128]{2,1,0:T(8,128)(2,1)S(1)}, bf16[1,128,128]{2,1,0:T(8,128)(2,1)S(1)}, u32[]{:S(2)}, u32[]{:S(2)}) collective-permute-start(bf16[1,128,128]{2,1,0:T(8,128)(2,1)S(1)} %get-tuple-element.52), channel_id=1, source_target_pairs={{0,4},{4,0},{8,12},{12,8},{16,20},{20,16},{24,28},{28,24},{1,5},{5... | collective-permute-start | bytes 98312 | tf_op jit(solution)/shard_map/ppermute | solution.py:24
  38.1 4.0 %collective-permute-start.13 = (bf16[1,128,128]{2,1,0:T(8,128)(2,1)S(1)}, bf16[1,128,128]{2,1,0:T(8,128)(2,1)S(1)}, u32[]{:S(2)}, u32[]{:S(2)}) collective-permute-start(bf16[1,128,128]{2,1,0:T(8,128)(2,1)S(1)} %get-tuple-element.53), channel_id=1, source_target_pairs={{0,4},{4,0},{8,12},{12,8},{16,20},{20,16},{24,28},{28,24},{1,5},{5... | collective-permute-start | bytes 98312 | tf_op jit(solution)/shard_map/ppermute | solution.py:24
  42.8 1.6 %collective-permute-start.15 = (bf16[64,2304]{1,0:T(8,128)(2,1)S(1)}, bf16[64,2304]{1,0:T(8,128)(2,1)S(1)}, u32[]{:S(2)}, u32[]{:S(2)}) collective-permute-start(bf16[64,2304]{1,0:T(8,128)(2,1)S(1)} %get-tuple-element.64), channel_id=1, source_target_pairs={{0,1},{1,0},{2,3},{3,2},{4,5},{5,4},{6,7},{7,6},{8,9},{9,8},{10,11... | collective-permute-start | bytes 884744 | tf_op jit(solution)/shard_map/ppermute | solution.py:24
  43.6 2.1 %collective-permute-start.14 = (bf16[64,2304]{1,0:T(8,128)(2,1)S(1)}, bf16[64,2304]{1,0:T(8,128)(2,1)S(1)}, u32[]{:S(2)}, u32[]{:S(2)}) collective-permute-start(bf16[64,2304]{1,0:T(8,128)(2,1)S(1)} %get-tuple-element.62), channel_id=1, source_target_pairs={{0,1},{1,0},{2,3},{3,2},{4,5},{5,4},{6,7},{7,6},{8,9},{9,8},{10,11... | collective-permute-start | bytes 884744 | tf_op jit(solution)/shard_map/ppermute | solution.py:24
  44.5 9.1 %collective-permute-start.16 = (bf16[64,2304]{1,0:T(8,128)(2,1)S(1)}, bf16[64,2304]{1,0:T(8,128)(2,1)S(1)}, u32[]{:S(2)}, u32[]{:S(2)}) collective-permute-start(bf16[64,2304]{1,0:T(8,128)(2,1)S(1)} %convert_add_fusion), channel_id=1, source_target_pairs={{0,2},{1,3},{2,0},{3,1},{4,6},{5,7},{6,4},{7,5},{8,10},{9,11},{10,... | collective-permute-start | bytes 884744 | tf_op jit(solution)/shard_map/ppermute | solution.py:24

commit v10 on v9

--- a/solution.py
+++ b/solution.py
@@ -36,10 +36,11 @@
 
 def pick_body(targets, *refs):
     *tail_refs, rim_ref = refs
-    rim = jnp.zeros(rim_ref.shape, f32)
+    rim = jnp.zeros(tail_refs[0].shape, f32)
+    above = jnp.zeros((rim_ref.shape[0] - rim.shape[0], rim.shape[1]), f32)
     for target, ref in zip(targets, tail_refs):
         rim = jnp.where(place("head") == target, ref[...].astype(f32), rim)
-    rim_ref[...] = rim.astype(rim_ref.dtype)
+    rim_ref[...] = jnp.concatenate([above, rim], axis=0).astype(rim_ref.dtype)
 
 
 def gathered(own, loaded):
@@ -50,7 +51,7 @@
     for bit in reversed(bits[1:]):
         for k in sorted(slabs):
             slabs[k ^ bit] = swapped(slabs[k], "head", bit)
-    tail = own[own.shape[0] - RIM :]
+    tail = own[own.shape[0] - RIM // 2 :]
     targets = [first if first == heads - 2 else first + 1 for first in range(0, heads, 2)][::-1]
     tails = [lax.ppermute(tail, ("seq", "head"), rim_route(target)) for target in targets]
     slabs[1] = swapped(own, "head", 1)
@@ -61,7 +62,7 @@
     for k, slab in zip(arrived, moved):
         slabs[k], slabs[k ^ 1] = slab, swapped(slab, "head", 1)
     rim = vmem_call(
-        functools.partial(pick_body, targets), jax.ShapeDtypeStruct(tail.shape, bf16), tails
+        functools.partial(pick_body, targets), jax.ShapeDtypeStruct((RIM, own.shape[1]), bf16), tails
     )
     return [slabs[k] for k in range(1, heads)], [rim, swapped(rim, "head", 1)], loaded
 
@@ -171,9 +172,15 @@
             at = begin - piece.start
             projected[c * heads + begin // size] = result[:, at : at + size]
 
-    for c in range(2):
-        for piece in pieces:
+    pending = [(c, piece) for piece in pieces for c in range(2)]
+    share = (pieces[0].stop - pieces[0].start) // size
+
+    def project_next(number):
+        for c, piece in pending[:number]:
             project(c, piece, weights[c, :, piece])
+        del pending[:number]
+
+    project_next(2)
     low = dot(rows_ref[RIM:, :], downs[...]).astype(bf16)
     gate_ref[...] = low[:, rank:]
     strength = jax.nn.sigmoid(dot(rows_ref[RIM:, :], betas[...], ((1,), (1,))))
@@ -207,10 +214,8 @@
         half = 0.5 * total
         return half + half * jnp.tanh(half)
 
-    for i, piece in enumerate(pieces):
-        streams[i].wait()
-        project(2, piece, value_weight[:, piece])
-
+    for copy in streams:
+        copy.wait()
     stops = []
     for h in range(heads):
         lanes = slice(h * size, (h + 1) * size)
@@ -236,6 +241,7 @@
             key_falls.append(key_fall)
             lefts.append(jnp.concatenate([keys.astype(bf16), queries.astype(bf16)], axis=0))
         stops.append((jnp.concatenate(stop, axis=0), jnp.exp(last)))
+        project_next(pl.cdiv(2, share))
         for a in range(chunks):
             rows = tiles[a]
             reach = (a * chunk // block + 1) * block
@@ -260,6 +266,13 @@
                 at >= to, scores[chunk:, inside], 0.0
             ).astype(bf16)
 
+    def value_side(h):
+        for rows in tiles:
+            sides[h, rows, size:] = convolved(2, rows, h).astype(bf16)
+
+    between = [functools.partial(project, 2, p, value_weight[:, p]) for p in pieces]
+    between += [functools.partial(value_side, h) for h in range(heads)]
+
     at, to = row[:block, :block], col[:block, :block]
     eye = jnp.where(at == to, 1.0, 0.0).astype(bf16)
     base = math.gcd(block, BASE)
@@ -279,6 +292,8 @@
             else:
                 more = dot(total, power)
             totals[n] = (total.astype(f32) + more).astype(bf16)
+        if between:
+            between.pop(0)()
     for (h, d), total in zip(corners, totals):
         inverse[h, d, :] = total
     width = base
@@ -295,11 +310,12 @@
             new = (chosen.astype(f32) - dot(half, inverse[h, d, :])).astype(bf16)
             for n, i in enumerate(odd):
                 inverse[h, d.start + i : d.start + i + width, :] = new[n * width : (n + 1) * width]
+        if between:
+            between.pop(0)()
         width *= 2
-
-    for h in range(heads):
-        for rows in tiles:
-            sides[h, rows, size:] = convolved(2, rows, h).astype(bf16)
+    for work in between:
+        work()
+
     for d in range(blocks):
         rows = slice(d * block, (d + 1) * block)
         for h in range(heads):

time: 54.6 us -> 53.6 us (0.982)
  waiting for transfers between devices: 19.5 us -> 18.3 us
  starting transfers between devices: 19.1 us -> 20 us
  Pallas kernels: 13.9 us -> 13.3 us
    ppermute x15, waiting for transfers between devices: 19.5 us -> 18.3 us  [swapped(): lax.ppermute(block, axis, [(i, i ^ bit) for i in range(lax.axis_size(axis...]
    ppermute x15, starting transfers between devices: 17.7 us -> 18.6 us  [swapped(): lax.ppermute(block, axis, [(i, i ^ bit) for i in range(lax.axis_size(axis...]
    pallas_call x14, Pallas kernels: 13.9 us -> 13.3 us  [vmem_call(): pl.pallas_call(body, out_shape=out_shape, in_specs=[pl.BlockSpec(memory_s...]
where the time goes in v10:
time: 53.6 us; the launch traced here: 53.4 us
  starting transfers between devices  20 us (37%)
  waiting for transfers between devices  18.3 us (34%)
  Pallas kernels  13.3 us (25%)
  other arithmetic  0.86 us (2%)
  local copies, waits for them, and re-layouts  0.82 us (2%)
    ppermute x15, starting transfers between devices, swapped(): lax.ppermute(block, axis, [(i, i ^ bit) for i in range(lax.axis_size(axis...  18.6 us
    ppermute x15, waiting for transfers between devices, swapped(): lax.ppermute(block, axis, [(i, i ^ bit) for i in range(lax.axis_size(axis...  18.3 us
    pallas_call x14, Pallas kernels, vmem_call(): pl.pallas_call(body, out_shape=out_shape, in_specs=[pl.BlockSpec(memory_s...  13.3 us
    ppermute x2, starting transfers between devices, gathered(): lax.ppermute(tail, ('seq', 'head'), rim_route(target))  1.32 us
  transfers between devices with their start and end apart: 17, of which 9 were waited for; matrix products, arithmetic and copies ran while one was open for 2% of the time, Pallas kernels for 10%

profile of v10, /device:TPU:0, one launch (start us, length us, event | category | flops | bytes accessed | tf_op | source)
XLA Modules:
  0.0 53.4 jit_solution(9723660033930202358)
XLA Ops:
  0.0 2.9 %collective-permute-start = (bf16[64,2304]{1,0:T(8,128)(2,1)}, bf16[64,2304]{1,0:T(8,128)(2,1)S(1)}, u32[]{:S(2)}, u32[]{:S(2)}) collective-permute-start(bf16[64,2304]{1,0:T(8,128)(2,1)} %hidden_ref.1), channel_id=1, source_target_pairs={{0,2},{1,3},{2,0},{3,1},{4,6},{5,7},{6,4},{7,5},{8,10},{9,11},{10,... | collective-permute-start | bytes 884744 | tf_op jit(solution)/shard_map/ppermute | solution.py:24
  2.9 0.8 %slice.3 = bf16[8,2304]{1,0:T(8,128)(2,1)S(1)} slice(bf16[64,2304]{1,0:T(8,128)(2,1)} %hidden_ref.1), slice={[56:64], [0:2304]} | slice | bytes 73728 | tf_op jit(solution)/shard_map/slice | solution.py:54
  3.7 0.7 %collective-permute-start.2 = (bf16[8,2304]{1,0:T(8,128)(2,1)S(1)}, bf16[8,2304]{1,0:T(8,128)(2,1)S(1)}, u32[]{:S(2)}, u32[]{:S(2)}) collective-permute-start(bf16[8,2304]{1,0:T(8,128)(2,1)S(1)} %slice.3), channel_id=1, source_target_pairs={{3,5},{7,9},{11,13},{15,17},{19,21},{23,25},{27,29}} | collective-permute-start | bytes 110600 | tf_op jit(solution)/shard_map/ppermute | solution.py:56
  4.4 0.7 %collective-permute-start.1 = (bf16[8,2304]{1,0:T(8,128)(2,1)S(1)}, bf16[8,2304]{1,0:T(8,128)(2,1)S(1)}, u32[]{:S(2)}, u32[]{:S(2)}) collective-permute-start(bf16[8,2304]{1,0:T(8,128)(2,1)S(1)} %slice.3), channel_id=1, source_target_pairs={{3,6},{7,10},{11,14},{15,18},{19,22},{23,26},{27,30}} | collective-permute-start | bytes 110600 | tf_op jit(solution)/shard_map/ppermute | solution.py:56
  5.1 0.1 collective-permute-start.4
  5.2 2.9 %shard_map.118 = (bf16[64,2304]{1,0:T(8,128)(2,1)S(1)}, bf16[2,2304,512]{2,1,0:T(8,128)(2,1)S(1)}, bf16[2304,256]{1,0:T(8,128)(2,1)S(1)}, bf16[4,2304]{1,0:T(4,128)(2,1)S(1)}) custom-call(bf16[64,2304]{1,0:T(8,128)(2,1)} %hidden_ref.1, bf16[2304,128]{1,0:T(8,128)(2,1)} %decay_down_ref.1, bf16[2304,128]{1,0:T(8,128)(2,1)} %gate_down_ref.1, ...), custom_call_target="tpu_custom_call" | custom-call | tf_op jit(solution)/shard_map/pallas_call | solution.py:74
  8.1 0.0 collective-permute-done.2.refs_1_
  8.1 0.0 collective-permute-done.1.refs_0_
  8.1 2.4 %collective-permute-done.refs_3_ = bf16[64,2304]{1,0:T(8,128)(2,1)S(1)} collective-permute-done((bf16[64,2304]{1,0:T(8,128)(2,1)}, bf16[64,2304]{1,0:T(8,128)(2,1)S(1)}, u32[]{:S(2)}, u32[]{:S(2)}) %collective-permute-start) | collective-permute-done | bytes 294944 | tf_op jit(solution)/shard_map/ppermute | solution.py:24
  10.6 0.0 collective-permute-start.5
  10.6 0.6 %collective-permute-start.3 = (bf16[16,2304]{1,0:T(8,128)(2,1)S(1)}, bf16[16,2304]{1,0:T(8,128)(2,1)S(1)}, u32[]{:S(2)}, u32[]{:S(2)}) collective-permute-start(bf16[16,2304]{1,0:T(8,128)(2,1)S(1)} %shard_map.119.refs_0_), channel_id=1, source_target_pairs={{0,1},{1,0},{2,3},{3,2},{4,5},{5,4},{6,7},{7,6},{8,9},{9,8},{10,11... | collective-permute-start | bytes 221192 | tf_op jit(solution)/shard_map/ppermute | solution.py:24
  11.1 0.0 collective-permute-done.4.refs_2_
  11.1 1.1 %collective-permute-done.3.refs_1_ = bf16[16,2304]{1,0:T(8,128)(2,1)S(1)} collective-permute-done((bf16[16,2304]{1,0:T(8,128)(2,1)S(1)}, bf16[16,2304]{1,0:T(8,128)(2,1)S(1)}, u32[]{:S(2)}, u32[]{:S(2)}) %collective-permute-start.3) | collective-permute-done | bytes 73760 | tf_op jit(solution)/shard_map/ppermute | solution.py:24
  12.2 0.0 collective-permute-done.5.refs_4_
  12.2 0.0 copy-start.1
  12.2 0.0 copy-start
  12.2 0.0 copy-start.2
  12.3 7.3 %shard_map.120 = (bf16[1,128,256]{2,1,0:T(8,128)(2,1)S(1)}, bf16[1,128,256]{2,1,0:T(8,128)(2,1)S(1)}, bf16[1,128,256]{2,1,0:T(8,128)(2,1)S(1)}, bf16[1,128,256]{...) custom-call(bf16[16,2304]{1,0:T(8,128)(2,1)S(1)} %shard_map.119.refs, ...), custom_call_target="tpu_custom_call" | custom-call | flops 2415919104 | bytes 9437184 | tf_op jit(solution)/shard_map/pallas_call | solution.py:74
  19.5 1.4 %collective-permute-start.6 = (bf16[1,128,256]{2,1,0:T(8,128)(2,1)S(1)}, bf16[1,128,256]{2,1,0:T(8,128)(2,1)S(1)}, u32[]{:S(2)}, u32[]{:S(2)}) collective-permute-start(bf16[1,128,256]{2,1,0:T(8,128)(2,1)S(1)} %get-tuple-element.47), channel_id=1, source_target_pairs={{0,4},{4,0},{8,12},{12,8},{16,20},{20,16},{24,28},{28,24},{1,5},{5... | collective-permute-start | bytes 196616 | tf_op jit(solution)/shard_map/ppermute | solution.py:24
  21.0 0.7 %collective-permute-start.9 = (bf16[1,128,256]{2,1,0:T(8,128)(2,1)S(1)}, bf16[1,128,256]{2,1,0:T(8,128)(2,1)S(1)}, u32[]{:S(2)}, u32[]{:S(2)}) collective-permute-start(bf16[1,128,256]{2,1,0:T(8,128)(2,1)S(1)} %get-tuple-element.50), channel_id=1, source_target_pairs={{0,4},{4,0},{8,12},{12,8},{16,20},{20,16},{24,28},{28,24},{1,5},{5... | collective-permute-start | bytes 196616 | tf_op jit(solution)/shard_map/ppermute | solution.py:24
  21.6 2.6 %collective-permute-done.6.far_ref.partner_ref = bf16[1,128,256]{2,1,0:T(8,128)(2,1)S(1)} collective-permute-done((bf16[1,128,256]{2,1,0:T(8,128)(2,1)S(1)}, bf16[1,128,256]{2,1,0:T(8,128)(2,1)S(1)}, u32[]{:S(2)}, u32[]{:S(2)}) %collective-permute-start.6) | collective-permute-done | bytes 65568 | tf_op jit(solution)/shard_map/ppermute | solution.py:24
  24.3 0.2 shard_map.121.own_ref
  24.4 1.8 %collective-permute-start.7 = (bf16[1,128,256]{2,1,0:T(8,128)(2,1)S(1)}, bf16[1,128,256]{2,1,0:T(8,128)(2,1)S(1)}, u32[]{:S(2)}, u32[]{:S(2)}) collective-permute-start(bf16[1,128,256]{2,1,0:T(8,128)(2,1)S(1)} %shard_map.121.own_ref), channel_id=1, source_target_pairs={{0,8},{4,12},{8,0},{12,4},{16,24},{20,28},{24,16},{28,20},{1,9},{5... | collective-permute-start | bytes 196616 | tf_op jit(solution)/shard_map/ppermute | solution.py:24
  26.3 0.0 collective-permute-done.9.far_ref.partner_ref
  26.3 0.2 shard_map.125.own_ref
  26.4 1.0 %collective-permute-start.10 = (bf16[1,128,256]{2,1,0:T(8,128)(2,1)S(1)}, bf16[1,128,256]{2,1,0:T(8,128)(2,1)S(1)}, u32[]{:S(2)}, u32[]{:S(2)}) collective-permute-start(bf16[1,128,256]{2,1,0:T(8,128)(2,1)S(1)} %shard_map.125.own_ref), channel_id=1, source_target_pairs={{0,8},{4,12},{8,0},{12,4},{16,24},{20,28},{24,16},{28,20},{1,9},{5... | collective-permute-start | bytes 196616 | tf_op jit(solution)/shard_map/ppermute | solution.py:24
  27.4 1.5 %collective-permute-done.7.far_ref = bf16[1,128,256]{2,1,0:T(8,128)(2,1)S(1)} collective-permute-done((bf16[1,128,256]{2,1,0:T(8,128)(2,1)S(1)}, bf16[1,128,256]{2,1,0:T(8,128)(2,1)S(1)}, u32[]{:S(2)}, u32[]{:S(2)}) %collective-permute-start.7) | collective-permute-done | bytes 65568 | tf_op jit(solution)/shard_map/ppermute | solution.py:24
  28.9 0.1 shard_map.123
  29.1 2.7 %collective-permute-start.8 = (bf16[1,128,128]{2,1,0:T(8,128)(2,1)S(1)}, bf16[1,128,128]{2,1,0:T(8,128)(2,1)S(1)}, u32[]{:S(2)}, u32[]{:S(2)}) collective-permute-start(bf16[1,128,128]{2,1,0:T(8,128)(2,1)S(1)} %shard_map.123), channel_id=1, source_target_pairs={{0,16},{4,20},{8,24},{12,28},{16,0},{20,4},{24,8},{28,12},{1,17},{... | collective-permute-start | bytes 98312 | tf_op jit(solution)/shard_map/ppermute | solution.py:24
  31.8 0.0 collective-permute-done.10.far_ref
  31.8 0.2 shard_map.127
  31.9 1.6 %collective-permute-start.11 = (bf16[1,128,128]{2,1,0:T(8,128)(2,1)S(1)}, bf16[1,128,128]{2,1,0:T(8,128)(2,1)S(1)}, u32[]{:S(2)}, u32[]{:S(2)}) collective-permute-start(bf16[1,128,128]{2,1,0:T(8,128)(2,1)S(1)} %shard_map.127), channel_id=1, source_target_pairs={{0,16},{4,20},{8,24},{12,28},{16,0},{20,4},{24,8},{28,12},{1,17},{... | collective-permute-start | bytes 98312 | tf_op jit(solution)/shard_map/ppermute | solution.py:24
  33.6 0.7 %collective-permute-done.8.far_ref = bf16[1,128,128]{2,1,0:T(8,128)(2,1)S(1)} collective-permute-done((bf16[1,128,128]{2,1,0:T(8,128)(2,1)S(1)}, bf16[1,128,128]{2,1,0:T(8,128)(2,1)S(1)}, u32[]{:S(2)}, u32[]{:S(2)}) %collective-permute-start.8) | collective-permute-done | bytes 32800 | tf_op jit(solution)/shard_map/ppermute | solution.py:24
  34.3 0.3 shard_map.124
  34.6 1.6 %collective-permute-start.12 = (bf16[1,128,128]{2,1,0:T(8,128)(2,1)S(1)}, bf16[1,128,128]{2,1,0:T(8,128)(2,1)S(1)}, u32[]{:S(2)}, u32[]{:S(2)}) collective-permute-start(bf16[1,128,128]{2,1,0:T(8,128)(2,1)S(1)} %get-tuple-element.52), channel_id=1, source_target_pairs={{0,4},{4,0},{8,12},{12,8},{16,20},{20,16},{24,28},{28,24},{1,5},{5... | collective-permute-start | bytes 98312 | tf_op jit(solution)/shard_map/ppermute | solution.py:24
  36.2 0.6 %collective-permute-done.11.far_ref = bf16[1,128,128]{2,1,0:T(8,128)(2,1)S(1)} collective-permute-done((bf16[1,128,128]{2,1,0:T(8,128)(2,1)S(1)}, bf16[1,128,128]{2,1,0:T(8,128)(2,1)S(1)}, u32[]{:S(2)}, u32[]{:S(2)}) %collective-permute-start.11) | collective-permute-done | bytes 32800 | tf_op jit(solution)/shard_map/ppermute | solution.py:24
  36.8 0.3 shard_map.128
  37.1 1.9 %collective-permute-start.13 = (bf16[1,128,128]{2,1,0:T(8,128)(2,1)S(1)}, bf16[1,128,128]{2,1,0:T(8,128)(2,1)S(1)}, u32[]{:S(2)}, u32[]{:S(2)}) collective-permute-start(bf16[1,128,128]{2,1,0:T(8,128)(2,1)S(1)} %get-tuple-element.53), channel_id=1, source_target_pairs={{0,4},{4,0},{8,12},{12,8},{16,20},{20,16},{24,28},{28,24},{1,5},{5... | collective-permute-start | bytes 98312 | tf_op jit(solution)/shard_map/ppermute | solution.py:24
  39.0 0.0 copy-done.1
  39.0 0.4 shard_map.129
  39.4 0.0 collective-permute-done.12.refs_2_
  39.4 1.7 %collective-permute-done.13.refs_3_ = bf16[1,128,128]{2,1,0:T(8,128)(2,1)S(1)} collective-permute-done((bf16[1,128,128]{2,1,0:T(8,128)(2,1)S(1)}, bf16[1,128,128]{2,1,0:T(8,128)(2,1)S(1)}, u32[]{:S(2)}, u32[]{:S(2)}) %collective-permute-start.13) | collective-permute-done | bytes 32800 | tf_op jit(solution)/shard_map/ppermute | solution.py:24
  41.1 0.0 copy-done
  41.1 0.0 copy-done.2
  41.1 0.7 %shard_map.131 = (f32[64,2304]{1,0:T(8,128)S(1)}, bf16[64,2304]{1,0:T(8,128)(2,1)S(1)}) custom-call(bf16[1,128,128]{2,1,0:T(8,128)(2,1)S(1)} %get-tuple-element.48.refs_0_, bf16[1,128,128]{2,1,0:T(8,128)(2,1)S(1)} %get-tuple-element.51.refs_1_, bf16[1,128,128]{2,1,0:T(8,128)(2,1)S(1)} %collective-permute-done.12.refs_2_, ...), custom_call_target="tpu_custom_call" | custom-call | flops 301989888 | bytes 2359296 | tf_op jit(solution)/shard_map/pallas_call | solution.py:74
  41.8 0.1 collective-permute-start.15
  41.9 0.7 %shard_map.130 = (f32[64,2304]{1,0:T(8,128)S(1)}, bf16[64,2304]{1,0:T(8,128)(2,1)S(1)}) custom-call(bf16[1,128,128]{2,1,0:T(8,128)(2,1)S(1)} %get-tuple-element.48.refs_0_, bf16[1,128,128]{2,1,0:T(8,128)(2,1)S(1)} %get-tuple-element.51.refs_1_, bf16[1,128,128]{2,1,0:T(8,128)(2,1)S(1)} %collective-permute-done.12.refs_2_, ...), custom_call_target="tpu_custom_call" | custom-call | flops 301989888 | bytes 2359296 | tf_op jit(solution)/shard_map/pallas_call | solution.py:74
  42.7 0.5 %collective-permute-start.14 = (bf16[64,2304]{1,0:T(8,128)(2,1)S(1)}, bf16[64,2304]{1,0:T(8,128)(2,1)S(1)}, u32[]{:S(2)}, u32[]{:S(2)}) collective-permute-start(bf16[64,2304]{1,0:T(8,128)(2,1)S(1)} %get-tuple-element.62), channel_id=1, source_target_pairs={{0,1},{1,0},{2,3},{3,2},{4,5},{5,4},{6,7},{7,6},{8,9},{9,8},{10,11... | collective-permute-start | bytes 884744 | tf_op jit(solution)/shard_map/ppermute | solution.py:24
  43.2 0.3 collective-permute-done.15
  43.5 0.1 convert_add_fusion
  43.5 1.6 %collective-permute-start.16 = (bf16[64,2304]{1,0:T(8,128)(2,1)S(1)}, bf16[64,2304]{1,0:T(8,128)(2,1)S(1)}, u32[]{:S(2)}, u32[]{:S(2)}) collective-permute-start(bf16[64,2304]{1,0:T(8,128)(2,1)S(1)} %convert_add_fusion), channel_id=1, source_target_pairs={{0,2},{1,3},{2,0},{3,1},{4,6},{5,7},{6,4},{7,5},{8,10},{9,11},{10,... | collective-permute-start | bytes 884744 | tf_op jit(solution)/shard_map/ppermute | solution.py:24
  45.2 0.0 collective-permute-done.14
  45.2 0.1 convert_add_fusion.1
  45.2 7.4 %collective-permute-done.16 = bf16[64,2304]{1,0:T(8,128)(2,1)S(1)} collective-permute-done((bf16[64,2304]{1,0:T(8,128)(2,1)S(1)}, bf16[64,2304]{1,0:T(8,128)(2,1)S(1)}, u32[]{:S(2)}, u32[]{:S(2)}) %collective-permute-start.16) | collective-permute-done | bytes 294944 | tf_op jit(solution)/shard_map/ppermute | solution.py:24
  52.7 0.8 %add_convert_fusion = bf16[64,2304]{1,0:T(8,128)(2,1)} fusion(f32[64,2304]{1,0:T(8,128)S(1)} %convert_add_fusion.1, bf16[64,2304]{1,0:T(8,128)(2,1)S(1)} %collective-permute-done.16), kind=kLoop, calls=%fused_computation | loop fusion | flops 442368 | bytes 1179648 | tf_op jit(solution)/shard_map/convert_element_type | solution.py:580
  (3 shorter events, 0.1 us)
Async XLA Ops:
  0.0 10.5 %collective-permute-start = (bf16[64,2304]{1,0:T(8,128)(2,1)}, bf16[64,2304]{1,0:T(8,128)(2,1)S(1)}, u32[]{:S(2)}, u32[]{:S(2)}) collective-permute-start(bf16[64,2304]{1,0:T(8,128)(2,1)} %hidden_ref.1), channel_id=1, source_target_pairs={{0,2},{1,3},{2,0},{3,1},{4,6},{5,7},{6,4},{7,5},{8,10},{9,11},{10,... | collective-permute-start | bytes 884744 | tf_op jit(solution)/shard_map/ppermute | solution.py:24
  3.7 4.3 %collective-permute-start.2 = (bf16[8,2304]{1,0:T(8,128)(2,1)S(1)}, bf16[8,2304]{1,0:T(8,128)(2,1)S(1)}, u32[]{:S(2)}, u32[]{:S(2)}) collective-permute-start(bf16[8,2304]{1,0:T(8,128)(2,1)S(1)} %slice.3), channel_id=1, source_target_pairs={{3,5},{7,9},{11,13},{15,17},{19,21},{23,25},{27,29}} | collective-permute-start | bytes 110600 | tf_op jit(solution)/shard_map/ppermute | solution.py:56
  4.4 3.7 %collective-permute-start.1 = (bf16[8,2304]{1,0:T(8,128)(2,1)S(1)}, bf16[8,2304]{1,0:T(8,128)(2,1)S(1)}, u32[]{:S(2)}, u32[]{:S(2)}) collective-permute-start(bf16[8,2304]{1,0:T(8,128)(2,1)S(1)} %slice.3), channel_id=1, source_target_pairs={{3,6},{7,10},{11,14},{15,18},{19,22},{23,26},{27,30}} | collective-permute-start | bytes 110600 | tf_op jit(solution)/shard_map/ppermute | solution.py:56
  5.1 6.1 %collective-permute-start.4 = (bf16[64,2304]{1,0:T(8,128)(2,1)}, bf16[64,2304]{1,0:T(8,128)(2,1)S(1)}, u32[]{:S(2)}, u32[]{:S(2)}) collective-permute-start(bf16[64,2304]{1,0:T(8,128)(2,1)} %hidden_ref.1), channel_id=1, source_target_pairs={{0,1},{1,0},{2,3},{3,2},{4,5},{5,4},{6,7},{7,6},{8,9},{9,8},{10,11... | collective-permute-start | bytes 884744 | tf_op jit(solution)/shard_map/ppermute | solution.py:24
  10.6 1.7 %collective-permute-start.5 = (bf16[64,2304]{1,0:T(8,128)(2,1)S(1)}, bf16[64,2304]{1,0:T(8,128)(2,1)S(1)}, u32[]{:S(2)}, u32[]{:S(2)}) collective-permute-start(bf16[64,2304]{1,0:T(8,128)(2,1)S(1)} %collective-permute-done.refs_3_), channel_id=1, source_target_pairs={{0,1},{1,0},{2,3},{3,2},{4,5},{5,4},{6,7},{7,6},{8,9},{9,8},{10,11... | collective-permute-start | bytes 884744 | tf_op jit(solution)/shard_map/ppermute | solution.py:24
  10.6 1.7 %collective-permute-start.3 = (bf16[16,2304]{1,0:T(8,128)(2,1)S(1)}, bf16[16,2304]{1,0:T(8,128)(2,1)S(1)}, u32[]{:S(2)}, u32[]{:S(2)}) collective-permute-start(bf16[16,2304]{1,0:T(8,128)(2,1)S(1)} %shard_map.119.refs_0_), channel_id=1, source_target_pairs={{0,1},{1,0},{2,3},{3,2},{4,5},{5,4},{6,7},{7,6},{8,9},{9,8},{10,11... | collective-permute-start | bytes 221192 | tf_op jit(solution)/shard_map/ppermute | solution.py:24
  12.2 26.8 %copy-start.1 = (bf16[128,512]{1,0:T(8,128)(2,1)S(1)}, bf16[128,512]{1,0:T(8,128)(2,1)}, u32[]{:S(2)}) copy-start(bf16[128,512]{1,0:T(8,128)(2,1)} %up_ref.1) | copy-start | bytes 393220
  12.2 28.8 %copy-start = (bf16[512,2304]{1,0:T(8,128)(2,1)S(1)}, bf16[512,2304]{1,0:T(8,128)(2,1)}, u32[]{:S(2)}) copy-start(bf16[512,2304]{1,0:T(8,128)(2,1)} %refs_8_.3) | copy-start | bytes 7077892
  12.2 28.8 %copy-start.2 = (f32[128]{0:T(128)S(1)}, f32[128]{0:T(128)}, u32[]{:S(2)}) copy-start(f32[128]{0:T(128)} %param.22) | copy-start | bytes 1540
  19.5 4.7 %collective-permute-start.6 = (bf16[1,128,256]{2,1,0:T(8,128)(2,1)S(1)}, bf16[1,128,256]{2,1,0:T(8,128)(2,1)S(1)}, u32[]{:S(2)}, u32[]{:S(2)}) collective-permute-start(bf16[1,128,256]{2,1,0:T(8,128)(2,1)S(1)} %get-tuple-element.47), channel_id=1, source_target_pairs={{0,4},{4,0},{8,12},{12,8},{16,20},{20,16},{24,28},{28,24},{1,5},{5... | collective-permute-start | bytes 196616 | tf_op jit(solution)/shard_map/ppermute | solution.py:24
  21.0 5.3 %collective-permute-start.9 = (bf16[1,128,256]{2,1,0:T(8,128)(2,1)S(1)}, bf16[1,128,256]{2,1,0:T(8,128)(2,1)S(1)}, u32[]{:S(2)}, u32[]{:S(2)}) collective-permute-start(bf16[1,128,256]{2,1,0:T(8,128)(2,1)S(1)} %get-tuple-element.50), channel_id=1, source_target_pairs={{0,4},{4,0},{8,12},{12,8},{16,20},{20,16},{24,28},{28,24},{1,5},{5... | collective-permute-start | bytes 196616 | tf_op jit(solution)/shard_map/ppermute | solution.py:24
  24.4 4.5 %collective-permute-start.7 = (bf16[1,128,256]{2,1,0:T(8,128)(2,1)S(1)}, bf16[1,128,256]{2,1,0:T(8,128)(2,1)S(1)}, u32[]{:S(2)}, u32[]{:S(2)}) collective-permute-start(bf16[1,128,256]{2,1,0:T(8,128)(2,1)S(1)} %shard_map.121.own_ref), channel_id=1, source_target_pairs={{0,8},{4,12},{8,0},{12,4},{16,24},{20,28},{24,16},{28,20},{1,9},{5... | collective-permute-start | bytes 196616 | tf_op jit(solution)/shard_map/ppermute | solution.py:24
  26.4 5.3 %collective-permute-start.10 = (bf16[1,128,256]{2,1,0:T(8,128)(2,1)S(1)}, bf16[1,128,256]{2,1,0:T(8,128)(2,1)S(1)}, u32[]{:S(2)}, u32[]{:S(2)}) collective-permute-start(bf16[1,128,256]{2,1,0:T(8,128)(2,1)S(1)} %shard_map.125.own_ref), channel_id=1, source_target_pairs={{0,8},{4,12},{8,0},{12,4},{16,24},{20,28},{24,16},{28,20},{1,9},{5... | collective-permute-start | bytes 196616 | tf_op jit(solution)/shard_map/ppermute | solution.py:24
  29.1 5.2 %collective-permute-start.8 = (bf16[1,128,128]{2,1,0:T(8,128)(2,1)S(1)}, bf16[1,128,128]{2,1,0:T(8,128)(2,1)S(1)}, u32[]{:S(2)}, u32[]{:S(2)}) collective-permute-start(bf16[1,128,128]{2,1,0:T(8,128)(2,1)S(1)} %shard_map.123), channel_id=1, source_target_pairs={{0,16},{4,20},{8,24},{12,28},{16,0},{20,4},{24,8},{28,12},{1,17},{... | collective-permute-start | bytes 98312 | tf_op jit(solution)/shard_map/ppermute | solution.py:24
  31.9 4.9 %collective-permute-start.11 = (bf16[1,128,128]{2,1,0:T(8,128)(2,1)S(1)}, bf16[1,128,128]{2,1,0:T(8,128)(2,1)S(1)}, u32[]{:S(2)}, u32[]{:S(2)}) collective-permute-start(bf16[1,128,128]{2,1,0:T(8,128)(2,1)S(1)} %shard_map.127), channel_id=1, source_target_pairs={{0,16},{4,20},{8,24},{12,28},{16,0},{20,4},{24,8},{28,12},{1,17},{... | collective-permute-start | bytes 98312 | tf_op jit(solution)/shard_map/ppermute | solution.py:24
  34.6 4.8 %collective-permute-start.12 = (bf16[1,128,128]{2,1,0:T(8,128)(2,1)S(1)}, bf16[1,128,128]{2,1,0:T(8,128)(2,1)S(1)}, u32[]{:S(2)}, u32[]{:S(2)}) collective-permute-start(bf16[1,128,128]{2,1,0:T(8,128)(2,1)S(1)} %get-tuple-element.52), channel_id=1, source_target_pairs={{0,4},{4,0},{8,12},{12,8},{16,20},{20,16},{24,28},{28,24},{1,5},{5... | collective-permute-start | bytes 98312 | tf_op jit(solution)/shard_map/ppermute | solution.py:24
  37.1 4.0 %collective-permute-start.13 = (bf16[1,128,128]{2,1,0:T(8,128)(2,1)S(1)}, bf16[1,128,128]{2,1,0:T(8,128)(2,1)S(1)}, u32[]{:S(2)}, u32[]{:S(2)}) collective-permute-start(bf16[1,128,128]{2,1,0:T(8,128)(2,1)S(1)} %get-tuple-element.53), channel_id=1, source_target_pairs={{0,4},{4,0},{8,12},{12,8},{16,20},{20,16},{24,28},{28,24},{1,5},{5... | collective-permute-start | bytes 98312 | tf_op jit(solution)/shard_map/ppermute | solution.py:24
  41.8 1.6 %collective-permute-start.15 = (bf16[64,2304]{1,0:T(8,128)(2,1)S(1)}, bf16[64,2304]{1,0:T(8,128)(2,1)S(1)}, u32[]{:S(2)}, u32[]{:S(2)}) collective-permute-start(bf16[64,2304]{1,0:T(8,128)(2,1)S(1)} %get-tuple-element.64), channel_id=1, source_target_pairs={{0,1},{1,0},{2,3},{3,2},{4,5},{5,4},{6,7},{7,6},{8,9},{9,8},{10,11... | collective-permute-start | bytes 884744 | tf_op jit(solution)/shard_map/ppermute | solution.py:24
  42.7 2.5 %collective-permute-start.14 = (bf16[64,2304]{1,0:T(8,128)(2,1)S(1)}, bf16[64,2304]{1,0:T(8,128)(2,1)S(1)}, u32[]{:S(2)}, u32[]{:S(2)}) collective-permute-start(bf16[64,2304]{1,0:T(8,128)(2,1)S(1)} %get-tuple-element.62), channel_id=1, source_target_pairs={{0,1},{1,0},{2,3},{3,2},{4,5},{5,4},{6,7},{7,6},{8,9},{9,8},{10,11... | collective-permute-start | bytes 884744 | tf_op jit(solution)/shard_map/ppermute | solution.py:24
  43.5 9.1 %collective-permute-start.16 = (bf16[64,2304]{1,0:T(8,128)(2,1)S(1)}, bf16[64,2304]{1,0:T(8,128)(2,1)S(1)}, u32[]{:S(2)}, u32[]{:S(2)}) collective-permute-start(bf16[64,2304]{1,0:T(8,128)(2,1)S(1)} %convert_add_fusion), channel_id=1, source_target_pairs={{0,2},{1,3},{2,0},{3,1},{4,6},{5,7},{6,4},{7,5},{8,10},{9,11},{10,... | collective-permute-start | bytes 884744 | tf_op jit(solution)/shard_map/ppermute | solution.py:24

commit v11 on v9

--- a/solution.py
+++ b/solution.py
@@ -1,4 +1,5 @@
 import functools
+import itertools
 import math
 
 import jax
@@ -36,10 +37,11 @@
 
 def pick_body(targets, *refs):
     *tail_refs, rim_ref = refs
-    rim = jnp.zeros(rim_ref.shape, f32)
+    rim = jnp.zeros(tail_refs[0].shape, f32)
+    above = jnp.zeros((rim_ref.shape[0] - rim.shape[0], rim.shape[1]), f32)
     for target, ref in zip(targets, tail_refs):
         rim = jnp.where(place("head") == target, ref[...].astype(f32), rim)
-    rim_ref[...] = rim.astype(rim_ref.dtype)
+    rim_ref[...] = jnp.concatenate([above, rim], axis=0).astype(rim_ref.dtype)
 
 
 def gathered(own, loaded):
@@ -50,7 +52,7 @@
     for bit in reversed(bits[1:]):
         for k in sorted(slabs):
             slabs[k ^ bit] = swapped(slabs[k], "head", bit)
-    tail = own[own.shape[0] - RIM :]
+    tail = own[own.shape[0] - RIM // 2 :]
     targets = [first if first == heads - 2 else first + 1 for first in range(0, heads, 2)][::-1]
     tails = [lax.ppermute(tail, ("seq", "head"), rim_route(target)) for target in targets]
     slabs[1] = swapped(own, "head", 1)
@@ -61,7 +63,7 @@
     for k, slab in zip(arrived, moved):
         slabs[k], slabs[k ^ 1] = slab, swapped(slab, "head", 1)
     rim = vmem_call(
-        functools.partial(pick_body, targets), jax.ShapeDtypeStruct(tail.shape, bf16), tails
+        functools.partial(pick_body, targets), jax.ShapeDtypeStruct((RIM, own.shape[1]), bf16), tails
     )
     return [slabs[k] for k in range(1, heads)], [rim, swapped(rim, "head", 1)], loaded
 
@@ -91,52 +93,56 @@
     return [slice(i, i + step) for i in range(0, width, step)]
 
 
-def load_body(
-    hidden_ref, decay_down_ref, gate_down_ref, beta_ref, weight_ref,
-    own_ref, weights, downs, betas, sems,
-):
-    rank = decay_down_ref.shape[1]
-    copies = [
-        pltpu.make_async_copy(hidden_ref, own_ref, sems.at[0]),
-        pltpu.make_async_copy(decay_down_ref, downs.at[:, pl.ds(0, rank)], sems.at[1]),
-        pltpu.make_async_copy(gate_down_ref, downs.at[:, pl.ds(rank, rank)], sems.at[2]),
-        pltpu.make_async_copy(beta_ref, betas, sems.at[3]),
-    ]
-    for c in range(2):
-        copies.append(pltpu.make_async_copy(weight_ref.at[c], weights.at[c], sems.at[4 + c]))
+def load_body(*refs):
+    (down_refs, whole_refs, weight_ref), refs = (refs[:2], refs[2:8], refs[8]), refs[9:]
+    downs, whole, weights, sems = refs[0], refs[1:7], refs[7], refs[8]
+    rank = down_refs[0].shape[1]
+    pairs = [(ref, downs.at[:, pl.ds(i * rank, rank)]) for i, ref in enumerate(down_refs)]
+    pairs += list(zip(whole_refs, whole))
+    pairs += [(weight_ref.at[c], weights.at[c]) for c in range(2)]
+    copies = [pltpu.make_async_copy(*pair, sems.at[i]) for i, pair in enumerate(pairs)]
     for copy in copies:
         copy.start()
     for copy in copies:
         copy.wait()
 
 
-def load(own, decay_down, gate_down, beta, weight):
-    width, rank = decay_down.shape
+def load(downs, whole, weight):
+    width, rank = downs[0].shape
     return vmem_call(
         load_body,
         (
-            jax.ShapeDtypeStruct(own.shape, bf16),
+            jax.ShapeDtypeStruct((width, 2 * rank), bf16),
+            *[jax.ShapeDtypeStruct(part.shape, part.dtype) for part in whole],
             jax.ShapeDtypeStruct((2, *weight.shape[1:]), bf16),
-            jax.ShapeDtypeStruct((width, 2 * rank), bf16),
-            jax.ShapeDtypeStruct(beta.shape, bf16),
         ),
-        (own, decay_down, gate_down, beta, weight),
-        scratch=[pltpu.SemaphoreType.DMA((6,))],
-        hbm=5,
+        (*downs, *whole, weight),
+        scratch=[pltpu.SemaphoreType.DMA((4 + len(whole),))],
+        hbm=3 + len(whole),
         grant=8,
     )
+
+
+def weave(main, *others):
+    for _ in main:
+        for other in others:
+            next(other, None)
+
+
+def drain(*steps):
+    for each in steps:
+        for _ in each:
+            pass
 
 
 def front_body(slab_count, *refs):
     (one_ref, two_ref, *slab_refs), refs = refs[: slab_count + 1], refs[slab_count + 1 :]
-    (own_rows_ref, weights, downs, betas), refs = refs[:4], refs[4:]
-    hbm_refs, refs = refs[:5], refs[5:]
+    (downs, own_rows_ref, betas, rates, decay_up_ref, bias_ref, conv_ref), refs = refs[:7], refs[7:]
+    (weights, weight_ref), refs = refs[:2], refs[2:]
     (own_refs, other_refs), refs = (refs[:GROUPS], refs[GROUPS : 2 * GROUPS]), refs[2 * GROUPS :]
     (solved_ref, attend_ref, start_ref, gate_ref), refs = refs[:4], refs[4:]
-    loaded, refs = refs[:5], refs[5:]
-    rows_ref, projected, running_ref, parts_ref, mixing, inverse, sides, sems = refs
-    rates, decay_up_ref, bias_ref, conv_ref, value_weight = loaded
-    weight_ref = hbm_refs[-1]
+    value_weight, rows_ref, projected, running_ref, parts_ref, *refs = refs
+    mixing, inverse, sides, sems = refs
     heads, count, size = start_ref.shape
     slab_rows = count // slab_count
     tap_count = conv_ref.shape[1]
@@ -145,77 +151,79 @@
     chunks = count // chunk
     block = math.gcd(count, 128)
     blocks = count // block
+    half = heads // 2
     here = place("head")
+    lanes_of = [slice(h * size, (h + 1) * size) for h in range(heads)]
+    tiles = [slice(a * chunk, (a + 1) * chunk) for a in range(chunks)]
+    pieces = column_pieces(heads * size)
 
     def rows_of(k):
         return pl.ds(pl.multiple_of(RIM + (here ^ k) * slab_rows, 16), slab_rows)
 
-    small = [pltpu.make_async_copy(hbm_refs[i], loaded[i], sems.at[i]) for i in range(4)]
-    pieces = column_pieces(heads * size)
     streams = []
     for i, piece in enumerate(pieces):
         streams.append(
-            pltpu.make_async_copy(
-                weight_ref.at[2, :, piece], value_weight.at[:, piece], sems.at[4 + i]
-            )
+            pltpu.make_async_copy(weight_ref.at[2, :, piece], value_weight.at[:, piece], sems.at[i])
         )
-    for copy in small + streams:
+    for copy in streams:
         copy.start()
     rows_ref[:RIM, :] = (one_ref[...].astype(f32) + two_ref[...].astype(f32)).astype(bf16)
     for k, ref in enumerate([own_rows_ref, *slab_refs]):
         rows_ref[rows_of(k), :] = ref[...]
 
-    def project(c, piece, weight):
+    def project(c, piece):
+        weight = value_weight[:, piece] if c == 2 else weights[c, :, piece]
         result = dot(rows_ref[...], weight)
         for begin in range(piece.start, piece.stop, size):
             at = begin - piece.start
             projected[c * heads + begin // size] = result[:, at : at + size]
 
-    for c in range(2):
-        for piece in pieces:
-            project(c, piece, weights[c, :, piece])
+    def projections(chosen):
+        for c, piece in chosen:
+            project(c, piece)
+            yield
+
+    def decays():
+        for h, lanes in enumerate(lanes_of):
+            rate = jnp.exp(jnp.broadcast_to(rates[:, h : h + 1], (1, size)))
+            for rows in tiles:
+                raw = running_ref[rows, lanes] + bias_ref[:, lanes]
+                softplus = jnp.maximum(raw, 0.0) + jnp.log(1.0 + jnp.exp(-jnp.abs(raw)))
+                log_decay = -rate * softplus
+                high = log_decay.astype(bf16)
+                parts_ref[rows, lanes] = high
+                rest = (log_decay - high.astype(f32)).astype(bf16)
+                parts_ref[count + rows.start : count + rows.stop, lanes] = rest
+            yield
+
     low = dot(rows_ref[RIM:, :], downs[...]).astype(bf16)
+    running_ref[...] = dot(low[:, :rank], decay_up_ref[...])
     gate_ref[...] = low[:, rank:]
     strength = jax.nn.sigmoid(dot(rows_ref[RIM:, :], betas[...], ((1,), (1,))))
-    for copy in small:
-        copy.wait()
-    running_ref[...] = dot(low[:, :rank], decay_up_ref[...])
-    tiles = [slice(a * chunk, (a + 1) * chunk) for a in range(chunks)]
-    for h in range(heads):
-        lanes = slice(h * size, (h + 1) * size)
-        rate = jnp.exp(jnp.full((1, size), rates[h], f32))
-        for rows in tiles:
-            raw = running_ref[rows, lanes] + bias_ref[:, lanes]
-            softplus = jnp.maximum(raw, 0.0) + jnp.log(1.0 + jnp.exp(-jnp.abs(raw)))
-            log_decay = -rate * softplus
-            high = log_decay.astype(bf16)
-            parts_ref[rows, lanes] = high
-            rest = (log_decay - high.astype(f32)).astype(bf16)
-            parts_ref[count + rows.start : count + rows.stop, lanes] = rest
+    first = [(c, pieces[0]) for c in range(2)]
+    weave(decays(), projections(first))
     row = lax.broadcasted_iota(jnp.int32, (count, count), 0)
     col = lax.broadcasted_iota(jnp.int32, (count, count), 1)
     lower = jnp.where(row >= col, 1.0, 0.0).astype(bf16)
     running_ref[...] = dot(jnp.concatenate([lower, lower], axis=1), parts_ref[...])
+    for copy in streams:
+        copy.wait()
 
     def convolved(c, rows, h):
-        taps = conv_ref[c].astype(f32)[:, h * size : (h + 1) * size]
+        taps = conv_ref[c].astype(f32)[:, lanes_of[h]]
         total = None
         for i in range(tap_count):
-            first = RIM - tap_count + 1 + i + rows.start
-            term = projected[c * heads + h, pl.ds(first, chunk), :] * taps[i : i + 1]
+            begin = RIM - tap_count + 1 + i + rows.start
+            term = projected[c * heads + h, pl.ds(begin, chunk), :] * taps[i : i + 1]
             total = term if total is None else total + term
-        half = 0.5 * total
-        return half + half * jnp.tanh(half)
-
-    for i, piece in enumerate(pieces):
-        streams[i].wait()
-        project(2, piece, value_weight[:, piece])
-
-    stops = []
-    for h in range(heads):
-        lanes = slice(h * size, (h + 1) * size)
+        part = 0.5 * total
+        return part + part * jnp.tanh(part)
+
+    middles, key_falls, stops, lefts = ([[] for _ in range(heads)] for _ in range(4))
+
+    def tiles_of(h):
+        lanes = lanes_of[h]
         last = running_ref[count - 1 : count, lanes]
-        middles, key_falls, stop, lefts = [], [], [], []
         for rows in tiles:
             running = running_ref[rows, lanes]
             middle = running[chunk // 2 : chunk // 2 + 1]
@@ -231,24 +239,25 @@
             key_fall = keys * strength[rows, h : h + 1] * jnp.exp(-above)
             keys = keys * rise
             sides[h, rows, :size] = (keys * entry).astype(bf16)
-            stop.append((key_fall * jnp.exp(last - middle)).astype(bf16))
-            middles.append(middle)
-            key_falls.append(key_fall)
-            lefts.append(jnp.concatenate([keys.astype(bf16), queries.astype(bf16)], axis=0))
-        stops.append((jnp.concatenate(stop, axis=0), jnp.exp(last)))
-        for a in range(chunks):
-            rows = tiles[a]
+            stops[h].append((key_fall * jnp.exp(last - middle)).astype(bf16))
+            middles[h].append(middle)
+            key_falls[h].append(key_fall)
+            lefts[h].append(jnp.concatenate([keys.astype(bf16), queries.astype(bf16)], axis=0))
+            yield
+
+    def scores_of(h):
+        for a, rows in enumerate(tiles):
             reach = (a * chunk // block + 1) * block
             falls = []
             for b in range(reach // chunk):
                 if b < a:
-                    falls.append(key_falls[b] * jnp.exp(middles[a] - middles[b]))
+                    falls.append(key_falls[h][b] * jnp.exp(middles[h][a] - middles[h][b]))
                 elif b == a:
-                    falls.append(key_falls[b])
+                    falls.append(key_falls[h][b])
                 else:
                     falls.append(jnp.zeros((chunk, size), f32))
             right = jnp.concatenate(falls, axis=0).astype(bf16)
-            scores = dot(lefts[a], right, ((1,), (1,)))
+            scores = dot(lefts[h][a], right, ((1,), (1,)))
             inside = slice(reach - block, reach)
             if reach > block:
                 before = slice(0, reach - block)
@@ -259,77 +268,108 @@
             attend_ref[h, rows, inside] = jnp.where(
                 at >= to, scores[chunk:, inside], 0.0
             ).astype(bf16)
+            yield
 
     at, to = row[:block, :block], col[:block, :block]
     eye = jnp.where(at == to, 1.0, 0.0).astype(bf16)
     base = math.gcd(block, BASE)
     near = jnp.where(at // base == to // base, -1.0, 0.0).astype(bf16)
-    corners = [(h, slice(d * block, (d + 1) * block)) for h in range(heads) for d in range(blocks)]
-    powers = [mixing[h, d, d] * near for h, d in corners]
-    totals = [power + eye for power in powers]
-    steps = (base - 1).bit_length() - 1
-    if steps:
-        powers = [dot(power, power).astype(bf16) for power in powers]
-    for step in range(steps):
-        for n in range(len(corners)):
-            power, total = powers[n], totals[n]
-            if step < steps - 1:
-                both = dot(jnp.concatenate([power, total], axis=0), power)
-                powers[n], more = both[:block].astype(bf16), both[block:]
-            else:
-                more = dot(total, power)
-            totals[n] = (total.astype(f32) + more).astype(bf16)
-    for (h, d), total in zip(corners, totals):
-        inverse[h, d, :] = total
-    width = base
-    while width < block:
-        odd = range(width, block, 2 * width)
-        pair_mask = (at // width % 2 == 1) & (to // width == at // width - 1)
-        pair_mask = jnp.where(pair_mask, 1.0, 0.0).astype(bf16)
-        halves = []
-        for h, d in corners:
-            parts = [inverse[h, d.start + i : d.start + i + width, :] for i in odd]
-            chosen = jnp.concatenate(parts, axis=0)
-            halves.append((chosen, dot(chosen, mixing[h, d, d] * pair_mask).astype(bf16)))
-        for (h, d), (chosen, half) in zip(corners, halves):
-            new = (chosen.astype(f32) - dot(half, inverse[h, d, :])).astype(bf16)
-            for n, i in enumerate(odd):
-                inverse[h, d.start + i : d.start + i + width, :] = new[n * width : (n + 1) * width]
-        width *= 2
-
-    for h in range(heads):
-        for rows in tiles:
-            sides[h, rows, size:] = convolved(2, rows, h).astype(bf16)
-    for d in range(blocks):
-        rows = slice(d * block, (d + 1) * block)
-        for h in range(heads):
-            side = sides[h, rows, :]
-            if d:
-                done = solved_ref[h, : d * block, :]
-                side = (side.astype(f32) - dot(mixing[h, rows, : d * block], done)).astype(bf16)
-            solved_ref[h, rows, :] = dot(inverse[h, rows, :], side).astype(bf16)
-    pairs = []
+
+    def inverse_of(chosen):
+        corners = [(h, slice(d * block, (d + 1) * block)) for h in chosen for d in range(blocks)]
+        powers = [mixing[h, d, d] * near for h, d in corners]
+        totals = [power + eye for power in powers]
+        steps = (base - 1).bit_length() - 1
+        if steps:
+            powers = [dot(power, power).astype(bf16) for power in powers]
+        yield
+        for step in range(steps):
+            for n in range(len(corners)):
+                power, total = powers[n], totals[n]
+                if step < steps - 1:
+                    both = dot(jnp.concatenate([power, total], axis=0), power)
+                    powers[n], more = both[:block].astype(bf16), both[block:]
+                else:
+                    more = dot(total, power)
+                totals[n] = (total.astype(f32) + more).astype(bf16)
+            yield
+        for (h, d), total in zip(corners, totals):
+            inverse[h, d, :] = total
+        width = base
+        while width < block:
+            odd = range(width, block, 2 * width)
+            pair_mask = (at // width % 2 == 1) & (to // width == at // width - 1)
+            pair_mask = jnp.where(pair_mask, 1.0, 0.0).astype(bf16)
+            halves = []
+            for h, d in corners:
+                parts = [inverse[h, d.start + i : d.start + i + width, :] for i in odd]
+                picked = jnp.concatenate(parts, axis=0)
+                halves.append((picked, dot(picked, mixing[h, d, d] * pair_mask).astype(bf16)))
+            yield
+            for (h, d), (picked, part) in zip(corners, halves):
+                new = (picked.astype(f32) - dot(part, inverse[h, d, :])).astype(bf16)
+                for n, i in enumerate(odd):
+                    inverse[h, d.start + i : d.start + i + width, :] = new[
+                        n * width : (n + 1) * width
+                    ]
+            yield
+            width *= 2
+
+    def values():
+        for piece in pieces:
+            project(2, piece)
+            yield
+            for h in range(piece.start // size, piece.stop // size):
+                for rows in tiles:
+                    sides[h, rows, size:] = convolved(2, rows, h).astype(bf16)
+                yield
+
+    pairs = [None] * heads
     unit = row[:size, :size] == col[:size, :size]
-    for h in range(heads):
-        stop, fade = stops[h]
-        moved = dot(stop, solved_ref[h], ((0,), (0,)))
-        diagonal = jnp.where(unit, jnp.broadcast_to(fade, (size, size)), 0.0)
-        pairs.append(jnp.concatenate([diagonal - moved[:, :size], moved[:, size:]], axis=1))
+
+    def solve(chosen):
+        for d in range(blocks):
+            rows = slice(d * block, (d + 1) * block)
+            for h in chosen:
+                side = sides[h, rows, :]
+                if d:
+                    done = solved_ref[h, : d * block, :]
+                    side = side.astype(f32) - dot(mixing[h, rows, : d * block], done)
+                    side = side.astype(bf16)
+                solved_ref[h, rows, :] = dot(inverse[h, rows, :], side).astype(bf16)
+            yield
+        for h in chosen:
+            moved = dot(jnp.concatenate(stops[h], axis=0), solved_ref[h], ((0,), (0,)))
+            fade = jnp.exp(running_ref[count - 1 : count, lanes_of[h]])
+            diagonal = jnp.where(unit, jnp.broadcast_to(fade, (size, size)), 0.0)
+            pairs[h] = jnp.concatenate([diagonal - moved[:, :size], moved[:, size:]], axis=1)
+        yield
+
+    ready, last = range(half), range(half, heads)
+    early, late, value_steps, solving = inverse_of(ready), inverse_of(last), values(), solve(ready)
+    weave(tiles_of(0), projections([(c, piece) for piece in pieces[1:] for c in range(2)]))
+    for h in range(1, heads):
+        scores = scores_of(h - 1)
+        weave(tiles_of(h), scores, *([early] if h > half else []))
+        drain(scores)
+    weave(scores_of(heads - 1), early, value_steps)
+    weave(early, value_steps)
+    drain(early)
+    weave(late, itertools.chain(value_steps, solving))
+    drain(value_steps, solving, solve(last))
     upper = place("seq", 1) == 1
-    for h in range(heads // 2):
-        low, high = pairs[h], pairs[heads // 2 + h]
+    for h in range(half):
+        low, high = pairs[h], pairs[half + h]
         group, at = divmod(h, own_refs[0].shape[0])
         own_refs[group][at] = jnp.where(upper, high, low).astype(bf16)
         other_refs[group][at] = jnp.where(upper, low, high).astype(bf16)
 
 
-def front(rims, slabs, fetched, loaded, weight, size):
+def front(rims, slabs, loaded, weight, size):
     slab_count, slab_rows = 1 + len(slabs), slabs[0].shape[0]
     count = slab_count * slab_rows
     _, width, channels = weight.shape
     heads, block = channels // size, math.gcd(count, 128)
-    buffers = [pltpu.SMEM(loaded[0].shape, f32)]
-    buffers += [pltpu.VMEM(part.shape, part.dtype) for part in loaded[1:]]
     return vmem_call(
         functools.partial(front_body, slab_count),
         (
@@ -337,11 +377,10 @@
             jax.ShapeDtypeStruct((heads, count, 2 * size), bf16),
             jax.ShapeDtypeStruct((heads, count, count), bf16),
             jax.ShapeDtypeStruct((heads, count, size), bf16),
-            jax.ShapeDtypeStruct((count, fetched[2].shape[1] // 2), bf16),
+            jax.ShapeDtypeStruct((count, loaded[0].shape[1] // 2), bf16),
         ),
-        (*rims, *slabs, *fetched, *loaded, weight),
+        (*rims, *slabs, *loaded, weight),
         scratch=[
-            *buffers,
             pltpu.VMEM((width, channels), bf16),
             pltpu.VMEM((RIM + count, width), bf16),
             pltpu.VMEM((3 * heads, RIM + count, size), f32),
@@ -350,9 +389,9 @@
             pltpu.VMEM((heads, count, count), bf16),
             pltpu.VMEM((heads, count, block), bf16),
             pltpu.VMEM((heads, count, 2 * size), bf16),
-            pltpu.SemaphoreType.DMA((4 + len(column_pieces(channels)),)),
+            pltpu.SemaphoreType.DMA((len(column_pieces(channels)),)),
         ],
-        hbm=1 + len(loaded),
+        hbm=1,
         grant=24,
         flops=2 * count * width * channels * 4,
         moved=2 * 4 * width * channels,
@@ -527,11 +566,13 @@
     channels = heads * size
     devices = lax.axis_size("head")
     weight = qkv_weight.transpose(1, 0, 2)
-    fetched = load(hidden_in, decay_down, gate_down, beta_weight.T, weight)
-    slabs, rims, fetched = gathered(hidden_in, fetched)
-    *pairs, solved, attend, start, gate_low = front(
-        rims, slabs, fetched, (decay_log, decay_up, dt_bias[None], conv_weight), weight, size
-    )
+    loaded = load(
+        (decay_down, gate_down),
+        (hidden_in, beta_weight.T, decay_log[None], decay_up, dt_bias[None], conv_weight),
+        weight,
+    )
+    slabs, rims, loaded = gathered(hidden_in, loaded)
+    *pairs, solved, attend, start, gate_low = front(rims, slabs, loaded, weight, size)
     count = start.shape[1]
     raised, output_rows, out_gate = vmem_call(
         rows_body,

time: 54.6 us -> 53.6 us (0.982)
  waiting for transfers between devices: 19.5 us -> 18 us
  starting transfers between devices: 19.1 us -> 20.1 us
    ppermute x15, waiting for transfers between devices: 19.5 us -> 18 us  [swapped(): lax.ppermute(block, axis, [(i, i ^ bit) for i in range(lax.axis_size(axis...]
    ppermute x15, starting transfers between devices: 17.7 us -> 18.8 us  [swapped(): lax.ppermute(block, axis, [(i, i ^ bit) for i in range(lax.axis_size(axis...]
where the time goes in v11:
time: 53.6 us; the launch traced here: 53.4 us
  starting transfers between devices  20.1 us (38%)
  waiting for transfers between devices  18 us (34%)
  Pallas kernels  13.4 us (25%)
  other arithmetic  0.88 us (2%)
  local copies, waits for them, and re-layouts  0.82 us (2%)
    ppermute x15, starting transfers between devices, swapped(): lax.ppermute(block, axis, [(i, i ^ bit) for i in range(lax.axis_size(axis...  18.8 us
    ppermute x15, waiting for transfers between devices, swapped(): lax.ppermute(block, axis, [(i, i ^ bit) for i in range(lax.axis_size(axis...  18 us
    pallas_call x14, Pallas kernels, vmem_call(): pl.pallas_call(body, out_shape=out_shape, in_specs=[pl.BlockSpec(memory_s...  13.4 us
    ppermute x2, starting transfers between devices, gathered(): lax.ppermute(tail, ('seq', 'head'), rim_route(target))  1.32 us
  transfers between devices with their start and end apart: 17, of which 9 were waited for; matrix products, arithmetic and copies ran while one was open for 2% of the time, Pallas kernels for 10%

profile of v11, /device:TPU:0, one launch (start us, length us, event | category | flops | bytes accessed | tf_op | source)
XLA Modules:
  0.0 53.4 jit_solution(5762271614718326482)
XLA Ops:
  0.0 2.9 %collective-permute-start = (bf16[64,2304]{1,0:T(8,128)(2,1)}, bf16[64,2304]{1,0:T(8,128)(2,1)S(1)}, u32[]{:S(2)}, u32[]{:S(2)}) collective-permute-start(bf16[64,2304]{1,0:T(8,128)(2,1)} %refs_2_.1), channel_id=1, source_target_pairs={{0,2},{1,3},{2,0},{3,1},{4,6},{5,7},{6,4},{7,5},{8,10},{9,11},{10,... | collective-permute-start | bytes 884744 | tf_op jit(solution)/shard_map/ppermute | solution.py:25
  2.9 0.8 %slice.3 = bf16[8,2304]{1,0:T(8,128)(2,1)S(1)} slice(bf16[64,2304]{1,0:T(8,128)(2,1)} %refs_2_.1), slice={[56:64], [0:2304]} | slice | bytes 73728 | tf_op jit(solution)/shard_map/slice | solution.py:55
  3.7 0.7 %collective-permute-start.2 = (bf16[8,2304]{1,0:T(8,128)(2,1)S(1)}, bf16[8,2304]{1,0:T(8,128)(2,1)S(1)}, u32[]{:S(2)}, u32[]{:S(2)}) collective-permute-start(bf16[8,2304]{1,0:T(8,128)(2,1)S(1)} %slice.3), channel_id=1, source_target_pairs={{3,5},{7,9},{11,13},{15,17},{19,21},{23,25},{27,29}} | collective-permute-start | bytes 110600 | tf_op jit(solution)/shard_map/ppermute | solution.py:57
  4.4 0.7 %collective-permute-start.1 = (bf16[8,2304]{1,0:T(8,128)(2,1)S(1)}, bf16[8,2304]{1,0:T(8,128)(2,1)S(1)}, u32[]{:S(2)}, u32[]{:S(2)}) collective-permute-start(bf16[8,2304]{1,0:T(8,128)(2,1)S(1)} %slice.3), channel_id=1, source_target_pairs={{3,6},{7,10},{11,14},{15,18},{19,22},{23,26},{27,30}} | collective-permute-start | bytes 110600 | tf_op jit(solution)/shard_map/ppermute | solution.py:57
  5.1 0.1 collective-permute-start.4
  5.2 3.0 %shard_map.118 = (bf16[2304,256]{1,0:T(8,128)(2,1)S(1)}, bf16[64,2304]{1,0:T(8,128)(2,1)S(1)}, bf16[4,2304]{1,0:T(4,128)(2,1)S(1)}, f32[1,4]{1,0:T(1,128)S(1)}, ...) custom-call(bf16[2304,128]{1,0:T(8,128)(2,1)} %refs_0_.1, ...), custom_call_target="tpu_custom_call" | custom-call | tf_op jit(solution)/shard_map/pallas_call | solution.py:75
  8.2 0.0 collective-permute-done.2.refs_1_
  8.2 0.0 collective-permute-done.1.refs_0_
  8.2 2.3 %collective-permute-done.refs_3_ = bf16[64,2304]{1,0:T(8,128)(2,1)S(1)} collective-permute-done((bf16[64,2304]{1,0:T(8,128)(2,1)}, bf16[64,2304]{1,0:T(8,128)(2,1)S(1)}, u32[]{:S(2)}, u32[]{:S(2)}) %collective-permute-start) | collective-permute-done | bytes 294944 | tf_op jit(solution)/shard_map/ppermute | solution.py:25
  10.6 0.0 collective-permute-start.5
  10.6 0.0 copy-start.1
  10.6 0.0 copy-start
  10.6 0.0 copy-start.2
  10.6 0.6 %collective-permute-start.3 = (bf16[16,2304]{1,0:T(8,128)(2,1)S(1)}, bf16[16,2304]{1,0:T(8,128)(2,1)S(1)}, u32[]{:S(2)}, u32[]{:S(2)}) collective-permute-start(bf16[16,2304]{1,0:T(8,128)(2,1)S(1)} %shard_map.119.refs_0_), channel_id=1, source_target_pairs={{0,1},{1,0},{2,3},{3,2},{4,5},{5,4},{6,7},{7,6},{8,9},{9,8},{10,11... | collective-permute-start | bytes 221192 | tf_op jit(solution)/shard_map/ppermute | solution.py:25
  11.2 0.0 collective-permute-done.4.refs_2_
  11.2 1.1 %collective-permute-done.3.refs_1_ = bf16[16,2304]{1,0:T(8,128)(2,1)S(1)} collective-permute-done((bf16[16,2304]{1,0:T(8,128)(2,1)S(1)}, bf16[16,2304]{1,0:T(8,128)(2,1)S(1)}, u32[]{:S(2)}, u32[]{:S(2)}) %collective-permute-start.3) | collective-permute-done | bytes 73760 | tf_op jit(solution)/shard_map/ppermute | solution.py:25
  12.2 0.0 collective-permute-done.5.refs_4_
  12.2 7.3 %shard_map.120 = (bf16[1,128,256]{2,1,0:T(8,128)(2,1)S(1)}, bf16[1,128,256]{2,1,0:T(8,128)(2,1)S(1)}, bf16[1,128,256]{2,1,0:T(8,128)(2,1)S(1)}, bf16[1,128,256]{...) custom-call(bf16[16,2304]{1,0:T(8,128)(2,1)S(1)} %shard_map.119.refs, ...), custom_call_target="tpu_custom_call" | custom-call | flops 2415919104 | bytes 9437184 | tf_op jit(solution)/shard_map/pallas_call | solution.py:75
  19.5 1.4 %collective-permute-start.6 = (bf16[1,128,256]{2,1,0:T(8,128)(2,1)S(1)}, bf16[1,128,256]{2,1,0:T(8,128)(2,1)S(1)}, u32[]{:S(2)}, u32[]{:S(2)}) collective-permute-start(bf16[1,128,256]{2,1,0:T(8,128)(2,1)S(1)} %get-tuple-element.63), channel_id=1, source_target_pairs={{0,4},{4,0},{8,12},{12,8},{16,20},{20,16},{24,28},{28,24},{1,5},{5... | collective-permute-start | bytes 196616 | tf_op jit(solution)/shard_map/ppermute | solution.py:25
  21.0 0.6 %collective-permute-start.9 = (bf16[1,128,256]{2,1,0:T(8,128)(2,1)S(1)}, bf16[1,128,256]{2,1,0:T(8,128)(2,1)S(1)}, u32[]{:S(2)}, u32[]{:S(2)}) collective-permute-start(bf16[1,128,256]{2,1,0:T(8,128)(2,1)S(1)} %get-tuple-element.66), channel_id=1, source_target_pairs={{0,4},{4,0},{8,12},{12,8},{16,20},{20,16},{24,28},{28,24},{1,5},{5... | collective-permute-start | bytes 196616 | tf_op jit(solution)/shard_map/ppermute | solution.py:25
  21.6 2.6 %collective-permute-done.6.far_ref.partner_ref = bf16[1,128,256]{2,1,0:T(8,128)(2,1)S(1)} collective-permute-done((bf16[1,128,256]{2,1,0:T(8,128)(2,1)S(1)}, bf16[1,128,256]{2,1,0:T(8,128)(2,1)S(1)}, u32[]{:S(2)}, u32[]{:S(2)}) %collective-permute-start.6) | collective-permute-done | bytes 65568 | tf_op jit(solution)/shard_map/ppermute | solution.py:25
  24.2 0.2 shard_map.121.own_ref
  24.4 1.8 %collective-permute-start.7 = (bf16[1,128,256]{2,1,0:T(8,128)(2,1)S(1)}, bf16[1,128,256]{2,1,0:T(8,128)(2,1)S(1)}, u32[]{:S(2)}, u32[]{:S(2)}) collective-permute-start(bf16[1,128,256]{2,1,0:T(8,128)(2,1)S(1)} %shard_map.121.own_ref), channel_id=1, source_target_pairs={{0,8},{4,12},{8,0},{12,4},{16,24},{20,28},{24,16},{28,20},{1,9},{5... | collective-permute-start | bytes 196616 | tf_op jit(solution)/shard_map/ppermute | solution.py:25
  26.2 0.0 collective-permute-done.9.far_ref.partner_ref
  26.2 0.2 shard_map.125.own_ref
  26.4 1.1 %collective-permute-start.10 = (bf16[1,128,256]{2,1,0:T(8,128)(2,1)S(1)}, bf16[1,128,256]{2,1,0:T(8,128)(2,1)S(1)}, u32[]{:S(2)}, u32[]{:S(2)}) collective-permute-start(bf16[1,128,256]{2,1,0:T(8,128)(2,1)S(1)} %shard_map.125.own_ref), channel_id=1, source_target_pairs={{0,8},{4,12},{8,0},{12,4},{16,24},{20,28},{24,16},{28,20},{1,9},{5... | collective-permute-start | bytes 196616 | tf_op jit(solution)/shard_map/ppermute | solution.py:25
  27.5 1.5 %collective-permute-done.7.far_ref = bf16[1,128,256]{2,1,0:T(8,128)(2,1)S(1)} collective-permute-done((bf16[1,128,256]{2,1,0:T(8,128)(2,1)S(1)}, bf16[1,128,256]{2,1,0:T(8,128)(2,1)S(1)}, u32[]{:S(2)}, u32[]{:S(2)}) %collective-permute-start.7) | collective-permute-done | bytes 65568 | tf_op jit(solution)/shard_map/ppermute | solution.py:25
  28.9 0.1 shard_map.123
  29.1 2.6 %collective-permute-start.8 = (bf16[1,128,128]{2,1,0:T(8,128)(2,1)S(1)}, bf16[1,128,128]{2,1,0:T(8,128)(2,1)S(1)}, u32[]{:S(2)}, u32[]{:S(2)}) collective-permute-start(bf16[1,128,128]{2,1,0:T(8,128)(2,1)S(1)} %shard_map.123), channel_id=1, source_target_pairs={{0,16},{4,20},{8,24},{12,28},{16,0},{20,4},{24,8},{28,12},{1,17},{... | collective-permute-start | bytes 98312 | tf_op jit(solution)/shard_map/ppermute | solution.py:25
  31.8 0.0 collective-permute-done.10.far_ref
  31.8 0.2 shard_map.127
  31.9 1.6 %collective-permute-start.11 = (bf16[1,128,128]{2,1,0:T(8,128)(2,1)S(1)}, bf16[1,128,128]{2,1,0:T(8,128)(2,1)S(1)}, u32[]{:S(2)}, u32[]{:S(2)}) collective-permute-start(bf16[1,128,128]{2,1,0:T(8,128)(2,1)S(1)} %shard_map.127), channel_id=1, source_target_pairs={{0,16},{4,20},{8,24},{12,28},{16,0},{20,4},{24,8},{28,12},{1,17},{... | collective-permute-start | bytes 98312 | tf_op jit(solution)/shard_map/ppermute | solution.py:25
  33.6 0.7 %collective-permute-done.8.far_ref = bf16[1,128,128]{2,1,0:T(8,128)(2,1)S(1)} collective-permute-done((bf16[1,128,128]{2,1,0:T(8,128)(2,1)S(1)}, bf16[1,128,128]{2,1,0:T(8,128)(2,1)S(1)}, u32[]{:S(2)}, u32[]{:S(2)}) %collective-permute-start.8) | collective-permute-done | bytes 32800 | tf_op jit(solution)/shard_map/ppermute | solution.py:25
  34.3 0.3 shard_map.124
  34.6 1.7 %collective-permute-start.12 = (bf16[1,128,128]{2,1,0:T(8,128)(2,1)S(1)}, bf16[1,128,128]{2,1,0:T(8,128)(2,1)S(1)}, u32[]{:S(2)}, u32[]{:S(2)}) collective-permute-start(bf16[1,128,128]{2,1,0:T(8,128)(2,1)S(1)} %get-tuple-element.68), channel_id=1, source_target_pairs={{0,4},{4,0},{8,12},{12,8},{16,20},{20,16},{24,28},{28,24},{1,5},{5... | collective-permute-start | bytes 98312 | tf_op jit(solution)/shard_map/ppermute | solution.py:25
  36.3 0.5 collective-permute-done.11.far_ref
  36.8 0.3 shard_map.128
  37.1 2.0 %collective-permute-start.13 = (bf16[1,128,128]{2,1,0:T(8,128)(2,1)S(1)}, bf16[1,128,128]{2,1,0:T(8,128)(2,1)S(1)}, u32[]{:S(2)}, u32[]{:S(2)}) collective-permute-start(bf16[1,128,128]{2,1,0:T(8,128)(2,1)S(1)} %get-tuple-element.69), channel_id=1, source_target_pairs={{0,4},{4,0},{8,12},{12,8},{16,20},{20,16},{24,28},{28,24},{1,5},{5... | collective-permute-start | bytes 98312 | tf_op jit(solution)/shard_map/ppermute | solution.py:25
  39.1 0.0 copy-done.1
  39.1 0.4 shard_map.129
  39.5 0.0 collective-permute-done.12.refs_2_
  39.5 1.6 %collective-permute-done.13.refs_3_ = bf16[1,128,128]{2,1,0:T(8,128)(2,1)S(1)} collective-permute-done((bf16[1,128,128]{2,1,0:T(8,128)(2,1)S(1)}, bf16[1,128,128]{2,1,0:T(8,128)(2,1)S(1)}, u32[]{:S(2)}, u32[]{:S(2)}) %collective-permute-start.13) | collective-permute-done | bytes 32800 | tf_op jit(solution)/shard_map/ppermute | solution.py:25
  41.1 0.0 copy-done
  41.1 0.0 copy-done.2
  41.1 0.7 %shard_map.131 = (f32[64,2304]{1,0:T(8,128)S(1)}, bf16[64,2304]{1,0:T(8,128)(2,1)S(1)}) custom-call(bf16[1,128,128]{2,1,0:T(8,128)(2,1)S(1)} %get-tuple-element.64.refs_0_, bf16[1,128,128]{2,1,0:T(8,128)(2,1)S(1)} %get-tuple-element.67.refs_1_, bf16[1,128,128]{2,1,0:T(8,128)(2,1)S(1)} %collective-permute-done.12.refs_2_, ...), custom_call_target="tpu_custom_call" | custom-call | flops 301989888 | bytes 2359296 | tf_op jit(solution)/shard_map/pallas_call | solution.py:75
  41.8 0.1 collective-permute-start.15
  41.9 0.7 %shard_map.130 = (f32[64,2304]{1,0:T(8,128)S(1)}, bf16[64,2304]{1,0:T(8,128)(2,1)S(1)}) custom-call(bf16[1,128,128]{2,1,0:T(8,128)(2,1)S(1)} %get-tuple-element.64.refs_0_, bf16[1,128,128]{2,1,0:T(8,128)(2,1)S(1)} %get-tuple-element.67.refs_1_, bf16[1,128,128]{2,1,0:T(8,128)(2,1)S(1)} %collective-permute-done.12.refs_2_, ...), custom_call_target="tpu_custom_call" | custom-call | flops 301989888 | bytes 2359296 | tf_op jit(solution)/shard_map/pallas_call | solution.py:75
  42.7 0.6 %collective-permute-start.14 = (bf16[64,2304]{1,0:T(8,128)(2,1)S(1)}, bf16[64,2304]{1,0:T(8,128)(2,1)S(1)}, u32[]{:S(2)}, u32[]{:S(2)}) collective-permute-start(bf16[64,2304]{1,0:T(8,128)(2,1)S(1)} %get-tuple-element.78), channel_id=1, source_target_pairs={{0,1},{1,0},{2,3},{3,2},{4,5},{5,4},{6,7},{7,6},{8,9},{9,8},{10,11... | collective-permute-start | bytes 884744 | tf_op jit(solution)/shard_map/ppermute | solution.py:25
  43.2 0.3 collective-permute-done.15
  43.5 0.1 convert_add_fusion
  43.5 1.7 %collective-permute-start.16 = (bf16[64,2304]{1,0:T(8,128)(2,1)S(1)}, bf16[64,2304]{1,0:T(8,128)(2,1)S(1)}, u32[]{:S(2)}, u32[]{:S(2)}) collective-permute-start(bf16[64,2304]{1,0:T(8,128)(2,1)S(1)} %convert_add_fusion), channel_id=1, source_target_pairs={{0,2},{1,3},{2,0},{3,1},{4,6},{5,7},{6,4},{7,5},{8,10},{9,11},{10,... | collective-permute-start | bytes 884744 | tf_op jit(solution)/shard_map/ppermute | solution.py:25
  45.2 0.0 collective-permute-done.14
  45.2 0.1 convert_add_fusion.1
  45.3 7.4 %collective-permute-done.16 = bf16[64,2304]{1,0:T(8,128)(2,1)S(1)} collective-permute-done((bf16[64,2304]{1,0:T(8,128)(2,1)S(1)}, bf16[64,2304]{1,0:T(8,128)(2,1)S(1)}, u32[]{:S(2)}, u32[]{:S(2)}) %collective-permute-start.16) | collective-permute-done | bytes 294944 | tf_op jit(solution)/shard_map/ppermute | solution.py:25
  52.6 0.8 %add_convert_fusion = bf16[64,2304]{1,0:T(8,128)(2,1)} fusion(f32[64,2304]{1,0:T(8,128)S(1)} %convert_add_fusion.1, bf16[64,2304]{1,0:T(8,128)(2,1)S(1)} %collective-permute-done.16), kind=kLoop, calls=%fused_computation | loop fusion | flops 442368 | bytes 1179648 | tf_op jit(solution)/shard_map/convert_element_type | solution.py:605
  (3 shorter events, 0.1 us)
Async XLA Ops:
  0.0 10.5 %collective-permute-start = (bf16[64,2304]{1,0:T(8,128)(2,1)}, bf16[64,2304]{1,0:T(8,128)(2,1)S(1)}, u32[]{:S(2)}, u32[]{:S(2)}) collective-permute-start(bf16[64,2304]{1,0:T(8,128)(2,1)} %refs_2_.1), channel_id=1, source_target_pairs={{0,2},{1,3},{2,0},{3,1},{4,6},{5,7},{6,4},{7,5},{8,10},{9,11},{10,... | collective-permute-start | bytes 884744 | tf_op jit(solution)/shard_map/ppermute | solution.py:25
  3.7 4.5 %collective-permute-start.2 = (bf16[8,2304]{1,0:T(8,128)(2,1)S(1)}, bf16[8,2304]{1,0:T(8,128)(2,1)S(1)}, u32[]{:S(2)}, u32[]{:S(2)}) collective-permute-start(bf16[8,2304]{1,0:T(8,128)(2,1)S(1)} %slice.3), channel_id=1, source_target_pairs={{3,5},{7,9},{11,13},{15,17},{19,21},{23,25},{27,29}} | collective-permute-start | bytes 110600 | tf_op jit(solution)/shard_map/ppermute | solution.py:57
  4.4 3.8 %collective-permute-start.1 = (bf16[8,2304]{1,0:T(8,128)(2,1)S(1)}, bf16[8,2304]{1,0:T(8,128)(2,1)S(1)}, u32[]{:S(2)}, u32[]{:S(2)}) collective-permute-start(bf16[8,2304]{1,0:T(8,128)(2,1)S(1)} %slice.3), channel_id=1, source_target_pairs={{3,6},{7,10},{11,14},{15,18},{19,22},{23,26},{27,30}} | collective-permute-start | bytes 110600 | tf_op jit(solution)/shard_map/ppermute | solution.py:57
  5.1 6.1 %collective-permute-start.4 = (bf16[64,2304]{1,0:T(8,128)(2,1)}, bf16[64,2304]{1,0:T(8,128)(2,1)S(1)}, u32[]{:S(2)}, u32[]{:S(2)}) collective-permute-start(bf16[64,2304]{1,0:T(8,128)(2,1)} %refs_2_.1), channel_id=1, source_target_pairs={{0,1},{1,0},{2,3},{3,2},{4,5},{5,4},{6,7},{7,6},{8,9},{9,8},{10,11... | collective-permute-start | bytes 884744 | tf_op jit(solution)/shard_map/ppermute | solution.py:25
  10.6 1.7 %collective-permute-start.5 = (bf16[64,2304]{1,0:T(8,128)(2,1)S(1)}, bf16[64,2304]{1,0:T(8,128)(2,1)S(1)}, u32[]{:S(2)}, u32[]{:S(2)}) collective-permute-start(bf16[64,2304]{1,0:T(8,128)(2,1)S(1)} %collective-permute-done.refs_3_), channel_id=1, source_target_pairs={{0,1},{1,0},{2,3},{3,2},{4,5},{5,4},{6,7},{7,6},{8,9},{9,8},{10,11... | collective-permute-start | bytes 884744 | tf_op jit(solution)/shard_map/ppermute | solution.py:25
  10.6 28.5 %copy-start.1 = (bf16[128,512]{1,0:T(8,128)(2,1)S(1)}, bf16[128,512]{1,0:T(8,128)(2,1)}, u32[]{:S(2)}) copy-start(bf16[128,512]{1,0:T(8,128)(2,1)} %up_ref.1) | copy-start | bytes 393220
  10.6 30.5 %copy-start = (bf16[512,2304]{1,0:T(8,128)(2,1)S(1)}, bf16[512,2304]{1,0:T(8,128)(2,1)}, u32[]{:S(2)}) copy-start(bf16[512,2304]{1,0:T(8,128)(2,1)} %refs_8_.3) | copy-start | bytes 7077892
  10.6 30.5 %copy-start.2 = (f32[128]{0:T(128)S(1)}, f32[128]{0:T(128)}, u32[]{:S(2)}) copy-start(f32[128]{0:T(128)} %param.22) | copy-start | bytes 1540
  10.6 1.6 %collective-permute-start.3 = (bf16[16,2304]{1,0:T(8,128)(2,1)S(1)}, bf16[16,2304]{1,0:T(8,128)(2,1)S(1)}, u32[]{:S(2)}, u32[]{:S(2)}) collective-permute-start(bf16[16,2304]{1,0:T(8,128)(2,1)S(1)} %shard_map.119.refs_0_), channel_id=1, source_target_pairs={{0,1},{1,0},{2,3},{3,2},{4,5},{5,4},{6,7},{7,6},{8,9},{9,8},{10,11... | collective-permute-start | bytes 221192 | tf_op jit(solution)/shard_map/ppermute | solution.py:25
  19.5 4.7 %collective-permute-start.6 = (bf16[1,128,256]{2,1,0:T(8,128)(2,1)S(1)}, bf16[1,128,256]{2,1,0:T(8,128)(2,1)S(1)}, u32[]{:S(2)}, u32[]{:S(2)}) collective-permute-start(bf16[1,128,256]{2,1,0:T(8,128)(2,1)S(1)} %get-tuple-element.63), channel_id=1, source_target_pairs={{0,4},{4,0},{8,12},{12,8},{16,20},{20,16},{24,28},{28,24},{1,5},{5... | collective-permute-start | bytes 196616 | tf_op jit(solution)/shard_map/ppermute | solution.py:25
  21.0 5.2 %collective-permute-start.9 = (bf16[1,128,256]{2,1,0:T(8,128)(2,1)S(1)}, bf16[1,128,256]{2,1,0:T(8,128)(2,1)S(1)}, u32[]{:S(2)}, u32[]{:S(2)}) collective-permute-start(bf16[1,128,256]{2,1,0:T(8,128)(2,1)S(1)} %get-tuple-element.66), channel_id=1, source_target_pairs={{0,4},{4,0},{8,12},{12,8},{16,20},{20,16},{24,28},{28,24},{1,5},{5... | collective-permute-start | bytes 196616 | tf_op jit(solution)/shard_map/ppermute | solution.py:25
  24.4 4.5 %collective-permute-start.7 = (bf16[1,128,256]{2,1,0:T(8,128)(2,1)S(1)}, bf16[1,128,256]{2,1,0:T(8,128)(2,1)S(1)}, u32[]{:S(2)}, u32[]{:S(2)}) collective-permute-start(bf16[1,128,256]{2,1,0:T(8,128)(2,1)S(1)} %shard_map.121.own_ref), channel_id=1, source_target_pairs={{0,8},{4,12},{8,0},{12,4},{16,24},{20,28},{24,16},{28,20},{1,9},{5... | collective-permute-start | bytes 196616 | tf_op jit(solution)/shard_map/ppermute | solution.py:25
  26.4 5.4 %collective-permute-start.10 = (bf16[1,128,256]{2,1,0:T(8,128)(2,1)S(1)}, bf16[1,128,256]{2,1,0:T(8,128)(2,1)S(1)}, u32[]{:S(2)}, u32[]{:S(2)}) collective-permute-start(bf16[1,128,256]{2,1,0:T(8,128)(2,1)S(1)} %shard_map.125.own_ref), channel_id=1, source_target_pairs={{0,8},{4,12},{8,0},{12,4},{16,24},{20,28},{24,16},{28,20},{1,9},{5... | collective-permute-start | bytes 196616 | tf_op jit(solution)/shard_map/ppermute | solution.py:25
  29.1 5.2 %collective-permute-start.8 = (bf16[1,128,128]{2,1,0:T(8,128)(2,1)S(1)}, bf16[1,128,128]{2,1,0:T(8,128)(2,1)S(1)}, u32[]{:S(2)}, u32[]{:S(2)}) collective-permute-start(bf16[1,128,128]{2,1,0:T(8,128)(2,1)S(1)} %shard_map.123), channel_id=1, source_target_pairs={{0,16},{4,20},{8,24},{12,28},{16,0},{20,4},{24,8},{28,12},{1,17},{... | collective-permute-start | bytes 98312 | tf_op jit(solution)/shard_map/ppermute | solution.py:25
  31.9 4.9 %collective-permute-start.11 = (bf16[1,128,128]{2,1,0:T(8,128)(2,1)S(1)}, bf16[1,128,128]{2,1,0:T(8,128)(2,1)S(1)}, u32[]{:S(2)}, u32[]{:S(2)}) collective-permute-start(bf16[1,128,128]{2,1,0:T(8,128)(2,1)S(1)} %shard_map.127), channel_id=1, source_target_pairs={{0,16},{4,20},{8,24},{12,28},{16,0},{20,4},{24,8},{28,12},{1,17},{... | collective-permute-start | bytes 98312 | tf_op jit(solution)/shard_map/ppermute | solution.py:25
  34.6 4.8 %collective-permute-start.12 = (bf16[1,128,128]{2,1,0:T(8,128)(2,1)S(1)}, bf16[1,128,128]{2,1,0:T(8,128)(2,1)S(1)}, u32[]{:S(2)}, u32[]{:S(2)}) collective-permute-start(bf16[1,128,128]{2,1,0:T(8,128)(2,1)S(1)} %get-tuple-element.68), channel_id=1, source_target_pairs={{0,4},{4,0},{8,12},{12,8},{16,20},{20,16},{24,28},{28,24},{1,5},{5... | collective-permute-start | bytes 98312 | tf_op jit(solution)/shard_map/ppermute | solution.py:25
  37.1 4.0 %collective-permute-start.13 = (bf16[1,128,128]{2,1,0:T(8,128)(2,1)S(1)}, bf16[1,128,128]{2,1,0:T(8,128)(2,1)S(1)}, u32[]{:S(2)}, u32[]{:S(2)}) collective-permute-start(bf16[1,128,128]{2,1,0:T(8,128)(2,1)S(1)} %get-tuple-element.69), channel_id=1, source_target_pairs={{0,4},{4,0},{8,12},{12,8},{16,20},{20,16},{24,28},{28,24},{1,5},{5... | collective-permute-start | bytes 98312 | tf_op jit(solution)/shard_map/ppermute | solution.py:25
  41.8 1.6 %collective-permute-start.15 = (bf16[64,2304]{1,0:T(8,128)(2,1)S(1)}, bf16[64,2304]{1,0:T(8,128)(2,1)S(1)}, u32[]{:S(2)}, u32[]{:S(2)}) collective-permute-start(bf16[64,2304]{1,0:T(8,128)(2,1)S(1)} %get-tuple-element.80), channel_id=1, source_target_pairs={{0,1},{1,0},{2,3},{3,2},{4,5},{5,4},{6,7},{7,6},{8,9},{9,8},{10,11... | collective-permute-start | bytes 884744 | tf_op jit(solution)/shard_map/ppermute | solution.py:25
  42.7 2.6 %collective-permute-start.14 = (bf16[64,2304]{1,0:T(8,128)(2,1)S(1)}, bf16[64,2304]{1,0:T(8,128)(2,1)S(1)}, u32[]{:S(2)}, u32[]{:S(2)}) collective-permute-start(bf16[64,2304]{1,0:T(8,128)(2,1)S(1)} %get-tuple-element.78), channel_id=1, source_target_pairs={{0,1},{1,0},{2,3},{3,2},{4,5},{5,4},{6,7},{7,6},{8,9},{9,8},{10,11... | collective-permute-start | bytes 884744 | tf_op jit(solution)/shard_map/ppermute | solution.py:25
  43.5 9.1 %collective-permute-start.16 = (bf16[64,2304]{1,0:T(8,128)(2,1)S(1)}, bf16[64,2304]{1,0:T(8,128)(2,1)S(1)}, u32[]{:S(2)}, u32[]{:S(2)}) collective-permute-start(bf16[64,2304]{1,0:T(8,128)(2,1)S(1)} %convert_add_fusion), channel_id=1, source_target_pairs={{0,2},{1,3},{2,0},{3,1},{4,6},{5,7},{6,4},{7,5},{8,10},{9,11},{10,... | collective-permute-start | bytes 884744 | tf_op jit(solution)/shard_map/ppermute | solution.py:25

commit v12 on v10

--- a/solution.py
+++ b/solution.py
@@ -482,46 +482,54 @@
     return keep, swapped(send, "seq", 1)
 
 
-def back_body(places, *refs):
+def norm_body(places, *refs):
     own_refs, other_refs, refs = refs[:GROUPS], refs[GROUPS : 2 * GROUPS], refs[2 * GROUPS :]
-    raised_ref, output_ref, gate_ref, gain_ref, weight_ref, keep_ref, *rest = refs
-    normed = rest[-1]
+    raised_ref, output_ref, gate_ref, gain_ref, *normed_refs = refs
     size = gain_ref.shape[1]
-    slab_rows = keep_ref.shape[0]
+    slab_rows = normed_refs[0].shape[0]
     share = own_refs[0].shape[0]
     half = GROUPS * share
     upper = place("seq", 1) == 1
-    for k, away in enumerate(places):
-        rows = pl.ds(pl.multiple_of((place("head") ^ away) * slab_rows, 16), slab_rows)
-        for h in range(raised_ref.shape[0]):
-            lanes = slice(h * size, (h + 1) * size)
-            group, at = divmod(h % half, share)
-            own, other = own_refs[group][at], other_refs[group][at]
-            state = jnp.where(upper, other, own) if h < half else jnp.where(upper, own, other)
+    for h in range(raised_ref.shape[0]):
+        lanes = slice(h * size, (h + 1) * size)
+        group, at = divmod(h % half, share)
+        own, other = own_refs[group][at], other_refs[group][at]
+        state = jnp.where(upper, other, own) if h < half else jnp.where(upper, own, other)
+        for away, normed_ref in zip(places, normed_refs):
+            rows = pl.ds(pl.multiple_of((place("head") ^ away) * slab_rows, 16), slab_rows)
             attended = dot(raised_ref[h, rows, :], state) + output_ref[rows, lanes]
             power = jnp.sum(attended * attended, -1, keepdims=True) * (1.0 / size)
-            normed[k * slab_rows : (k + 1) * slab_rows, lanes] = (
+            normed_ref[:, lanes] = (
                 attended * lax.rsqrt(power + 1e-05) * gain_ref[...] * gate_ref[rows, lanes]
             ).astype(bf16)
-    total = dot(normed[...], weight_ref[...])
-    keep_ref[...] = total[:slab_rows]
-    if len(rest) > 1:
-        rest[0][...] = total[slab_rows:].astype(bf16)
-
-
-def back(places, states, raised, output_rows, out_gate, gain, weight, slab_rows):
-    slab_count, width = len(places), weight.shape[1]
-    shapes = [jax.ShapeDtypeStruct((slab_rows, width), f32)]
-    if slab_count > 1:
-        shapes.append(jax.ShapeDtypeStruct((slab_rows, width), bf16))
+
+
+def normed_rows(places, states, raised, output_rows, out_gate, gain, slab_rows):
+    shape = jax.ShapeDtypeStruct((slab_rows, output_rows.shape[1]), bf16)
     return vmem_call(
-        functools.partial(back_body, places),
-        shapes,
-        (*states, raised, output_rows, out_gate, gain, weight),
-        scratch=[pltpu.VMEM((slab_count * slab_rows, weight.shape[0]), bf16)],
-        grant=10,
-        flops=2 * slab_count * slab_rows * weight.shape[0] * width,
-        moved=2 * weight.shape[0] * width,
+        functools.partial(norm_body, places),
+        [shape] * len(places),
+        (*states, raised, output_rows, out_gate, gain),
+        grant=6,
+        flops=2 * len(places) * slab_rows * output_rows.shape[1] * gain.shape[1],
+        moved=8 * output_rows.size,
+    )
+
+
+def product_body(one_ref, two_ref, own_ref, other_ref, out_ref):
+    total = dot(one_ref[...], own_ref[...]) + dot(two_ref[...], other_ref[...])
+    out_ref[...] = total.astype(out_ref.dtype)
+
+
+def product_rows(one, two, own_weight, other_weight, dtype):
+    rows, width = one.shape[0], own_weight.shape[1]
+    return vmem_call(
+        product_body,
+        jax.ShapeDtypeStruct((rows, width), dtype),
+        (one, two, own_weight, other_weight),
+        grant=8,
+        flops=4 * rows * own_weight.size,
+        moved=4 * own_weight.size,
     )
 
 
@@ -545,10 +553,13 @@
     weight = qkv_weight.transpose(1, 0, 2)
     fetched = load(hidden_in, decay_down, gate_down, beta_weight.T, weight)
     slabs, rims, fetched = gathered(hidden_in, fetched)
+    rims, late_weight = lax.optimization_barrier((rims, out_weight))
+    near_weight = swapped(late_weight, "head", 1)
     *pairs, solved, attend, start, gate_low = front(
         rims, slabs, fetched, (decay_log, decay_up, dt_bias[None], conv_weight), weight, size
     )
     count = start.shape[1]
+    attend, near_weight = lax.optimization_barrier((attend, near_weight))
     raised, output_rows, out_gate = vmem_call(
         rows_body,
         (
@@ -565,17 +576,18 @@
     states = [own for own, _ in states] + [other for _, other in states]
     slab_rows = count // devices
     sums = {}
-    for g in reversed(range(max(devices // 2, 1))):
-        places = [2 * g, 2 * g + 1][:devices]
-        keep, *send = back(
-            places, states, raised, output_rows, out_gate, norm_gain[None], out_weight, slab_rows
+    for g in reversed(range(devices // 2)):
+        keep, send = normed_rows(
+            [2 * g, 2 * g + 1], states, raised, output_rows, out_gate, norm_gain[None], slab_rows
         )
-        near = [swapped(part, "head", 1).astype(f32) for part in send]
-        sums[g] = [lax.optimization_barrier(sum([keep] + near))]
+        received = swapped(send, "head", 1)
+        sums[g] = [product_rows(keep, received, out_weight, near_weight, bf16 if g else f32)]
     for bit in bits_of(devices)[1:]:
         for g in sorted(sums):
             if 2 * g & bit:
-                arrived = swapped(sum(sums.pop(g)).astype(bf16), "head", bit)
+                parts = sums.pop(g)
+                parts = parts[0] if len(parts) == 1 else sum(p.astype(f32) for p in parts)
+                arrived = swapped(parts.astype(bf16), "head", bit)
                 sums[g ^ bit // 2].append(arrived.astype(f32))
     return sum(sums[0]).astype(bf16)
 

time: 53.6 us -> 58.8 us (1.097)
  waiting for transfers between devices: 18.3 us -> 22.7 us
  Pallas kernels: 13.3 us -> 14.4 us
    ppermute x15 -> x16, waiting for transfers between devices: 18.3 us -> 22.7 us  [swapped(): lax.ppermute(block, axis, [(i, i ^ bit) for i in range(lax.axis_size(axis...]
    pallas_call x14 -> x16, Pallas kernels: 13.3 us -> 14.4 us  [vmem_call(): pl.pallas_call(body, out_shape=out_shape, in_specs=[pl.BlockSpec(memory_s...]
    ppermute x15 -> x16, starting transfers between devices: 18.6 us -> 18.4 us  [swapped(): lax.ppermute(block, axis, [(i, i ^ bit) for i in range(lax.axis_size(axis...]
  transfers between devices with their start and end apart: 17 -> 18, of which waited for: 9 -> 12; matrix products, arithmetic and copies ran while one was open for 2% -> 1% of each run, Pallas kernels for 10% -> 22%
where the time goes in v12:
time: 58.8 us; the launch traced here: 58.6 us
  waiting for transfers between devices  22.7 us (39%)
  starting transfers between devices  19.7 us (34%)
  Pallas kernels  14.4 us (24%)
  local copies, waits for them, and re-layouts  0.83 us (1%)
  other arithmetic  0.76 us (1%)
    ppermute x16, waiting for transfers between devices, swapped(): lax.ppermute(block, axis, [(i, i ^ bit) for i in range(lax.axis_size(axis...  22.7 us
    ppermute x16, starting transfers between devices, swapped(): lax.ppermute(block, axis, [(i, i ^ bit) for i in range(lax.axis_size(axis...  18.4 us
    pallas_call x16, Pallas kernels, vmem_call(): pl.pallas_call(body, out_shape=out_shape, in_specs=[pl.BlockSpec(memory_s...  14.4 us
    ppermute x2, starting transfers between devices, gathered(): lax.ppermute(tail, ('seq', 'head'), rim_route(target))  1.32 us
  transfers between devices with their start and end apart: 18, of which 12 were waited for; matrix products, arithmetic and copies ran while one was open for 1% of the time, Pallas kernels for 22%

profile of v12, /device:TPU:0, one launch (start us, length us, event | category | flops | bytes accessed | tf_op | source)
XLA Modules:
  0.0 58.6 jit_solution(4533837043448777485)
XLA Ops:
  0.0 2.9 %collective-permute-start = (bf16[64,2304]{1,0:T(8,128)(2,1)}, bf16[64,2304]{1,0:T(8,128)(2,1)S(1)}, u32[]{:S(2)}, u32[]{:S(2)}) collective-permute-start(bf16[64,2304]{1,0:T(8,128)(2,1)} %hidden_ref.1), channel_id=1, source_target_pairs={{0,2},{1,3},{2,0},{3,1},{4,6},{5,7},{6,4},{7,5},{8,10},{9,11},{10,... | collective-permute-start | bytes 884744 | tf_op jit(solution)/shard_map/ppermute | solution.py:24
  2.9 0.8 %slice.3 = bf16[8,2304]{1,0:T(8,128)(2,1)S(1)} slice(bf16[64,2304]{1,0:T(8,128)(2,1)} %hidden_ref.1), slice={[56:64], [0:2304]} | slice | bytes 73728 | tf_op jit(solution)/shard_map/slice | solution.py:54
  3.7 0.7 %collective-permute-start.2 = (bf16[8,2304]{1,0:T(8,128)(2,1)S(1)}, bf16[8,2304]{1,0:T(8,128)(2,1)S(1)}, u32[]{:S(2)}, u32[]{:S(2)}) collective-permute-start(bf16[8,2304]{1,0:T(8,128)(2,1)S(1)} %slice.3), channel_id=1, source_target_pairs={{3,5},{7,9},{11,13},{15,17},{19,21},{23,25},{27,29}} | collective-permute-start | bytes 110600 | tf_op jit(solution)/shard_map/ppermute | solution.py:56
  4.4 0.7 %collective-permute-start.1 = (bf16[8,2304]{1,0:T(8,128)(2,1)S(1)}, bf16[8,2304]{1,0:T(8,128)(2,1)S(1)}, u32[]{:S(2)}, u32[]{:S(2)}) collective-permute-start(bf16[8,2304]{1,0:T(8,128)(2,1)S(1)} %slice.3), channel_id=1, source_target_pairs={{3,6},{7,10},{11,14},{15,18},{19,22},{23,26},{27,30}} | collective-permute-start | bytes 110600 | tf_op jit(solution)/shard_map/ppermute | solution.py:56
  5.1 0.0 copy-start
  5.1 0.0 copy-start.3
  5.1 3.0 %shard_map.118 = (bf16[64,2304]{1,0:T(8,128)(2,1)S(1)}, bf16[2,2304,512]{2,1,0:T(8,128)(2,1)S(1)}, bf16[2304,256]{1,0:T(8,128)(2,1)S(1)}, bf16[4,2304]{1,0:T(4,128)(2,1)S(1)}) custom-call(bf16[64,2304]{1,0:T(8,128)(2,1)} %hidden_ref.1, bf16[2304,128]{1,0:T(8,128)(2,1)} %decay_down_ref.1, bf16[2304,128]{1,0:T(8,128)(2,1)} %gate_down_ref.1, ...), custom_call_target="tpu_custom_call" | custom-call | tf_op jit(solution)/shard_map/pallas_call | solution.py:74
  8.1 0.0 collective-permute-done.2.refs_1_
  8.2 0.0 collective-permute-done.1.refs_0_
  8.2 2.4 %collective-permute-done.refs_3_ = bf16[64,2304]{1,0:T(8,128)(2,1)S(1)} collective-permute-done((bf16[64,2304]{1,0:T(8,128)(2,1)}, bf16[64,2304]{1,0:T(8,128)(2,1)S(1)}, u32[]{:S(2)}, u32[]{:S(2)}) %collective-permute-start) | collective-permute-done | bytes 294944 | tf_op jit(solution)/shard_map/ppermute | solution.py:24
  10.6 0.1 collective-permute-start.3
  10.6 1.3 %collective-permute-done.3.refs_1_ = bf16[16,2304]{1,0:T(8,128)(2,1)S(1)} collective-permute-done((bf16[16,2304]{1,0:T(8,128)(2,1)S(1)}, bf16[16,2304]{1,0:T(8,128)(2,1)S(1)}, u32[]{:S(2)}, u32[]{:S(2)}) %collective-permute-start.3) | collective-permute-done | bytes 73760 | tf_op jit(solution)/shard_map/ppermute | solution.py:24
  11.9 0.0 copy-done
  11.9 0.2 collective-permute-start.14
  12.1 0.0 copy-done.3
  12.1 0.4 collective-permute-start.4
  12.4 0.2 collective-permute-start.5
  12.6 4.3 %collective-permute-done.4.refs_2_ = bf16[64,2304]{1,0:T(8,128)(2,1)S(1)} collective-permute-done((bf16[64,2304]{1,0:T(8,128)(2,1)S(1)}, bf16[64,2304]{1,0:T(8,128)(2,1)S(1)}, u32[]{:S(2)}, u32[]{:S(2)}) %collective-permute-start.4) | collective-permute-done | bytes 294944 | tf_op jit(solution)/shard_map/ppermute | solution.py:24
  16.9 0.4 collective-permute-done.5.refs_4_
  17.3 0.0 copy-start.1
  17.3 7.3 %shard_map.120 = (bf16[1,128,256]{2,1,0:T(8,128)(2,1)S(1)}, bf16[1,128,256]{2,1,0:T(8,128)(2,1)S(1)}, bf16[1,128,256]{2,1,0:T(8,128)(2,1)S(1)}, bf16[1,128,256]{...) custom-call(bf16[16,2304]{1,0:T(8,128)(2,1)S(1)} %shard_map.119.refs, ...), custom_call_target="tpu_custom_call" | custom-call | flops 2415919104 | bytes 9437184 | tf_op jit(solution)/shard_map/pallas_call | solution.py:74
  24.6 0.0 copy-start.2
  24.6 1.4 %collective-permute-start.6 = (bf16[1,128,256]{2,1,0:T(8,128)(2,1)S(1)}, bf16[1,128,256]{2,1,0:T(8,128)(2,1)S(1)}, u32[]{:S(2)}, u32[]{:S(2)}) collective-permute-start(bf16[1,128,256]{2,1,0:T(8,128)(2,1)S(1)} %get-tuple-element.54), channel_id=1, source_target_pairs={{0,4},{4,0},{8,12},{12,8},{16,20},{20,16},{24,28},{28,24},{1,5},{5... | collective-permute-start | bytes 196616 | tf_op jit(solution)/shard_map/ppermute | solution.py:24
  26.0 0.6 %collective-permute-start.9 = (bf16[1,128,256]{2,1,0:T(8,128)(2,1)S(1)}, bf16[1,128,256]{2,1,0:T(8,128)(2,1)S(1)}, u32[]{:S(2)}, u32[]{:S(2)}) collective-permute-start(bf16[1,128,256]{2,1,0:T(8,128)(2,1)S(1)} %get-tuple-element.57), channel_id=1, source_target_pairs={{0,4},{4,0},{8,12},{12,8},{16,20},{20,16},{24,28},{28,24},{1,5},{5... | collective-permute-start | bytes 196616 | tf_op jit(solution)/shard_map/ppermute | solution.py:24
  26.7 2.6 %collective-permute-done.6.far_ref.partner_ref = bf16[1,128,256]{2,1,0:T(8,128)(2,1)S(1)} collective-permute-done((bf16[1,128,256]{2,1,0:T(8,128)(2,1)S(1)}, bf16[1,128,256]{2,1,0:T(8,128)(2,1)S(1)}, u32[]{:S(2)}, u32[]{:S(2)}) %collective-permute-start.6) | collective-permute-done | bytes 65568 | tf_op jit(solution)/shard_map/ppermute | solution.py:24
  29.3 0.2 shard_map.121.own_ref
  29.5 1.8 %collective-permute-start.7 = (bf16[1,128,256]{2,1,0:T(8,128)(2,1)S(1)}, bf16[1,128,256]{2,1,0:T(8,128)(2,1)S(1)}, u32[]{:S(2)}, u32[]{:S(2)}) collective-permute-start(bf16[1,128,256]{2,1,0:T(8,128)(2,1)S(1)} %shard_map.121.own_ref), channel_id=1, source_target_pairs={{0,8},{4,12},{8,0},{12,4},{16,24},{20,28},{24,16},{28,20},{1,9},{5... | collective-permute-start | bytes 196616 | tf_op jit(solution)/shard_map/ppermute | solution.py:24
  31.3 0.0 collective-permute-done.9.far_ref.partner_ref
  31.3 0.2 shard_map.125.own_ref
  31.5 1.0 %collective-permute-start.10 = (bf16[1,128,256]{2,1,0:T(8,128)(2,1)S(1)}, bf16[1,128,256]{2,1,0:T(8,128)(2,1)S(1)}, u32[]{:S(2)}, u32[]{:S(2)}) collective-permute-start(bf16[1,128,256]{2,1,0:T(8,128)(2,1)S(1)} %shard_map.125.own_ref), channel_id=1, source_target_pairs={{0,8},{4,12},{8,0},{12,4},{16,24},{20,28},{24,16},{28,20},{1,9},{5... | collective-permute-start | bytes 196616 | tf_op jit(solution)/shard_map/ppermute | solution.py:24
  32.5 1.5 %collective-permute-done.7.far_ref = bf16[1,128,256]{2,1,0:T(8,128)(2,1)S(1)} collective-permute-done((bf16[1,128,256]{2,1,0:T(8,128)(2,1)S(1)}, bf16[1,128,256]{2,1,0:T(8,128)(2,1)S(1)}, u32[]{:S(2)}, u32[]{:S(2)}) %collective-permute-start.7) | collective-permute-done | bytes 65568 | tf_op jit(solution)/shard_map/ppermute | solution.py:24
  34.0 0.1 shard_map.123
  34.1 2.7 %collective-permute-start.8 = (bf16[1,128,128]{2,1,0:T(8,128)(2,1)S(1)}, bf16[1,128,128]{2,1,0:T(8,128)(2,1)S(1)}, u32[]{:S(2)}, u32[]{:S(2)}) collective-permute-start(bf16[1,128,128]{2,1,0:T(8,128)(2,1)S(1)} %shard_map.123), channel_id=1, source_target_pairs={{0,16},{4,20},{8,24},{12,28},{16,0},{20,4},{24,8},{28,12},{1,17},{... | collective-permute-start | bytes 98312 | tf_op jit(solution)/shard_map/ppermute | solution.py:24
  36.8 0.0 collective-permute-done.10.far_ref
  36.8 0.2 shard_map.127
  37.0 1.6 %collective-permute-start.11 = (bf16[1,128,128]{2,1,0:T(8,128)(2,1)S(1)}, bf16[1,128,128]{2,1,0:T(8,128)(2,1)S(1)}, u32[]{:S(2)}, u32[]{:S(2)}) collective-permute-start(bf16[1,128,128]{2,1,0:T(8,128)(2,1)S(1)} %shard_map.127), channel_id=1, source_target_pairs={{0,16},{4,20},{8,24},{12,28},{16,0},{20,4},{24,8},{28,12},{1,17},{... | collective-permute-start | bytes 98312 | tf_op jit(solution)/shard_map/ppermute | solution.py:24
  38.7 0.7 %collective-permute-done.8.far_ref = bf16[1,128,128]{2,1,0:T(8,128)(2,1)S(1)} collective-permute-done((bf16[1,128,128]{2,1,0:T(8,128)(2,1)S(1)}, bf16[1,128,128]{2,1,0:T(8,128)(2,1)S(1)}, u32[]{:S(2)}, u32[]{:S(2)}) %collective-permute-start.8) | collective-permute-done | bytes 32800 | tf_op jit(solution)/shard_map/ppermute | solution.py:24
  39.4 0.3 shard_map.124
  39.6 1.6 %collective-permute-start.12 = (bf16[1,128,128]{2,1,0:T(8,128)(2,1)S(1)}, bf16[1,128,128]{2,1,0:T(8,128)(2,1)S(1)}, u32[]{:S(2)}, u32[]{:S(2)}) collective-permute-start(bf16[1,128,128]{2,1,0:T(8,128)(2,1)S(1)} %get-tuple-element.59), channel_id=1, source_target_pairs={{0,4},{4,0},{8,12},{12,8},{16,20},{20,16},{24,28},{28,24},{1,5},{5... | collective-permute-start | bytes 98312 | tf_op jit(solution)/shard_map/ppermute | solution.py:24
  41.2 0.6 %collective-permute-done.11.far_ref = bf16[1,128,128]{2,1,0:T(8,128)(2,1)S(1)} collective-permute-done((bf16[1,128,128]{2,1,0:T(8,128)(2,1)S(1)}, bf16[1,128,128]{2,1,0:T(8,128)(2,1)S(1)}, u32[]{:S(2)}, u32[]{:S(2)}) %collective-permute-start.11) | collective-permute-done | bytes 32800 | tf_op jit(solution)/shard_map/ppermute | solution.py:24
  41.9 0.3 shard_map.128
  42.2 1.9 %collective-permute-start.13 = (bf16[1,128,128]{2,1,0:T(8,128)(2,1)S(1)}, bf16[1,128,128]{2,1,0:T(8,128)(2,1)S(1)}, u32[]{:S(2)}, u32[]{:S(2)}) collective-permute-start(bf16[1,128,128]{2,1,0:T(8,128)(2,1)S(1)} %get-tuple-element.60), channel_id=1, source_target_pairs={{0,4},{4,0},{8,12},{12,8},{16,20},{20,16},{24,28},{28,24},{1,5},{5... | collective-permute-start | bytes 98312 | tf_op jit(solution)/shard_map/ppermute | solution.py:24
  44.0 0.0 collective-permute-done.14.other_ref
  44.1 0.0 copy-done.1
  44.1 0.4 shard_map.129
  44.4 0.0 collective-permute-done.12.refs_2_
  44.4 1.7 %collective-permute-done.13.refs_3_ = bf16[1,128,128]{2,1,0:T(8,128)(2,1)S(1)} collective-permute-done((bf16[1,128,128]{2,1,0:T(8,128)(2,1)S(1)}, bf16[1,128,128]{2,1,0:T(8,128)(2,1)S(1)}, u32[]{:S(2)}, u32[]{:S(2)}) %collective-permute-start.13) | collective-permute-done | bytes 32800 | tf_op jit(solution)/shard_map/ppermute | solution.py:24
  46.1 0.0 copy-done.2
  46.1 0.3 shard_map.132
  46.5 0.1 collective-permute-start.16
  46.5 1.2 %collective-permute-done.16.two_ref = bf16[64,512]{1,0:T(8,128)(2,1)S(1)} collective-permute-done((bf16[64,512]{1,0:T(8,128)(2,1)S(1)}, bf16[64,512]{1,0:T(8,128)(2,1)S(1)}, u32[]{:S(2)}, u32[]{:S(2)}) %collective-permute-start.16) | collective-permute-done | bytes 65568 | tf_op jit(solution)/shard_map/ppermute | solution.py:24
  47.8 0.9 %shard_map.133 = bf16[64,2304]{1,0:T(8,128)(2,1)S(1)} custom-call(bf16[64,512]{1,0:T(8,128)(2,1)S(1)} %get-tuple-element.73.one_ref, bf16[64,512]{1,0:T(8,128)(2,1)S(1)} %collective-permute-done.16.two_ref, bf16[512,2304]{1,0:T(8,128)(2,1)S(1)} %copy-done, bf16[512,2304]{1,0:T(8,128)(2,1)S(1)} %collective-permute-done.14.other_ref), custom_call_target="tpu_custom_call" | custom-call | flops 301989888 | bytes 4718592 | tf_op jit(solution)/shard_map/pallas_call | solution.py:74
  48.7 1.8 %collective-permute-start.17 = (bf16[64,2304]{1,0:T(8,128)(2,1)S(1)}, bf16[64,2304]{1,0:T(8,128)(2,1)S(1)}, u32[]{:S(2)}, u32[]{:S(2)}) collective-permute-start(bf16[64,2304]{1,0:T(8,128)(2,1)S(1)} %shard_map.133), channel_id=1, source_target_pairs={{0,2},{1,3},{2,0},{3,1},{4,6},{5,7},{6,4},{7,5},{8,10},{9,11},{10,... | collective-permute-start | bytes 884744 | tf_op jit(solution)/shard_map/ppermute | solution.py:24
  50.5 0.3 shard_map.130
  50.8 0.1 collective-permute-start.15
  50.9 1.2 %collective-permute-done.15.two_ref = bf16[64,512]{1,0:T(8,128)(2,1)S(1)} collective-permute-done((bf16[64,512]{1,0:T(8,128)(2,1)S(1)}, bf16[64,512]{1,0:T(8,128)(2,1)S(1)}, u32[]{:S(2)}, u32[]{:S(2)}) %collective-permute-start.15) | collective-permute-done | bytes 65568 | tf_op jit(solution)/shard_map/ppermute | solution.py:24
  52.1 0.9 %shard_map.131 = f32[64,2304]{1,0:T(8,128)S(1)} custom-call(bf16[64,512]{1,0:T(8,128)(2,1)S(1)} %get-tuple-element.70.one_ref, bf16[64,512]{1,0:T(8,128)(2,1)S(1)} %collective-permute-done.15.two_ref, bf16[512,2304]{1,0:T(8,128)(2,1)S(1)} %copy-done, bf16[512,2304]{1,0:T(8,128)(2,1)S(1)} %collective-permute-done.14.other_ref), custom_call_target="tpu_custom_call" | custom-call | flops 301989888 | bytes 4718592 | tf_op jit(solution)/shard_map/pallas_call | solution.py:74
  53.0 4.8 %collective-permute-done.17 = bf16[64,2304]{1,0:T(8,128)(2,1)S(1)} collective-permute-done((bf16[64,2304]{1,0:T(8,128)(2,1)S(1)}, bf16[64,2304]{1,0:T(8,128)(2,1)S(1)}, u32[]{:S(2)}, u32[]{:S(2)}) %collective-permute-start.17) | collective-permute-done | bytes 294944 | tf_op jit(solution)/shard_map/ppermute | solution.py:24
  57.8 0.8 %add_convert_fusion = bf16[64,2304]{1,0:T(8,128)(2,1)} fusion(f32[64,2304]{1,0:T(8,128)S(1)} %shard_map.131, bf16[64,2304]{1,0:T(8,128)(2,1)S(1)} %collective-permute-done.17), kind=kLoop, calls=%fused_computation | loop fusion | flops 442368 | bytes 1179648 | tf_op jit(solution)/shard_map/convert_element_type | solution.py:592
  (3 shorter events, 0.1 us)
Async XLA Ops:
  0.0 10.5 %collective-permute-start = (bf16[64,2304]{1,0:T(8,128)(2,1)}, bf16[64,2304]{1,0:T(8,128)(2,1)S(1)}, u32[]{:S(2)}, u32[]{:S(2)}) collective-permute-start(bf16[64,2304]{1,0:T(8,128)(2,1)} %hidden_ref.1), channel_id=1, source_target_pairs={{0,2},{1,3},{2,0},{3,1},{4,6},{5,7},{6,4},{7,5},{8,10},{9,11},{10,... | collective-permute-start | bytes 884744 | tf_op jit(solution)/shard_map/ppermute | solution.py:24
  3.7 4.4 %collective-permute-start.2 = (bf16[8,2304]{1,0:T(8,128)(2,1)S(1)}, bf16[8,2304]{1,0:T(8,128)(2,1)S(1)}, u32[]{:S(2)}, u32[]{:S(2)}) collective-permute-start(bf16[8,2304]{1,0:T(8,128)(2,1)S(1)} %slice.3), channel_id=1, source_target_pairs={{3,5},{7,9},{11,13},{15,17},{19,21},{23,25},{27,29}} | collective-permute-start | bytes 110600 | tf_op jit(solution)/shard_map/ppermute | solution.py:56
  4.4 3.8 %collective-permute-start.1 = (bf16[8,2304]{1,0:T(8,128)(2,1)S(1)}, bf16[8,2304]{1,0:T(8,128)(2,1)S(1)}, u32[]{:S(2)}, u32[]{:S(2)}) collective-permute-start(bf16[8,2304]{1,0:T(8,128)(2,1)S(1)} %slice.3), channel_id=1, source_target_pairs={{3,6},{7,10},{11,14},{15,18},{19,22},{23,26},{27,30}} | collective-permute-start | bytes 110600 | tf_op jit(solution)/shard_map/ppermute | solution.py:56
  5.1 6.8 %copy-start = (bf16[512,2304]{1,0:T(8,128)(2,1)S(1)}, bf16[512,2304]{1,0:T(8,128)(2,1)}, u32[]{:S(2)}) copy-start(bf16[512,2304]{1,0:T(8,128)(2,1)} %own_ref.3) | copy-start | bytes 7077892
  5.1 7.0 %copy-start.3 = (bf16[64,2304]{1,0:T(8,128)(2,1)S(1)}, bf16[64,2304]{1,0:T(8,128)(2,1)}, u32[]{:S(2)}) copy-start(bf16[64,2304]{1,0:T(8,128)(2,1)} %hidden_ref.1) | copy-start | bytes 884740
  10.6 1.3 %collective-permute-start.3 = (bf16[16,2304]{1,0:T(8,128)(2,1)S(1)}, bf16[16,2304]{1,0:T(8,128)(2,1)S(1)}, u32[]{:S(2)}, u32[]{:S(2)}) collective-permute-start(bf16[16,2304]{1,0:T(8,128)(2,1)S(1)} %shard_map.119.refs_0_), channel_id=1, source_target_pairs={{0,1},{1,0},{2,3},{3,2},{4,5},{5,4},{6,7},{7,6},{8,9},{9,8},{10,11... | collective-permute-start | bytes 221192 | tf_op jit(solution)/shard_map/ppermute | solution.py:24
  11.9 32.1 %collective-permute-start.14 = (bf16[512,2304]{1,0:T(8,128)(2,1)S(1)}, bf16[512,2304]{1,0:T(8,128)(2,1)S(1)}, u32[]{:S(2)}, u32[]{:S(2)}) collective-permute-start(bf16[512,2304]{1,0:T(8,128)(2,1)S(1)} %copy-done), channel_id=1, source_target_pairs={{0,1},{1,0},{2,3},{3,2},{4,5},{5,4},{6,7},{7,6},{8,9},{9,8},{10,11... | collective-permute-start | bytes 7077896 | tf_op jit(solution)/shard_map/ppermute | solution.py:24
  12.1 4.8 %collective-permute-start.4 = (bf16[64,2304]{1,0:T(8,128)(2,1)S(1)}, bf16[64,2304]{1,0:T(8,128)(2,1)S(1)}, u32[]{:S(2)}, u32[]{:S(2)}) collective-permute-start(bf16[64,2304]{1,0:T(8,128)(2,1)S(1)} %copy-done.3), channel_id=1, source_target_pairs={{0,1},{1,0},{2,3},{3,2},{4,5},{5,4},{6,7},{7,6},{8,9},{9,8},{10,11... | collective-permute-start | bytes 884744 | tf_op jit(solution)/shard_map/ppermute | solution.py:24
  12.4 4.9 %collective-permute-start.5 = (bf16[64,2304]{1,0:T(8,128)(2,1)S(1)}, bf16[64,2304]{1,0:T(8,128)(2,1)S(1)}, u32[]{:S(2)}, u32[]{:S(2)}) collective-permute-start(bf16[64,2304]{1,0:T(8,128)(2,1)S(1)} %collective-permute-done.refs_3_), channel_id=1, source_target_pairs={{0,1},{1,0},{2,3},{3,2},{4,5},{5,4},{6,7},{7,6},{8,9},{9,8},{10,11... | collective-permute-start | bytes 884744 | tf_op jit(solution)/shard_map/ppermute | solution.py:24
  17.3 26.8 %copy-start.1 = (bf16[128,512]{1,0:T(8,128)(2,1)S(1)}, bf16[128,512]{1,0:T(8,128)(2,1)}, u32[]{:S(2)}) copy-start(bf16[128,512]{1,0:T(8,128)(2,1)} %up_ref.1) | copy-start | bytes 393220
  24.6 21.6 %copy-start.2 = (f32[128]{0:T(128)S(1)}, f32[128]{0:T(128)}, u32[]{:S(2)}) copy-start(f32[128]{0:T(128)} %param.22) | copy-start | bytes 1540
  24.6 4.7 %collective-permute-start.6 = (bf16[1,128,256]{2,1,0:T(8,128)(2,1)S(1)}, bf16[1,128,256]{2,1,0:T(8,128)(2,1)S(1)}, u32[]{:S(2)}, u32[]{:S(2)}) collective-permute-start(bf16[1,128,256]{2,1,0:T(8,128)(2,1)S(1)} %get-tuple-element.54), channel_id=1, source_target_pairs={{0,4},{4,0},{8,12},{12,8},{16,20},{20,16},{24,28},{28,24},{1,5},{5... | collective-permute-start | bytes 196616 | tf_op jit(solution)/shard_map/ppermute | solution.py:24
  26.0 5.3 %collective-permute-start.9 = (bf16[1,128,256]{2,1,0:T(8,128)(2,1)S(1)}, bf16[1,128,256]{2,1,0:T(8,128)(2,1)S(1)}, u32[]{:S(2)}, u32[]{:S(2)}) collective-permute-start(bf16[1,128,256]{2,1,0:T(8,128)(2,1)S(1)} %get-tuple-element.57), channel_id=1, source_target_pairs={{0,4},{4,0},{8,12},{12,8},{16,20},{20,16},{24,28},{28,24},{1,5},{5... | collective-permute-start | bytes 196616 | tf_op jit(solution)/shard_map/ppermute | solution.py:24
  29.5 4.5 %collective-permute-start.7 = (bf16[1,128,256]{2,1,0:T(8,128)(2,1)S(1)}, bf16[1,128,256]{2,1,0:T(8,128)(2,1)S(1)}, u32[]{:S(2)}, u32[]{:S(2)}) collective-permute-start(bf16[1,128,256]{2,1,0:T(8,128)(2,1)S(1)} %shard_map.121.own_ref), channel_id=1, source_target_pairs={{0,8},{4,12},{8,0},{12,4},{16,24},{20,28},{24,16},{28,20},{1,9},{5... | collective-permute-start | bytes 196616 | tf_op jit(solution)/shard_map/ppermute | solution.py:24
  31.5 5.3 %collective-permute-start.10 = (bf16[1,128,256]{2,1,0:T(8,128)(2,1)S(1)}, bf16[1,128,256]{2,1,0:T(8,128)(2,1)S(1)}, u32[]{:S(2)}, u32[]{:S(2)}) collective-permute-start(bf16[1,128,256]{2,1,0:T(8,128)(2,1)S(1)} %shard_map.125.own_ref), channel_id=1, source_target_pairs={{0,8},{4,12},{8,0},{12,4},{16,24},{20,28},{24,16},{28,20},{1,9},{5... | collective-permute-start | bytes 196616 | tf_op jit(solution)/shard_map/ppermute | solution.py:24
  34.1 5.2 %collective-permute-start.8 = (bf16[1,128,128]{2,1,0:T(8,128)(2,1)S(1)}, bf16[1,128,128]{2,1,0:T(8,128)(2,1)S(1)}, u32[]{:S(2)}, u32[]{:S(2)}) collective-permute-start(bf16[1,128,128]{2,1,0:T(8,128)(2,1)S(1)} %shard_map.123), channel_id=1, source_target_pairs={{0,16},{4,20},{8,24},{12,28},{16,0},{20,4},{24,8},{28,12},{1,17},{... | collective-permute-start | bytes 98312 | tf_op jit(solution)/shard_map/ppermute | solution.py:24
  37.0 4.9 %collective-permute-start.11 = (bf16[1,128,128]{2,1,0:T(8,128)(2,1)S(1)}, bf16[1,128,128]{2,1,0:T(8,128)(2,1)S(1)}, u32[]{:S(2)}, u32[]{:S(2)}) collective-permute-start(bf16[1,128,128]{2,1,0:T(8,128)(2,1)S(1)} %shard_map.127), channel_id=1, source_target_pairs={{0,16},{4,20},{8,24},{12,28},{16,0},{20,4},{24,8},{28,12},{1,17},{... | collective-permute-start | bytes 98312 | tf_op jit(solution)/shard_map/ppermute | solution.py:24
  39.6 4.8 %collective-permute-start.12 = (bf16[1,128,128]{2,1,0:T(8,128)(2,1)S(1)}, bf16[1,128,128]{2,1,0:T(8,128)(2,1)S(1)}, u32[]{:S(2)}, u32[]{:S(2)}) collective-permute-start(bf16[1,128,128]{2,1,0:T(8,128)(2,1)S(1)} %get-tuple-element.59), channel_id=1, source_target_pairs={{0,4},{4,0},{8,12},{12,8},{16,20},{20,16},{24,28},{28,24},{1,5},{5... | collective-permute-start | bytes 98312 | tf_op jit(solution)/shard_map/ppermute | solution.py:24
  42.2 4.0 %collective-permute-start.13 = (bf16[1,128,128]{2,1,0:T(8,128)(2,1)S(1)}, bf16[1,128,128]{2,1,0:T(8,128)(2,1)S(1)}, u32[]{:S(2)}, u32[]{:S(2)}) collective-permute-start(bf16[1,128,128]{2,1,0:T(8,128)(2,1)S(1)} %get-tuple-element.60), channel_id=1, source_target_pairs={{0,4},{4,0},{8,12},{12,8},{16,20},{20,16},{24,28},{28,24},{1,5},{5... | collective-permute-start | bytes 98312 | tf_op jit(solution)/shard_map/ppermute | solution.py:24
  46.5 1.3 %collective-permute-start.16 = (bf16[64,512]{1,0:T(8,128)(2,1)S(1)}, bf16[64,512]{1,0:T(8,128)(2,1)S(1)}, u32[]{:S(2)}, u32[]{:S(2)}) collective-permute-start(bf16[64,512]{1,0:T(8,128)(2,1)S(1)} %get-tuple-element.74), channel_id=1, source_target_pairs={{0,1},{1,0},{2,3},{3,2},{4,5},{5,4},{6,7},{7,6},{8,9},{9,8},{10,11... | collective-permute-start | bytes 196616 | tf_op jit(solution)/shard_map/ppermute | solution.py:24
  48.7 9.1 %collective-permute-start.17 = (bf16[64,2304]{1,0:T(8,128)(2,1)S(1)}, bf16[64,2304]{1,0:T(8,128)(2,1)S(1)}, u32[]{:S(2)}, u32[]{:S(2)}) collective-permute-start(bf16[64,2304]{1,0:T(8,128)(2,1)S(1)} %shard_map.133), channel_id=1, source_target_pairs={{0,2},{1,3},{2,0},{3,1},{4,6},{5,7},{6,4},{7,5},{8,10},{9,11},{10,... | collective-permute-start | bytes 884744 | tf_op jit(solution)/shard_map/ppermute | solution.py:24
  50.8 1.3 %collective-permute-start.15 = (bf16[64,512]{1,0:T(8,128)(2,1)S(1)}, bf16[64,512]{1,0:T(8,128)(2,1)S(1)}, u32[]{:S(2)}, u32[]{:S(2)}) collective-permute-start(bf16[64,512]{1,0:T(8,128)(2,1)S(1)} %get-tuple-element.71), channel_id=1, source_target_pairs={{0,1},{1,0},{2,3},{3,2},{4,5},{5,4},{6,7},{7,6},{8,9},{9,8},{10,11... | collective-permute-start | bytes 196616 | tf_op jit(solution)/shard_map/ppermute | solution.py:24

commit v13 on v10

--- a/solution.py
+++ b/solution.py
@@ -93,25 +93,27 @@
 
 
 def load_body(
-    hidden_ref, decay_down_ref, gate_down_ref, beta_ref, weight_ref,
-    own_ref, weights, downs, betas, sems,
+    hidden_ref, decay_down_ref, beta_ref, weight_ref, own_ref, weights, downs, betas, sems
 ):
-    rank = decay_down_ref.shape[1]
+    rank, heads = decay_down_ref.shape[1], beta_ref.shape[0]
+    beta = pltpu.make_async_copy(beta_ref, betas, sems.at[0])
     copies = [
-        pltpu.make_async_copy(hidden_ref, own_ref, sems.at[0]),
-        pltpu.make_async_copy(decay_down_ref, downs.at[:, pl.ds(0, rank)], sems.at[1]),
-        pltpu.make_async_copy(gate_down_ref, downs.at[:, pl.ds(rank, rank)], sems.at[2]),
-        pltpu.make_async_copy(beta_ref, betas, sems.at[3]),
+        pltpu.make_async_copy(hidden_ref, own_ref, sems.at[1]),
+        pltpu.make_async_copy(decay_down_ref, downs.at[:, pl.ds(0, rank)], sems.at[2]),
     ]
     for c in range(2):
-        copies.append(pltpu.make_async_copy(weight_ref.at[c], weights.at[c], sems.at[4 + c]))
-    for copy in copies:
+        copies.append(pltpu.make_async_copy(weight_ref.at[c], weights.at[c], sems.at[3 + c]))
+    for copy in [beta] + copies:
         copy.start()
+    beta.wait()
+    below = jnp.zeros((rank - heads, betas.shape[1]), f32)
+    wide = jnp.concatenate([betas[...].astype(f32), below], axis=0)
+    downs[:, rank:] = wide.T.astype(bf16)
     for copy in copies:
         copy.wait()
 
 
-def load(own, decay_down, gate_down, beta, weight):
+def load(own, decay_down, beta, weight):
     width, rank = decay_down.shape
     return vmem_call(
         load_body,
@@ -119,23 +121,22 @@
             jax.ShapeDtypeStruct(own.shape, bf16),
             jax.ShapeDtypeStruct((2, *weight.shape[1:]), bf16),
             jax.ShapeDtypeStruct((width, 2 * rank), bf16),
-            jax.ShapeDtypeStruct(beta.shape, bf16),
         ),
-        (own, decay_down, gate_down, beta, weight),
-        scratch=[pltpu.SemaphoreType.DMA((6,))],
-        hbm=5,
-        grant=8,
+        (own, decay_down, beta, weight),
+        scratch=[pltpu.VMEM(beta.shape, bf16), pltpu.SemaphoreType.DMA((5,))],
+        hbm=4,
+        grant=12,
     )
 
 
 def front_body(slab_count, *refs):
     (one_ref, two_ref, *slab_refs), refs = refs[: slab_count + 1], refs[slab_count + 1 :]
-    (own_rows_ref, weights, downs, betas), refs = refs[:4], refs[4:]
+    (own_rows_ref, weights, downs), refs = refs[:3], refs[3:]
     hbm_refs, refs = refs[:5], refs[5:]
     (own_refs, other_refs), refs = (refs[:GROUPS], refs[GROUPS : 2 * GROUPS]), refs[2 * GROUPS :]
-    (solved_ref, attend_ref, start_ref, gate_ref), refs = refs[:4], refs[4:]
+    (solved_ref, attend_ref, start_ref, rows_ref), refs = refs[:4], refs[4:]
     loaded, refs = refs[:5], refs[5:]
-    rows_ref, projected, running_ref, parts_ref, mixing, inverse, sides, sems = refs
+    projected, running_ref, parts_ref, mixing, inverse, sides, sems = refs
     rates, decay_up_ref, bias_ref, conv_ref, value_weight = loaded
     weight_ref = hbm_refs[-1]
     heads, count, size = start_ref.shape
@@ -181,12 +182,11 @@
         del pending[:number]
 
     project_next(2)
-    low = dot(rows_ref[RIM:, :], downs[...]).astype(bf16)
-    gate_ref[...] = low[:, rank:]
-    strength = jax.nn.sigmoid(dot(rows_ref[RIM:, :], betas[...], ((1,), (1,))))
+    low = dot(rows_ref[RIM:, :], downs[...])
+    strength = jax.nn.sigmoid(low[:, rank:])
     for copy in small:
         copy.wait()
-    running_ref[...] = dot(low[:, :rank], decay_up_ref[...])
+    running_ref[...] = dot(low[:, :rank].astype(bf16), decay_up_ref[...])
     tiles = [slice(a * chunk, (a + 1) * chunk) for a in range(chunks)]
     for h in range(heads):
         lanes = slice(h * size, (h + 1) * size)
@@ -353,13 +353,12 @@
             jax.ShapeDtypeStruct((heads, count, 2 * size), bf16),
             jax.ShapeDtypeStruct((heads, count, count), bf16),
             jax.ShapeDtypeStruct((heads, count, size), bf16),
-            jax.ShapeDtypeStruct((count, fetched[2].shape[1] // 2), bf16),
+            jax.ShapeDtypeStruct((RIM + count, width), bf16),
         ),
         (*rims, *slabs, *fetched, *loaded, weight),
         scratch=[
             *buffers,
             pltpu.VMEM((width, channels), bf16),
-            pltpu.VMEM((RIM + count, width), bf16),
             pltpu.VMEM((3 * heads, RIM + count, size), f32),
             pltpu.VMEM((count, channels), f32),
             pltpu.VMEM((2 * count, channels), bf16),
@@ -375,9 +374,12 @@
     )
 
 
-def rows_body(attend_ref, solved_ref, start_ref, low_ref, up_ref, raised_ref, output_ref, gate_ref):
+def rows_body(
+    attend_ref, solved_ref, start_ref, rows_ref, down_ref, up_ref, raised_ref, output_ref, gate_ref
+):
     heads, _, size = start_ref.shape
-    gate_ref[...] = jax.nn.sigmoid(dot(low_ref[...], up_ref[...]))
+    low = dot(rows_ref[RIM:, :], down_ref[...]).astype(bf16)
+    gate_ref[...] = jax.nn.sigmoid(dot(low, up_ref[...]))
     count = attend_ref.shape[1]
     block = math.gcd(count, 128)
     for h in range(heads):
@@ -482,45 +484,37 @@
     return keep, swapped(send, "seq", 1)
 
 
-def back_body(places, *refs):
+def back_body(away, *refs):
     own_refs, other_refs, refs = refs[:GROUPS], refs[GROUPS : 2 * GROUPS], refs[2 * GROUPS :]
-    raised_ref, output_ref, gate_ref, gain_ref, weight_ref, keep_ref, *rest = refs
-    normed = rest[-1]
+    raised_ref, output_ref, gate_ref, gain_ref, weight_ref, out_ref, normed = refs
     size = gain_ref.shape[1]
-    slab_rows = keep_ref.shape[0]
+    slab_rows = out_ref.shape[0]
     share = own_refs[0].shape[0]
     half = GROUPS * share
     upper = place("seq", 1) == 1
-    for k, away in enumerate(places):
-        rows = pl.ds(pl.multiple_of((place("head") ^ away) * slab_rows, 16), slab_rows)
-        for h in range(raised_ref.shape[0]):
-            lanes = slice(h * size, (h + 1) * size)
-            group, at = divmod(h % half, share)
-            own, other = own_refs[group][at], other_refs[group][at]
-            state = jnp.where(upper, other, own) if h < half else jnp.where(upper, own, other)
-            attended = dot(raised_ref[h, rows, :], state) + output_ref[rows, lanes]
-            power = jnp.sum(attended * attended, -1, keepdims=True) * (1.0 / size)
-            normed[k * slab_rows : (k + 1) * slab_rows, lanes] = (
-                attended * lax.rsqrt(power + 1e-05) * gain_ref[...] * gate_ref[rows, lanes]
-            ).astype(bf16)
-    total = dot(normed[...], weight_ref[...])
-    keep_ref[...] = total[:slab_rows]
-    if len(rest) > 1:
-        rest[0][...] = total[slab_rows:].astype(bf16)
-
-
-def back(places, states, raised, output_rows, out_gate, gain, weight, slab_rows):
-    slab_count, width = len(places), weight.shape[1]
-    shapes = [jax.ShapeDtypeStruct((slab_rows, width), f32)]
-    if slab_count > 1:
-        shapes.append(jax.ShapeDtypeStruct((slab_rows, width), bf16))
+    rows = pl.ds(pl.multiple_of((place("head") ^ away) * slab_rows, 16), slab_rows)
+    for h in range(raised_ref.shape[0]):
+        lanes = slice(h * size, (h + 1) * size)
+        group, at = divmod(h % half, share)
+        own, other = own_refs[group][at], other_refs[group][at]
+        state = jnp.where(upper, other, own) if h < half else jnp.where(upper, own, other)
+        attended = dot(raised_ref[h, rows, :], state) + output_ref[rows, lanes]
+        power = jnp.sum(attended * attended, -1, keepdims=True) * (1.0 / size)
+        normed[:, lanes] = (
+            attended * lax.rsqrt(power + 1e-05) * gain_ref[...] * gate_ref[rows, lanes]
+        ).astype(bf16)
+    out_ref[...] = dot(normed[...], weight_ref[...]).astype(out_ref.dtype)
+
+
+def back(away, states, raised, output_rows, out_gate, gain, weight, slab_rows, dtype):
+    width = weight.shape[1]
     return vmem_call(
-        functools.partial(back_body, places),
-        shapes,
+        functools.partial(back_body, away),
+        jax.ShapeDtypeStruct((slab_rows, width), dtype),
         (*states, raised, output_rows, out_gate, gain, weight),
-        scratch=[pltpu.VMEM((slab_count * slab_rows, weight.shape[0]), bf16)],
+        scratch=[pltpu.VMEM((slab_rows, weight.shape[0]), bf16)],
         grant=10,
-        flops=2 * slab_count * slab_rows * weight.shape[0] * width,
+        flops=2 * slab_rows * weight.shape[0] * width,
         moved=2 * weight.shape[0] * width,
     )
 
@@ -543,9 +537,9 @@
     channels = heads * size
     devices = lax.axis_size("head")
     weight = qkv_weight.transpose(1, 0, 2)
-    fetched = load(hidden_in, decay_down, gate_down, beta_weight.T, weight)
+    fetched = load(hidden_in, decay_down, beta_weight.T, weight)
     slabs, rims, fetched = gathered(hidden_in, fetched)
-    *pairs, solved, attend, start, gate_low = front(
+    *pairs, solved, attend, start, rows = front(
         rims, slabs, fetched, (decay_log, decay_up, dt_bias[None], conv_weight), weight, size
     )
     count = start.shape[1]
@@ -556,7 +550,7 @@
             jax.ShapeDtypeStruct((count, channels), f32),
             jax.ShapeDtypeStruct((count, channels), f32),
         ),
-        (attend, solved, start, gate_low, gate_up),
+        (attend, solved, start, rows, gate_down, gate_up),
         grant=8,
         flops=2 * heads * count * count * 2 * size,
         moved=4 * heads * count * count,
@@ -565,13 +559,10 @@
     states = [own for own, _ in states] + [other for _, other in states]
     slab_rows = count // devices
     sums = {}
-    for g in reversed(range(max(devices // 2, 1))):
-        places = [2 * g, 2 * g + 1][:devices]
-        keep, *send = back(
-            places, states, raised, output_rows, out_gate, norm_gain[None], out_weight, slab_rows
-        )
-        near = [swapped(part, "head", 1).astype(f32) for part in send]
-        sums[g] = [lax.optimization_barrier(sum([keep] + near))]
+    for g in reversed(range(devices // 2)):
+        rest = (states, raised, output_rows, out_gate, norm_gain[None], out_weight, slab_rows)
+        near = swapped(back(2 * g + 1, *rest, bf16), "head", 1).astype(f32)
+        sums[g] = [lax.optimization_barrier(back(2 * g, *rest, f32) + near)]
     for bit in bits_of(devices)[1:]:
         for g in sorted(sums):
             if 2 * g & bit:

time: 53.6 us -> 54.3 us (1.013)
  Pallas kernels: 13.3 us -> 14.6 us
  waiting for transfers between devices: 18.3 us -> 17.7 us
    pallas_call x14 -> x16, Pallas kernels: 13.3 us -> 14.6 us  [vmem_call(): pl.pallas_call(body, out_shape=out_shape, in_specs=[pl.BlockSpec(memory_s...]
    ppermute x15, waiting for transfers between devices: 18.3 us -> 17.7 us  [swapped(): lax.ppermute(block, axis, [(i, i ^ bit) for i in range(lax.axis_size(axis...]
  transfers between devices with their start and end apart: 17 -> 17, of which waited for: 9 -> 8; matrix products, arithmetic and copies ran while one was open for 2% -> 2% of each run, Pallas kernels for 10% -> 13%
where the time goes in v13:
time: 54.3 us; the launch traced here: 54.1 us
  starting transfers between devices  19.8 us (36%)
  waiting for transfers between devices  17.7 us (33%)
  Pallas kernels  14.6 us (27%)
  other arithmetic  0.89 us (2%)
  local copies, waits for them, and re-layouts  0.82 us (2%)
    ppermute x15, starting transfers between devices, swapped(): lax.ppermute(block, axis, [(i, i ^ bit) for i in range(lax.axis_size(axis...  18.5 us
    ppermute x15, waiting for transfers between devices, swapped(): lax.ppermute(block, axis, [(i, i ^ bit) for i in range(lax.axis_size(axis...  17.7 us
    pallas_call x16, Pallas kernels, vmem_call(): pl.pallas_call(body, out_shape=out_shape, in_specs=[pl.BlockSpec(memory_s...  14.6 us
    ppermute x2, starting transfers between devices, gathered(): lax.ppermute(tail, ('seq', 'head'), rim_route(target))  1.32 us
  transfers between devices with their start and end apart: 17, of which 8 were waited for; matrix products, arithmetic and copies ran while one was open for 2% of the time, Pallas kernels for 13%

profile of v13, /device:TPU:0, one launch (start us, length us, event | category | flops | bytes accessed | tf_op | source)
XLA Modules:
  0.0 54.1 jit_solution(9454080621318490617)
XLA Ops:
  0.0 2.9 %collective-permute-start = (bf16[64,2304]{1,0:T(8,128)(2,1)}, bf16[64,2304]{1,0:T(8,128)(2,1)S(1)}, u32[]{:S(2)}, u32[]{:S(2)}) collective-permute-start(bf16[64,2304]{1,0:T(8,128)(2,1)} %hidden_ref.1), channel_id=1, source_target_pairs={{0,2},{1,3},{2,0},{3,1},{4,6},{5,7},{6,4},{7,5},{8,10},{9,11},{10,... | collective-permute-start | bytes 884744 | tf_op jit(solution)/shard_map/ppermute | solution.py:24
  2.9 0.8 %slice.3 = bf16[8,2304]{1,0:T(8,128)(2,1)S(1)} slice(bf16[64,2304]{1,0:T(8,128)(2,1)} %hidden_ref.1), slice={[56:64], [0:2304]} | slice | bytes 73728 | tf_op jit(solution)/shard_map/slice | solution.py:54
  3.7 0.7 %collective-permute-start.2 = (bf16[8,2304]{1,0:T(8,128)(2,1)S(1)}, bf16[8,2304]{1,0:T(8,128)(2,1)S(1)}, u32[]{:S(2)}, u32[]{:S(2)}) collective-permute-start(bf16[8,2304]{1,0:T(8,128)(2,1)S(1)} %slice.3), channel_id=1, source_target_pairs={{3,5},{7,9},{11,13},{15,17},{19,21},{23,25},{27,29}} | collective-permute-start | bytes 110600 | tf_op jit(solution)/shard_map/ppermute | solution.py:56
  4.4 0.7 %collective-permute-start.1 = (bf16[8,2304]{1,0:T(8,128)(2,1)S(1)}, bf16[8,2304]{1,0:T(8,128)(2,1)S(1)}, u32[]{:S(2)}, u32[]{:S(2)}) collective-permute-start(bf16[8,2304]{1,0:T(8,128)(2,1)S(1)} %slice.3), channel_id=1, source_target_pairs={{3,6},{7,10},{11,14},{15,18},{19,22},{23,26},{27,30}} | collective-permute-start | bytes 110600 | tf_op jit(solution)/shard_map/ppermute | solution.py:56
  5.1 0.1 collective-permute-start.4
  5.2 2.7 %shard_map.118 = (bf16[64,2304]{1,0:T(8,128)(2,1)S(1)}, bf16[2,2304,512]{2,1,0:T(8,128)(2,1)S(1)}, bf16[2304,256]{1,0:T(8,128)(2,1)S(1)}) custom-call(bf16[64,2304]{1,0:T(8,128)(2,1)} %hidden_ref.1, bf16[2304,128]{1,0:T(8,128)(2,1)} %decay_down_ref.1, bf16[4,2304]{1,0:T(4,128)(2,1)} %bitcast.10, bf16[3,2304,512]{2,1,0:T(8,128)(2,1)} %bitcast.8), custom_call_target="tpu_custom_call" | custom-call | tf_op jit(solution)/shard_map/pallas_call | solution.py:74
  7.9 0.0 collective-permute-done.2.refs_1_
  7.9 0.0 collective-permute-done.1.refs_0_
  7.9 2.6 %collective-permute-done.refs_3_ = bf16[64,2304]{1,0:T(8,128)(2,1)S(1)} collective-permute-done((bf16[64,2304]{1,0:T(8,128)(2,1)}, bf16[64,2304]{1,0:T(8,128)(2,1)S(1)}, u32[]{:S(2)}, u32[]{:S(2)}) %collective-permute-start) | collective-permute-done | bytes 294944 | tf_op jit(solution)/shard_map/ppermute | solution.py:24
  10.6 0.0 collective-permute-start.5
  10.6 0.6 %collective-permute-start.3 = (bf16[16,2304]{1,0:T(8,128)(2,1)S(1)}, bf16[16,2304]{1,0:T(8,128)(2,1)S(1)}, u32[]{:S(2)}, u32[]{:S(2)}) collective-permute-start(bf16[16,2304]{1,0:T(8,128)(2,1)S(1)} %shard_map.119.refs_0_), channel_id=1, source_target_pairs={{0,1},{1,0},{2,3},{3,2},{4,5},{5,4},{6,7},{7,6},{8,9},{9,8},{10,11... | collective-permute-start | bytes 221192 | tf_op jit(solution)/shard_map/ppermute | solution.py:24
  11.1 0.0 collective-permute-done.4.refs_2_
  11.1 1.1 %collective-permute-done.3.refs_1_ = bf16[16,2304]{1,0:T(8,128)(2,1)S(1)} collective-permute-done((bf16[16,2304]{1,0:T(8,128)(2,1)S(1)}, bf16[16,2304]{1,0:T(8,128)(2,1)S(1)}, u32[]{:S(2)}, u32[]{:S(2)}) %collective-permute-start.3) | collective-permute-done | bytes 73760 | tf_op jit(solution)/shard_map/ppermute | solution.py:24
  12.2 0.0 collective-permute-done.5.refs_4_
  12.2 0.0 copy-start.1
  12.2 0.0 copy-start.2
  12.2 7.0 %shard_map.120 = (bf16[1,128,256]{2,1,0:T(8,128)(2,1)S(1)}, bf16[1,128,256]{2,1,0:T(8,128)(2,1)S(1)}, bf16[1,128,256]{2,1,0:T(8,128)(2,1)S(1)}, bf16[1,128,256]{...) custom-call(bf16[16,2304]{1,0:T(8,128)(2,1)S(1)} %shard_map.119.refs, ...), custom_call_target="tpu_custom_call" | custom-call | flops 2415919104 | bytes 9437184 | tf_op jit(solution)/shard_map/pallas_call | solution.py:74
  19.3 1.4 %collective-permute-start.6 = (bf16[1,128,256]{2,1,0:T(8,128)(2,1)S(1)}, bf16[1,128,256]{2,1,0:T(8,128)(2,1)S(1)}, u32[]{:S(2)}, u32[]{:S(2)}) collective-permute-start(bf16[1,128,256]{2,1,0:T(8,128)(2,1)S(1)} %get-tuple-element.39), channel_id=1, source_target_pairs={{0,4},{4,0},{8,12},{12,8},{16,20},{20,16},{24,28},{28,24},{1,5},{5... | collective-permute-start | bytes 196616 | tf_op jit(solution)/shard_map/ppermute | solution.py:24
  20.7 0.6 %collective-permute-start.9 = (bf16[1,128,256]{2,1,0:T(8,128)(2,1)S(1)}, bf16[1,128,256]{2,1,0:T(8,128)(2,1)S(1)}, u32[]{:S(2)}, u32[]{:S(2)}) collective-permute-start(bf16[1,128,256]{2,1,0:T(8,128)(2,1)S(1)} %get-tuple-element.42), channel_id=1, source_target_pairs={{0,4},{4,0},{8,12},{12,8},{16,20},{20,16},{24,28},{28,24},{1,5},{5... | collective-permute-start | bytes 196616 | tf_op jit(solution)/shard_map/ppermute | solution.py:24
  21.4 2.6 %collective-permute-done.6.far_ref.partner_ref = bf16[1,128,256]{2,1,0:T(8,128)(2,1)S(1)} collective-permute-done((bf16[1,128,256]{2,1,0:T(8,128)(2,1)S(1)}, bf16[1,128,256]{2,1,0:T(8,128)(2,1)S(1)}, u32[]{:S(2)}, u32[]{:S(2)}) %collective-permute-start.6) | collective-permute-done | bytes 65568 | tf_op jit(solution)/shard_map/ppermute | solution.py:24
  24.0 0.0 copy-start
  24.0 0.0 copy-start.3
  24.0 0.2 shard_map.121.own_ref
  24.2 1.8 %collective-permute-start.7 = (bf16[1,128,256]{2,1,0:T(8,128)(2,1)S(1)}, bf16[1,128,256]{2,1,0:T(8,128)(2,1)S(1)}, u32[]{:S(2)}, u32[]{:S(2)}) collective-permute-start(bf16[1,128,256]{2,1,0:T(8,128)(2,1)S(1)} %shard_map.121.own_ref), channel_id=1, source_target_pairs={{0,8},{4,12},{8,0},{12,4},{16,24},{20,28},{24,16},{28,20},{1,9},{5... | collective-permute-start | bytes 196616 | tf_op jit(solution)/shard_map/ppermute | solution.py:24
  26.0 0.0 collective-permute-done.9.far_ref.partner_ref
  26.0 0.2 shard_map.125.own_ref
  26.2 1.0 %collective-permute-start.10 = (bf16[1,128,256]{2,1,0:T(8,128)(2,1)S(1)}, bf16[1,128,256]{2,1,0:T(8,128)(2,1)S(1)}, u32[]{:S(2)}, u32[]{:S(2)}) collective-permute-start(bf16[1,128,256]{2,1,0:T(8,128)(2,1)S(1)} %shard_map.125.own_ref), channel_id=1, source_target_pairs={{0,8},{4,12},{8,0},{12,4},{16,24},{20,28},{24,16},{28,20},{1,9},{5... | collective-permute-start | bytes 196616 | tf_op jit(solution)/shard_map/ppermute | solution.py:24
  27.2 1.5 %collective-permute-done.7.far_ref = bf16[1,128,256]{2,1,0:T(8,128)(2,1)S(1)} collective-permute-done((bf16[1,128,256]{2,1,0:T(8,128)(2,1)S(1)}, bf16[1,128,256]{2,1,0:T(8,128)(2,1)S(1)}, u32[]{:S(2)}, u32[]{:S(2)}) %collective-permute-start.7) | collective-permute-done | bytes 65568 | tf_op jit(solution)/shard_map/ppermute | solution.py:24
  28.7 0.1 shard_map.123
  28.9 2.7 %collective-permute-start.8 = (bf16[1,128,128]{2,1,0:T(8,128)(2,1)S(1)}, bf16[1,128,128]{2,1,0:T(8,128)(2,1)S(1)}, u32[]{:S(2)}, u32[]{:S(2)}) collective-permute-start(bf16[1,128,128]{2,1,0:T(8,128)(2,1)S(1)} %shard_map.123), channel_id=1, source_target_pairs={{0,16},{4,20},{8,24},{12,28},{16,0},{20,4},{24,8},{28,12},{1,17},{... | collective-permute-start | bytes 98312 | tf_op jit(solution)/shard_map/ppermute | solution.py:24
  31.5 0.0 collective-permute-done.10.far_ref
  31.5 0.2 shard_map.127
  31.7 1.7 %collective-permute-start.11 = (bf16[1,128,128]{2,1,0:T(8,128)(2,1)S(1)}, bf16[1,128,128]{2,1,0:T(8,128)(2,1)S(1)}, u32[]{:S(2)}, u32[]{:S(2)}) collective-permute-start(bf16[1,128,128]{2,1,0:T(8,128)(2,1)S(1)} %shard_map.127), channel_id=1, source_target_pairs={{0,16},{4,20},{8,24},{12,28},{16,0},{20,4},{24,8},{28,12},{1,17},{... | collective-permute-start | bytes 98312 | tf_op jit(solution)/shard_map/ppermute | solution.py:24
  33.4 0.7 %collective-permute-done.8.far_ref = bf16[1,128,128]{2,1,0:T(8,128)(2,1)S(1)} collective-permute-done((bf16[1,128,128]{2,1,0:T(8,128)(2,1)S(1)}, bf16[1,128,128]{2,1,0:T(8,128)(2,1)S(1)}, u32[]{:S(2)}, u32[]{:S(2)}) %collective-permute-start.8) | collective-permute-done | bytes 32800 | tf_op jit(solution)/shard_map/ppermute | solution.py:24
  34.1 0.3 shard_map.124
  34.4 1.6 %collective-permute-start.12 = (bf16[1,128,128]{2,1,0:T(8,128)(2,1)S(1)}, bf16[1,128,128]{2,1,0:T(8,128)(2,1)S(1)}, u32[]{:S(2)}, u32[]{:S(2)}) collective-permute-start(bf16[1,128,128]{2,1,0:T(8,128)(2,1)S(1)} %get-tuple-element.44), channel_id=1, source_target_pairs={{0,4},{4,0},{8,12},{12,8},{16,20},{20,16},{24,28},{28,24},{1,5},{5... | collective-permute-start | bytes 98312 | tf_op jit(solution)/shard_map/ppermute | solution.py:24
  36.0 0.6 %collective-permute-done.11.far_ref = bf16[1,128,128]{2,1,0:T(8,128)(2,1)S(1)} collective-permute-done((bf16[1,128,128]{2,1,0:T(8,128)(2,1)S(1)}, bf16[1,128,128]{2,1,0:T(8,128)(2,1)S(1)}, u32[]{:S(2)}, u32[]{:S(2)}) %collective-permute-start.11) | collective-permute-done | bytes 32800 | tf_op jit(solution)/shard_map/ppermute | solution.py:24
  36.6 0.3 shard_map.128
  36.9 2.0 %collective-permute-start.13 = (bf16[1,128,128]{2,1,0:T(8,128)(2,1)S(1)}, bf16[1,128,128]{2,1,0:T(8,128)(2,1)S(1)}, u32[]{:S(2)}, u32[]{:S(2)}) collective-permute-start(bf16[1,128,128]{2,1,0:T(8,128)(2,1)S(1)} %get-tuple-element.45), channel_id=1, source_target_pairs={{0,4},{4,0},{8,12},{12,8},{16,20},{20,16},{24,28},{28,24},{1,5},{5... | collective-permute-start | bytes 98312 | tf_op jit(solution)/shard_map/ppermute | solution.py:24
  38.8 0.0 copy-done.1
  38.8 0.0 copy-done.2
  38.8 0.8 %shard_map.129 = (bf16[4,256,128]{2,1,0:T(8,128)(2,1)S(1)}, f32[256,512]{1,0:T(8,128)S(1)}, f32[256,512]{1,0:T(8,128)S(1)}) custom-call(bf16[4,256,256]{2,1,0:T(8,128)(2,1)S(1)} %get-tuple-element.46.attend_ref, bf16[4,256,256]{2,1,0:T(8,128)(2,1)S(1)} %get-tuple-element.47.solved_ref, bf16[4,256,128]{2,1,0:T(8,128)(2,1)S(1)} %get-tuple-element.48.start_ref, ...), custom_call_target="tpu_custom_call" | custom-call | flops 134217728 | bytes 1048576 | tf_op jit(solution)/shard_map/pallas_call | solution.py:74
  39.6 0.0 collective-permute-done.12.refs_2_
  39.6 1.2 %collective-permute-done.13.refs_3_ = bf16[1,128,128]{2,1,0:T(8,128)(2,1)S(1)} collective-permute-done((bf16[1,128,128]{2,1,0:T(8,128)(2,1)S(1)}, bf16[1,128,128]{2,1,0:T(8,128)(2,1)S(1)}, u32[]{:S(2)}, u32[]{:S(2)}) %collective-permute-start.13) | collective-permute-done | bytes 32800 | tf_op jit(solution)/shard_map/ppermute | solution.py:24
  40.8 0.0 copy-done
  40.8 0.0 copy-done.3
  40.8 0.7 %shard_map.133 = bf16[64,2304]{1,0:T(8,128)(2,1)S(1)} custom-call(bf16[1,128,128]{2,1,0:T(8,128)(2,1)S(1)} %get-tuple-element.40.refs_0_, bf16[1,128,128]{2,1,0:T(8,128)(2,1)S(1)} %get-tuple-element.43.refs_1_, bf16[1,128,128]{2,1,0:T(8,128)(2,1)S(1)} %collective-permute-done.12.refs_2_, bf16[1,128,128]{2,1,0:T(8,128)(2,1)S(1)} %collective-permute-done.13.refs_3_, ...), custom_call_target="tpu_custom_call" | custom-call | flops 150994944 | bytes 2359296 | tf_op jit(solution)/shard_map/pallas_call | solution.py:74
  41.5 0.1 collective-permute-start.15
  41.6 0.7 %shard_map.131 = bf16[64,2304]{1,0:T(8,128)(2,1)S(1)} custom-call(bf16[1,128,128]{2,1,0:T(8,128)(2,1)S(1)} %get-tuple-element.40.refs_0_, bf16[1,128,128]{2,1,0:T(8,128)(2,1)S(1)} %get-tuple-element.43.refs_1_, bf16[1,128,128]{2,1,0:T(8,128)(2,1)S(1)} %collective-permute-done.12.refs_2_, bf16[1,128,128]{2,1,0:T(8,128)(2,1)S(1)} %collective-permute-done.13.refs_3_, ...), custom_call_target="tpu_custom_call" | custom-call | flops 150994944 | bytes 2359296 | tf_op jit(solution)/shard_map/pallas_call | solution.py:74
  42.3 0.6 %collective-permute-start.14 = (bf16[64,2304]{1,0:T(8,128)(2,1)S(1)}, bf16[64,2304]{1,0:T(8,128)(2,1)S(1)}, u32[]{:S(2)}, u32[]{:S(2)}) collective-permute-start(bf16[64,2304]{1,0:T(8,128)(2,1)S(1)} %shard_map.131), channel_id=1, source_target_pairs={{0,1},{1,0},{2,3},{3,2},{4,5},{5,4},{6,7},{7,6},{8,9},{9,8},{10,11... | collective-permute-start | bytes 884744 | tf_op jit(solution)/shard_map/ppermute | solution.py:24
  42.9 0.7 %shard_map.132 = f32[64,2304]{1,0:T(8,128)S(1)} custom-call(bf16[1,128,128]{2,1,0:T(8,128)(2,1)S(1)} %get-tuple-element.40.refs_0_, bf16[1,128,128]{2,1,0:T(8,128)(2,1)S(1)} %get-tuple-element.43.refs_1_, bf16[1,128,128]{2,1,0:T(8,128)(2,1)S(1)} %collective-permute-done.12.refs_2_, bf16[1,128,128]{2,1,0:T(8,128)(2,1)S(1)} %collective-permute-done.13.refs_3_, ...), custom_call_target="tpu_custom_call" | custom-call | flops 150994944 | bytes 2359296 | tf_op jit(solution)/shard_map/pallas_call | solution.py:74
  43.5 0.7 %shard_map.130 = f32[64,2304]{1,0:T(8,128)S(1)} custom-call(bf16[1,128,128]{2,1,0:T(8,128)(2,1)S(1)} %get-tuple-element.40.refs_0_, bf16[1,128,128]{2,1,0:T(8,128)(2,1)S(1)} %get-tuple-element.43.refs_1_, bf16[1,128,128]{2,1,0:T(8,128)(2,1)S(1)} %collective-permute-done.12.refs_2_, bf16[1,128,128]{2,1,0:T(8,128)(2,1)S(1)} %collective-permute-done.13.refs_3_, ...), custom_call_target="tpu_custom_call" | custom-call | flops 150994944 | bytes 2359296 | tf_op jit(solution)/shard_map/pallas_call | solution.py:74
  44.2 0.0 collective-permute-done.15
  44.3 0.1 convert_add_fusion
  44.3 1.5 %collective-permute-start.16 = (bf16[64,2304]{1,0:T(8,128)(2,1)S(1)}, bf16[64,2304]{1,0:T(8,128)(2,1)S(1)}, u32[]{:S(2)}, u32[]{:S(2)}) collective-permute-start(bf16[64,2304]{1,0:T(8,128)(2,1)S(1)} %convert_add_fusion), channel_id=1, source_target_pairs={{0,2},{1,3},{2,0},{3,1},{4,6},{5,7},{6,4},{7,5},{8,10},{9,11},{10,... | collective-permute-start | bytes 884744 | tf_op jit(solution)/shard_map/ppermute | solution.py:24
  45.8 0.0 collective-permute-done.14
  45.8 0.1 convert_add_fusion.1
  45.9 7.5 %collective-permute-done.16 = bf16[64,2304]{1,0:T(8,128)(2,1)S(1)} collective-permute-done((bf16[64,2304]{1,0:T(8,128)(2,1)S(1)}, bf16[64,2304]{1,0:T(8,128)(2,1)S(1)}, u32[]{:S(2)}, u32[]{:S(2)}) %collective-permute-start.16) | collective-permute-done | bytes 294944 | tf_op jit(solution)/shard_map/ppermute | solution.py:24
  53.3 0.8 %add_convert_fusion = bf16[64,2304]{1,0:T(8,128)(2,1)} fusion(f32[64,2304]{1,0:T(8,128)S(1)} %convert_add_fusion.1, bf16[64,2304]{1,0:T(8,128)(2,1)S(1)} %collective-permute-done.16), kind=kLoop, calls=%fused_computation | loop fusion | flops 442368 | bytes 1179648 | tf_op jit(solution)/shard_map/convert_element_type | solution.py:571
  (3 shorter events, 0.1 us)
Async XLA Ops:
  0.0 10.5 %collective-permute-start = (bf16[64,2304]{1,0:T(8,128)(2,1)}, bf16[64,2304]{1,0:T(8,128)(2,1)S(1)}, u32[]{:S(2)}, u32[]{:S(2)}) collective-permute-start(bf16[64,2304]{1,0:T(8,128)(2,1)} %hidden_ref.1), channel_id=1, source_target_pairs={{0,2},{1,3},{2,0},{3,1},{4,6},{5,7},{6,4},{7,5},{8,10},{9,11},{10,... | collective-permute-start | bytes 884744 | tf_op jit(solution)/shard_map/ppermute | solution.py:24
  3.7 4.2 %collective-permute-start.2 = (bf16[8,2304]{1,0:T(8,128)(2,1)S(1)}, bf16[8,2304]{1,0:T(8,128)(2,1)S(1)}, u32[]{:S(2)}, u32[]{:S(2)}) collective-permute-start(bf16[8,2304]{1,0:T(8,128)(2,1)S(1)} %slice.3), channel_id=1, source_target_pairs={{3,5},{7,9},{11,13},{15,17},{19,21},{23,25},{27,29}} | collective-permute-start | bytes 110600 | tf_op jit(solution)/shard_map/ppermute | solution.py:56
  4.4 3.5 %collective-permute-start.1 = (bf16[8,2304]{1,0:T(8,128)(2,1)S(1)}, bf16[8,2304]{1,0:T(8,128)(2,1)S(1)}, u32[]{:S(2)}, u32[]{:S(2)}) collective-permute-start(bf16[8,2304]{1,0:T(8,128)(2,1)S(1)} %slice.3), channel_id=1, source_target_pairs={{3,6},{7,10},{11,14},{15,18},{19,22},{23,26},{27,30}} | collective-permute-start | bytes 110600 | tf_op jit(solution)/shard_map/ppermute | solution.py:56
  5.1 6.1 %collective-permute-start.4 = (bf16[64,2304]{1,0:T(8,128)(2,1)}, bf16[64,2304]{1,0:T(8,128)(2,1)S(1)}, u32[]{:S(2)}, u32[]{:S(2)}) collective-permute-start(bf16[64,2304]{1,0:T(8,128)(2,1)} %hidden_ref.1), channel_id=1, source_target_pairs={{0,1},{1,0},{2,3},{3,2},{4,5},{5,4},{6,7},{7,6},{8,9},{9,8},{10,11... | collective-permute-start | bytes 884744 | tf_op jit(solution)/shard_map/ppermute | solution.py:24
  10.6 1.7 %collective-permute-start.5 = (bf16[64,2304]{1,0:T(8,128)(2,1)S(1)}, bf16[64,2304]{1,0:T(8,128)(2,1)S(1)}, u32[]{:S(2)}, u32[]{:S(2)}) collective-permute-start(bf16[64,2304]{1,0:T(8,128)(2,1)S(1)} %collective-permute-done.refs_3_), channel_id=1, source_target_pairs={{0,1},{1,0},{2,3},{3,2},{4,5},{5,4},{6,7},{7,6},{8,9},{9,8},{10,11... | collective-permute-start | bytes 884744 | tf_op jit(solution)/shard_map/ppermute | solution.py:24
  10.6 1.7 %collective-permute-start.3 = (bf16[16,2304]{1,0:T(8,128)(2,1)S(1)}, bf16[16,2304]{1,0:T(8,128)(2,1)S(1)}, u32[]{:S(2)}, u32[]{:S(2)}) collective-permute-start(bf16[16,2304]{1,0:T(8,128)(2,1)S(1)} %shard_map.119.refs_0_), channel_id=1, source_target_pairs={{0,1},{1,0},{2,3},{3,2},{4,5},{5,4},{6,7},{7,6},{8,9},{9,8},{10,11... | collective-permute-start | bytes 221192 | tf_op jit(solution)/shard_map/ppermute | solution.py:24
  12.2 26.6 %copy-start.1 = (bf16[2304,128]{1,0:T(8,128)(2,1)S(1)}, bf16[2304,128]{1,0:T(8,128)(2,1)}, u32[]{:S(2)}) copy-start(bf16[2304,128]{1,0:T(8,128)(2,1)} %down_ref.1) | copy-start | bytes 1769476
  12.2 26.6 %copy-start.2 = (bf16[128,512]{1,0:T(8,128)(2,1)S(1)}, bf16[128,512]{1,0:T(8,128)(2,1)}, u32[]{:S(2)}) copy-start(bf16[128,512]{1,0:T(8,128)(2,1)} %up_ref.1) | copy-start | bytes 393220
  19.3 4.7 %collective-permute-start.6 = (bf16[1,128,256]{2,1,0:T(8,128)(2,1)S(1)}, bf16[1,128,256]{2,1,0:T(8,128)(2,1)S(1)}, u32[]{:S(2)}, u32[]{:S(2)}) collective-permute-start(bf16[1,128,256]{2,1,0:T(8,128)(2,1)S(1)} %get-tuple-element.39), channel_id=1, source_target_pairs={{0,4},{4,0},{8,12},{12,8},{16,20},{20,16},{24,28},{28,24},{1,5},{5... | collective-permute-start | bytes 196616 | tf_op jit(solution)/shard_map/ppermute | solution.py:24
  20.7 5.3 %collective-permute-start.9 = (bf16[1,128,256]{2,1,0:T(8,128)(2,1)S(1)}, bf16[1,128,256]{2,1,0:T(8,128)(2,1)S(1)}, u32[]{:S(2)}, u32[]{:S(2)}) collective-permute-start(bf16[1,128,256]{2,1,0:T(8,128)(2,1)S(1)} %get-tuple-element.42), channel_id=1, source_target_pairs={{0,4},{4,0},{8,12},{12,8},{16,20},{20,16},{24,28},{28,24},{1,5},{5... | collective-permute-start | bytes 196616 | tf_op jit(solution)/shard_map/ppermute | solution.py:24
  24.0 16.8 %copy-start = (bf16[512,2304]{1,0:T(8,128)(2,1)S(1)}, bf16[512,2304]{1,0:T(8,128)(2,1)}, u32[]{:S(2)}) copy-start(bf16[512,2304]{1,0:T(8,128)(2,1)} %refs_8_.9) | copy-start | bytes 7077892
  24.0 16.8 %copy-start.3 = (f32[128]{0:T(128)S(1)}, f32[128]{0:T(128)}, u32[]{:S(2)}) copy-start(f32[128]{0:T(128)} %param.22) | copy-start | bytes 1540
  24.2 4.5 %collective-permute-start.7 = (bf16[1,128,256]{2,1,0:T(8,128)(2,1)S(1)}, bf16[1,128,256]{2,1,0:T(8,128)(2,1)S(1)}, u32[]{:S(2)}, u32[]{:S(2)}) collective-permute-start(bf16[1,128,256]{2,1,0:T(8,128)(2,1)S(1)} %shard_map.121.own_ref), channel_id=1, source_target_pairs={{0,8},{4,12},{8,0},{12,4},{16,24},{20,28},{24,16},{28,20},{1,9},{5... | collective-permute-start | bytes 196616 | tf_op jit(solution)/shard_map/ppermute | solution.py:24
  26.2 5.3 %collective-permute-start.10 = (bf16[1,128,256]{2,1,0:T(8,128)(2,1)S(1)}, bf16[1,128,256]{2,1,0:T(8,128)(2,1)S(1)}, u32[]{:S(2)}, u32[]{:S(2)}) collective-permute-start(bf16[1,128,256]{2,1,0:T(8,128)(2,1)S(1)} %shard_map.125.own_ref), channel_id=1, source_target_pairs={{0,8},{4,12},{8,0},{12,4},{16,24},{20,28},{24,16},{28,20},{1,9},{5... | collective-permute-start | bytes 196616 | tf_op jit(solution)/shard_map/ppermute | solution.py:24
  28.9 5.2 %collective-permute-start.8 = (bf16[1,128,128]{2,1,0:T(8,128)(2,1)S(1)}, bf16[1,128,128]{2,1,0:T(8,128)(2,1)S(1)}, u32[]{:S(2)}, u32[]{:S(2)}) collective-permute-start(bf16[1,128,128]{2,1,0:T(8,128)(2,1)S(1)} %shard_map.123), channel_id=1, source_target_pairs={{0,16},{4,20},{8,24},{12,28},{16,0},{20,4},{24,8},{28,12},{1,17},{... | collective-permute-start | bytes 98312 | tf_op jit(solution)/shard_map/ppermute | solution.py:24
  31.7 4.9 %collective-permute-start.11 = (bf16[1,128,128]{2,1,0:T(8,128)(2,1)S(1)}, bf16[1,128,128]{2,1,0:T(8,128)(2,1)S(1)}, u32[]{:S(2)}, u32[]{:S(2)}) collective-permute-start(bf16[1,128,128]{2,1,0:T(8,128)(2,1)S(1)} %shard_map.127), channel_id=1, source_target_pairs={{0,16},{4,20},{8,24},{12,28},{16,0},{20,4},{24,8},{28,12},{1,17},{... | collective-permute-start | bytes 98312 | tf_op jit(solution)/shard_map/ppermute | solution.py:24
  34.4 5.3 %collective-permute-start.12 = (bf16[1,128,128]{2,1,0:T(8,128)(2,1)S(1)}, bf16[1,128,128]{2,1,0:T(8,128)(2,1)S(1)}, u32[]{:S(2)}, u32[]{:S(2)}) collective-permute-start(bf16[1,128,128]{2,1,0:T(8,128)(2,1)S(1)} %get-tuple-element.44), channel_id=1, source_target_pairs={{0,4},{4,0},{8,12},{12,8},{16,20},{20,16},{24,28},{28,24},{1,5},{5... | collective-permute-start | bytes 98312 | tf_op jit(solution)/shard_map/ppermute | solution.py:24
  36.9 4.0 %collective-permute-start.13 = (bf16[1,128,128]{2,1,0:T(8,128)(2,1)S(1)}, bf16[1,128,128]{2,1,0:T(8,128)(2,1)S(1)}, u32[]{:S(2)}, u32[]{:S(2)}) collective-permute-start(bf16[1,128,128]{2,1,0:T(8,128)(2,1)S(1)} %get-tuple-element.45), channel_id=1, source_target_pairs={{0,4},{4,0},{8,12},{12,8},{16,20},{20,16},{24,28},{28,24},{1,5},{5... | collective-permute-start | bytes 98312 | tf_op jit(solution)/shard_map/ppermute | solution.py:24
  41.5 2.7 %collective-permute-start.15 = (bf16[64,2304]{1,0:T(8,128)(2,1)S(1)}, bf16[64,2304]{1,0:T(8,128)(2,1)S(1)}, u32[]{:S(2)}, u32[]{:S(2)}) collective-permute-start(bf16[64,2304]{1,0:T(8,128)(2,1)S(1)} %shard_map.133), channel_id=1, source_target_pairs={{0,1},{1,0},{2,3},{3,2},{4,5},{5,4},{6,7},{7,6},{8,9},{9,8},{10,11... | collective-permute-start | bytes 884744 | tf_op jit(solution)/shard_map/ppermute | solution.py:24
  42.3 3.5 %collective-permute-start.14 = (bf16[64,2304]{1,0:T(8,128)(2,1)S(1)}, bf16[64,2304]{1,0:T(8,128)(2,1)S(1)}, u32[]{:S(2)}, u32[]{:S(2)}) collective-permute-start(bf16[64,2304]{1,0:T(8,128)(2,1)S(1)} %shard_map.131), channel_id=1, source_target_pairs={{0,1},{1,0},{2,3},{3,2},{4,5},{5,4},{6,7},{7,6},{8,9},{9,8},{10,11... | collective-permute-start | bytes 884744 | tf_op jit(solution)/shard_map/ppermute | solution.py:24
  44.3 9.0 %collective-permute-start.16 = (bf16[64,2304]{1,0:T(8,128)(2,1)S(1)}, bf16[64,2304]{1,0:T(8,128)(2,1)S(1)}, u32[]{:S(2)}, u32[]{:S(2)}) collective-permute-start(bf16[64,2304]{1,0:T(8,128)(2,1)S(1)} %convert_add_fusion), channel_id=1, source_target_pairs={{0,2},{1,3},{2,0},{3,1},{4,6},{5,7},{6,4},{7,5},{8,10},{9,11},{10,... | collective-permute-start | bytes 884744 | tf_op jit(solution)/shard_map/ppermute | solution.py:24

commit v14 on v10

--- a/solution.py
+++ b/solution.py
@@ -93,25 +93,27 @@
 
 
 def load_body(
-    hidden_ref, decay_down_ref, gate_down_ref, beta_ref, weight_ref,
-    own_ref, weights, downs, betas, sems,
+    hidden_ref, decay_down_ref, beta_ref, weight_ref, own_ref, weights, downs, betas, sems
 ):
-    rank = decay_down_ref.shape[1]
+    rank, heads = decay_down_ref.shape[1], beta_ref.shape[0]
+    beta = pltpu.make_async_copy(beta_ref, betas, sems.at[0])
     copies = [
-        pltpu.make_async_copy(hidden_ref, own_ref, sems.at[0]),
-        pltpu.make_async_copy(decay_down_ref, downs.at[:, pl.ds(0, rank)], sems.at[1]),
-        pltpu.make_async_copy(gate_down_ref, downs.at[:, pl.ds(rank, rank)], sems.at[2]),
-        pltpu.make_async_copy(beta_ref, betas, sems.at[3]),
+        pltpu.make_async_copy(hidden_ref, own_ref, sems.at[1]),
+        pltpu.make_async_copy(decay_down_ref, downs.at[:, pl.ds(0, rank)], sems.at[2]),
     ]
     for c in range(2):
-        copies.append(pltpu.make_async_copy(weight_ref.at[c], weights.at[c], sems.at[4 + c]))
-    for copy in copies:
+        copies.append(pltpu.make_async_copy(weight_ref.at[c], weights.at[c], sems.at[3 + c]))
+    for copy in [beta] + copies:
         copy.start()
+    beta.wait()
+    below = jnp.zeros((rank - heads, betas.shape[1]), f32)
+    wide = jnp.concatenate([betas[...].astype(f32), below], axis=0)
+    downs[:, rank:] = wide.T.astype(bf16)
     for copy in copies:
         copy.wait()
 
 
-def load(own, decay_down, gate_down, beta, weight):
+def load(own, decay_down, beta, weight):
     width, rank = decay_down.shape
     return vmem_call(
         load_body,
@@ -119,23 +121,22 @@
             jax.ShapeDtypeStruct(own.shape, bf16),
             jax.ShapeDtypeStruct((2, *weight.shape[1:]), bf16),
             jax.ShapeDtypeStruct((width, 2 * rank), bf16),
-            jax.ShapeDtypeStruct(beta.shape, bf16),
         ),
-        (own, decay_down, gate_down, beta, weight),
-        scratch=[pltpu.SemaphoreType.DMA((6,))],
-        hbm=5,
-        grant=8,
+        (own, decay_down, beta, weight),
+        scratch=[pltpu.VMEM(beta.shape, bf16), pltpu.SemaphoreType.DMA((5,))],
+        hbm=4,
+        grant=12,
     )
 
 
 def front_body(slab_count, *refs):
     (one_ref, two_ref, *slab_refs), refs = refs[: slab_count + 1], refs[slab_count + 1 :]
-    (own_rows_ref, weights, downs, betas), refs = refs[:4], refs[4:]
+    (own_rows_ref, weights, downs), refs = refs[:3], refs[3:]
     hbm_refs, refs = refs[:5], refs[5:]
     (own_refs, other_refs), refs = (refs[:GROUPS], refs[GROUPS : 2 * GROUPS]), refs[2 * GROUPS :]
-    (solved_ref, attend_ref, start_ref, gate_ref), refs = refs[:4], refs[4:]
+    (solved_ref, attend_ref, start_ref, rows_ref), refs = refs[:4], refs[4:]
     loaded, refs = refs[:5], refs[5:]
-    rows_ref, projected, running_ref, parts_ref, mixing, inverse, sides, sems = refs
+    projected, running_ref, parts_ref, mixing, inverse, sides, sems = refs
     rates, decay_up_ref, bias_ref, conv_ref, value_weight = loaded
     weight_ref = hbm_refs[-1]
     heads, count, size = start_ref.shape
@@ -181,12 +182,11 @@
         del pending[:number]
 
     project_next(2)
-    low = dot(rows_ref[RIM:, :], downs[...]).astype(bf16)
-    gate_ref[...] = low[:, rank:]
-    strength = jax.nn.sigmoid(dot(rows_ref[RIM:, :], betas[...], ((1,), (1,))))
+    low = dot(rows_ref[RIM:, :], downs[...])
+    strength = jax.nn.sigmoid(low[:, rank:])
     for copy in small:
         copy.wait()
-    running_ref[...] = dot(low[:, :rank], decay_up_ref[...])
+    running_ref[...] = dot(low[:, :rank].astype(bf16), decay_up_ref[...])
     tiles = [slice(a * chunk, (a + 1) * chunk) for a in range(chunks)]
     for h in range(heads):
         lanes = slice(h * size, (h + 1) * size)
@@ -353,13 +353,12 @@
             jax.ShapeDtypeStruct((heads, count, 2 * size), bf16),
             jax.ShapeDtypeStruct((heads, count, count), bf16),
             jax.ShapeDtypeStruct((heads, count, size), bf16),
-            jax.ShapeDtypeStruct((count, fetched[2].shape[1] // 2), bf16),
+            jax.ShapeDtypeStruct((RIM + count, width), bf16),
         ),
         (*rims, *slabs, *fetched, *loaded, weight),
         scratch=[
             *buffers,
             pltpu.VMEM((width, channels), bf16),
-            pltpu.VMEM((RIM + count, width), bf16),
             pltpu.VMEM((3 * heads, RIM + count, size), f32),
             pltpu.VMEM((count, channels), f32),
             pltpu.VMEM((2 * count, channels), bf16),
@@ -375,9 +374,12 @@
     )
 
 
-def rows_body(attend_ref, solved_ref, start_ref, low_ref, up_ref, raised_ref, output_ref, gate_ref):
+def rows_body(
+    attend_ref, solved_ref, start_ref, rows_ref, down_ref, up_ref, raised_ref, output_ref, gate_ref
+):
     heads, _, size = start_ref.shape
-    gate_ref[...] = jax.nn.sigmoid(dot(low_ref[...], up_ref[...]))
+    low = dot(rows_ref[RIM:, :], down_ref[...]).astype(bf16)
+    gate_ref[...] = jax.nn.sigmoid(dot(low, up_ref[...]))
     count = attend_ref.shape[1]
     block = math.gcd(count, 128)
     for h in range(heads):
@@ -543,9 +545,9 @@
     channels = heads * size
     devices = lax.axis_size("head")
     weight = qkv_weight.transpose(1, 0, 2)
-    fetched = load(hidden_in, decay_down, gate_down, beta_weight.T, weight)
+    fetched = load(hidden_in, decay_down, beta_weight.T, weight)
     slabs, rims, fetched = gathered(hidden_in, fetched)
-    *pairs, solved, attend, start, gate_low = front(
+    *pairs, solved, attend, start, rows = front(
         rims, slabs, fetched, (decay_log, decay_up, dt_bias[None], conv_weight), weight, size
     )
     count = start.shape[1]
@@ -556,7 +558,7 @@
             jax.ShapeDtypeStruct((count, channels), f32),
             jax.ShapeDtypeStruct((count, channels), f32),
         ),
-        (attend, solved, start, gate_low, gate_up),
+        (attend, solved, start, rows, gate_down, gate_up),
         grant=8,
         flops=2 * heads * count * count * 2 * size,
         moved=4 * heads * count * count,

time: 53.6 us -> 53.4 us (level)
  no operation moved by 1% of the time
where the time goes in v14:
time: 53.4 us; the launch traced here: 53.2 us
  starting transfers between devices  19.8 us (37%)
  waiting for transfers between devices  18.1 us (34%)
  Pallas kernels  13.3 us (25%)
  other arithmetic  0.88 us (2%)
  local copies, waits for them, and re-layouts  0.82 us (2%)
    ppermute x15, starting transfers between devices, swapped(): lax.ppermute(block, axis, [(i, i ^ bit) for i in range(lax.axis_size(axis...  18.5 us
    ppermute x15, waiting for transfers between devices, swapped(): lax.ppermute(block, axis, [(i, i ^ bit) for i in range(lax.axis_size(axis...  18.1 us
    pallas_call x14, Pallas kernels, vmem_call(): pl.pallas_call(body, out_shape=out_shape, in_specs=[pl.BlockSpec(memory_s...  13.3 us
    ppermute x2, starting transfers between devices, gathered(): lax.ppermute(tail, ('seq', 'head'), rim_route(target))  1.32 us
  transfers between devices with their start and end apart: 17, of which 9 were waited for; matrix products, arithmetic and copies ran while one was open for 2% of the time, Pallas kernels for 10%

profile of v14, /device:TPU:0, one launch (start us, length us, event | category | flops | bytes accessed | tf_op | source)
XLA Modules:
  0.0 53.2 jit_solution(2658602112583470827)
XLA Ops:
  0.0 2.9 %collective-permute-start = (bf16[64,2304]{1,0:T(8,128)(2,1)}, bf16[64,2304]{1,0:T(8,128)(2,1)S(1)}, u32[]{:S(2)}, u32[]{:S(2)}) collective-permute-start(bf16[64,2304]{1,0:T(8,128)(2,1)} %hidden_ref.1), channel_id=1, source_target_pairs={{0,2},{1,3},{2,0},{3,1},{4,6},{5,7},{6,4},{7,5},{8,10},{9,11},{10,... | collective-permute-start | bytes 884744 | tf_op jit(solution)/shard_map/ppermute | solution.py:24
  2.9 0.8 %slice.3 = bf16[8,2304]{1,0:T(8,128)(2,1)S(1)} slice(bf16[64,2304]{1,0:T(8,128)(2,1)} %hidden_ref.1), slice={[56:64], [0:2304]} | slice | bytes 73728 | tf_op jit(solution)/shard_map/slice | solution.py:54
  3.7 0.7 %collective-permute-start.2 = (bf16[8,2304]{1,0:T(8,128)(2,1)S(1)}, bf16[8,2304]{1,0:T(8,128)(2,1)S(1)}, u32[]{:S(2)}, u32[]{:S(2)}) collective-permute-start(bf16[8,2304]{1,0:T(8,128)(2,1)S(1)} %slice.3), channel_id=1, source_target_pairs={{3,5},{7,9},{11,13},{15,17},{19,21},{23,25},{27,29}} | collective-permute-start | bytes 110600 | tf_op jit(solution)/shard_map/ppermute | solution.py:56
  4.4 0.7 %collective-permute-start.1 = (bf16[8,2304]{1,0:T(8,128)(2,1)S(1)}, bf16[8,2304]{1,0:T(8,128)(2,1)S(1)}, u32[]{:S(2)}, u32[]{:S(2)}) collective-permute-start(bf16[8,2304]{1,0:T(8,128)(2,1)S(1)} %slice.3), channel_id=1, source_target_pairs={{3,6},{7,10},{11,14},{15,18},{19,22},{23,26},{27,30}} | collective-permute-start | bytes 110600 | tf_op jit(solution)/shard_map/ppermute | solution.py:56
  5.1 0.1 collective-permute-start.4
  5.2 2.7 %shard_map.118 = (bf16[64,2304]{1,0:T(8,128)(2,1)S(1)}, bf16[2,2304,512]{2,1,0:T(8,128)(2,1)S(1)}, bf16[2304,256]{1,0:T(8,128)(2,1)S(1)}) custom-call(bf16[64,2304]{1,0:T(8,128)(2,1)} %hidden_ref.1, bf16[2304,128]{1,0:T(8,128)(2,1)} %decay_down_ref.1, bf16[4,2304]{1,0:T(4,128)(2,1)} %bitcast.8, bf16[3,2304,512]{2,1,0:T(8,128)(2,1)} %bitcast.6), custom_call_target="tpu_custom_call" | custom-call | tf_op jit(solution)/shard_map/pallas_call | solution.py:74
  7.9 0.0 collective-permute-done.2.refs_1_
  7.9 0.0 collective-permute-done.1.refs_0_
  7.9 2.6 %collective-permute-done.refs_3_ = bf16[64,2304]{1,0:T(8,128)(2,1)S(1)} collective-permute-done((bf16[64,2304]{1,0:T(8,128)(2,1)}, bf16[64,2304]{1,0:T(8,128)(2,1)S(1)}, u32[]{:S(2)}, u32[]{:S(2)}) %collective-permute-start) | collective-permute-done | bytes 294944 | tf_op jit(solution)/shard_map/ppermute | solution.py:24
  10.6 0.0 collective-permute-start.5
  10.6 0.6 %collective-permute-start.3 = (bf16[16,2304]{1,0:T(8,128)(2,1)S(1)}, bf16[16,2304]{1,0:T(8,128)(2,1)S(1)}, u32[]{:S(2)}, u32[]{:S(2)}) collective-permute-start(bf16[16,2304]{1,0:T(8,128)(2,1)S(1)} %shard_map.119.refs_0_), channel_id=1, source_target_pairs={{0,1},{1,0},{2,3},{3,2},{4,5},{5,4},{6,7},{7,6},{8,9},{9,8},{10,11... | collective-permute-start | bytes 221192 | tf_op jit(solution)/shard_map/ppermute | solution.py:24
  11.1 0.0 collective-permute-done.4.refs_2_
  11.1 1.1 %collective-permute-done.3.refs_1_ = bf16[16,2304]{1,0:T(8,128)(2,1)S(1)} collective-permute-done((bf16[16,2304]{1,0:T(8,128)(2,1)S(1)}, bf16[16,2304]{1,0:T(8,128)(2,1)S(1)}, u32[]{:S(2)}, u32[]{:S(2)}) %collective-permute-start.3) | collective-permute-done | bytes 73760 | tf_op jit(solution)/shard_map/ppermute | solution.py:24
  12.2 0.0 collective-permute-done.5.refs_4_
  12.2 0.0 copy-start.1
  12.2 0.0 copy-start.2
  12.2 7.0 %shard_map.120 = (bf16[1,128,256]{2,1,0:T(8,128)(2,1)S(1)}, bf16[1,128,256]{2,1,0:T(8,128)(2,1)S(1)}, bf16[1,128,256]{2,1,0:T(8,128)(2,1)S(1)}, bf16[1,128,256]{...) custom-call(bf16[16,2304]{1,0:T(8,128)(2,1)S(1)} %shard_map.119.refs, ...), custom_call_target="tpu_custom_call" | custom-call | flops 2415919104 | bytes 9437184 | tf_op jit(solution)/shard_map/pallas_call | solution.py:74
  19.3 1.4 %collective-permute-start.6 = (bf16[1,128,256]{2,1,0:T(8,128)(2,1)S(1)}, bf16[1,128,256]{2,1,0:T(8,128)(2,1)S(1)}, u32[]{:S(2)}, u32[]{:S(2)}) collective-permute-start(bf16[1,128,256]{2,1,0:T(8,128)(2,1)S(1)} %get-tuple-element.43), channel_id=1, source_target_pairs={{0,4},{4,0},{8,12},{12,8},{16,20},{20,16},{24,28},{28,24},{1,5},{5... | collective-permute-start | bytes 196616 | tf_op jit(solution)/shard_map/ppermute | solution.py:24
  20.7 0.6 %collective-permute-start.9 = (bf16[1,128,256]{2,1,0:T(8,128)(2,1)S(1)}, bf16[1,128,256]{2,1,0:T(8,128)(2,1)S(1)}, u32[]{:S(2)}, u32[]{:S(2)}) collective-permute-start(bf16[1,128,256]{2,1,0:T(8,128)(2,1)S(1)} %get-tuple-element.46), channel_id=1, source_target_pairs={{0,4},{4,0},{8,12},{12,8},{16,20},{20,16},{24,28},{28,24},{1,5},{5... | collective-permute-start | bytes 196616 | tf_op jit(solution)/shard_map/ppermute | solution.py:24
  21.4 2.6 %collective-permute-done.6.far_ref.partner_ref = bf16[1,128,256]{2,1,0:T(8,128)(2,1)S(1)} collective-permute-done((bf16[1,128,256]{2,1,0:T(8,128)(2,1)S(1)}, bf16[1,128,256]{2,1,0:T(8,128)(2,1)S(1)}, u32[]{:S(2)}, u32[]{:S(2)}) %collective-permute-start.6) | collective-permute-done | bytes 65568 | tf_op jit(solution)/shard_map/ppermute | solution.py:24
  24.0 0.0 copy-start
  24.0 0.0 copy-start.3
  24.0 0.2 shard_map.121.own_ref
  24.2 1.8 %collective-permute-start.7 = (bf16[1,128,256]{2,1,0:T(8,128)(2,1)S(1)}, bf16[1,128,256]{2,1,0:T(8,128)(2,1)S(1)}, u32[]{:S(2)}, u32[]{:S(2)}) collective-permute-start(bf16[1,128,256]{2,1,0:T(8,128)(2,1)S(1)} %shard_map.121.own_ref), channel_id=1, source_target_pairs={{0,8},{4,12},{8,0},{12,4},{16,24},{20,28},{24,16},{28,20},{1,9},{5... | collective-permute-start | bytes 196616 | tf_op jit(solution)/shard_map/ppermute | solution.py:24
  26.0 0.0 collective-permute-done.9.far_ref.partner_ref
  26.0 0.2 shard_map.125.own_ref
  26.2 1.0 %collective-permute-start.10 = (bf16[1,128,256]{2,1,0:T(8,128)(2,1)S(1)}, bf16[1,128,256]{2,1,0:T(8,128)(2,1)S(1)}, u32[]{:S(2)}, u32[]{:S(2)}) collective-permute-start(bf16[1,128,256]{2,1,0:T(8,128)(2,1)S(1)} %shard_map.125.own_ref), channel_id=1, source_target_pairs={{0,8},{4,12},{8,0},{12,4},{16,24},{20,28},{24,16},{28,20},{1,9},{5... | collective-permute-start | bytes 196616 | tf_op jit(solution)/shard_map/ppermute | solution.py:24
  27.2 1.5 %collective-permute-done.7.far_ref = bf16[1,128,256]{2,1,0:T(8,128)(2,1)S(1)} collective-permute-done((bf16[1,128,256]{2,1,0:T(8,128)(2,1)S(1)}, bf16[1,128,256]{2,1,0:T(8,128)(2,1)S(1)}, u32[]{:S(2)}, u32[]{:S(2)}) %collective-permute-start.7) | collective-permute-done | bytes 65568 | tf_op jit(solution)/shard_map/ppermute | solution.py:24
  28.7 0.1 shard_map.123
  28.9 2.7 %collective-permute-start.8 = (bf16[1,128,128]{2,1,0:T(8,128)(2,1)S(1)}, bf16[1,128,128]{2,1,0:T(8,128)(2,1)S(1)}, u32[]{:S(2)}, u32[]{:S(2)}) collective-permute-start(bf16[1,128,128]{2,1,0:T(8,128)(2,1)S(1)} %shard_map.123), channel_id=1, source_target_pairs={{0,16},{4,20},{8,24},{12,28},{16,0},{20,4},{24,8},{28,12},{1,17},{... | collective-permute-start | bytes 98312 | tf_op jit(solution)/shard_map/ppermute | solution.py:24
  31.5 0.0 collective-permute-done.10.far_ref
  31.5 0.2 shard_map.127
  31.7 1.7 %collective-permute-start.11 = (bf16[1,128,128]{2,1,0:T(8,128)(2,1)S(1)}, bf16[1,128,128]{2,1,0:T(8,128)(2,1)S(1)}, u32[]{:S(2)}, u32[]{:S(2)}) collective-permute-start(bf16[1,128,128]{2,1,0:T(8,128)(2,1)S(1)} %shard_map.127), channel_id=1, source_target_pairs={{0,16},{4,20},{8,24},{12,28},{16,0},{20,4},{24,8},{28,12},{1,17},{... | collective-permute-start | bytes 98312 | tf_op jit(solution)/shard_map/ppermute | solution.py:24
  33.4 0.7 %collective-permute-done.8.far_ref = bf16[1,128,128]{2,1,0:T(8,128)(2,1)S(1)} collective-permute-done((bf16[1,128,128]{2,1,0:T(8,128)(2,1)S(1)}, bf16[1,128,128]{2,1,0:T(8,128)(2,1)S(1)}, u32[]{:S(2)}, u32[]{:S(2)}) %collective-permute-start.8) | collective-permute-done | bytes 32800 | tf_op jit(solution)/shard_map/ppermute | solution.py:24
  34.1 0.3 shard_map.124
  34.4 1.6 %collective-permute-start.12 = (bf16[1,128,128]{2,1,0:T(8,128)(2,1)S(1)}, bf16[1,128,128]{2,1,0:T(8,128)(2,1)S(1)}, u32[]{:S(2)}, u32[]{:S(2)}) collective-permute-start(bf16[1,128,128]{2,1,0:T(8,128)(2,1)S(1)} %get-tuple-element.48), channel_id=1, source_target_pairs={{0,4},{4,0},{8,12},{12,8},{16,20},{20,16},{24,28},{28,24},{1,5},{5... | collective-permute-start | bytes 98312 | tf_op jit(solution)/shard_map/ppermute | solution.py:24
  36.0 0.6 %collective-permute-done.11.far_ref = bf16[1,128,128]{2,1,0:T(8,128)(2,1)S(1)} collective-permute-done((bf16[1,128,128]{2,1,0:T(8,128)(2,1)S(1)}, bf16[1,128,128]{2,1,0:T(8,128)(2,1)S(1)}, u32[]{:S(2)}, u32[]{:S(2)}) %collective-permute-start.11) | collective-permute-done | bytes 32800 | tf_op jit(solution)/shard_map/ppermute | solution.py:24
  36.6 0.3 shard_map.128
  36.9 2.0 %collective-permute-start.13 = (bf16[1,128,128]{2,1,0:T(8,128)(2,1)S(1)}, bf16[1,128,128]{2,1,0:T(8,128)(2,1)S(1)}, u32[]{:S(2)}, u32[]{:S(2)}) collective-permute-start(bf16[1,128,128]{2,1,0:T(8,128)(2,1)S(1)} %get-tuple-element.49), channel_id=1, source_target_pairs={{0,4},{4,0},{8,12},{12,8},{16,20},{20,16},{24,28},{28,24},{1,5},{5... | collective-permute-start | bytes 98312 | tf_op jit(solution)/shard_map/ppermute | solution.py:24
  38.8 0.0 copy-done.1
  38.8 0.0 copy-done.2
  38.8 0.8 %shard_map.129 = (bf16[4,256,128]{2,1,0:T(8,128)(2,1)S(1)}, f32[256,512]{1,0:T(8,128)S(1)}, f32[256,512]{1,0:T(8,128)S(1)}) custom-call(bf16[4,256,256]{2,1,0:T(8,128)(2,1)S(1)} %get-tuple-element.50.attend_ref, bf16[4,256,256]{2,1,0:T(8,128)(2,1)S(1)} %get-tuple-element.51.solved_ref, bf16[4,256,128]{2,1,0:T(8,128)(2,1)S(1)} %get-tuple-element.52.start_ref, ...), custom_call_target="tpu_custom_call" | custom-call | flops 134217728 | bytes 1048576 | tf_op jit(solution)/shard_map/pallas_call | solution.py:74
  39.6 0.0 collective-permute-done.12.refs_2_
  39.6 1.2 %collective-permute-done.13.refs_3_ = bf16[1,128,128]{2,1,0:T(8,128)(2,1)S(1)} collective-permute-done((bf16[1,128,128]{2,1,0:T(8,128)(2,1)S(1)}, bf16[1,128,128]{2,1,0:T(8,128)(2,1)S(1)}, u32[]{:S(2)}, u32[]{:S(2)}) %collective-permute-start.13) | collective-permute-done | bytes 32800 | tf_op jit(solution)/shard_map/ppermute | solution.py:24
  40.8 0.0 copy-done
  40.8 0.0 copy-done.3
  40.8 0.7 %shard_map.131 = (f32[64,2304]{1,0:T(8,128)S(1)}, bf16[64,2304]{1,0:T(8,128)(2,1)S(1)}) custom-call(bf16[1,128,128]{2,1,0:T(8,128)(2,1)S(1)} %get-tuple-element.44.refs_0_, bf16[1,128,128]{2,1,0:T(8,128)(2,1)S(1)} %get-tuple-element.47.refs_1_, bf16[1,128,128]{2,1,0:T(8,128)(2,1)S(1)} %collective-permute-done.12.refs_2_, ...), custom_call_target="tpu_custom_call" | custom-call | flops 301989888 | bytes 2359296 | tf_op jit(solution)/shard_map/pallas_call | solution.py:74
  41.6 0.1 collective-permute-start.15
  41.7 0.7 %shard_map.130 = (f32[64,2304]{1,0:T(8,128)S(1)}, bf16[64,2304]{1,0:T(8,128)(2,1)S(1)}) custom-call(bf16[1,128,128]{2,1,0:T(8,128)(2,1)S(1)} %get-tuple-element.44.refs_0_, bf16[1,128,128]{2,1,0:T(8,128)(2,1)S(1)} %get-tuple-element.47.refs_1_, bf16[1,128,128]{2,1,0:T(8,128)(2,1)S(1)} %collective-permute-done.12.refs_2_, ...), custom_call_target="tpu_custom_call" | custom-call | flops 301989888 | bytes 2359296 | tf_op jit(solution)/shard_map/pallas_call | solution.py:74
  42.4 0.6 %collective-permute-start.14 = (bf16[64,2304]{1,0:T(8,128)(2,1)S(1)}, bf16[64,2304]{1,0:T(8,128)(2,1)S(1)}, u32[]{:S(2)}, u32[]{:S(2)}) collective-permute-start(bf16[64,2304]{1,0:T(8,128)(2,1)S(1)} %get-tuple-element.58), channel_id=1, source_target_pairs={{0,1},{1,0},{2,3},{3,2},{4,5},{5,4},{6,7},{7,6},{8,9},{9,8},{10,11... | collective-permute-start | bytes 884744 | tf_op jit(solution)/shard_map/ppermute | solution.py:24
  43.0 0.3 collective-permute-done.15
  43.2 0.1 convert_add_fusion
  43.3 1.5 %collective-permute-start.16 = (bf16[64,2304]{1,0:T(8,128)(2,1)S(1)}, bf16[64,2304]{1,0:T(8,128)(2,1)S(1)}, u32[]{:S(2)}, u32[]{:S(2)}) collective-permute-start(bf16[64,2304]{1,0:T(8,128)(2,1)S(1)} %convert_add_fusion), channel_id=1, source_target_pairs={{0,2},{1,3},{2,0},{3,1},{4,6},{5,7},{6,4},{7,5},{8,10},{9,11},{10,... | collective-permute-start | bytes 884744 | tf_op jit(solution)/shard_map/ppermute | solution.py:24
  44.8 0.0 collective-permute-done.14
  44.8 0.1 convert_add_fusion.1
  44.8 7.6 %collective-permute-done.16 = bf16[64,2304]{1,0:T(8,128)(2,1)S(1)} collective-permute-done((bf16[64,2304]{1,0:T(8,128)(2,1)S(1)}, bf16[64,2304]{1,0:T(8,128)(2,1)S(1)}, u32[]{:S(2)}, u32[]{:S(2)}) %collective-permute-start.16) | collective-permute-done | bytes 294944 | tf_op jit(solution)/shard_map/ppermute | solution.py:24
  52.4 0.8 %add_convert_fusion = bf16[64,2304]{1,0:T(8,128)(2,1)} fusion(f32[64,2304]{1,0:T(8,128)S(1)} %convert_add_fusion.1, bf16[64,2304]{1,0:T(8,128)(2,1)S(1)} %collective-permute-done.16), kind=kLoop, calls=%fused_computation | loop fusion | flops 442368 | bytes 1179648 | tf_op jit(solution)/shard_map/convert_element_type | solution.py:582
  (3 shorter events, 0.1 us)
Async XLA Ops:
  0.0 10.5 %collective-permute-start = (bf16[64,2304]{1,0:T(8,128)(2,1)}, bf16[64,2304]{1,0:T(8,128)(2,1)S(1)}, u32[]{:S(2)}, u32[]{:S(2)}) collective-permute-start(bf16[64,2304]{1,0:T(8,128)(2,1)} %hidden_ref.1), channel_id=1, source_target_pairs={{0,2},{1,3},{2,0},{3,1},{4,6},{5,7},{6,4},{7,5},{8,10},{9,11},{10,... | collective-permute-start | bytes 884744 | tf_op jit(solution)/shard_map/ppermute | solution.py:24
  3.7 4.2 %collective-permute-start.2 = (bf16[8,2304]{1,0:T(8,128)(2,1)S(1)}, bf16[8,2304]{1,0:T(8,128)(2,1)S(1)}, u32[]{:S(2)}, u32[]{:S(2)}) collective-permute-start(bf16[8,2304]{1,0:T(8,128)(2,1)S(1)} %slice.3), channel_id=1, source_target_pairs={{3,5},{7,9},{11,13},{15,17},{19,21},{23,25},{27,29}} | collective-permute-start | bytes 110600 | tf_op jit(solution)/shard_map/ppermute | solution.py:56
  4.4 3.5 %collective-permute-start.1 = (bf16[8,2304]{1,0:T(8,128)(2,1)S(1)}, bf16[8,2304]{1,0:T(8,128)(2,1)S(1)}, u32[]{:S(2)}, u32[]{:S(2)}) collective-permute-start(bf16[8,2304]{1,0:T(8,128)(2,1)S(1)} %slice.3), channel_id=1, source_target_pairs={{3,6},{7,10},{11,14},{15,18},{19,22},{23,26},{27,30}} | collective-permute-start | bytes 110600 | tf_op jit(solution)/shard_map/ppermute | solution.py:56
  5.1 6.1 %collective-permute-start.4 = (bf16[64,2304]{1,0:T(8,128)(2,1)}, bf16[64,2304]{1,0:T(8,128)(2,1)S(1)}, u32[]{:S(2)}, u32[]{:S(2)}) collective-permute-start(bf16[64,2304]{1,0:T(8,128)(2,1)} %hidden_ref.1), channel_id=1, source_target_pairs={{0,1},{1,0},{2,3},{3,2},{4,5},{5,4},{6,7},{7,6},{8,9},{9,8},{10,11... | collective-permute-start | bytes 884744 | tf_op jit(solution)/shard_map/ppermute | solution.py:24
  10.6 1.7 %collective-permute-start.5 = (bf16[64,2304]{1,0:T(8,128)(2,1)S(1)}, bf16[64,2304]{1,0:T(8,128)(2,1)S(1)}, u32[]{:S(2)}, u32[]{:S(2)}) collective-permute-start(bf16[64,2304]{1,0:T(8,128)(2,1)S(1)} %collective-permute-done.refs_3_), channel_id=1, source_target_pairs={{0,1},{1,0},{2,3},{3,2},{4,5},{5,4},{6,7},{7,6},{8,9},{9,8},{10,11... | collective-permute-start | bytes 884744 | tf_op jit(solution)/shard_map/ppermute | solution.py:24
  10.6 1.7 %collective-permute-start.3 = (bf16[16,2304]{1,0:T(8,128)(2,1)S(1)}, bf16[16,2304]{1,0:T(8,128)(2,1)S(1)}, u32[]{:S(2)}, u32[]{:S(2)}) collective-permute-start(bf16[16,2304]{1,0:T(8,128)(2,1)S(1)} %shard_map.119.refs_0_), channel_id=1, source_target_pairs={{0,1},{1,0},{2,3},{3,2},{4,5},{5,4},{6,7},{7,6},{8,9},{9,8},{10,11... | collective-permute-start | bytes 221192 | tf_op jit(solution)/shard_map/ppermute | solution.py:24
  12.2 26.6 %copy-start.1 = (bf16[2304,128]{1,0:T(8,128)(2,1)S(1)}, bf16[2304,128]{1,0:T(8,128)(2,1)}, u32[]{:S(2)}) copy-start(bf16[2304,128]{1,0:T(8,128)(2,1)} %down_ref.1) | copy-start | bytes 1769476
  12.2 26.6 %copy-start.2 = (bf16[128,512]{1,0:T(8,128)(2,1)S(1)}, bf16[128,512]{1,0:T(8,128)(2,1)}, u32[]{:S(2)}) copy-start(bf16[128,512]{1,0:T(8,128)(2,1)} %up_ref.1) | copy-start | bytes 393220
  19.3 4.7 %collective-permute-start.6 = (bf16[1,128,256]{2,1,0:T(8,128)(2,1)S(1)}, bf16[1,128,256]{2,1,0:T(8,128)(2,1)S(1)}, u32[]{:S(2)}, u32[]{:S(2)}) collective-permute-start(bf16[1,128,256]{2,1,0:T(8,128)(2,1)S(1)} %get-tuple-element.43), channel_id=1, source_target_pairs={{0,4},{4,0},{8,12},{12,8},{16,20},{20,16},{24,28},{28,24},{1,5},{5... | collective-permute-start | bytes 196616 | tf_op jit(solution)/shard_map/ppermute | solution.py:24
  20.7 5.3 %collective-permute-start.9 = (bf16[1,128,256]{2,1,0:T(8,128)(2,1)S(1)}, bf16[1,128,256]{2,1,0:T(8,128)(2,1)S(1)}, u32[]{:S(2)}, u32[]{:S(2)}) collective-permute-start(bf16[1,128,256]{2,1,0:T(8,128)(2,1)S(1)} %get-tuple-element.46), channel_id=1, source_target_pairs={{0,4},{4,0},{8,12},{12,8},{16,20},{20,16},{24,28},{28,24},{1,5},{5... | collective-permute-start | bytes 196616 | tf_op jit(solution)/shard_map/ppermute | solution.py:24
  24.0 16.8 %copy-start = (bf16[512,2304]{1,0:T(8,128)(2,1)S(1)}, bf16[512,2304]{1,0:T(8,128)(2,1)}, u32[]{:S(2)}) copy-start(bf16[512,2304]{1,0:T(8,128)(2,1)} %refs_8_.5) | copy-start | bytes 7077892
  24.0 16.8 %copy-start.3 = (f32[128]{0:T(128)S(1)}, f32[128]{0:T(128)}, u32[]{:S(2)}) copy-start(f32[128]{0:T(128)} %param.22) | copy-start | bytes 1540
  24.2 4.5 %collective-permute-start.7 = (bf16[1,128,256]{2,1,0:T(8,128)(2,1)S(1)}, bf16[1,128,256]{2,1,0:T(8,128)(2,1)S(1)}, u32[]{:S(2)}, u32[]{:S(2)}) collective-permute-start(bf16[1,128,256]{2,1,0:T(8,128)(2,1)S(1)} %shard_map.121.own_ref), channel_id=1, source_target_pairs={{0,8},{4,12},{8,0},{12,4},{16,24},{20,28},{24,16},{28,20},{1,9},{5... | collective-permute-start | bytes 196616 | tf_op jit(solution)/shard_map/ppermute | solution.py:24
  26.2 5.3 %collective-permute-start.10 = (bf16[1,128,256]{2,1,0:T(8,128)(2,1)S(1)}, bf16[1,128,256]{2,1,0:T(8,128)(2,1)S(1)}, u32[]{:S(2)}, u32[]{:S(2)}) collective-permute-start(bf16[1,128,256]{2,1,0:T(8,128)(2,1)S(1)} %shard_map.125.own_ref), channel_id=1, source_target_pairs={{0,8},{4,12},{8,0},{12,4},{16,24},{20,28},{24,16},{28,20},{1,9},{5... | collective-permute-start | bytes 196616 | tf_op jit(solution)/shard_map/ppermute | solution.py:24
  28.9 5.2 %collective-permute-start.8 = (bf16[1,128,128]{2,1,0:T(8,128)(2,1)S(1)}, bf16[1,128,128]{2,1,0:T(8,128)(2,1)S(1)}, u32[]{:S(2)}, u32[]{:S(2)}) collective-permute-start(bf16[1,128,128]{2,1,0:T(8,128)(2,1)S(1)} %shard_map.123), channel_id=1, source_target_pairs={{0,16},{4,20},{8,24},{12,28},{16,0},{20,4},{24,8},{28,12},{1,17},{... | collective-permute-start | bytes 98312 | tf_op jit(solution)/shard_map/ppermute | solution.py:24
  31.7 4.9 %collective-permute-start.11 = (bf16[1,128,128]{2,1,0:T(8,128)(2,1)S(1)}, bf16[1,128,128]{2,1,0:T(8,128)(2,1)S(1)}, u32[]{:S(2)}, u32[]{:S(2)}) collective-permute-start(bf16[1,128,128]{2,1,0:T(8,128)(2,1)S(1)} %shard_map.127), channel_id=1, source_target_pairs={{0,16},{4,20},{8,24},{12,28},{16,0},{20,4},{24,8},{28,12},{1,17},{... | collective-permute-start | bytes 98312 | tf_op jit(solution)/shard_map/ppermute | solution.py:24
  34.4 5.3 %collective-permute-start.12 = (bf16[1,128,128]{2,1,0:T(8,128)(2,1)S(1)}, bf16[1,128,128]{2,1,0:T(8,128)(2,1)S(1)}, u32[]{:S(2)}, u32[]{:S(2)}) collective-permute-start(bf16[1,128,128]{2,1,0:T(8,128)(2,1)S(1)} %get-tuple-element.48), channel_id=1, source_target_pairs={{0,4},{4,0},{8,12},{12,8},{16,20},{20,16},{24,28},{28,24},{1,5},{5... | collective-permute-start | bytes 98312 | tf_op jit(solution)/shard_map/ppermute | solution.py:24
  36.9 4.0 %collective-permute-start.13 = (bf16[1,128,128]{2,1,0:T(8,128)(2,1)S(1)}, bf16[1,128,128]{2,1,0:T(8,128)(2,1)S(1)}, u32[]{:S(2)}, u32[]{:S(2)}) collective-permute-start(bf16[1,128,128]{2,1,0:T(8,128)(2,1)S(1)} %get-tuple-element.49), channel_id=1, source_target_pairs={{0,4},{4,0},{8,12},{12,8},{16,20},{20,16},{24,28},{28,24},{1,5},{5... | collective-permute-start | bytes 98312 | tf_op jit(solution)/shard_map/ppermute | solution.py:24
  41.6 1.6 %collective-permute-start.15 = (bf16[64,2304]{1,0:T(8,128)(2,1)S(1)}, bf16[64,2304]{1,0:T(8,128)(2,1)S(1)}, u32[]{:S(2)}, u32[]{:S(2)}) collective-permute-start(bf16[64,2304]{1,0:T(8,128)(2,1)S(1)} %get-tuple-element.60), channel_id=1, source_target_pairs={{0,1},{1,0},{2,3},{3,2},{4,5},{5,4},{6,7},{7,6},{8,9},{9,8},{10,11... | collective-permute-start | bytes 884744 | tf_op jit(solution)/shard_map/ppermute | solution.py:24
  42.4 2.4 %collective-permute-start.14 = (bf16[64,2304]{1,0:T(8,128)(2,1)S(1)}, bf16[64,2304]{1,0:T(8,128)(2,1)S(1)}, u32[]{:S(2)}, u32[]{:S(2)}) collective-permute-start(bf16[64,2304]{1,0:T(8,128)(2,1)S(1)} %get-tuple-element.58), channel_id=1, source_target_pairs={{0,1},{1,0},{2,3},{3,2},{4,5},{5,4},{6,7},{7,6},{8,9},{9,8},{10,11... | collective-permute-start | bytes 884744 | tf_op jit(solution)/shard_map/ppermute | solution.py:24
  43.3 9.1 %collective-permute-start.16 = (bf16[64,2304]{1,0:T(8,128)(2,1)S(1)}, bf16[64,2304]{1,0:T(8,128)(2,1)S(1)}, u32[]{:S(2)}, u32[]{:S(2)}) collective-permute-start(bf16[64,2304]{1,0:T(8,128)(2,1)S(1)} %convert_add_fusion), channel_id=1, source_target_pairs={{0,2},{1,3},{2,0},{3,1},{4,6},{5,7},{6,4},{7,5},{8,10},{9,11},{10,... | collective-permute-start | bytes 884744 | tf_op jit(solution)/shard_map/ppermute | solution.py:24

commit v15 on v14

--- a/solution.py
+++ b/solution.py
@@ -10,7 +10,7 @@
 
 RIM = 16
 BASE = 16
-GROUPS = 2
+GROUPS = 1
 MIB = 1024 * 1024
 f32 = jnp.float32
 bf16 = jnp.bfloat16

time: 53.4 us -> 52.8 us (0.989)
  starting transfers between devices: 19.8 us -> 14.8 us
  waiting for transfers between devices: 18.1 us -> 23.1 us
    ppermute x15 -> x11, starting transfers between devices: 18.5 us -> 13.5 us  [swapped(): lax.ppermute(block, axis, [(i, i ^ bit) for i in range(lax.axis_size(axis...]
    ppermute x15 -> x11, waiting for transfers between devices: 18.1 us -> 23.1 us  [swapped(): lax.ppermute(block, axis, [(i, i ^ bit) for i in range(lax.axis_size(axis...]
    pallas_call x14 -> x10, Pallas kernels: 13.3 us -> 12.8 us  [vmem_call(): pl.pallas_call(body, out_shape=out_shape, in_specs=[pl.BlockSpec(memory_s...]
  transfers between devices with their start and end apart: 17 -> 13, of which waited for: 9 -> 8; matrix products, arithmetic and copies ran while one was open for 2% -> 2% of each run, Pallas kernels for 10% -> 8%
where the time goes in v15:
time: 52.8 us; the launch traced here: 52.6 us
  waiting for transfers between devices  23.1 us (44%)
  starting transfers between devices  14.8 us (28%)
  Pallas kernels  12.8 us (24%)
  other arithmetic  0.88 us (2%)
  local copies, waits for them, and re-layouts  0.82 us (2%)
    ppermute x11, waiting for transfers between devices, swapped(): lax.ppermute(block, axis, [(i, i ^ bit) for i in range(lax.axis_size(axis...  23.1 us
    ppermute x11, starting transfers between devices, swapped(): lax.ppermute(block, axis, [(i, i ^ bit) for i in range(lax.axis_size(axis...  13.5 us
    pallas_call x10, Pallas kernels, vmem_call(): pl.pallas_call(body, out_shape=out_shape, in_specs=[pl.BlockSpec(memory_s...  12.8 us
    ppermute x2, starting transfers between devices, gathered(): lax.ppermute(tail, ('seq', 'head'), rim_route(target))  1.32 us
  transfers between devices with their start and end apart: 13, of which 8 were waited for; matrix products, arithmetic and copies ran while one was open for 2% of the time, Pallas kernels for 8%

profile of v15, /device:TPU:0, one launch (start us, length us, event | category | flops | bytes accessed | tf_op | source)
XLA Modules:
  0.0 52.6 jit_solution(2070060113719055380)
XLA Ops:
  0.0 2.9 %collective-permute-start = (bf16[64,2304]{1,0:T(8,128)(2,1)}, bf16[64,2304]{1,0:T(8,128)(2,1)S(1)}, u32[]{:S(2)}, u32[]{:S(2)}) collective-permute-start(bf16[64,2304]{1,0:T(8,128)(2,1)} %hidden_ref.1), channel_id=1, source_target_pairs={{0,2},{1,3},{2,0},{3,1},{4,6},{5,7},{6,4},{7,5},{8,10},{9,11},{10,... | collective-permute-start | bytes 884744 | tf_op jit(solution)/shard_map/ppermute | solution.py:24
  2.9 0.8 %slice.3 = bf16[8,2304]{1,0:T(8,128)(2,1)S(1)} slice(bf16[64,2304]{1,0:T(8,128)(2,1)} %hidden_ref.1), slice={[56:64], [0:2304]} | slice | bytes 73728 | tf_op jit(solution)/shard_map/slice | solution.py:54
  3.7 0.7 %collective-permute-start.2 = (bf16[8,2304]{1,0:T(8,128)(2,1)S(1)}, bf16[8,2304]{1,0:T(8,128)(2,1)S(1)}, u32[]{:S(2)}, u32[]{:S(2)}) collective-permute-start(bf16[8,2304]{1,0:T(8,128)(2,1)S(1)} %slice.3), channel_id=1, source_target_pairs={{3,5},{7,9},{11,13},{15,17},{19,21},{23,25},{27,29}} | collective-permute-start | bytes 110600 | tf_op jit(solution)/shard_map/ppermute | solution.py:56
  4.4 0.7 %collective-permute-start.1 = (bf16[8,2304]{1,0:T(8,128)(2,1)S(1)}, bf16[8,2304]{1,0:T(8,128)(2,1)S(1)}, u32[]{:S(2)}, u32[]{:S(2)}) collective-permute-start(bf16[8,2304]{1,0:T(8,128)(2,1)S(1)} %slice.3), channel_id=1, source_target_pairs={{3,6},{7,10},{11,14},{15,18},{19,22},{23,26},{27,30}} | collective-permute-start | bytes 110600 | tf_op jit(solution)/shard_map/ppermute | solution.py:56
  5.1 0.1 collective-permute-start.4
  5.2 2.7 %shard_map.118 = (bf16[64,2304]{1,0:T(8,128)(2,1)S(1)}, bf16[2,2304,512]{2,1,0:T(8,128)(2,1)S(1)}, bf16[2304,256]{1,0:T(8,128)(2,1)S(1)}) custom-call(bf16[64,2304]{1,0:T(8,128)(2,1)} %hidden_ref.1, bf16[2304,128]{1,0:T(8,128)(2,1)} %decay_down_ref.1, bf16[4,2304]{1,0:T(4,128)(2,1)} %bitcast.8, bf16[3,2304,512]{2,1,0:T(8,128)(2,1)} %bitcast.6), custom_call_target="tpu_custom_call" | custom-call | tf_op jit(solution)/shard_map/pallas_call | solution.py:74
  7.9 0.0 collective-permute-done.2.refs_1_
  7.9 0.0 collective-permute-done.1.refs_0_
  7.9 2.6 %collective-permute-done.refs_3_ = bf16[64,2304]{1,0:T(8,128)(2,1)S(1)} collective-permute-done((bf16[64,2304]{1,0:T(8,128)(2,1)}, bf16[64,2304]{1,0:T(8,128)(2,1)S(1)}, u32[]{:S(2)}, u32[]{:S(2)}) %collective-permute-start) | collective-permute-done | bytes 294944 | tf_op jit(solution)/shard_map/ppermute | solution.py:24
  10.6 0.0 collective-permute-start.5
  10.6 0.6 %collective-permute-start.3 = (bf16[16,2304]{1,0:T(8,128)(2,1)S(1)}, bf16[16,2304]{1,0:T(8,128)(2,1)S(1)}, u32[]{:S(2)}, u32[]{:S(2)}) collective-permute-start(bf16[16,2304]{1,0:T(8,128)(2,1)S(1)} %shard_map.119.refs_0_), channel_id=1, source_target_pairs={{0,1},{1,0},{2,3},{3,2},{4,5},{5,4},{6,7},{7,6},{8,9},{9,8},{10,11... | collective-permute-start | bytes 221192 | tf_op jit(solution)/shard_map/ppermute | solution.py:24
  11.1 0.0 collective-permute-done.4.refs_2_
  11.1 1.1 %collective-permute-done.3.refs_1_ = bf16[16,2304]{1,0:T(8,128)(2,1)S(1)} collective-permute-done((bf16[16,2304]{1,0:T(8,128)(2,1)S(1)}, bf16[16,2304]{1,0:T(8,128)(2,1)S(1)}, u32[]{:S(2)}, u32[]{:S(2)}) %collective-permute-start.3) | collective-permute-done | bytes 73760 | tf_op jit(solution)/shard_map/ppermute | solution.py:24
  12.2 0.0 collective-permute-done.5.refs_4_
  12.2 0.0 copy-start.1
  12.2 0.0 copy-start.2
  12.2 7.1 %shard_map.120 = (bf16[2,128,256]{2,1,0:T(8,128)(2,1)S(1)}, bf16[2,128,256]{2,1,0:T(8,128)(2,1)S(1)}, bf16[4,256,256]{2,1,0:T(8,128)(2,1)S(1)}, bf16[4,256,256]{...) custom-call(bf16[16,2304]{1,0:T(8,128)(2,1)S(1)} %shard_map.119.refs_0_, ...), custom_call_target="tpu_custom_call" | custom-call | flops 2415919104 | bytes 9437184 | tf_op jit(solution)/shard_map/pallas_call | solution.py:74
  19.3 1.4 %collective-permute-start.6 = (bf16[2,128,256]{2,1,0:T(8,128)(2,1)S(1)}, bf16[2,128,256]{2,1,0:T(8,128)(2,1)S(1)}, u32[]{:S(2)}, u32[]{:S(2)}) collective-permute-start(bf16[2,128,256]{2,1,0:T(8,128)(2,1)S(1)} %get-tuple-element.39), channel_id=1, source_target_pairs={{0,4},{4,0},{8,12},{12,8},{16,20},{20,16},{24,28},{28,24},{1,5},{5... | collective-permute-start | bytes 393224 | tf_op jit(solution)/shard_map/ppermute | solution.py:24
  20.7 4.2 %collective-permute-done.6.far_ref.partner_ref = bf16[2,128,256]{2,1,0:T(8,128)(2,1)S(1)} collective-permute-done((bf16[2,128,256]{2,1,0:T(8,128)(2,1)S(1)}, bf16[2,128,256]{2,1,0:T(8,128)(2,1)S(1)}, u32[]{:S(2)}, u32[]{:S(2)}) %collective-permute-start.6) | collective-permute-done | bytes 131104 | tf_op jit(solution)/shard_map/ppermute | solution.py:24
  24.9 0.0 copy-start
  24.9 0.0 copy-start.3
  24.9 0.2 shard_map.121.own_ref
  25.1 1.9 %collective-permute-start.7 = (bf16[2,128,256]{2,1,0:T(8,128)(2,1)S(1)}, bf16[2,128,256]{2,1,0:T(8,128)(2,1)S(1)}, u32[]{:S(2)}, u32[]{:S(2)}) collective-permute-start(bf16[2,128,256]{2,1,0:T(8,128)(2,1)S(1)} %shard_map.121.own_ref), channel_id=1, source_target_pairs={{0,8},{4,12},{8,0},{12,4},{16,24},{20,28},{24,16},{28,20},{1,9},{5... | collective-permute-start | bytes 393224 | tf_op jit(solution)/shard_map/ppermute | solution.py:24
  27.0 3.1 %collective-permute-done.7.far_ref = bf16[2,128,256]{2,1,0:T(8,128)(2,1)S(1)} collective-permute-done((bf16[2,128,256]{2,1,0:T(8,128)(2,1)S(1)}, bf16[2,128,256]{2,1,0:T(8,128)(2,1)S(1)}, u32[]{:S(2)}, u32[]{:S(2)}) %collective-permute-start.7) | collective-permute-done | bytes 131104 | tf_op jit(solution)/shard_map/ppermute | solution.py:24
  30.2 0.2 shard_map.123
  30.4 2.9 %collective-permute-start.8 = (bf16[2,128,128]{2,1,0:T(8,128)(2,1)S(1)}, bf16[2,128,128]{2,1,0:T(8,128)(2,1)S(1)}, u32[]{:S(2)}, u32[]{:S(2)}) collective-permute-start(bf16[2,128,128]{2,1,0:T(8,128)(2,1)S(1)} %shard_map.123), channel_id=1, source_target_pairs={{0,16},{4,20},{8,24},{12,28},{16,0},{20,4},{24,8},{28,12},{1,17},{... | collective-permute-start | bytes 196616 | tf_op jit(solution)/shard_map/ppermute | solution.py:24
  33.3 2.3 %collective-permute-done.8.far_ref = bf16[2,128,128]{2,1,0:T(8,128)(2,1)S(1)} collective-permute-done((bf16[2,128,128]{2,1,0:T(8,128)(2,1)S(1)}, bf16[2,128,128]{2,1,0:T(8,128)(2,1)S(1)}, u32[]{:S(2)}, u32[]{:S(2)}) %collective-permute-start.8) | collective-permute-done | bytes 65568 | tf_op jit(solution)/shard_map/ppermute | solution.py:24
  35.6 0.3 shard_map.124
  35.9 1.5 %collective-permute-start.9 = (bf16[2,128,128]{2,1,0:T(8,128)(2,1)S(1)}, bf16[2,128,128]{2,1,0:T(8,128)(2,1)S(1)}, u32[]{:S(2)}, u32[]{:S(2)}) collective-permute-start(bf16[2,128,128]{2,1,0:T(8,128)(2,1)S(1)} %get-tuple-element.41), channel_id=1, source_target_pairs={{0,4},{4,0},{8,12},{12,8},{16,20},{20,16},{24,28},{28,24},{1,5},{5... | collective-permute-start | bytes 196616 | tf_op jit(solution)/shard_map/ppermute | solution.py:24
  37.4 0.0 copy-done.1
  37.4 0.0 copy-done.2
  37.4 0.8 %shard_map.125 = (bf16[4,256,128]{2,1,0:T(8,128)(2,1)S(1)}, f32[256,512]{1,0:T(8,128)S(1)}, f32[256,512]{1,0:T(8,128)S(1)}) custom-call(bf16[4,256,256]{2,1,0:T(8,128)(2,1)S(1)} %get-tuple-element.42.attend_ref, bf16[4,256,256]{2,1,0:T(8,128)(2,1)S(1)} %get-tuple-element.43.solved_ref, bf16[4,256,128]{2,1,0:T(8,128)(2,1)S(1)} %get-tuple-element.44.start_ref, ...), custom_call_target="tpu_custom_call" | custom-call | flops 134217728 | bytes 1048576 | tf_op jit(solution)/shard_map/pallas_call | solution.py:74
  38.2 2.0 %collective-permute-done.9.refs_1_ = bf16[2,128,128]{2,1,0:T(8,128)(2,1)S(1)} collective-permute-done((bf16[2,128,128]{2,1,0:T(8,128)(2,1)S(1)}, bf16[2,128,128]{2,1,0:T(8,128)(2,1)S(1)}, u32[]{:S(2)}, u32[]{:S(2)}) %collective-permute-start.9) | collective-permute-done | bytes 65568 | tf_op jit(solution)/shard_map/ppermute | solution.py:24
  40.2 0.0 copy-done
  40.2 0.0 copy-done.3
  40.2 0.7 %shard_map.127 = (f32[64,2304]{1,0:T(8,128)S(1)}, bf16[64,2304]{1,0:T(8,128)(2,1)S(1)}) custom-call(bf16[2,128,128]{2,1,0:T(8,128)(2,1)S(1)} %get-tuple-element.40.refs_0_, bf16[2,128,128]{2,1,0:T(8,128)(2,1)S(1)} %collective-permute-done.9.refs_1_, bf16[4,256,128]{2,1,0:T(8,128)(2,1)S(1)} %get-tuple-element.46.refs_2_, ...), custom_call_target="tpu_custom_call" | custom-call | flops 301989888 | bytes 2359296 | tf_op jit(solution)/shard_map/pallas_call | solution.py:74
  41.0 0.1 collective-permute-start.11
  41.1 0.7 %shard_map.126 = (f32[64,2304]{1,0:T(8,128)S(1)}, bf16[64,2304]{1,0:T(8,128)(2,1)S(1)}) custom-call(bf16[2,128,128]{2,1,0:T(8,128)(2,1)S(1)} %get-tuple-element.40.refs_0_, bf16[2,128,128]{2,1,0:T(8,128)(2,1)S(1)} %collective-permute-done.9.refs_1_, bf16[4,256,128]{2,1,0:T(8,128)(2,1)S(1)} %get-tuple-element.46.refs_2_, ...), custom_call_target="tpu_custom_call" | custom-call | flops 301989888 | bytes 2359296 | tf_op jit(solution)/shard_map/pallas_call | solution.py:74
  41.8 0.5 %collective-permute-start.10 = (bf16[64,2304]{1,0:T(8,128)(2,1)S(1)}, bf16[64,2304]{1,0:T(8,128)(2,1)S(1)}, u32[]{:S(2)}, u32[]{:S(2)}) collective-permute-start(bf16[64,2304]{1,0:T(8,128)(2,1)S(1)} %get-tuple-element.50), channel_id=1, source_target_pairs={{0,1},{1,0},{2,3},{3,2},{4,5},{5,4},{6,7},{7,6},{8,9},{9,8},{10,11... | collective-permute-start | bytes 884744 | tf_op jit(solution)/shard_map/ppermute | solution.py:24
  42.4 0.3 collective-permute-done.11
  42.6 0.1 convert_add_fusion
  42.7 1.6 %collective-permute-start.12 = (bf16[64,2304]{1,0:T(8,128)(2,1)S(1)}, bf16[64,2304]{1,0:T(8,128)(2,1)S(1)}, u32[]{:S(2)}, u32[]{:S(2)}) collective-permute-start(bf16[64,2304]{1,0:T(8,128)(2,1)S(1)} %convert_add_fusion), channel_id=1, source_target_pairs={{0,2},{1,3},{2,0},{3,1},{4,6},{5,7},{6,4},{7,5},{8,10},{9,11},{10,... | collective-permute-start | bytes 884744 | tf_op jit(solution)/shard_map/ppermute | solution.py:24
  44.3 0.0 collective-permute-done.10
  44.3 0.1 convert_add_fusion.1
  44.4 7.5 %collective-permute-done.12 = bf16[64,2304]{1,0:T(8,128)(2,1)S(1)} collective-permute-done((bf16[64,2304]{1,0:T(8,128)(2,1)S(1)}, bf16[64,2304]{1,0:T(8,128)(2,1)S(1)}, u32[]{:S(2)}, u32[]{:S(2)}) %collective-permute-start.12) | collective-permute-done | bytes 294944 | tf_op jit(solution)/shard_map/ppermute | solution.py:24
  51.8 0.8 %add_convert_fusion = bf16[64,2304]{1,0:T(8,128)(2,1)} fusion(f32[64,2304]{1,0:T(8,128)S(1)} %convert_add_fusion.1, bf16[64,2304]{1,0:T(8,128)(2,1)S(1)} %collective-permute-done.12), kind=kLoop, calls=%fused_computation | loop fusion | flops 442368 | bytes 1179648 | tf_op jit(solution)/shard_map/convert_element_type | solution.py:582
  (2 shorter events, 0.1 us)
Async XLA Ops:
  0.0 10.5 %collective-permute-start = (bf16[64,2304]{1,0:T(8,128)(2,1)}, bf16[64,2304]{1,0:T(8,128)(2,1)S(1)}, u32[]{:S(2)}, u32[]{:S(2)}) collective-permute-start(bf16[64,2304]{1,0:T(8,128)(2,1)} %hidden_ref.1), channel_id=1, source_target_pairs={{0,2},{1,3},{2,0},{3,1},{4,6},{5,7},{6,4},{7,5},{8,10},{9,11},{10,... | collective-permute-start | bytes 884744 | tf_op jit(solution)/shard_map/ppermute | solution.py:24
  3.7 4.2 %collective-permute-start.2 = (bf16[8,2304]{1,0:T(8,128)(2,1)S(1)}, bf16[8,2304]{1,0:T(8,128)(2,1)S(1)}, u32[]{:S(2)}, u32[]{:S(2)}) collective-permute-start(bf16[8,2304]{1,0:T(8,128)(2,1)S(1)} %slice.3), channel_id=1, source_target_pairs={{3,5},{7,9},{11,13},{15,17},{19,21},{23,25},{27,29}} | collective-permute-start | bytes 110600 | tf_op jit(solution)/shard_map/ppermute | solution.py:56
  4.4 3.5 %collective-permute-start.1 = (bf16[8,2304]{1,0:T(8,128)(2,1)S(1)}, bf16[8,2304]{1,0:T(8,128)(2,1)S(1)}, u32[]{:S(2)}, u32[]{:S(2)}) collective-permute-start(bf16[8,2304]{1,0:T(8,128)(2,1)S(1)} %slice.3), channel_id=1, source_target_pairs={{3,6},{7,10},{11,14},{15,18},{19,22},{23,26},{27,30}} | collective-permute-start | bytes 110600 | tf_op jit(solution)/shard_map/ppermute | solution.py:56
  5.1 6.1 %collective-permute-start.4 = (bf16[64,2304]{1,0:T(8,128)(2,1)}, bf16[64,2304]{1,0:T(8,128)(2,1)S(1)}, u32[]{:S(2)}, u32[]{:S(2)}) collective-permute-start(bf16[64,2304]{1,0:T(8,128)(2,1)} %hidden_ref.1), channel_id=1, source_target_pairs={{0,1},{1,0},{2,3},{3,2},{4,5},{5,4},{6,7},{7,6},{8,9},{9,8},{10,11... | collective-permute-start | bytes 884744 | tf_op jit(solution)/shard_map/ppermute | solution.py:24
  10.6 1.7 %collective-permute-start.5 = (bf16[64,2304]{1,0:T(8,128)(2,1)S(1)}, bf16[64,2304]{1,0:T(8,128)(2,1)S(1)}, u32[]{:S(2)}, u32[]{:S(2)}) collective-permute-start(bf16[64,2304]{1,0:T(8,128)(2,1)S(1)} %collective-permute-done.refs_3_), channel_id=1, source_target_pairs={{0,1},{1,0},{2,3},{3,2},{4,5},{5,4},{6,7},{7,6},{8,9},{9,8},{10,11... | collective-permute-start | bytes 884744 | tf_op jit(solution)/shard_map/ppermute | solution.py:24
  10.6 1.7 %collective-permute-start.3 = (bf16[16,2304]{1,0:T(8,128)(2,1)S(1)}, bf16[16,2304]{1,0:T(8,128)(2,1)S(1)}, u32[]{:S(2)}, u32[]{:S(2)}) collective-permute-start(bf16[16,2304]{1,0:T(8,128)(2,1)S(1)} %shard_map.119.refs_0_), channel_id=1, source_target_pairs={{0,1},{1,0},{2,3},{3,2},{4,5},{5,4},{6,7},{7,6},{8,9},{9,8},{10,11... | collective-permute-start | bytes 221192 | tf_op jit(solution)/shard_map/ppermute | solution.py:24
  12.2 25.2 %copy-start.1 = (bf16[2304,128]{1,0:T(8,128)(2,1)S(1)}, bf16[2304,128]{1,0:T(8,128)(2,1)}, u32[]{:S(2)}) copy-start(bf16[2304,128]{1,0:T(8,128)(2,1)} %down_ref.1) | copy-start | bytes 1769476
  12.2 25.2 %copy-start.2 = (bf16[128,512]{1,0:T(8,128)(2,1)S(1)}, bf16[128,512]{1,0:T(8,128)(2,1)}, u32[]{:S(2)}) copy-start(bf16[128,512]{1,0:T(8,128)(2,1)} %up_ref.1) | copy-start | bytes 393220
  19.3 5.6 %collective-permute-start.6 = (bf16[2,128,256]{2,1,0:T(8,128)(2,1)S(1)}, bf16[2,128,256]{2,1,0:T(8,128)(2,1)S(1)}, u32[]{:S(2)}, u32[]{:S(2)}) collective-permute-start(bf16[2,128,256]{2,1,0:T(8,128)(2,1)S(1)} %get-tuple-element.39), channel_id=1, source_target_pairs={{0,4},{4,0},{8,12},{12,8},{16,20},{20,16},{24,28},{28,24},{1,5},{5... | collective-permute-start | bytes 393224 | tf_op jit(solution)/shard_map/ppermute | solution.py:24
  24.9 15.3 %copy-start = (bf16[512,2304]{1,0:T(8,128)(2,1)S(1)}, bf16[512,2304]{1,0:T(8,128)(2,1)}, u32[]{:S(2)}) copy-start(bf16[512,2304]{1,0:T(8,128)(2,1)} %refs_6_.3) | copy-start | bytes 7077892
  24.9 15.3 %copy-start.3 = (f32[128]{0:T(128)S(1)}, f32[128]{0:T(128)}, u32[]{:S(2)}) copy-start(f32[128]{0:T(128)} %param.22) | copy-start | bytes 1540
  25.1 5.0 %collective-permute-start.7 = (bf16[2,128,256]{2,1,0:T(8,128)(2,1)S(1)}, bf16[2,128,256]{2,1,0:T(8,128)(2,1)S(1)}, u32[]{:S(2)}, u32[]{:S(2)}) collective-permute-start(bf16[2,128,256]{2,1,0:T(8,128)(2,1)S(1)} %shard_map.121.own_ref), channel_id=1, source_target_pairs={{0,8},{4,12},{8,0},{12,4},{16,24},{20,28},{24,16},{28,20},{1,9},{5... | collective-permute-start | bytes 393224 | tf_op jit(solution)/shard_map/ppermute | solution.py:24
  30.4 5.2 %collective-permute-start.8 = (bf16[2,128,128]{2,1,0:T(8,128)(2,1)S(1)}, bf16[2,128,128]{2,1,0:T(8,128)(2,1)S(1)}, u32[]{:S(2)}, u32[]{:S(2)}) collective-permute-start(bf16[2,128,128]{2,1,0:T(8,128)(2,1)S(1)} %shard_map.123), channel_id=1, source_target_pairs={{0,16},{4,20},{8,24},{12,28},{16,0},{20,4},{24,8},{28,12},{1,17},{... | collective-permute-start | bytes 196616 | tf_op jit(solution)/shard_map/ppermute | solution.py:24
  35.9 4.3 %collective-permute-start.9 = (bf16[2,128,128]{2,1,0:T(8,128)(2,1)S(1)}, bf16[2,128,128]{2,1,0:T(8,128)(2,1)S(1)}, u32[]{:S(2)}, u32[]{:S(2)}) collective-permute-start(bf16[2,128,128]{2,1,0:T(8,128)(2,1)S(1)} %get-tuple-element.41), channel_id=1, source_target_pairs={{0,4},{4,0},{8,12},{12,8},{16,20},{20,16},{24,28},{28,24},{1,5},{5... | collective-permute-start | bytes 196616 | tf_op jit(solution)/shard_map/ppermute | solution.py:24
  41.0 1.6 %collective-permute-start.11 = (bf16[64,2304]{1,0:T(8,128)(2,1)S(1)}, bf16[64,2304]{1,0:T(8,128)(2,1)S(1)}, u32[]{:S(2)}, u32[]{:S(2)}) collective-permute-start(bf16[64,2304]{1,0:T(8,128)(2,1)S(1)} %get-tuple-element.52), channel_id=1, source_target_pairs={{0,1},{1,0},{2,3},{3,2},{4,5},{5,4},{6,7},{7,6},{8,9},{9,8},{10,11... | collective-permute-start | bytes 884744 | tf_op jit(solution)/shard_map/ppermute | solution.py:24
  41.8 2.5 %collective-permute-start.10 = (bf16[64,2304]{1,0:T(8,128)(2,1)S(1)}, bf16[64,2304]{1,0:T(8,128)(2,1)S(1)}, u32[]{:S(2)}, u32[]{:S(2)}) collective-permute-start(bf16[64,2304]{1,0:T(8,128)(2,1)S(1)} %get-tuple-element.50), channel_id=1, source_target_pairs={{0,1},{1,0},{2,3},{3,2},{4,5},{5,4},{6,7},{7,6},{8,9},{9,8},{10,11... | collective-permute-start | bytes 884744 | tf_op jit(solution)/shard_map/ppermute | solution.py:24
  42.7 9.1 %collective-permute-start.12 = (bf16[64,2304]{1,0:T(8,128)(2,1)S(1)}, bf16[64,2304]{1,0:T(8,128)(2,1)S(1)}, u32[]{:S(2)}, u32[]{:S(2)}) collective-permute-start(bf16[64,2304]{1,0:T(8,128)(2,1)S(1)} %convert_add_fusion), channel_id=1, source_target_pairs={{0,2},{1,3},{2,0},{3,1},{4,6},{5,7},{6,4},{7,5},{8,10},{9,11},{10,... | collective-permute-start | bytes 884744 | tf_op jit(solution)/shard_map/ppermute | solution.py:24

commit v16 on v15

--- a/solution.py
+++ b/solution.py
@@ -88,7 +88,7 @@
 
 
 def column_pieces(width):
-    step = math.gcd(width, 256)
+    step = math.gcd(width, 512)
     return [slice(i, i + step) for i in range(0, width, step)]
 
 

time: 52.8 us -> 52.7 us (level)
  no operation moved by 1% of the time
where the time goes in v16:
time: 52.7 us; the launch traced here: 52.5 us
  waiting for transfers between devices  23.1 us (44%)
  starting transfers between devices  14.9 us (28%)
  Pallas kernels  12.7 us (24%)
  other arithmetic  0.88 us (2%)
  local copies, waits for them, and re-layouts  0.82 us (2%)
    ppermute x11, waiting for transfers between devices, swapped(): lax.ppermute(block, axis, [(i, i ^ bit) for i in range(lax.axis_size(axis...  23.1 us
    ppermute x11, starting transfers between devices, swapped(): lax.ppermute(block, axis, [(i, i ^ bit) for i in range(lax.axis_size(axis...  13.6 us
    pallas_call x10, Pallas kernels, vmem_call(): pl.pallas_call(body, out_shape=out_shape, in_specs=[pl.BlockSpec(memory_s...  12.7 us
    ppermute x2, starting transfers between devices, gathered(): lax.ppermute(tail, ('seq', 'head'), rim_route(target))  1.32 us
  transfers between devices with their start and end apart: 13, of which 8 were waited for; matrix products, arithmetic and copies ran while one was open for 2% of the time, Pallas kernels for 8%

profile of v16, /device:TPU:0, one launch (start us, length us, event | category | flops | bytes accessed | tf_op | source)
XLA Modules:
  0.0 52.5 jit_solution(6247771467864383574)
XLA Ops:
  0.0 2.9 %collective-permute-start = (bf16[64,2304]{1,0:T(8,128)(2,1)}, bf16[64,2304]{1,0:T(8,128)(2,1)S(1)}, u32[]{:S(2)}, u32[]{:S(2)}) collective-permute-start(bf16[64,2304]{1,0:T(8,128)(2,1)} %hidden_ref.1), channel_id=1, source_target_pairs={{0,2},{1,3},{2,0},{3,1},{4,6},{5,7},{6,4},{7,5},{8,10},{9,11},{10,... | collective-permute-start | bytes 884744 | tf_op jit(solution)/shard_map/ppermute | solution.py:24
  2.9 0.8 %slice.3 = bf16[8,2304]{1,0:T(8,128)(2,1)S(1)} slice(bf16[64,2304]{1,0:T(8,128)(2,1)} %hidden_ref.1), slice={[56:64], [0:2304]} | slice | bytes 73728 | tf_op jit(solution)/shard_map/slice | solution.py:54
  3.7 0.7 %collective-permute-start.2 = (bf16[8,2304]{1,0:T(8,128)(2,1)S(1)}, bf16[8,2304]{1,0:T(8,128)(2,1)S(1)}, u32[]{:S(2)}, u32[]{:S(2)}) collective-permute-start(bf16[8,2304]{1,0:T(8,128)(2,1)S(1)} %slice.3), channel_id=1, source_target_pairs={{3,5},{7,9},{11,13},{15,17},{19,21},{23,25},{27,29}} | collective-permute-start | bytes 110600 | tf_op jit(solution)/shard_map/ppermute | solution.py:56
  4.4 0.7 %collective-permute-start.1 = (bf16[8,2304]{1,0:T(8,128)(2,1)S(1)}, bf16[8,2304]{1,0:T(8,128)(2,1)S(1)}, u32[]{:S(2)}, u32[]{:S(2)}) collective-permute-start(bf16[8,2304]{1,0:T(8,128)(2,1)S(1)} %slice.3), channel_id=1, source_target_pairs={{3,6},{7,10},{11,14},{15,18},{19,22},{23,26},{27,30}} | collective-permute-start | bytes 110600 | tf_op jit(solution)/shard_map/ppermute | solution.py:56
  5.1 0.1 collective-permute-start.4
  5.2 2.7 %shard_map.118 = (bf16[64,2304]{1,0:T(8,128)(2,1)S(1)}, bf16[2,2304,512]{2,1,0:T(8,128)(2,1)S(1)}, bf16[2304,256]{1,0:T(8,128)(2,1)S(1)}) custom-call(bf16[64,2304]{1,0:T(8,128)(2,1)} %hidden_ref.1, bf16[2304,128]{1,0:T(8,128)(2,1)} %decay_down_ref.1, bf16[4,2304]{1,0:T(4,128)(2,1)} %bitcast.8, bf16[3,2304,512]{2,1,0:T(8,128)(2,1)} %bitcast.6), custom_call_target="tpu_custom_call" | custom-call | tf_op jit(solution)/shard_map/pallas_call | solution.py:74
  7.9 0.0 collective-permute-done.2.refs_1_
  7.9 0.0 collective-permute-done.1.refs_0_
  7.9 2.6 %collective-permute-done.refs_3_ = bf16[64,2304]{1,0:T(8,128)(2,1)S(1)} collective-permute-done((bf16[64,2304]{1,0:T(8,128)(2,1)}, bf16[64,2304]{1,0:T(8,128)(2,1)S(1)}, u32[]{:S(2)}, u32[]{:S(2)}) %collective-permute-start) | collective-permute-done | bytes 294944 | tf_op jit(solution)/shard_map/ppermute | solution.py:24
  10.6 0.0 collective-permute-start.5
  10.6 0.6 %collective-permute-start.3 = (bf16[16,2304]{1,0:T(8,128)(2,1)S(1)}, bf16[16,2304]{1,0:T(8,128)(2,1)S(1)}, u32[]{:S(2)}, u32[]{:S(2)}) collective-permute-start(bf16[16,2304]{1,0:T(8,128)(2,1)S(1)} %shard_map.119.refs_0_), channel_id=1, source_target_pairs={{0,1},{1,0},{2,3},{3,2},{4,5},{5,4},{6,7},{7,6},{8,9},{9,8},{10,11... | collective-permute-start | bytes 221192 | tf_op jit(solution)/shard_map/ppermute | solution.py:24
  11.1 0.0 collective-permute-done.4.refs_2_
  11.1 1.1 %collective-permute-done.3.refs_1_ = bf16[16,2304]{1,0:T(8,128)(2,1)S(1)} collective-permute-done((bf16[16,2304]{1,0:T(8,128)(2,1)S(1)}, bf16[16,2304]{1,0:T(8,128)(2,1)S(1)}, u32[]{:S(2)}, u32[]{:S(2)}) %collective-permute-start.3) | collective-permute-done | bytes 73760 | tf_op jit(solution)/shard_map/ppermute | solution.py:24
  12.2 0.0 collective-permute-done.5.refs_4_
  12.2 0.0 copy-start.1
  12.2 0.0 copy-start.2
  12.2 6.9 %shard_map.120 = (bf16[2,128,256]{2,1,0:T(8,128)(2,1)S(1)}, bf16[2,128,256]{2,1,0:T(8,128)(2,1)S(1)}, bf16[4,256,256]{2,1,0:T(8,128)(2,1)S(1)}, bf16[4,256,256]{...) custom-call(bf16[16,2304]{1,0:T(8,128)(2,1)S(1)} %shard_map.119.refs_0_, ...), custom_call_target="tpu_custom_call" | custom-call | flops 2415919104 | bytes 9437184 | tf_op jit(solution)/shard_map/pallas_call | solution.py:74
  19.2 1.4 %collective-permute-start.6 = (bf16[2,128,256]{2,1,0:T(8,128)(2,1)S(1)}, bf16[2,128,256]{2,1,0:T(8,128)(2,1)S(1)}, u32[]{:S(2)}, u32[]{:S(2)}) collective-permute-start(bf16[2,128,256]{2,1,0:T(8,128)(2,1)S(1)} %get-tuple-element.39), channel_id=1, source_target_pairs={{0,4},{4,0},{8,12},{12,8},{16,20},{20,16},{24,28},{28,24},{1,5},{5... | collective-permute-start | bytes 393224 | tf_op jit(solution)/shard_map/ppermute | solution.py:24
  20.6 4.2 %collective-permute-done.6.far_ref.partner_ref = bf16[2,128,256]{2,1,0:T(8,128)(2,1)S(1)} collective-permute-done((bf16[2,128,256]{2,1,0:T(8,128)(2,1)S(1)}, bf16[2,128,256]{2,1,0:T(8,128)(2,1)S(1)}, u32[]{:S(2)}, u32[]{:S(2)}) %collective-permute-start.6) | collective-permute-done | bytes 131104 | tf_op jit(solution)/shard_map/ppermute | solution.py:24
  24.8 0.0 copy-start
  24.8 0.0 copy-start.3
  24.8 0.2 shard_map.121.own_ref
  25.0 1.9 %collective-permute-start.7 = (bf16[2,128,256]{2,1,0:T(8,128)(2,1)S(1)}, bf16[2,128,256]{2,1,0:T(8,128)(2,1)S(1)}, u32[]{:S(2)}, u32[]{:S(2)}) collective-permute-start(bf16[2,128,256]{2,1,0:T(8,128)(2,1)S(1)} %shard_map.121.own_ref), channel_id=1, source_target_pairs={{0,8},{4,12},{8,0},{12,4},{16,24},{20,28},{24,16},{28,20},{1,9},{5... | collective-permute-start | bytes 393224 | tf_op jit(solution)/shard_map/ppermute | solution.py:24
  26.9 3.1 %collective-permute-done.7.far_ref = bf16[2,128,256]{2,1,0:T(8,128)(2,1)S(1)} collective-permute-done((bf16[2,128,256]{2,1,0:T(8,128)(2,1)S(1)}, bf16[2,128,256]{2,1,0:T(8,128)(2,1)S(1)}, u32[]{:S(2)}, u32[]{:S(2)}) %collective-permute-start.7) | collective-permute-done | bytes 131104 | tf_op jit(solution)/shard_map/ppermute | solution.py:24
  30.1 0.2 shard_map.123
  30.3 2.9 %collective-permute-start.8 = (bf16[2,128,128]{2,1,0:T(8,128)(2,1)S(1)}, bf16[2,128,128]{2,1,0:T(8,128)(2,1)S(1)}, u32[]{:S(2)}, u32[]{:S(2)}) collective-permute-start(bf16[2,128,128]{2,1,0:T(8,128)(2,1)S(1)} %shard_map.123), channel_id=1, source_target_pairs={{0,16},{4,20},{8,24},{12,28},{16,0},{20,4},{24,8},{28,12},{1,17},{... | collective-permute-start | bytes 196616 | tf_op jit(solution)/shard_map/ppermute | solution.py:24
  33.2 2.3 %collective-permute-done.8.far_ref = bf16[2,128,128]{2,1,0:T(8,128)(2,1)S(1)} collective-permute-done((bf16[2,128,128]{2,1,0:T(8,128)(2,1)S(1)}, bf16[2,128,128]{2,1,0:T(8,128)(2,1)S(1)}, u32[]{:S(2)}, u32[]{:S(2)}) %collective-permute-start.8) | collective-permute-done | bytes 65568 | tf_op jit(solution)/shard_map/ppermute | solution.py:24
  35.5 0.3 shard_map.124
  35.8 1.5 %collective-permute-start.9 = (bf16[2,128,128]{2,1,0:T(8,128)(2,1)S(1)}, bf16[2,128,128]{2,1,0:T(8,128)(2,1)S(1)}, u32[]{:S(2)}, u32[]{:S(2)}) collective-permute-start(bf16[2,128,128]{2,1,0:T(8,128)(2,1)S(1)} %get-tuple-element.41), channel_id=1, source_target_pairs={{0,4},{4,0},{8,12},{12,8},{16,20},{20,16},{24,28},{28,24},{1,5},{5... | collective-permute-start | bytes 196616 | tf_op jit(solution)/shard_map/ppermute | solution.py:24
  37.3 0.0 copy-done.1
  37.3 0.0 copy-done.2
  37.3 0.8 %shard_map.125 = (bf16[4,256,128]{2,1,0:T(8,128)(2,1)S(1)}, f32[256,512]{1,0:T(8,128)S(1)}, f32[256,512]{1,0:T(8,128)S(1)}) custom-call(bf16[4,256,256]{2,1,0:T(8,128)(2,1)S(1)} %get-tuple-element.42.attend_ref, bf16[4,256,256]{2,1,0:T(8,128)(2,1)S(1)} %get-tuple-element.43.solved_ref, bf16[4,256,128]{2,1,0:T(8,128)(2,1)S(1)} %get-tuple-element.44.start_ref, ...), custom_call_target="tpu_custom_call" | custom-call | flops 134217728 | bytes 1048576 | tf_op jit(solution)/shard_map/pallas_call | solution.py:74
  38.1 2.0 %collective-permute-done.9.refs_1_ = bf16[2,128,128]{2,1,0:T(8,128)(2,1)S(1)} collective-permute-done((bf16[2,128,128]{2,1,0:T(8,128)(2,1)S(1)}, bf16[2,128,128]{2,1,0:T(8,128)(2,1)S(1)}, u32[]{:S(2)}, u32[]{:S(2)}) %collective-permute-start.9) | collective-permute-done | bytes 65568 | tf_op jit(solution)/shard_map/ppermute | solution.py:24
  40.1 0.0 copy-done
  40.1 0.0 copy-done.3
  40.1 0.7 %shard_map.127 = (f32[64,2304]{1,0:T(8,128)S(1)}, bf16[64,2304]{1,0:T(8,128)(2,1)S(1)}) custom-call(bf16[2,128,128]{2,1,0:T(8,128)(2,1)S(1)} %get-tuple-element.40.refs_0_, bf16[2,128,128]{2,1,0:T(8,128)(2,1)S(1)} %collective-permute-done.9.refs_1_, bf16[4,256,128]{2,1,0:T(8,128)(2,1)S(1)} %get-tuple-element.46.refs_2_, ...), custom_call_target="tpu_custom_call" | custom-call | flops 301989888 | bytes 2359296 | tf_op jit(solution)/shard_map/pallas_call | solution.py:74
  40.9 0.1 collective-permute-start.11
  41.0 0.7 %shard_map.126 = (f32[64,2304]{1,0:T(8,128)S(1)}, bf16[64,2304]{1,0:T(8,128)(2,1)S(1)}) custom-call(bf16[2,128,128]{2,1,0:T(8,128)(2,1)S(1)} %get-tuple-element.40.refs_0_, bf16[2,128,128]{2,1,0:T(8,128)(2,1)S(1)} %collective-permute-done.9.refs_1_, bf16[4,256,128]{2,1,0:T(8,128)(2,1)S(1)} %get-tuple-element.46.refs_2_, ...), custom_call_target="tpu_custom_call" | custom-call | flops 301989888 | bytes 2359296 | tf_op jit(solution)/shard_map/pallas_call | solution.py:74
  41.7 0.5 %collective-permute-start.10 = (bf16[64,2304]{1,0:T(8,128)(2,1)S(1)}, bf16[64,2304]{1,0:T(8,128)(2,1)S(1)}, u32[]{:S(2)}, u32[]{:S(2)}) collective-permute-start(bf16[64,2304]{1,0:T(8,128)(2,1)S(1)} %get-tuple-element.50), channel_id=1, source_target_pairs={{0,1},{1,0},{2,3},{3,2},{4,5},{5,4},{6,7},{7,6},{8,9},{9,8},{10,11... | collective-permute-start | bytes 884744 | tf_op jit(solution)/shard_map/ppermute | solution.py:24
  42.3 0.3 collective-permute-done.11
  42.5 0.1 convert_add_fusion
  42.6 1.6 %collective-permute-start.12 = (bf16[64,2304]{1,0:T(8,128)(2,1)S(1)}, bf16[64,2304]{1,0:T(8,128)(2,1)S(1)}, u32[]{:S(2)}, u32[]{:S(2)}) collective-permute-start(bf16[64,2304]{1,0:T(8,128)(2,1)S(1)} %convert_add_fusion), channel_id=1, source_target_pairs={{0,2},{1,3},{2,0},{3,1},{4,6},{5,7},{6,4},{7,5},{8,10},{9,11},{10,... | collective-permute-start | bytes 884744 | tf_op jit(solution)/shard_map/ppermute | solution.py:24
  44.2 0.0 collective-permute-done.10
  44.2 0.1 convert_add_fusion.1
  44.3 7.5 %collective-permute-done.12 = bf16[64,2304]{1,0:T(8,128)(2,1)S(1)} collective-permute-done((bf16[64,2304]{1,0:T(8,128)(2,1)S(1)}, bf16[64,2304]{1,0:T(8,128)(2,1)S(1)}, u32[]{:S(2)}, u32[]{:S(2)}) %collective-permute-start.12) | collective-permute-done | bytes 294944 | tf_op jit(solution)/shard_map/ppermute | solution.py:24
  51.7 0.8 %add_convert_fusion = bf16[64,2304]{1,0:T(8,128)(2,1)} fusion(f32[64,2304]{1,0:T(8,128)S(1)} %convert_add_fusion.1, bf16[64,2304]{1,0:T(8,128)(2,1)S(1)} %collective-permute-done.12), kind=kLoop, calls=%fused_computation | loop fusion | flops 442368 | bytes 1179648 | tf_op jit(solution)/shard_map/convert_element_type | solution.py:582
  (2 shorter events, 0.1 us)
Async XLA Ops:
  0.0 10.5 %collective-permute-start = (bf16[64,2304]{1,0:T(8,128)(2,1)}, bf16[64,2304]{1,0:T(8,128)(2,1)S(1)}, u32[]{:S(2)}, u32[]{:S(2)}) collective-permute-start(bf16[64,2304]{1,0:T(8,128)(2,1)} %hidden_ref.1), channel_id=1, source_target_pairs={{0,2},{1,3},{2,0},{3,1},{4,6},{5,7},{6,4},{7,5},{8,10},{9,11},{10,... | collective-permute-start | bytes 884744 | tf_op jit(solution)/shard_map/ppermute | solution.py:24
  3.7 4.2 %collective-permute-start.2 = (bf16[8,2304]{1,0:T(8,128)(2,1)S(1)}, bf16[8,2304]{1,0:T(8,128)(2,1)S(1)}, u32[]{:S(2)}, u32[]{:S(2)}) collective-permute-start(bf16[8,2304]{1,0:T(8,128)(2,1)S(1)} %slice.3), channel_id=1, source_target_pairs={{3,5},{7,9},{11,13},{15,17},{19,21},{23,25},{27,29}} | collective-permute-start | bytes 110600 | tf_op jit(solution)/shard_map/ppermute | solution.py:56
  4.4 3.5 %collective-permute-start.1 = (bf16[8,2304]{1,0:T(8,128)(2,1)S(1)}, bf16[8,2304]{1,0:T(8,128)(2,1)S(1)}, u32[]{:S(2)}, u32[]{:S(2)}) collective-permute-start(bf16[8,2304]{1,0:T(8,128)(2,1)S(1)} %slice.3), channel_id=1, source_target_pairs={{3,6},{7,10},{11,14},{15,18},{19,22},{23,26},{27,30}} | collective-permute-start | bytes 110600 | tf_op jit(solution)/shard_map/ppermute | solution.py:56
  5.1 6.1 %collective-permute-start.4 = (bf16[64,2304]{1,0:T(8,128)(2,1)}, bf16[64,2304]{1,0:T(8,128)(2,1)S(1)}, u32[]{:S(2)}, u32[]{:S(2)}) collective-permute-start(bf16[64,2304]{1,0:T(8,128)(2,1)} %hidden_ref.1), channel_id=1, source_target_pairs={{0,1},{1,0},{2,3},{3,2},{4,5},{5,4},{6,7},{7,6},{8,9},{9,8},{10,11... | collective-permute-start | bytes 884744 | tf_op jit(solution)/shard_map/ppermute | solution.py:24
  10.6 1.7 %collective-permute-start.5 = (bf16[64,2304]{1,0:T(8,128)(2,1)S(1)}, bf16[64,2304]{1,0:T(8,128)(2,1)S(1)}, u32[]{:S(2)}, u32[]{:S(2)}) collective-permute-start(bf16[64,2304]{1,0:T(8,128)(2,1)S(1)} %collective-permute-done.refs_3_), channel_id=1, source_target_pairs={{0,1},{1,0},{2,3},{3,2},{4,5},{5,4},{6,7},{7,6},{8,9},{9,8},{10,11... | collective-permute-start | bytes 884744 | tf_op jit(solution)/shard_map/ppermute | solution.py:24
  10.6 1.7 %collective-permute-start.3 = (bf16[16,2304]{1,0:T(8,128)(2,1)S(1)}, bf16[16,2304]{1,0:T(8,128)(2,1)S(1)}, u32[]{:S(2)}, u32[]{:S(2)}) collective-permute-start(bf16[16,2304]{1,0:T(8,128)(2,1)S(1)} %shard_map.119.refs_0_), channel_id=1, source_target_pairs={{0,1},{1,0},{2,3},{3,2},{4,5},{5,4},{6,7},{7,6},{8,9},{9,8},{10,11... | collective-permute-start | bytes 221192 | tf_op jit(solution)/shard_map/ppermute | solution.py:24
  12.2 25.1 %copy-start.1 = (bf16[2304,128]{1,0:T(8,128)(2,1)S(1)}, bf16[2304,128]{1,0:T(8,128)(2,1)}, u32[]{:S(2)}) copy-start(bf16[2304,128]{1,0:T(8,128)(2,1)} %down_ref.1) | copy-start | bytes 1769476
  12.2 25.1 %copy-start.2 = (bf16[128,512]{1,0:T(8,128)(2,1)S(1)}, bf16[128,512]{1,0:T(8,128)(2,1)}, u32[]{:S(2)}) copy-start(bf16[128,512]{1,0:T(8,128)(2,1)} %up_ref.1) | copy-start | bytes 393220
  19.2 5.6 %collective-permute-start.6 = (bf16[2,128,256]{2,1,0:T(8,128)(2,1)S(1)}, bf16[2,128,256]{2,1,0:T(8,128)(2,1)S(1)}, u32[]{:S(2)}, u32[]{:S(2)}) collective-permute-start(bf16[2,128,256]{2,1,0:T(8,128)(2,1)S(1)} %get-tuple-element.39), channel_id=1, source_target_pairs={{0,4},{4,0},{8,12},{12,8},{16,20},{20,16},{24,28},{28,24},{1,5},{5... | collective-permute-start | bytes 393224 | tf_op jit(solution)/shard_map/ppermute | solution.py:24
  24.8 15.3 %copy-start = (bf16[512,2304]{1,0:T(8,128)(2,1)S(1)}, bf16[512,2304]{1,0:T(8,128)(2,1)}, u32[]{:S(2)}) copy-start(bf16[512,2304]{1,0:T(8,128)(2,1)} %refs_6_.3) | copy-start | bytes 7077892
  24.8 15.3 %copy-start.3 = (f32[128]{0:T(128)S(1)}, f32[128]{0:T(128)}, u32[]{:S(2)}) copy-start(f32[128]{0:T(128)} %param.22) | copy-start | bytes 1540
  25.0 5.0 %collective-permute-start.7 = (bf16[2,128,256]{2,1,0:T(8,128)(2,1)S(1)}, bf16[2,128,256]{2,1,0:T(8,128)(2,1)S(1)}, u32[]{:S(2)}, u32[]{:S(2)}) collective-permute-start(bf16[2,128,256]{2,1,0:T(8,128)(2,1)S(1)} %shard_map.121.own_ref), channel_id=1, source_target_pairs={{0,8},{4,12},{8,0},{12,4},{16,24},{20,28},{24,16},{28,20},{1,9},{5... | collective-permute-start | bytes 393224 | tf_op jit(solution)/shard_map/ppermute | solution.py:24
  30.3 5.2 %collective-permute-start.8 = (bf16[2,128,128]{2,1,0:T(8,128)(2,1)S(1)}, bf16[2,128,128]{2,1,0:T(8,128)(2,1)S(1)}, u32[]{:S(2)}, u32[]{:S(2)}) collective-permute-start(bf16[2,128,128]{2,1,0:T(8,128)(2,1)S(1)} %shard_map.123), channel_id=1, source_target_pairs={{0,16},{4,20},{8,24},{12,28},{16,0},{20,4},{24,8},{28,12},{1,17},{... | collective-permute-start | bytes 196616 | tf_op jit(solution)/shard_map/ppermute | solution.py:24
  35.8 4.3 %collective-permute-start.9 = (bf16[2,128,128]{2,1,0:T(8,128)(2,1)S(1)}, bf16[2,128,128]{2,1,0:T(8,128)(2,1)S(1)}, u32[]{:S(2)}, u32[]{:S(2)}) collective-permute-start(bf16[2,128,128]{2,1,0:T(8,128)(2,1)S(1)} %get-tuple-element.41), channel_id=1, source_target_pairs={{0,4},{4,0},{8,12},{12,8},{16,20},{20,16},{24,28},{28,24},{1,5},{5... | collective-permute-start | bytes 196616 | tf_op jit(solution)/shard_map/ppermute | solution.py:24
  40.9 1.6 %collective-permute-start.11 = (bf16[64,2304]{1,0:T(8,128)(2,1)S(1)}, bf16[64,2304]{1,0:T(8,128)(2,1)S(1)}, u32[]{:S(2)}, u32[]{:S(2)}) collective-permute-start(bf16[64,2304]{1,0:T(8,128)(2,1)S(1)} %get-tuple-element.52), channel_id=1, source_target_pairs={{0,1},{1,0},{2,3},{3,2},{4,5},{5,4},{6,7},{7,6},{8,9},{9,8},{10,11... | collective-permute-start | bytes 884744 | tf_op jit(solution)/shard_map/ppermute | solution.py:24
  41.7 2.5 %collective-permute-start.10 = (bf16[64,2304]{1,0:T(8,128)(2,1)S(1)}, bf16[64,2304]{1,0:T(8,128)(2,1)S(1)}, u32[]{:S(2)}, u32[]{:S(2)}) collective-permute-start(bf16[64,2304]{1,0:T(8,128)(2,1)S(1)} %get-tuple-element.50), channel_id=1, source_target_pairs={{0,1},{1,0},{2,3},{3,2},{4,5},{5,4},{6,7},{7,6},{8,9},{9,8},{10,11... | collective-permute-start | bytes 884744 | tf_op jit(solution)/shard_map/ppermute | solution.py:24
  42.6 9.1 %collective-permute-start.12 = (bf16[64,2304]{1,0:T(8,128)(2,1)S(1)}, bf16[64,2304]{1,0:T(8,128)(2,1)S(1)}, u32[]{:S(2)}, u32[]{:S(2)}) collective-permute-start(bf16[64,2304]{1,0:T(8,128)(2,1)S(1)} %convert_add_fusion), channel_id=1, source_target_pairs={{0,2},{1,3},{2,0},{3,1},{4,6},{5,7},{6,4},{7,5},{8,10},{9,11},{10,... | collective-permute-start | bytes 884744 | tf_op jit(solution)/shard_map/ppermute | solution.py:24
